TPU v7x, 32 devices: a whole 2x2x4 slice. The times are simulated.
32 devices in a mesh: grp: 4 (over y, core), box: 8 (over z, x).
Axes of the slice: x: 2, y: 2, z: 4, core: 2. Of those that a mesh axis runs over, the one named last changes fastest.
Arguments:
- load: float32 [64, 4, 8, 512], P(None, 'grp', 'box'), may hold values from -6 to 6
- leaf_load_map: float32 [4, 8, 128, 512], P('grp', 'box'), may hold values from -0.25 to 0.25
- leaf_out_map: float32 [4, 8, 128, 128], P('grp', 'box'), may hold values from -0.5 to 0.5
- leaf_field_map: float32 [4, 8, 512, 640], P('grp', 'box'), may hold values from -0.25 to 0.25
- x_solve: float32 [3, 4, 8, 64, 64], P(None, 'grp', 'box'), as said below
- x_out: float32 [3, 4, 8, 128, 64], P(None, 'grp', 'box'), may hold values from -0.375 to 0.375
- x_in: float32 [3, 4, 8, 64, 128], P(None, 'grp', 'box'), may hold values from -0.25 to 0.25
- y_solve: float32 [2, 4, 8, 64, 512], P(None, 'grp', 'box'), as said below
- y_out: float32 [2, 4, 8, 128, 512], P(None, 'grp', 'box'), may hold values from -0.125 to 0.125
- y_in: float32 [2, 4, 8, 512, 128], P(None, 'grp', 'box'), may hold values from -0.21875 to 0.21875
- reflect: float32 [4, 8, 128], P('grp', 'box'), may hold values from -0.9 to 0.9
Outputs:
- field_vals: float32 [64, 4, 8, 512], P(None, 'grp', 'box')
- edge_trace: float32 [64, 4, 8, 128], P(None, 'grp', 'box')
Inputs may be any that keep to these rules, and one draw needn't show every extreme that they name: x_solve[j, r, c] is the same matrix for all c with the same c // 2^(j+1). y_solve[j, r, c] is the same matrix for all r with the same r // 2^(j+1).
All inputs are finite; a program needn't handle non-finite values.
Results may differ from a plain program's by a relative error of at most 0.00011.
Values sent between devices are 32-bit elements; how exact they have to be, the bound alone decides.
No kernel may reach another device: no remote copies, remote signals or barrier semaphores. Data moves between devices by JAX's collectives and lax.ppermute only.
A program may use at most 64 MiB of HBM per device.

v0:
```python
import jax
import jax.numpy as jnp
from jax import lax
from jax.sharding import PartitionSpec as P

precise = lax.Precision.HIGHEST


def partner(x, axis, bit):
    return lax.ppermute(x, axis, [(i, i ^ 1 << bit) for i in range(lax.axis_size(axis))])


def with_halo(block, sides, width):
    for axis, dim in sides:
        count = lax.axis_size(axis)
        forward = [(i, i + 1) for i in range(count - 1)]
        backward = [(target, source) for source, target in forward]
        low = lax.ppermute(
            lax.slice_in_dim(block, block.shape[dim] - width, None, axis=dim), axis, forward
        )
        high = lax.ppermute(lax.slice_in_dim(block, 0, width, axis=dim), axis, backward)
        block = jnp.concatenate([low, block, high], axis=dim)
    return block


def edge_of(source, edge_no, edge_len):
    return source[:, edge_no * edge_len : (edge_no + 1) * edge_len]


def with_edge(source, edge_no, edge_len, values):
    return jnp.concatenate(
        [source[:, : edge_no * edge_len], values, source[:, (edge_no + 1) * edge_len :]], axis=1
    )


def column_total(partial_value, merge_level):
    for bit_no in range(merge_level + 1):
        partial_value = partial_value + partner(partial_value, "box", bit_no)
    return partial_value


def row_total(partial_value, merge_level):
    for bit_no in range(merge_level + 1):
        partial_value = partial_value + partner(partial_value, "grp", bit_no)
    return partial_value


def local(
    load,
    leaf_load_map,
    leaf_out_map,
    leaf_field_map,
    x_solve,
    x_out,
    x_in,
    y_solve,
    y_out,
    y_in,
    reflect,
):
    edge_len = leaf_out_map.shape[-1] // 4
    my_column = lax.axis_index("box")
    my_row = lax.axis_index("grp")
    col_count = lax.axis_size("box")
    row_count = lax.axis_size("grp")
    x_levels = col_count.bit_length() - 1
    y_levels = row_count.bit_length() - 1
    load_here = load[:, 0, 0, :]
    start_out = jnp.einsum("wk,ek->we", load_here, leaf_load_map[0, 0], precision=precise)
    outgoing_now = start_out
    x_keep = []
    for merge_level in range(x_levels):
        group_span = 2 ** (merge_level + 1)
        left_cut = my_column // group_span * group_span + group_span // 2 - 1
        contrib = jnp.concatenate(
            [
                jnp.where(my_column == left_cut, edge_of(outgoing_now, 1, edge_len), 0.0),
                jnp.where(my_column == left_cut + 1, edge_of(outgoing_now, 3, edge_len), 0.0),
            ],
            axis=1,
        )
        cut_data = column_total(contrib, merge_level)
        solved = jnp.einsum("wk,jk->wj", cut_data, x_solve[merge_level, 0, 0], precision=precise)
        x_keep.append(solved)
        outgoing_now = outgoing_now + jnp.einsum(
            "wj,ej->we", solved, x_out[merge_level, 0, 0], precision=precise
        )
    y_keep = []
    for merge_level in range(y_levels):
        group_span = 2 ** (merge_level + 1)
        low_cut = my_row // group_span * group_span + group_span // 2 - 1
        contrib = jnp.concatenate(
            [
                jnp.where(my_row == low_cut, edge_of(outgoing_now, 2, edge_len), 0.0),
                jnp.where(my_row == low_cut + 1, edge_of(outgoing_now, 0, edge_len), 0.0),
            ],
            axis=1,
        )
        column_part = row_total(contrib, merge_level)
        solve_rows = y_solve[merge_level, 0, 0]

        def solve_piece(carry, piece, start, solve_rows=solve_rows):
            return jnp.einsum("wk,jk->wj", piece, solve_rows, precision=precise)

        solved = solve_piece(
            jnp.zeros_like(column_part),
            lax.all_gather(column_part, "box", axis=1, tiled=True),
            jnp.int32(0),
        )
        y_keep.append(solved)
        out_rows = y_out[merge_level, 0, 0]

        def spread_piece(carry, piece, start, out_rows=out_rows):
            return carry + jnp.einsum("wj,ej->we", piece, out_rows, precision=precise)

        outgoing_now = spread_piece(
            outgoing_now, lax.all_gather(solved, "box", axis=1, tiled=True), jnp.int32(0)
        )
    edge_ids = jnp.arange(4 * edge_len) // edge_len
    on_boundary = (
        (edge_ids == 0) & (my_row == 0)
        | (edge_ids == 1) & (my_column == col_count - 1)
        | (edge_ids == 2) & (my_row == row_count - 1)
        | (edge_ids == 3) & (my_column == 0)
    )
    incoming = jnp.where(on_boundary[None, :], outgoing_now * reflect[0, 0][None, :], 0.0)
    for merge_level in reversed(range(y_levels)):
        group_span = 2 ** (merge_level + 1)
        low_cut = my_row // group_span * group_span + group_span // 2 - 1
        in_rows = y_in[merge_level, 0, 0]

        def cut_term(start, count, in_rows=in_rows, incoming=incoming):
            return jnp.einsum(
                "we,cke->cwk", incoming, in_rows.reshape(count, 2 * edge_len, -1), precision=precise
            )

        own_rows = lax.psum_scatter(
            cut_term(jnp.int32(0), 1 * lax.axis_size("box")), "box", scatter_dimension=0, tiled=True
        )[0]
        summed_in = row_total(own_rows, merge_level)
        cut_in = y_keep[merge_level] + summed_in
        incoming = with_edge(
            incoming,
            2,
            edge_len,
            jnp.where(my_row == low_cut, cut_in[:, :edge_len], edge_of(incoming, 2, edge_len)),
        )
        incoming = with_edge(
            incoming,
            0,
            edge_len,
            jnp.where(my_row == low_cut + 1, cut_in[:, edge_len:], edge_of(incoming, 0, edge_len)),
        )
    for merge_level in reversed(range(x_levels)):
        group_span = 2 ** (merge_level + 1)
        left_cut = my_column // group_span * group_span + group_span // 2 - 1
        cut_terms = jnp.einsum("we,ke->wk", incoming, x_in[merge_level, 0, 0], precision=precise)
        summed_in = column_total(cut_terms, merge_level)
        cut_in = x_keep[merge_level] + summed_in
        incoming = with_edge(
            incoming,
            1,
            edge_len,
            jnp.where(my_column == left_cut, cut_in[:, :edge_len], edge_of(incoming, 1, edge_len)),
        )
        incoming = with_edge(
            incoming,
            3,
            edge_len,
            jnp.where(
                my_column == left_cut + 1, cut_in[:, edge_len:], edge_of(incoming, 3, edge_len)
            ),
        )
    field_vals = jnp.einsum(
        "wk,ik->wi",
        jnp.concatenate([incoming, load_here], axis=1),
        leaf_field_map[0, 0],
        precision=precise,
    )
    outgoing_end = (
        jnp.einsum("wk,ek->we", incoming, leaf_out_map[0, 0], precision=precise) + start_out
    )
    trace_raw = incoming - outgoing_end
    rim_cells = with_halo(trace_raw[:, None, None, :], (("grp", 1), ("box", 2)), 1)
    east_nb = edge_of(rim_cells[:, 1, 2, :], 3, edge_len)
    west_nb = edge_of(rim_cells[:, 1, 0, :], 1, edge_len)
    north_nb = edge_of(rim_cells[:, 2, 1, :], 0, edge_len)
    south_nb = edge_of(rim_cells[:, 0, 1, :], 2, edge_len)
    bottom_edge = edge_of(trace_raw, 0, edge_len)
    right_edge = edge_of(trace_raw, 1, edge_len)
    top_edge = edge_of(trace_raw, 2, edge_len)
    left_edge = edge_of(trace_raw, 3, edge_len)
    new_bottom = jnp.where(my_row > 0, 0.5 * (bottom_edge + south_nb), bottom_edge)
    new_right = jnp.where(my_column < col_count - 1, 0.5 * (right_edge + east_nb), right_edge)
    new_top = jnp.where(my_row < row_count - 1, 0.5 * (top_edge + north_nb), top_edge)
    new_left = jnp.where(my_column > 0, 0.5 * (left_edge + west_nb), left_edge)
    edge_trace = jnp.concatenate([new_bottom, new_right, new_top, new_left], axis=1)
    return (field_vals[:, None, None, :], edge_trace[:, None, None, :])


def solution(mesh):
    return jax.shard_map(
        local,
        mesh=mesh,
        in_specs=(
            P(None, "grp", "box", None),
            P("grp", "box", None, None),
            P("grp", "box", None, None),
            P("grp", "box", None, None),
            P(None, "grp", "box", None, None),
            P(None, "grp", "box", None, None),
            P(None, "grp", "box", None, None),
            P(None, "grp", "box", None, None),
            P(None, "grp", "box", None, None),
            P(None, "grp", "box", None, None),
            P("grp", "box", None),
        ),
        out_specs=(P(None, "grp", "box", None), P(None, "grp", "box", None)),
        check_vma=False,
    )
```

profile of v0, /device:TPU:9, one launch (start us, length us, event | category | flops | bytes accessed | tf_op | source)
XLA Modules:
  0.0 356.6 jit_solution(292700751152068959)
XLA Ops:
  16.8 2.7 collective-permute-done.2
  21.3 1.8 collective-permute-done.3
  23.3 2.8 collective-permute-done.4
  26.1 2.4 collective-permute-start.5
  30.4 7.3 %collective-permute-start.6 = (f32[64,64]{1,0:T(8,128)S(1)}, f32[64,64]{1,0:T(8,128)S(1)}, u32[]{:S(2)}, u32[]{:S(2)}) collective-permute-start(f32[64,64]{1,0:T(8,128)S(1)} %pad_maximum_fusion.5), channel_id=1, source_target_pairs={{0,8},{8,0},{16,24},{24,16},{1,9},{9,1},{17,25},{25,17},{2,10},{10... | collective-permute-start | bytes 49160 | tf_op jit(solution)/shard_map/ppermute | solution.py:10
  38.7 22.2 %all_gather.12 = f32[64,512]{0,1:T(8,128)S(1)} all-gather(f32[64,64]{0,1:T(8,128)S(1)} %copy.26), channel_id=1, replica_groups=mesh['grp'=4,'box'=8] {'box'}, dimensions={1}, use_global_device_ids=true | all-gather | bytes 147456 | tf_op jit(solution)/shard_map/all_gather | solution.py:107
  61.2 24.6 %all_gather.13 = f32[64,512]{0,1:T(8,128)S(1)} all-gather(f32[64,64]{0,1:T(8,128)S(1)} %fusion.16), channel_id=1, replica_groups=mesh['grp'=4,'box'=8] {'box'}, dimensions={1}, use_global_device_ids=true | all-gather | bytes 147456 | tf_op jit(solution)/shard_map/all_gather | solution.py:117
  86.5 12.8 %collective-permute-start.7 = (f32[64,64]{1,0:T(8,128)S(1)}, f32[64,64]{1,0:T(8,128)S(1)}, u32[]{:S(2)}, u32[]{:S(2)}) collective-permute-start(f32[64,64]{1,0:T(8,128)S(1)} %pad_maximum_fusion.6), channel_id=1, source_target_pairs={{0,8},{8,0},{16,24},{24,16},{1,9},{9,1},{17,25},{25,17},{2,10},{10... | collective-permute-start | bytes 49160 | tf_op jit(solution)/shard_map/ppermute | solution.py:10
  103.2 24.4 %all_gather.14 = f32[64,512]{0,1:T(8,128)S(1)} all-gather(f32[64,64]{0,1:T(8,128)S(1)} %copy.27), channel_id=1, replica_groups=mesh['grp'=4,'box'=8] {'box'}, dimensions={1}, use_global_device_ids=true | all-gather | bytes 147456 | tf_op jit(solution)/shard_map/all_gather | solution.py:107
  127.8 24.5 %all_gather.15 = f32[64,512]{0,1:T(8,128)S(1)} all-gather(f32[64,64]{0,1:T(8,128)S(1)} %fusion.14), channel_id=1, replica_groups=mesh['grp'=4,'box'=8] {'box'}, dimensions={1}, use_global_device_ids=true | all-gather | bytes 147456 | tf_op jit(solution)/shard_map/all_gather | solution.py:117
  154.6 76.3 %reduce-scatter.3.cloned.1.call-done = f32[1,64,64]{2,1,0:T(8,128)} async-done(((f32[8,64,64]{2,1,0:T(8,128)}), f32[1,64,64]{2,1,0:T(8,128)}) %reduce-scatter.3.cloned.1.call-update) | async-done | bytes 16400 | tf_op jit(solution)/shard_map/reduce_scatter | solution.py:137
  230.9 2.7 collective-permute-start.9
  239.9 59.4 %reduce-scatter.5.cloned.1.call-done = f32[1,64,64]{2,1,0:T(8,128)} async-done(((f32[8,64,64]{2,1,0:T(8,128)}), f32[1,64,64]{2,1,0:T(8,128)}) %reduce-scatter.5.cloned.1.call-update) | async-done | bytes 16400 | tf_op jit(solution)/shard_map/reduce_scatter | solution.py:137
  299.3 2.6 collective-permute-start.11
  307.2 2.4 collective-permute-done.13
  311.0 2.3 collective-permute-done.14
  314.9 1.8 collective-permute-done.15
  317.1 2.3 collective-permute-done.16
  323.0 10.0 %collective-permute-start.18 = (f32[64,1,1,128]{3,0,2,1:T(8,128)S(1)}, f32[64,1,1,128]{3,0,2,1:T(8,128)S(1)}, u32[]{:S(2)}, u32[]{:S(2)}) collective-permute-start(f32[64,1,1,128]{3,0,2,1:T(8,128)S(1)} %bitcast.96), channel_id=1, source_target_pairs={{0,8},{8,16},{16,24},{1,9},{9,17},{17,25},{2,10},{10,18},{18,26},{... | collective-permute-start | bytes 98312 | tf_op jit(solution)/shard_map/ppermute | solution.py:18
  333.1 1.9 collective-permute-start.19
  335.1 3.2 collective-permute-done.19
  338.3 3.1 collective-permute-start.21
  343.6 3.1 collective-permute-start.20
  346.7 2.2 collective-permute-done.20
  (116 shorter events, 43.4 us)
Async XLA Ops:
  7.2 223.7 %reduce-scatter.3.cloned.1.call-start = ((), (), s32[]{:S(2)}) async-start(), calls=%async_computation.2 | async-start | bytes 294912 | tf_op jit(solution)/shard_map/reduce_scatter | solution.py:137
  9.0 2.8 collective-permute-start
  13.9 2.8 collective-permute-start.1
  16.7 2.8 collective-permute-start.2
  20.1 3.1 collective-permute-start.3
  23.3 2.8 collective-permute-start.4
  26.1 3.7 %collective-permute-start.5 = (f32[64,64]{1,0:T(8,128)S(1)}, f32[64,64]{1,0:T(8,128)S(1)}, u32[]{:S(2)}, u32[]{:S(2)}) collective-permute-start(f32[64,64]{1,0:T(8,128)S(1)} %add.174), channel_id=1, source_target_pairs={{0,4},{1,5},{2,6},{3,7},{4,0},{5,1},{6,2},{7,3},{8,12},{9,13},{10,... | collective-permute-start | bytes 49160 | tf_op jit(solution)/shard_map/ppermute | solution.py:10
  30.4 8.1 %collective-permute-start.6 = (f32[64,64]{1,0:T(8,128)S(1)}, f32[64,64]{1,0:T(8,128)S(1)}, u32[]{:S(2)}, u32[]{:S(2)}) collective-permute-start(f32[64,64]{1,0:T(8,128)S(1)} %pad_maximum_fusion.5), channel_id=1, source_target_pairs={{0,8},{8,0},{16,24},{24,16},{1,9},{9,1},{17,25},{25,17},{2,10},{10... | collective-permute-start | bytes 49160 | tf_op jit(solution)/shard_map/ppermute | solution.py:10
  86.5 13.7 %collective-permute-start.7 = (f32[64,64]{1,0:T(8,128)S(1)}, f32[64,64]{1,0:T(8,128)S(1)}, u32[]{:S(2)}, u32[]{:S(2)}) collective-permute-start(f32[64,64]{1,0:T(8,128)S(1)} %pad_maximum_fusion.6), channel_id=1, source_target_pairs={{0,8},{8,0},{16,24},{24,16},{1,9},{9,1},{17,25},{25,17},{2,10},{10... | collective-permute-start | bytes 49160 | tf_op jit(solution)/shard_map/ppermute | solution.py:10
  100.3 2.8 collective-permute-start.8
  154.5 144.8 %reduce-scatter.5.cloned.1.call-start = ((), (), s32[]{:S(2)}) async-start(), calls=%async_computation.3 | async-start | bytes 294912 | tf_op jit(solution)/shard_map/reduce_scatter | solution.py:137
  230.9 3.8 %collective-permute-start.9 = (f32[64,64]{1,0:T(8,128)}, f32[64,64]{1,0:T(8,128)S(1)}, u32[]{:S(2)}, u32[]{:S(2)}) collective-permute-start(f32[64,64]{1,0:T(8,128)} %bitcast.105), channel_id=1, source_target_pairs={{0,8},{8,0},{16,24},{24,16},{1,9},{9,1},{17,25},{25,17},{2,10},{10... | collective-permute-start | bytes 49160 | tf_op jit(solution)/shard_map/ppermute | solution.py:10
  235.4 2.8 collective-permute-start.10
  299.3 3.6 %collective-permute-start.11 = (f32[64,64]{1,0:T(8,128)}, f32[64,64]{1,0:T(8,128)S(1)}, u32[]{:S(2)}, u32[]{:S(2)}) collective-permute-start(f32[64,64]{1,0:T(8,128)} %bitcast.107), channel_id=1, source_target_pairs={{0,8},{8,0},{16,24},{24,16},{1,9},{9,1},{17,25},{25,17},{2,10},{10... | collective-permute-start | bytes 49160 | tf_op jit(solution)/shard_map/ppermute | solution.py:10
  304.0 2.8 collective-permute-start.12
  306.9 2.8 collective-permute-start.13
  309.6 3.7 %collective-permute-start.14 = (f32[64,64]{1,0:T(8,128)S(1)}, f32[64,64]{1,0:T(8,128)S(1)}, u32[]{:S(2)}, u32[]{:S(2)}) collective-permute-start(f32[64,64]{1,0:T(8,128)S(1)} %add.189), channel_id=1, source_target_pairs={{0,4},{1,5},{2,6},{3,7},{4,0},{5,1},{6,2},{7,3},{8,12},{9,13},{10,... | collective-permute-start | bytes 49160 | tf_op jit(solution)/shard_map/ppermute | solution.py:10
  313.7 3.0 collective-permute-start.15
  316.7 2.8 collective-permute-start.16
  319.8 2.8 collective-permute-start.17
  323.0 12.1 %collective-permute-start.18 = (f32[64,1,1,128]{3,0,2,1:T(8,128)S(1)}, f32[64,1,1,128]{3,0,2,1:T(8,128)S(1)}, u32[]{:S(2)}, u32[]{:S(2)}) collective-permute-start(f32[64,1,1,128]{3,0,2,1:T(8,128)S(1)} %bitcast.96), channel_id=1, source_target_pairs={{0,8},{8,16},{16,24},{1,9},{9,17},{17,25},{2,10},{10,18},{18,26},{... | collective-permute-start | bytes 98312 | tf_op jit(solution)/shard_map/ppermute | solution.py:18
  333.1 5.2 %collective-permute-start.19 = (f32[64,1,1,128]{3,0,2,1:T(8,128)S(1)}, f32[64,1,1,128]{3,0,2,1:T(8,128)S(1)}, u32[]{:S(2)}, u32[]{:S(2)}) collective-permute-start(f32[64,1,1,128]{3,0,2,1:T(8,128)S(1)} %bitcast.97), channel_id=1, source_target_pairs={{8,0},{16,8},{24,16},{9,1},{17,9},{25,17},{10,2},{18,10},{26,18},{... | collective-permute-start | bytes 98312 | tf_op jit(solution)/shard_map/ppermute | solution.py:21
  338.3 8.4 %collective-permute-start.21 = (f32[64,3,1,128]{3,0,2,1:T(8,128)S(1)}, f32[64,3,1,128]{3,0,2,1:T(8,128)S(1)}, u32[]{:S(2)}, u32[]{:S(2)}) collective-permute-start(f32[64,3,1,128]{3,0,2,1:T(8,128)S(1)} %pad_maximum_fusion), channel_id=1, source_target_pairs={{0,1},{1,2},{2,3},{3,4},{4,5},{5,6},{6,7},{8,9},{9,10},{10,11},{11... | collective-permute-start | bytes 294920 | tf_op jit(solution)/shard_map/ppermute | solution.py:18
  343.6 5.3 %collective-permute-start.20 = (f32[64,3,1,128]{3,0,2,1:T(8,128)S(1)}, f32[64,3,1,128]{3,0,2,1:T(8,128)S(1)}, u32[]{:S(2)}, u32[]{:S(2)}) collective-permute-start(f32[64,3,1,128]{3,0,2,1:T(8,128)S(1)} %pad_maximum_fusion), channel_id=1, source_target_pairs={{1,0},{2,1},{3,2},{4,3},{5,4},{6,5},{7,6},{9,8},{10,9},{11,10},{12... | collective-permute-start | bytes 294920 | tf_op jit(solution)/shard_map/ppermute | solution.py:21
  (10 other events, 887.3 us)
Sparse Core Ops, SparseCore 0:
  154.7 76.1 reduce-scatter.2
  240.1 59.1 reduce-scatter.4
where the time goes:
time: 358 us; the launch traced here: 357 us
  waiting for transfers between devices  172 us (48%)
  blocking collectives  95.6 us (27%)
  starting transfers between devices  57.9 us (16%)
  between operations  14.5 us (4%)
  matrix products  11.6 us (3%)
  other arithmetic  4.03 us (1%)
    reduce_scatter x2, waiting for transfers between devices, local(): lax.psum_scatter(cut_term(jnp.int32(0), 1 * lax.axis_size('box')), 'box',...  136 us
    all_gather x2, blocking collectives, local(): lax.all_gather(solved, 'box', axis=1, tiled=True)  49.1 us
    all_gather x2, blocking collectives, local(): lax.all_gather(column_part, 'box', axis=1, tiled=True)  46.6 us
    ppermute x18, starting transfers between devices, partner(): lax.ppermute(x, axis, [(i, i ^ 1 << bit) for i in range(lax.axis_size(axi...  39.7 us
    ppermute x18, waiting for transfers between devices, partner(): lax.ppermute(x, axis, [(i, i ^ 1 << bit) for i in range(lax.axis_size(axi...  30.5 us
    ppermute x2, starting transfers between devices, with_halo(): lax.ppermute(lax.slice_in_dim(block, block.shape[dim] - width, None, axis...  13.1 us
  transfers between devices with their start and end apart: 24, of which 22 were waited for; matrix products, arithmetic and copies ran while one was open for 1% of the time, Pallas kernels for 0%

commit v1 on v0

v1 whole, which is shorter than its diff:
```python
import functools

import jax
import jax.numpy as jnp
from jax import lax
from jax.experimental import pallas as pl
from jax.experimental.pallas import tpu as pltpu
from jax.sharding import Mesh, PartitionSpec as P

f32 = jnp.float32
LANES = 128


def dot_t(a, b):
    dims = (((1,), (1,)), ((), ()))

    def parts(x):
        high = x.astype(jnp.bfloat16)
        return high, (x - high.astype(f32)).astype(jnp.bfloat16)

    def product(x, y):
        return lax.dot_general(x, y, dims, preferred_element_type=f32)

    a_high, a_low = parts(a)
    b_high, b_low = parts(b)
    return product(a_high, b_high) + (product(a_high, b_low) + product(a_low, b_high))


def fused(body, outs, *args, scratch=()):
    vmem = pl.BlockSpec(memory_space=pltpu.VMEM)
    return pl.pallas_call(
        body,
        out_shape=[jax.ShapeDtypeStruct(s, f32) for s in outs],
        in_specs=[vmem] * len(args),
        out_specs=[vmem] * len(outs),
        scratch_shapes=[pltpu.VMEM(s, f32) for s in scratch],
        compiler_params=pltpu.CompilerParams(vmem_limit_bytes=12 << 20),
    )(*args)


def packed(x, width):
    runs = LANES // width
    rows = x.shape[0] // runs
    return jnp.concatenate([x[i * rows : (i + 1) * rows] for i in range(runs)], axis=1)


def unpacked(x, width):
    return jnp.concatenate(
        [x[:, i * width : (i + 1) * width] for i in range(x.shape[1] // width)], axis=0
    )


def pad_lanes(x, lanes):
    if x.shape[1] == lanes:
        return x
    return jnp.concatenate([x, jnp.zeros((x.shape[0], lanes - x.shape[1]), f32)], axis=1)


def local(
    row_axes,
    load,
    leaf_load_map,
    leaf_out_map,
    leaf_field_map,
    x_solve,
    x_out,
    x_in,
    y_solve,
    y_out,
    y_in,
    reflect,
):
    edge = leaf_out_map.shape[-1] // 4
    cols = lax.axis_size("box")
    rows = 1
    for axis in row_axes:
        rows *= lax.axis_size(axis)
    x_levels = x_solve.shape[0]
    y_levels = y_solve.shape[0]
    waves = load.shape[0]
    leaf = 4 * edge
    pair = 2 * edge
    iface = cols * pair
    load_here = load[:, 0, 0, :]
    inner = load_here.shape[1]

    def my_column():
        return lax.axis_index("box")

    def my_row():
        return lax.axis_index(row_axes)

    def bit(value, level):
        return (value >> level) & 1

    def edge_of(x, number):
        return x[:, number * edge : (number + 1) * edge]

    def exchange_shape(level):
        kept = x_levels - 1 - level
        lanes = max(pair + kept * edge, kept * pair)
        lanes = -(-lanes // LANES) * LANES
        return (waves + (edge if kept else 0), lanes)

    def store_exchange(out, left, right, in_cols, out_rows):
        lanes = out.shape[1]
        out[:waves] = pad_lanes(jnp.concatenate([left, right] + in_cols, axis=1), lanes)
        if out_rows:
            out[waves:] = pad_lanes(jnp.concatenate(out_rows, axis=1), lanes)

    def start_body(load_ref, map_ref, xo_ref, xi_ref, h_ref, out_ref):
        h = dot_t(load_ref[...], map_ref[...])
        h_ref[...] = h
        is_right = bit(my_column(), 0) == 1
        in_cols, out_rows = [], []
        for k in range(x_levels - 1):
            xo, xi = xo_ref[k], xi_ref[k]
            in_cols.append(jnp.where(is_right, edge_of(xi, 1), edge_of(xi, 3)))
            out_rows.append(jnp.where(is_right, xo[edge : 2 * edge], xo[3 * edge :]))
        store_exchange(out_ref, edge_of(h, 3), edge_of(h, 1), in_cols, out_rows)

    h0, to_send = fused(
        start_body,
        [(waves, leaf), exchange_shape(0)],
        load_here,
        leaf_load_map[0, 0],
        x_out[:, 0, 0],
        x_in[:, 0, 0],
    )
    from_load = jnp.einsum(
        "wk,ik->wi", load_here, leaf_field_map[0, 0, :, leaf:], precision=lax.Precision.HIGH
    )

    def x_body(level, h_ref, own_ref, got_ref, solve_ref, xo_ref, h_out, w_out, *rest):
        kept = x_levels - 1 - level
        is_right = bit(my_column(), level) == 1
        own, got = own_ref[:waves], got_ref[:waves]
        left_child = jnp.where(is_right, got, own)
        right_child = jnp.where(is_right, own, got)
        v = jnp.concatenate([left_child[:, edge:pair], right_child[:, :edge]], axis=1)
        w = dot_t(v, solve_ref[...])
        w_out[...] = w
        if kept:
            next_ref, ends_ref = rest
            left_rows = jnp.where(is_right, got_ref[waves:], own_ref[waves:])
            right_rows = jnp.where(is_right, own_ref[waves:], got_ref[waves:])
            spread = dot_t(
                w, jnp.concatenate([xo_ref[...], left_rows[:, :pair], right_rows[:, :pair]], axis=0)
            )
            h_out[...] = h_ref[...] + spread[:, :leaf]
            left = left_child[:, :edge] + spread[:, leaf : leaf + edge]
            right = right_child[:, edge:pair] + spread[:, leaf + edge :]
            ends_ref[...] = jnp.concatenate(
                [left_child[:, pair : pair + edge], right_child[:, pair : pair + edge]], axis=1
            )
            next_right = bit(my_column(), level + 1) == 1
            in_all = jnp.where(next_right, right_child, left_child)
            out_all = jnp.where(next_right, right_rows, left_rows)
            store_exchange(
                next_ref,
                left,
                right,
                [in_all[:, pair + k * edge : pair + (k + 1) * edge] for k in range(1, kept)],
                [out_all[:, k * pair : (k + 1) * pair] for k in range(1, kept)],
            )
        else:
            h_out[...] = h_ref[...] + dot_t(w, xo_ref[...])

    h = h0
    x_keep, ends = [], []
    for level in range(x_levels):
        got = lax.ppermute(to_send, "box", [(i, i ^ (1 << level)) for i in range(cols)])
        outs = [(waves, leaf), (waves, pair)]
        if level < x_levels - 1:
            outs += [exchange_shape(level + 1), (pair, pair)]
        h, w, *rest = fused(
            functools.partial(x_body, level),
            outs,
            h,
            to_send,
            got,
            x_solve[level, 0, 0],
            x_out[level, 0, 0],
        )
        x_keep.append(w)
        if rest:
            to_send, end = rest
            ends.append(end)

    def group(level):
        return tuple(row_axes[y_levels - 1 - level :]) + ("box",)

    def span(level):
        return 2 << level

    def swap(x, level):
        return lax.all_to_all(x, group(level), 0, 0, tiled=True)

    def offer_shape(level):
        size = span(level)
        return (size * cols, waves // size * edge // LANES, LANES)

    def store_offer(level, h, out):
        size = span(level)
        share = waves // size
        facing = jnp.where(
            lax.rem(my_row(), size) == size // 2 - 1, edge_of(h, 2), edge_of(h, 0)
        )
        for target in range(size):
            piece = packed(facing[target * share : (target + 1) * share], edge)
            out[target * cols : (target + 1) * cols] = jnp.broadcast_to(piece, (cols,) + piece.shape)

    def offer_body(level, h_ref, out_ref):
        store_offer(level, h_ref[...], out_ref)

    def solve_body(level, got_ref, solve_ref, out_ref, v_ref):
        size = span(level)
        low = (size // 2 - 1) * cols
        run = got_ref.shape[1]
        for side in range(2):
            for c in range(cols):
                piece = got_ref[low + side * cols + c]
                for k in range(LANES // edge):
                    start = c * pair + side * edge
                    v_ref[k * run : (k + 1) * run, start : start + edge] = edge_of(piece, k)
        w = packed(dot_t(v_ref[...], solve_ref[...]), pair)
        out_ref[...] = jnp.broadcast_to(w, out_ref.shape)

    def own_columns(w_all):
        own = w_all[:, :pair]
        for c in range(1, cols):
            own = jnp.where(my_column() == c, w_all[:, c * pair : (c + 1) * pair], own)
        return own

    def gather_w(level, got_ref, w_ref):
        size = span(level)
        share = waves // size
        run = got_ref.shape[1]
        for target in range(size):
            for c in range(cols):
                piece = got_ref[target * cols + c]
                for k in range(LANES // pair):
                    start = target * share + k * run
                    w_ref[start : start + run, c * pair : (c + 1) * pair] = piece[
                        :, k * pair : (k + 1) * pair
                    ]
        return w_ref[...]

    def spread_body(level, h_ref, got_ref, yo_ref, h_out, w_out, next_ref, w_ref):
        w_all = gather_w(level, got_ref, w_ref)
        w_out[...] = own_columns(w_all)
        h = h_ref[...] + dot_t(w_all, yo_ref[...])
        h_out[...] = h
        store_offer(level + 1, h, next_ref)

    def halves(level):
        return span(level) // 2

    def terms_shape(level):
        return (span(level) * cols, waves // halves(level) * edge // LANES, LANES)

    def store_terms(level, g, yi_ref, out):
        terms = dot_t(g, yi_ref[...])
        half = halves(level)
        share = waves // half
        for side in range(2):
            for c in range(cols):
                start = c * pair + side * edge
                piece = terms[:, start : start + edge]
                for part in range(half):
                    out[(side * half + part) * cols + c] = packed(
                        piece[part * share : (part + 1) * share], edge
                    )

    def turn_body(level, h_ref, got_ref, yo_ref, yi_ref, reflect_ref, w_out, g_out, out_ref, w_ref):
        w_all = gather_w(level, got_ref, w_ref)
        w_out[...] = own_columns(w_all)
        h = h_ref[...] + dot_t(w_all, yo_ref[...])
        lane = lax.broadcasted_iota(jnp.int32, (1, leaf), 1)

        def side(number):
            return (lane >= number * edge) & (lane < (number + 1) * edge)

        outer = (
            side(0) & (my_row() == 0)
            | side(1) & (my_column() == cols - 1)
            | side(2) & (my_row() == rows - 1)
            | side(3) & (my_column() == 0)
        )
        g = jnp.where(outer, h * reflect_ref[...], 0.0)
        g_out[...] = g
        store_terms(level, g, yi_ref, out_ref)

    def sum_body(got_ref, out_ref):
        out_ref[...] = jnp.sum(got_ref[...], axis=0)

    def with_row_edge(level, g, w, q):
        size = span(level)
        place = lax.rem(my_row(), size)
        is_low = place == size // 2 - 1
        is_high = place == size // 2
        value = jnp.where(place < size // 2, w[:, :edge], w[:, edge:]) + q
        bottom = jnp.where(is_high, value, edge_of(g, 0))
        top = jnp.where(is_low, value, edge_of(g, 2))
        return jnp.concatenate([bottom, edge_of(g, 1), top, edge_of(g, 3)], axis=1)

    def row_down_body(level, g_ref, w_ref, sum_ref, yi_ref, g_out, out_ref):
        g = with_row_edge(level, g_ref[...], w_ref[...], unpacked_parts(level, sum_ref))
        g_out[...] = g
        store_terms(level - 1, g, yi_ref, out_ref)

    def unpacked_parts(level, sum_ref):
        run = waves // halves(level) * edge // LANES
        return jnp.concatenate(
            [unpacked(sum_ref[i * run : (i + 1) * run], edge) for i in range(halves(level))], axis=0
        )

    def collect(total, level):
        for axis_no in range(level):
            axis = row_axes[y_levels - 1 - axis_no]
            other = lax.ppermute(total, axis, [(0, 1), (1, 0)])
            first = lax.axis_index(axis) == 0
            total = jnp.concatenate(
                [jnp.where(first, total, other), jnp.where(first, other, total)], axis=0
            )
        return total

    x_lanes = -(-x_levels * edge // LANES) * LANES

    def x_terms_body(g_ref, w_ref, sum_ref, xi_ref, g_out, out_ref):
        g = with_row_edge(0, g_ref[...], w_ref[...], unpacked_parts(0, sum_ref))
        g_out[...] = g
        terms = [dot_t(g, xi_ref[k]) for k in range(x_levels)]
        for c in range(cols):
            picked = []
            for k in range(x_levels):
                start = bit(c, k) * edge
                same = my_column() >> (k + 1) == c >> (k + 1)
                picked.append(jnp.where(same, terms[k][:, start : start + edge], 0.0))
            out_ref[c] = pad_lanes(jnp.concatenate(picked, axis=1), x_lanes)

    def finish_body(g_ref, h0_ref, got_ref, keep_ref, ends_ref, lo_ref, g_out, t_out, *faces):
        g = g_ref[...]
        q = jnp.sum(got_ref[...], axis=0)
        gl = jnp.zeros((waves, edge), f32)
        gr = gl
        for level in reversed(range(x_levels)):
            is_right = bit(my_column(), level) == 1
            keep = keep_ref[level]
            value = edge_of(q, level) + jnp.where(is_right, keep[:, edge:], keep[:, :edge])
            if level < x_levels - 1:
                end = ends_ref[level]
                end = jnp.where(is_right, end[edge:], end[:edge])
                value = value + dot_t(jnp.concatenate([gl, gr], axis=1), end)
            gl = jnp.where(is_right, value, gl)
            gr = jnp.where(is_right, gr, value)
        g = jnp.concatenate(
            [edge_of(g, 0), edge_of(g, 1) + gr, edge_of(g, 2), edge_of(g, 3) + gl], axis=1
        )
        g_out[...] = g
        t = g - (dot_t(g, lo_ref[...]) + h0_ref[...])
        t_out[...] = t
        odd_col = bit(my_column(), 0) == 1
        odd_row = bit(my_row(), 0) == 1
        bottom, right, top, left = (packed(edge_of(t, i), edge) for i in range(4))
        faces[0][...] = jnp.where(odd_col, left, right)
        faces[1][...] = jnp.where(odd_col, right, left)
        faces[2][...] = jnp.where(odd_row, bottom, top)
        faces[3][...] = jnp.where(odd_row, top, bottom)

    def trace_body(t_ref, a_ref, b_ref, c_ref, d_ref, out_ref):
        t = t_ref[...]
        odd_col = bit(my_column(), 0) == 1
        odd_row = bit(my_row(), 0) == 1
        near_x, far_x, near_y, far_y = (
            unpacked(ref[...], edge) for ref in (a_ref, b_ref, c_ref, d_ref)
        )
        east = jnp.where(odd_col, far_x, near_x)
        west = jnp.where(odd_col, near_x, far_x)
        north = jnp.where(odd_row, far_y, near_y)
        south = jnp.where(odd_row, near_y, far_y)

        def mean(shared, own, other):
            return jnp.where(shared, 0.5 * (own + other), own)

        out_ref[...] = jnp.concatenate(
            [
                mean(my_row() > 0, edge_of(t, 0), south),
                mean(my_column() < cols - 1, edge_of(t, 1), east),
                mean(my_row() < rows - 1, edge_of(t, 2), north),
                mean(my_column() > 0, edge_of(t, 3), west),
            ],
            axis=1,
        )

    (offer,) = fused(functools.partial(offer_body, 0), [offer_shape(0)], h)
    y_keep = []
    for level in range(y_levels):
        share = waves // span(level)
        (w_offer,) = fused(
            functools.partial(solve_body, level),
            [(span(level) * cols, share * pair // LANES, LANES)],
            swap(offer, level),
            y_solve[level, 0, 0],
            scratch=[(share, iface)],
        )
        got = swap(w_offer, level)
        if level < y_levels - 1:
            h, w, offer = fused(
                functools.partial(spread_body, level),
                [(waves, leaf), (waves, pair), offer_shape(level + 1)],
                h,
                got,
                y_out[level, 0, 0],
                scratch=[(waves, iface)],
            )
        else:
            w, g, terms = fused(
                functools.partial(turn_body, level),
                [(waves, pair), (waves, leaf), terms_shape(level)],
                h,
                got,
                y_out[level, 0, 0],
                y_in[level, 0, 0],
                reflect[0],
                scratch=[(waves, iface)],
            )
        y_keep.append(w)
    for level in reversed(range(y_levels)):
        (total,) = fused(sum_body, [terms_shape(level)[1:]], swap(terms, level))
        total = collect(total, level)
        if level > 0:
            g, terms = fused(
                functools.partial(row_down_body, level),
                [(waves, leaf), terms_shape(level - 1)],
                g,
                y_keep[level],
                total,
                y_in[level - 1, 0, 0],
            )
    g, terms = fused(
        x_terms_body,
        [(waves, leaf), (cols, waves, x_lanes)],
        g,
        y_keep[0],
        total,
        x_in[:, 0, 0],
    )
    got = lax.all_to_all(terms, "box", 0, 0, tiled=True)
    face = (waves * edge // LANES, LANES)
    g, t, *faces = fused(
        finish_body,
        [(waves, leaf), (waves, leaf)] + [face] * 4,
        g,
        h0,
        got,
        jnp.stack(x_keep),
        jnp.stack(ends),
        leaf_out_map[0, 0],
    )

    def near(count):
        return [(i, i ^ 1) for i in range(count)]

    def far(count):
        one_way = [(i, i + 1) for i in range(1, count - 1, 2)]
        return one_way + [(j, i) for i, j in one_way]

    seen = [
        lax.ppermute(faces[0], "box", near(cols)),
        lax.ppermute(faces[1], "box", far(cols)),
        lax.ppermute(faces[2], row_axes, near(rows)),
        lax.ppermute(faces[3], row_axes, far(rows)),
    ]
    field_vals = from_load + jnp.einsum(
        "wk,ik->wi", g, leaf_field_map[0, 0, :, :leaf], precision=lax.Precision.HIGH
    )
    (edge_trace,) = fused(trace_body, [(waves, leaf)], t, *seen)
    return (field_vals[:, None, None, :], edge_trace[:, None, None, :])


def solution(mesh):
    rows, cols = mesh.devices.shape
    bits = rows.bit_length() - 1
    row_axes = tuple(f"row{i}" for i in reversed(range(bits)))
    split = Mesh(mesh.devices.reshape((2,) * bits + (cols,)), row_axes + ("box",))
    late = P(None, row_axes, "box")
    early = P(row_axes, "box")
    return jax.shard_map(
        functools.partial(local, row_axes),
        mesh=split,
        in_specs=(late, early, early, early) + (late,) * 6 + (early,),
        out_specs=(late, late),
        check_vma=False,
    )
```

time: 358 us -> 116 us (0.32)
  waiting for transfers between devices: 172 us -> 31.1 us
  blocking collectives: 95.6 us -> 29.7 us
  starting transfers between devices: 57.9 us -> 38 us
  between operations: 14.5 us -> 0.9 us
  matrix products: 11.6 us -> 0.87 us
  Pallas kernels: 0 us -> 9.27 us
  other arithmetic: 4.03 us -> 0.03 us
  local copies, waits for them, and re-layouts: 1.51 us -> 5.09 us
    reduce_scatter x2 -> x0, waiting for transfers between devices: 136 us -> none  [local(): lax.psum_scatter(cut_term(jnp.int32(0), 1 * lax.axis_size('box')), 'box',...]
    all_gather x4 -> x0, blocking collectives: 95.6 us -> none  [the longest x2 49.1 us: local(): lax.all_gather(solved, 'box', axis=1, tiled=True)]
    ppermute x22 -> x8, starting transfers between devices: 57.8 us -> 14.2 us  [the longest x3 3.72 us: local(): lax.ppermute(to_send, 'box', [(i, i ^ 1 << level) for i in range(cols)])]
    all_to_all x0 -> x3, blocking collectives: none -> 29.7 us  [swap(): return lax.all_to_all(x, group(level), 0, 0, tiled=True)]
    ppermute x22 -> x8, waiting for transfers between devices: 35.9 us -> 7.63 us  [the longest x3 5.68 us: local(): lax.ppermute(to_send, 'box', [(i, i ^ 1 << level) for i in range(cols)])]
    all_to_all x0 -> x4, starting transfers between devices: none -> 23.8 us  [the longest x3 19.5 us: swap(): return lax.all_to_all(x, group(level), 0, 0, tiled=True)]
    all_to_all x0 -> x4, waiting for transfers between devices: none -> 23.4 us  [the longest x3 17.2 us: swap(): return lax.all_to_all(x, group(level), 0, 0, tiled=True)]
    dot_general x18 -> x2, matrix products: 11.6 us -> 0.87 us  [the longest x1 0.61 us: local(): jnp.einsum('wk,ik->wi', load_here, leaf_field_map[0, 0, :, leaf:], precis...]
  transfers between devices with their start and end apart: 24 -> 12, of which waited for: 22 -> 9; matrix products, arithmetic and copies ran while one was open for 1% -> 2% of each run, Pallas kernels for 0% -> 0%
where the time goes in v1:
time: 116 us; the launch traced here: 115 us
  starting transfers between devices  38 us (33%)
  waiting for transfers between devices  31.1 us (27%)
  blocking collectives  29.7 us (26%)
  Pallas kernels  9.27 us (8%)
  local copies, waits for them, and re-layouts  5.09 us (4%)
    all_to_all x3, blocking collectives, swap(): return lax.all_to_all(x, group(level), 0, 0, tiled=True)  29.7 us
    all_to_all x3, starting transfers between devices, swap(): return lax.all_to_all(x, group(level), 0, 0, tiled=True)  19.5 us
    all_to_all x3, waiting for transfers between devices, swap(): return lax.all_to_all(x, group(level), 0, 0, tiled=True)  17.2 us
    pallas_call x15, Pallas kernels, fused(): pl.pallas_call(body, out_shape=[jax.ShapeDtypeStruct(s, f32) for s in out...  9.27 us
    all_to_all x1, waiting for transfers between devices, local(): got = lax.all_to_all(terms, 'box', 0, 0, tiled=True)  6.21 us
    ppermute x3, waiting for transfers between devices, local(): lax.ppermute(to_send, 'box', [(i, i ^ 1 << level) for i in range(cols)])  5.68 us
    unnamed x30, local copies, waits for them, and re-layouts  4.98 us
    all_to_all x1, starting transfers between devices, local(): got = lax.all_to_all(terms, 'box', 0, 0, tiled=True)  4.36 us
  transfers between devices with their start and end apart: 12, of which 9 were waited for; matrix products, arithmetic and copies ran while one was open for 2% of the time, Pallas kernels for 0%

profile of v1, /device:TPU:9, one launch (start us, length us, event | category | flops | bytes accessed | tf_op | source)
XLA Modules:
  0.0 115.0 jit_solution(504681548016770107)
XLA Ops:
  0.6 1.1 copy.13
  4.9 1.3 %collective-permute-start = (f32[96,128]{1,0:T(8,128)S(1)}, f32[96,128]{1,0:T(8,128)S(1)}, u32[]{:S(2)}, u32[]{:S(2)}) collective-permute-start(f32[96,128]{1,0:T(8,128)S(1)} %get-tuple-element.31.own_ref), channel_id=1, source_target_pairs={{0,1},{1,0},{2,3},{3,2},{4,5},{5,4},{6,7},{7,6},{8,9},{9,8},{10,11... | collective-permute-start | bytes 147464 | tf_op jit(solution)/shard_map/ppermute | solution.py:172
  6.3 1.6 %collective-permute-done.got_ref = f32[96,128]{1,0:T(8,128)S(1)} collective-permute-done((f32[96,128]{1,0:T(8,128)S(1)}, f32[96,128]{1,0:T(8,128)S(1)}, u32[]{:S(2)}, u32[]{:S(2)}) %collective-permute-start) | collective-permute-done | bytes 49184 | tf_op jit(solution)/shard_map/ppermute | solution.py:172
  8.5 2.8 %collective-permute-done.1.got_ref = f32[96,128]{1,0:T(8,128)S(1)} collective-permute-done((f32[96,128]{1,0:T(8,128)S(1)}, f32[96,128]{1,0:T(8,128)S(1)}, u32[]{:S(2)}, u32[]{:S(2)}) %collective-permute-start.1) | collective-permute-done | bytes 49184 | tf_op jit(solution)/shard_map/ppermute | solution.py:172
  11.8 2.4 %collective-permute-start.2 = (f32[64,128]{1,0:T(8,128)S(1)}, f32[64,128]{1,0:T(8,128)S(1)}, u32[]{:S(2)}, u32[]{:S(2)}) collective-permute-start(f32[64,128]{1,0:T(8,128)S(1)} %get-tuple-element.35.own_ref), channel_id=1, source_target_pairs={{0,4},{1,5},{2,6},{3,7},{4,0},{5,1},{6,2},{7,3},{8,12},{9,13},{10,... | collective-permute-start | bytes 98312 | tf_op jit(solution)/shard_map/ppermute | solution.py:172
  14.2 1.3 %collective-permute-done.2.got_ref = f32[64,128]{1,0:T(8,128)S(1)} collective-permute-done((f32[64,128]{1,0:T(8,128)S(1)}, f32[64,128]{1,0:T(8,128)S(1)}, u32[]{:S(2)}, u32[]{:S(2)}) %collective-permute-start.2) | collective-permute-done | bytes 32800 | tf_op jit(solution)/shard_map/ppermute | solution.py:172
  16.7 10.3 %all-to-all-start = ((f32[16,8,128]{2,1,0:T(8,128)}), f32[16,8,128]{2,1,0:T(8,128)S(1)}, u32[]{:S(2)}, u32[]{:S(2)}) async-start(f32[16,8,128]{2,1,0:T(8,128)} %shard_map.126), calls=%async_computation | async-start | bytes 131072 | tf_op jit(solution)/shard_map/all_to_all | solution.py:197
  27.0 4.9 %all-to-all-done.got_ref = f32[16,8,128]{2,1,0:T(8,128)S(1)} async-done(((f32[16,8,128]{2,1,0:T(8,128)}), f32[16,8,128]{2,1,0:T(8,128)S(1)}, u32[]{:S(2)}, u32[]{:S(2)}) %all-to-all-start) | async-done | bytes 65568 | tf_op jit(solution)/shard_map/all_to_all | solution.py:197
  32.9 5.3 %all-to-all-start.1 = ((f32[16,16,128]{2,1,0:T(8,128)}), f32[16,16,128]{2,1,0:T(8,128)S(1)}, u32[]{:S(2)}, u32[]{:S(2)}) async-start(f32[16,16,128]{2,1,0:T(8,128)} %shard_map.127), calls=%async_computation.1 | async-start | bytes 262144 | tf_op jit(solution)/shard_map/all_to_all | solution.py:197
  38.3 5.8 %all-to-all-done.1.got_ref = f32[16,16,128]{2,1,0:T(8,128)S(1)} async-done(((f32[16,16,128]{2,1,0:T(8,128)}), f32[16,16,128]{2,1,0:T(8,128)S(1)}, u32[]{:S(2)}, u32[]{:S(2)}) %all-to-all-start.1) | async-done | bytes 131104 | tf_op jit(solution)/shard_map/all_to_all | solution.py:197
  44.8 9.9 %all_to_all.35.got_ref = f32[32,4,128]{2,1,0:T(4,128)S(1)} all-to-all(f32[32,4,128]{2,1,0:T(4,128)S(1)} %get-tuple-element.38), channel_id=1, replica_groups=mesh['row1'=2,'row0'=2,'box'=8] {'row1','row0','box'}, dimensions={0} | all-to-all | bytes 131072 | tf_op jit(solution)/shard_map/all_to_all | solution.py:197
  54.6 1.0 shard_map.129
  55.6 3.9 %all-to-all-start.3 = ((f32[32,8,128]{2,1,0:T(8,128)}), f32[32,8,128]{2,1,0:T(8,128)S(1)}, u32[]{:S(2)}, u32[]{:S(2)}) async-start(f32[32,8,128]{2,1,0:T(8,128)} %shard_map.129), calls=%async_computation.3 | async-start | bytes 262144 | tf_op jit(solution)/shard_map/all_to_all | solution.py:197
  59.6 6.5 %all-to-all-done.3.got_ref = f32[32,8,128]{2,1,0:T(8,128)S(1)} async-done(((f32[32,8,128]{2,1,0:T(8,128)}), f32[32,8,128]{2,1,0:T(8,128)S(1)}, u32[]{:S(2)}, u32[]{:S(2)}) %all-to-all-start.3) | async-done | bytes 131104 | tf_op jit(solution)/shard_map/all_to_all | solution.py:197
  66.8 9.9 %all_to_all.36.got_ref = f32[32,8,128]{2,1,0:T(8,128)S(1)} all-to-all(f32[32,8,128]{2,1,0:T(8,128)S(1)} %get-tuple-element.41), channel_id=1, replica_groups=mesh['row1'=2,'row0'=2,'box'=8] {'row1','row0','box'}, dimensions={0} | all-to-all | bytes 262144 | tf_op jit(solution)/shard_map/all_to_all | solution.py:197
  79.0 9.9 %all_to_all.37.got_ref = f32[16,16,128]{2,1,0:T(8,128)S(1)} all-to-all(f32[16,16,128]{2,1,0:T(8,128)S(1)} %get-tuple-element.44), channel_id=1, replica_groups=mesh['row1'=2,'row0'=2,'box'=8] {'row0','box'}, dimensions={0} | all-to-all | bytes 262144 | tf_op jit(solution)/shard_map/all_to_all | solution.py:197
  89.0 1.1 shard_map.134
  90.1 4.4 %all-to-all-start.6 = ((f32[8,64,128]{2,1,0:T(8,128)}), f32[8,64,128]{2,1,0:T(8,128)S(1)}, u32[]{:S(2)}, u32[]{:S(2)}) async-start(f32[8,64,128]{2,1,0:T(8,128)} %get-tuple-element.46), calls=%async_computation.6 | async-start | bytes 524288 | tf_op jit(solution)/shard_map/all_to_all | solution.py:449
  94.5 6.2 %all-to-all-done.6.got_ref = f32[8,64,128]{2,1,0:T(8,128)S(1)} async-done(((f32[8,64,128]{2,1,0:T(8,128)}), f32[8,64,128]{2,1,0:T(8,128)S(1)}, u32[]{:S(2)}, u32[]{:S(2)}) %all-to-all-start.6) | async-done | bytes 262176 | tf_op jit(solution)/shard_map/all_to_all | solution.py:449
  100.7 1.1 shard_map.135
  102.7 3.3 %collective-permute-start.5 = (f32[16,128]{1,0:T(8,128)S(1)}, f32[16,128]{1,0:T(8,128)S(1)}, u32[]{:S(2)}, u32[]{:S(2)}) collective-permute-start(f32[16,128]{1,0:T(8,128)S(1)} %get-tuple-element.55), channel_id=1, source_target_pairs={{1,2},{3,4},{5,6},{2,1},{4,3},{6,5},{9,10},{11,12},{13,14},{10,9},... | collective-permute-start | bytes 24584 | tf_op jit(solution)/shard_map/ppermute | solution.py:471
  106.0 3.2 %collective-permute-start.6 = (f32[16,128]{1,0:T(8,128)S(1)}, f32[16,128]{1,0:T(8,128)S(1)}, u32[]{:S(2)}, u32[]{:S(2)}) collective-permute-start(f32[16,128]{1,0:T(8,128)S(1)} %get-tuple-element.56), channel_id=1, source_target_pairs={{0,8},{8,0},{16,24},{24,16},{1,9},{9,1},{17,25},{25,17},{2,10},{10... | collective-permute-start | bytes 24584 | tf_op jit(solution)/shard_map/ppermute | solution.py:472
  109.2 2.1 %collective-permute-start.7 = (f32[16,128]{1,0:T(8,128)S(1)}, f32[16,128]{1,0:T(8,128)S(1)}, u32[]{:S(2)}, u32[]{:S(2)}) collective-permute-start(f32[16,128]{1,0:T(8,128)S(1)} %get-tuple-element.57), channel_id=1, source_target_pairs={{8,16},{16,8},{9,17},{17,9},{10,18},{18,10},{11,19},{19,11},{12,20... | collective-permute-start | bytes 24584 | tf_op jit(solution)/shard_map/ppermute | solution.py:473
  113.1 1.1 collective-permute-done.7.d_ref
  (59 shorter events, 13.8 us)
Async XLA Ops:
  0.6 5.5 %copy-start.9 = (f32[3,1,1,128,64]{3,4,2,1,0:T(8,128)S(1)}, f32[3,1,1,128,64]{3,4,2,1,0:T(8,128)}, u32[]{:S(2)}) copy-start(f32[3,1,1,128,64]{3,4,2,1,0:T(8,128)} %param.16) | copy-start | bytes 294916
  0.6 5.5 %copy-start.11 = (f32[3,1,1,64,64]{4,3,2,1,0:T(8,128)S(1)}, f32[3,1,1,64,64]{4,3,2,1,0:T(8,128)}, u32[]{:S(2)}) copy-start(f32[3,1,1,64,64]{4,3,2,1,0:T(8,128)} %param.15) | copy-start | bytes 147460
  1.7 25.2 %copy-start.10 = (f32[2,1,1,64,512]{4,3,2,1,0:T(8,128)S(1)}, f32[2,1,1,64,512]{4,3,2,1,0:T(8,128)}, u32[]{:S(2)}) copy-start(f32[2,1,1,64,512]{4,3,2,1,0:T(8,128)} %param.18) | copy-start | bytes 786436
  2.7 0.9 copy-start
  3.6 0.9 copy-start.2
  4.9 33.4 %copy-start.6 = (f32[2,1,1,128,512]{4,3,2,1,0:T(8,128)S(1)}, f32[2,1,1,128,512]{4,3,2,1,0:T(8,128)}, u32[]{:S(2)}) copy-start(f32[2,1,1,128,512]{4,3,2,1,0:T(8,128)} %param.19) | copy-start | bytes 1572868
  4.9 3.0 %collective-permute-start = (f32[96,128]{1,0:T(8,128)S(1)}, f32[96,128]{1,0:T(8,128)S(1)}, u32[]{:S(2)}, u32[]{:S(2)}) collective-permute-start(f32[96,128]{1,0:T(8,128)S(1)} %get-tuple-element.31.own_ref), channel_id=1, source_target_pairs={{0,1},{1,0},{2,3},{3,2},{4,5},{5,4},{6,7},{7,6},{8,9},{9,8},{10,11... | collective-permute-start | bytes 147464 | tf_op jit(solution)/shard_map/ppermute | solution.py:172
  8.3 3.0 %collective-permute-start.1 = (f32[96,128]{1,0:T(8,128)S(1)}, f32[96,128]{1,0:T(8,128)S(1)}, u32[]{:S(2)}, u32[]{:S(2)}) collective-permute-start(f32[96,128]{1,0:T(8,128)S(1)} %get-tuple-element.33.own_ref), channel_id=1, source_target_pairs={{0,2},{1,3},{2,0},{3,1},{4,6},{5,7},{6,4},{7,5},{8,10},{9,11},{10,... | collective-permute-start | bytes 147464 | tf_op jit(solution)/shard_map/ppermute | solution.py:172
  11.8 3.7 %collective-permute-start.2 = (f32[64,128]{1,0:T(8,128)S(1)}, f32[64,128]{1,0:T(8,128)S(1)}, u32[]{:S(2)}, u32[]{:S(2)}) collective-permute-start(f32[64,128]{1,0:T(8,128)S(1)} %get-tuple-element.35.own_ref), channel_id=1, source_target_pairs={{0,4},{1,5},{2,6},{3,7},{4,0},{5,1},{6,2},{7,3},{8,12},{9,13},{10,... | collective-permute-start | bytes 98312 | tf_op jit(solution)/shard_map/ppermute | solution.py:172
  16.7 15.2 %all-to-all-start = ((f32[16,8,128]{2,1,0:T(8,128)}), f32[16,8,128]{2,1,0:T(8,128)S(1)}, u32[]{:S(2)}, u32[]{:S(2)}) async-start(f32[16,8,128]{2,1,0:T(8,128)} %shard_map.126), calls=%async_computation | async-start | bytes 131072 | tf_op jit(solution)/shard_map/all_to_all | solution.py:197
  32.9 26.6 %copy-start.7 = (f32[2,1,1,512,128]{4,3,2,1,0:T(8,128)S(1)}, f32[2,1,1,512,128]{4,3,2,1,0:T(8,128)}, u32[]{:S(2)}) copy-start(f32[2,1,1,512,128]{4,3,2,1,0:T(8,128)} %param.20) | copy-start | bytes 1572868
  32.9 11.2 %all-to-all-start.1 = ((f32[16,16,128]{2,1,0:T(8,128)}), f32[16,16,128]{2,1,0:T(8,128)S(1)}, u32[]{:S(2)}, u32[]{:S(2)}) async-start(f32[16,16,128]{2,1,0:T(8,128)} %shard_map.127), calls=%async_computation.1 | async-start | bytes 262144 | tf_op jit(solution)/shard_map/all_to_all | solution.py:197
  38.3 27.8 %copy-start.4 = (f32[1,1,128]{2,1,0:T(1,128)S(1)}, f32[1,1,128]{2,1,0:T(1,128)}, u32[]{:S(2)}) copy-start(f32[1,1,128]{2,1,0:T(1,128)} %param.21) | copy-start | bytes 1540
  55.6 10.5 %all-to-all-start.3 = ((f32[32,8,128]{2,1,0:T(8,128)}), f32[32,8,128]{2,1,0:T(8,128)S(1)}, u32[]{:S(2)}, u32[]{:S(2)}) async-start(f32[32,8,128]{2,1,0:T(8,128)} %shard_map.129), calls=%async_computation.3 | async-start | bytes 262144 | tf_op jit(solution)/shard_map/all_to_all | solution.py:197
  59.5 29.4 %copy-start.1 = (f32[3,1,1,64,128]{4,3,2,1,0:T(8,128)S(1)}, f32[3,1,1,64,128]{4,3,2,1,0:T(8,128)}, u32[]{:S(2)}) copy-start(f32[3,1,1,64,128]{4,3,2,1,0:T(8,128)} %param.17) | copy-start | bytes 294916
  66.1 34.6 %copy-start.3 = (f32[1,1,128,128]{3,2,1,0:T(8,128)S(1)}, f32[1,1,128,128]{3,2,1,0:T(8,128)}, u32[]{:S(2)}) copy-start(f32[1,1,128,128]{3,2,1,0:T(8,128)} %param.13) | copy-start | bytes 196612
  76.7 34.6 %copy-start.5 = (f32[1,1,512,640]{3,2,1,0:T(8,128)S(1)}, f32[1,1,512,640]{3,2,1,0:T(8,128)}, u32[]{:S(2)}) copy-start(f32[1,1,512,640]{3,2,1,0:T(8,128)} %param.14) | copy-start | bytes 3932164
  76.8 1.7 %collective-permute-start.3 = (f32[8,128]{1,0:T(8,128)S(1)}, f32[8,128]{1,0:T(8,128)S(1)}, u32[]{:S(2)}, u32[]{:S(2)}) collective-permute-start(f32[8,128]{1,0:T(8,128)S(1)} %shard_map.131), channel_id=1, source_target_pairs={{0,8},{8,0},{1,9},{9,1},{2,10},{10,2},{3,11},{11,3},{4,12},{12,4},... | collective-permute-start | bytes 12296 | tf_op jit(solution)/shard_map/ppermute | solution.py:321
  78.5 33.2 %copy-start.8 = (f32[64,1,1,512]{3,2,1,0:T(1,128)S(1)}, f32[64,1,1,512]{3,2,1,0:T(1,128)}, u32[]{:S(2)}) copy-start(f32[64,1,1,512]{3,2,1,0:T(1,128)} %param.11) | copy-start | bytes 393220
  90.1 10.6 %all-to-all-start.6 = ((f32[8,64,128]{2,1,0:T(8,128)}), f32[8,64,128]{2,1,0:T(8,128)S(1)}, u32[]{:S(2)}, u32[]{:S(2)}) async-start(f32[8,64,128]{2,1,0:T(8,128)} %get-tuple-element.46), calls=%async_computation.6 | async-start | bytes 524288 | tf_op jit(solution)/shard_map/all_to_all | solution.py:449
  101.8 11.3 %collective-permute-start.4 = (f32[16,128]{1,0:T(8,128)S(1)}, f32[16,128]{1,0:T(8,128)S(1)}, u32[]{:S(2)}, u32[]{:S(2)}) collective-permute-start(f32[16,128]{1,0:T(8,128)S(1)} %get-tuple-element.54), channel_id=1, source_target_pairs={{0,1},{1,0},{2,3},{3,2},{4,5},{5,4},{6,7},{7,6},{8,9},{9,8},{10,11... | collective-permute-start | bytes 24584 | tf_op jit(solution)/shard_map/ppermute | solution.py:470
  102.7 10.3 %collective-permute-start.5 = (f32[16,128]{1,0:T(8,128)S(1)}, f32[16,128]{1,0:T(8,128)S(1)}, u32[]{:S(2)}, u32[]{:S(2)}) collective-permute-start(f32[16,128]{1,0:T(8,128)S(1)} %get-tuple-element.55), channel_id=1, source_target_pairs={{1,2},{3,4},{5,6},{2,1},{4,3},{6,5},{9,10},{11,12},{13,14},{10,9},... | collective-permute-start | bytes 24584 | tf_op jit(solution)/shard_map/ppermute | solution.py:471
  106.0 7.0 %collective-permute-start.6 = (f32[16,128]{1,0:T(8,128)S(1)}, f32[16,128]{1,0:T(8,128)S(1)}, u32[]{:S(2)}, u32[]{:S(2)}) collective-permute-start(f32[16,128]{1,0:T(8,128)S(1)} %get-tuple-element.56), channel_id=1, source_target_pairs={{0,8},{8,0},{16,24},{24,16},{1,9},{9,1},{17,25},{25,17},{2,10},{10... | collective-permute-start | bytes 24584 | tf_op jit(solution)/shard_map/ppermute | solution.py:472
  109.2 5.0 %collective-permute-start.7 = (f32[16,128]{1,0:T(8,128)S(1)}, f32[16,128]{1,0:T(8,128)S(1)}, u32[]{:S(2)}, u32[]{:S(2)}) collective-permute-start(f32[16,128]{1,0:T(8,128)S(1)} %get-tuple-element.57), channel_id=1, source_target_pairs={{8,16},{16,8},{9,17},{17,9},{10,18},{18,10},{11,19},{19,11},{12,20... | collective-permute-start | bytes 24584 | tf_op jit(solution)/shard_map/ppermute | solution.py:473

commit v2 on v1

--- a/solution.py
+++ b/solution.py
@@ -1,4 +1,5 @@
 import functools
+import math
 
 import jax
 import jax.numpy as jnp
@@ -9,10 +10,11 @@
 
 f32 = jnp.float32
 LANES = 128
-
-
-def dot_t(a, b):
-    dims = (((1,), (1,)), ((), ()))
+START_ROOM = 60 << 20
+
+
+def dot(a, b, over=0):
+    dims = (((1,), (over,)), ((), ()))
 
     def parts(x):
         high = x.astype(jnp.bfloat16)
@@ -24,13 +26,17 @@
     a_high, a_low = parts(a)
     b_high, b_low = parts(b)
     return product(a_high, b_high) + (product(a_high, b_low) + product(a_low, b_high))
+
+
+def dot_t(a, b):
+    return dot(a, b, 1)
 
 
 def fused(body, outs, *args, scratch=()):
     vmem = pl.BlockSpec(memory_space=pltpu.VMEM)
     return pl.pallas_call(
         body,
-        out_shape=[jax.ShapeDtypeStruct(s, f32) for s in outs],
+        out_shape=[pltpu.VMEM(s, f32) for s in outs],
         in_specs=[vmem] * len(args),
         out_specs=[vmem] * len(outs),
         scratch_shapes=[pltpu.VMEM(s, f32) for s in scratch],
@@ -97,36 +103,62 @@
         return x[:, number * edge : (number + 1) * edge]
 
     def exchange_shape(level):
-        kept = x_levels - 1 - level
-        lanes = max(pair + kept * edge, kept * pair)
-        lanes = -(-lanes // LANES) * LANES
-        return (waves + (edge if kept else 0), lanes)
-
-    def store_exchange(out, left, right, in_cols, out_rows):
-        lanes = out.shape[1]
-        out[:waves] = pad_lanes(jnp.concatenate([left, right] + in_cols, axis=1), lanes)
-        if out_rows:
-            out[waves:] = pad_lanes(jnp.concatenate(out_rows, axis=1), lanes)
-
-    def start_body(load_ref, map_ref, xo_ref, xi_ref, h_ref, out_ref):
-        h = dot_t(load_ref[...], map_ref[...])
+        lanes = (2 + 2 * (x_levels - 1 - level)) * edge
+        return (pair, -(-lanes // LANES) * LANES)
+
+    def pieces_of(x, first, count):
+        return [edge_of(x, first + i) for i in range(count)]
+
+    kept_from_start = [x_solve, jnp.swapaxes(x_out, 3, 4), x_in, y_solve, y_out, y_in]
+    kept_from_start = [x[:, 0, 0] for x in kept_from_start] + [leaf_out_map[0, 0]]
+
+    def start_body(load_any, map_any, *refs):
+        count = len(kept_from_start)
+        sources, (h_ref, out_ref) = refs[:count], refs[count : count + 2]
+        targets = refs[count + 2 : 2 * count + 2]
+        load_v, map_v, sems = refs[2 * count + 2 :]
+        pairs = [(load_any, load_v), (map_any, map_v)] + list(zip(sources, targets))
+        order = [0, 1, 4, 3, 2, 5, 6, 7, 8]
+        copies = [pltpu.make_async_copy(a, b, sems.at[i]) for i, (a, b) in enumerate(pairs)]
+        for i in order:
+            copies[i].start()
+        copies[0].wait()
+        copies[1].wait()
+        h = dot_t(load_v[...].reshape(waves, inner), map_v[...])
         h_ref[...] = h
+        copies[4].wait()
+        copies[3].wait()
+        xo, xi = targets[1], targets[2]
         is_right = bit(my_column(), 0) == 1
-        in_cols, out_rows = [], []
-        for k in range(x_levels - 1):
-            xo, xi = xo_ref[k], xi_ref[k]
-            in_cols.append(jnp.where(is_right, edge_of(xi, 1), edge_of(xi, 3)))
-            out_rows.append(jnp.where(is_right, xo[edge : 2 * edge], xo[3 * edge :]))
-        store_exchange(out_ref, edge_of(h, 3), edge_of(h, 1), in_cols, out_rows)
-
-    h0, to_send = fused(
+        travelling = [
+            jnp.where(is_right, edge_of(x[k], 1), edge_of(x[k], 3))
+            for x in (xi, xo)
+            for k in range(x_levels - 1)
+        ]
+        out_ref[...] = pad_lanes(
+            jnp.concatenate([edge_of(h, 3), edge_of(h, 1)] + travelling, axis=1), out_ref.shape[1]
+        )
+        for i in order[4:]:
+            copies[i].wait()
+
+    anywhere, vmem = (pl.BlockSpec(memory_space=m) for m in (pl.ANY, pltpu.VMEM))
+    count = len(kept_from_start)
+    outs = [(waves, leaf), exchange_shape(0)] + [x.shape for x in kept_from_start]
+    h0, to_send, *placed = pl.pallas_call(
         start_body,
-        [(waves, leaf), exchange_shape(0)],
-        load_here,
-        leaf_load_map[0, 0],
-        x_out[:, 0, 0],
-        x_in[:, 0, 0],
-    )
+        out_shape=[pltpu.VMEM(s, f32) for s in outs],
+        in_specs=[anywhere] * (count + 2),
+        out_specs=[vmem] * (count + 2),
+        scratch_shapes=[
+            pltpu.VMEM(load.shape, f32),
+            pltpu.VMEM((leaf, inner), f32),
+            pltpu.SemaphoreType.DMA((count + 2,)),
+        ],
+        compiler_params=pltpu.CompilerParams(
+            vmem_limit_bytes=START_ROOM - sum(4 * math.prod(s) for s in outs)
+        ),
+    )(load, leaf_load_map[0, 0], *kept_from_start)
+    xs_all, xo_all, xi_all, ys_all, yo_all, yi_all, out_map = placed
     from_load = jnp.einsum(
         "wk,ik->wi", load_here, leaf_field_map[0, 0, :, leaf:], precision=lax.Precision.HIGH
     )
@@ -134,37 +166,29 @@
     def x_body(level, h_ref, own_ref, got_ref, solve_ref, xo_ref, h_out, w_out, *rest):
         kept = x_levels - 1 - level
         is_right = bit(my_column(), level) == 1
-        own, got = own_ref[:waves], got_ref[:waves]
+        own, got = own_ref[...], got_ref[...]
         left_child = jnp.where(is_right, got, own)
         right_child = jnp.where(is_right, own, got)
-        v = jnp.concatenate([left_child[:, edge:pair], right_child[:, :edge]], axis=1)
-        w = dot_t(v, solve_ref[...])
+        v = jnp.concatenate([edge_of(left_child, 1), edge_of(right_child, 0)], axis=1)
+        w = dot_t(v, solve_ref[level])
         w_out[...] = w
         if kept:
             next_ref, ends_ref = rest
-            left_rows = jnp.where(is_right, got_ref[waves:], own_ref[waves:])
-            right_rows = jnp.where(is_right, own_ref[waves:], got_ref[waves:])
-            spread = dot_t(
-                w, jnp.concatenate([xo_ref[...], left_rows[:, :pair], right_rows[:, :pair]], axis=0)
+            outer = [edge_of(x, 2 + kept) for x in (left_child, right_child)]
+            spread = dot(w, jnp.concatenate([xo_ref[level]] + outer, axis=1))
+            h_out[...] = h_ref[...] + spread[:, :leaf]
+            left = edge_of(left_child, 0) + edge_of(spread, 4)
+            right = edge_of(right_child, 1) + edge_of(spread, 5)
+            ends_ref[...] = jnp.concatenate(
+                [edge_of(left_child, 2), edge_of(right_child, 2)], axis=1
             )
-            h_out[...] = h_ref[...] + spread[:, :leaf]
-            left = left_child[:, :edge] + spread[:, leaf : leaf + edge]
-            right = right_child[:, edge:pair] + spread[:, leaf + edge :]
-            ends_ref[...] = jnp.concatenate(
-                [left_child[:, pair : pair + edge], right_child[:, pair : pair + edge]], axis=1
-            )
-            next_right = bit(my_column(), level + 1) == 1
-            in_all = jnp.where(next_right, right_child, left_child)
-            out_all = jnp.where(next_right, right_rows, left_rows)
-            store_exchange(
-                next_ref,
-                left,
-                right,
-                [in_all[:, pair + k * edge : pair + (k + 1) * edge] for k in range(1, kept)],
-                [out_all[:, k * pair : (k + 1) * pair] for k in range(1, kept)],
+            mine = jnp.where(bit(my_column(), level + 1) == 1, right_child, left_child)
+            travelling = pieces_of(mine, 3, kept - 1) + pieces_of(mine, 3 + kept, kept - 1)
+            next_ref[...] = pad_lanes(
+                jnp.concatenate([left, right] + travelling, axis=1), next_ref.shape[1]
             )
         else:
-            h_out[...] = h_ref[...] + dot_t(w, xo_ref[...])
+            h_out[...] = h_ref[...] + dot(w, xo_ref[level])
 
     h = h0
     x_keep, ends = [], []
@@ -174,13 +198,7 @@
         if level < x_levels - 1:
             outs += [exchange_shape(level + 1), (pair, pair)]
         h, w, *rest = fused(
-            functools.partial(x_body, level),
-            outs,
-            h,
-            to_send,
-            got,
-            x_solve[level, 0, 0],
-            x_out[level, 0, 0],
+            functools.partial(x_body, level), outs, h, to_send, got, xs_all, xo_all
         )
         x_keep.append(w)
         if rest:
@@ -223,7 +241,7 @@
                 for k in range(LANES // edge):
                     start = c * pair + side * edge
                     v_ref[k * run : (k + 1) * run, start : start + edge] = edge_of(piece, k)
-        w = packed(dot_t(v_ref[...], solve_ref[...]), pair)
+        w = packed(dot_t(v_ref[...], solve_ref[level]), pair)
         out_ref[...] = jnp.broadcast_to(w, out_ref.shape)
 
     def own_columns(w_all):
@@ -249,7 +267,7 @@
     def spread_body(level, h_ref, got_ref, yo_ref, h_out, w_out, next_ref, w_ref):
         w_all = gather_w(level, got_ref, w_ref)
         w_out[...] = own_columns(w_all)
-        h = h_ref[...] + dot_t(w_all, yo_ref[...])
+        h = h_ref[...] + dot_t(w_all, yo_ref[level])
         h_out[...] = h
         store_offer(level + 1, h, next_ref)
 
@@ -260,7 +278,7 @@
         return (span(level) * cols, waves // halves(level) * edge // LANES, LANES)
 
     def store_terms(level, g, yi_ref, out):
-        terms = dot_t(g, yi_ref[...])
+        terms = dot_t(g, yi_ref[level])
         half = halves(level)
         share = waves // half
         for side in range(2):
@@ -275,7 +293,7 @@
     def turn_body(level, h_ref, got_ref, yo_ref, yi_ref, reflect_ref, w_out, g_out, out_ref, w_ref):
         w_all = gather_w(level, got_ref, w_ref)
         w_out[...] = own_columns(w_all)
-        h = h_ref[...] + dot_t(w_all, yo_ref[...])
+        h = h_ref[...] + dot_t(w_all, yo_ref[level])
         lane = lax.broadcasted_iota(jnp.int32, (1, leaf), 1)
 
         def side(number):
@@ -339,17 +357,19 @@
                 picked.append(jnp.where(same, terms[k][:, start : start + edge], 0.0))
             out_ref[c] = pad_lanes(jnp.concatenate(picked, axis=1), x_lanes)
 
-    def finish_body(g_ref, h0_ref, got_ref, keep_ref, ends_ref, lo_ref, g_out, t_out, *faces):
+    def finish_body(g_ref, h0_ref, got_ref, lo_ref, *refs):
+        keep_ref, ends_ref = refs[:x_levels], refs[x_levels : 2 * x_levels - 1]
+        g_out, t_out, *faces = refs[2 * x_levels - 1 :]
         g = g_ref[...]
         q = jnp.sum(got_ref[...], axis=0)
         gl = jnp.zeros((waves, edge), f32)
         gr = gl
         for level in reversed(range(x_levels)):
             is_right = bit(my_column(), level) == 1
-            keep = keep_ref[level]
+            keep = keep_ref[level][...]
             value = edge_of(q, level) + jnp.where(is_right, keep[:, edge:], keep[:, :edge])
             if level < x_levels - 1:
-                end = ends_ref[level]
+                end = ends_ref[level][...]
                 end = jnp.where(is_right, end[edge:], end[:edge])
                 value = value + dot_t(jnp.concatenate([gl, gr], axis=1), end)
             gl = jnp.where(is_right, value, gl)
@@ -401,7 +421,7 @@
             functools.partial(solve_body, level),
             [(span(level) * cols, share * pair // LANES, LANES)],
             swap(offer, level),
-            y_solve[level, 0, 0],
+            ys_all,
             scratch=[(share, iface)],
         )
         got = swap(w_offer, level)
@@ -411,7 +431,7 @@
                 [(waves, leaf), (waves, pair), offer_shape(level + 1)],
                 h,
                 got,
-                y_out[level, 0, 0],
+                yo_all,
                 scratch=[(waves, iface)],
             )
         else:
@@ -420,8 +440,8 @@
                 [(waves, pair), (waves, leaf), terms_shape(level)],
                 h,
                 got,
-                y_out[level, 0, 0],
-                y_in[level, 0, 0],
+                yo_all,
+                yi_all,
                 reflect[0],
                 scratch=[(waves, iface)],
             )
@@ -436,7 +456,7 @@
                 g,
                 y_keep[level],
                 total,
-                y_in[level - 1, 0, 0],
+                yi_all,
             )
     g, terms = fused(
         x_terms_body,
@@ -444,7 +464,7 @@
         g,
         y_keep[0],
         total,
-        x_in[:, 0, 0],
+        xi_all,
     )
     got = lax.all_to_all(terms, "box", 0, 0, tiled=True)
     face = (waves * edge // LANES, LANES)
@@ -454,9 +474,9 @@
         g,
         h0,
         got,
-        jnp.stack(x_keep),
-        jnp.stack(ends),
-        leaf_out_map[0, 0],
+        out_map,
+        *x_keep,
+        *ends,
     )
 
     def near(count):

time: 116 us -> 109 us (0.940)
  blocking collectives: 29.7 us -> 64.5 us
  starting transfers between devices: 38 us -> 18.6 us
  waiting for transfers between devices: 31.1 us -> 14.2 us
  local copies, waits for them, and re-layouts: 5.09 us -> 1.43 us
    all_to_all x3 -> x6, blocking collectives: 29.7 us -> 64.5 us  [swap(): return lax.all_to_all(x, group(level), 0, 0, tiled=True)]
    all_to_all x3 -> x0, starting transfers between devices: 19.5 us -> none  [swap(): return lax.all_to_all(x, group(level), 0, 0, tiled=True)]
    all_to_all x3 -> x0, waiting for transfers between devices: 17.2 us -> none  [swap(): return lax.all_to_all(x, group(level), 0, 0, tiled=True)]
    unnamed x30 -> x8, local copies, waits for them, and re-layouts: 4.98 us -> 1.43 us
  transfers between devices with their start and end apart: 12 -> 9, of which waited for: 9 -> 6; matrix products, arithmetic and copies ran while one was open for 2% -> 2% of each run, Pallas kernels for 0% -> 0%
where the time goes in v2:
time: 109 us; the launch traced here: 108 us
  blocking collectives  64.5 us (59%)
  starting transfers between devices  18.6 us (17%)
  waiting for transfers between devices  14.2 us (13%)
  Pallas kernels  8.12 us (7%)
  local copies, waits for them, and re-layouts  1.43 us (1%)
    all_to_all x6, blocking collectives, swap(): return lax.all_to_all(x, group(level), 0, 0, tiled=True)  64.5 us
    pallas_call x14, Pallas kernels, fused(): pl.pallas_call(body, out_shape=[pltpu.VMEM(s, f32) for s in outs], in_spe...  6.25 us
    ppermute x3, waiting for transfers between devices, local(): lax.ppermute(to_send, 'box', [(i, i ^ 1 << level) for i in range(cols)])  6.01 us
    all_to_all x1, waiting for transfers between devices, local(): got = lax.all_to_all(terms, 'box', 0, 0, tiled=True)  5.6 us
    all_to_all x1, starting transfers between devices, local(): got = lax.all_to_all(terms, 'box', 0, 0, tiled=True)  4.36 us
    ppermute x3, starting transfers between devices, local(): lax.ppermute(to_send, 'box', [(i, i ^ 1 << level) for i in range(cols)])  3.72 us
    ppermute x1, starting transfers between devices, local(): lax.ppermute(faces[1], 'box', far(cols))  3.28 us
    ppermute x1, starting transfers between devices, local(): lax.ppermute(faces[2], row_axes, near(rows))  3.2 us
  transfers between devices with their start and end apart: 9, of which 6 were waited for; matrix products, arithmetic and copies ran while one was open for 2% of the time, Pallas kernels for 0%

profile of v2, /device:TPU:9, one launch (start us, length us, event | category | flops | bytes accessed | tf_op | source)
XLA Modules:
  0.0 108.5 jit_solution(59782768770000496)
XLA Ops:
  0.6 1.9 %shard_map.122 = (f32[64,128]{1,0:T(8,128)S(1)}, f32[64,256]{1,0:T(8,128)S(1)}, f32[3,64,64]{2,1,0:T(8,128)S(1)}, f32[3,64,128]{2,1,0:T(8,128)S(1)}, f32[3,64,12...) custom-call(f32[64,1,1,512]{3,2,1,0:T(1,128)} %load_any.1, ...), custom_call_target="tpu_custom_call" | custom-call | tf_op jit(solution)/shard_map/pallas_call | solution.py:147
  2.5 1.3 %collective-permute-start = (f32[64,256]{1,0:T(8,128)S(1)}, f32[64,256]{1,0:T(8,128)S(1)}, u32[]{:S(2)}, u32[]{:S(2)}) collective-permute-start(f32[64,256]{1,0:T(8,128)S(1)} %get-tuple-element.38.own_ref), channel_id=1, source_target_pairs={{0,1},{1,0},{2,3},{3,2},{4,5},{5,4},{6,7},{7,6},{8,9},{9,8},{10,11... | collective-permute-start | bytes 196616 | tf_op jit(solution)/shard_map/ppermute | solution.py:196
  3.8 1.9 %collective-permute-done.got_ref = f32[64,256]{1,0:T(8,128)S(1)} collective-permute-done((f32[64,256]{1,0:T(8,128)S(1)}, f32[64,256]{1,0:T(8,128)S(1)}, u32[]{:S(2)}, u32[]{:S(2)}) %collective-permute-start) | collective-permute-done | bytes 65568 | tf_op jit(solution)/shard_map/ppermute | solution.py:196
  6.2 2.8 %collective-permute-done.1.got_ref = f32[64,128]{1,0:T(8,128)S(1)} collective-permute-done((f32[64,128]{1,0:T(8,128)S(1)}, f32[64,128]{1,0:T(8,128)S(1)}, u32[]{:S(2)}, u32[]{:S(2)}) %collective-permute-start.1) | collective-permute-done | bytes 32800 | tf_op jit(solution)/shard_map/ppermute | solution.py:196
  9.3 2.4 %collective-permute-start.2 = (f32[64,128]{1,0:T(8,128)S(1)}, f32[64,128]{1,0:T(8,128)S(1)}, u32[]{:S(2)}, u32[]{:S(2)}) collective-permute-start(f32[64,128]{1,0:T(8,128)S(1)} %get-tuple-element.44.own_ref), channel_id=1, source_target_pairs={{0,4},{1,5},{2,6},{3,7},{4,0},{5,1},{6,2},{7,3},{8,12},{9,13},{10,... | collective-permute-start | bytes 98312 | tf_op jit(solution)/shard_map/ppermute | solution.py:196
  11.7 1.4 %collective-permute-done.2.got_ref = f32[64,128]{1,0:T(8,128)S(1)} collective-permute-done((f32[64,128]{1,0:T(8,128)S(1)}, f32[64,128]{1,0:T(8,128)S(1)}, u32[]{:S(2)}, u32[]{:S(2)}) %collective-permute-start.2) | collective-permute-done | bytes 32800 | tf_op jit(solution)/shard_map/ppermute | solution.py:196
  13.6 15.0 %all_to_all.35.got_ref = f32[16,8,128]{2,1,0:T(8,128)S(1)} all-to-all(f32[16,8,128]{2,1,0:T(8,128)S(1)} %shard_map.126), channel_id=1, replica_groups=mesh['row1'=2,'row0'=2,'box'=8] {'row0','box'}, dimensions={0} | all-to-all | bytes 131072 | tf_op jit(solution)/shard_map/all_to_all | solution.py:215
  29.0 10.1 %all_to_all.36.got_ref = f32[16,16,128]{2,1,0:T(8,128)S(1)} all-to-all(f32[16,16,128]{2,1,0:T(8,128)S(1)} %shard_map.127), channel_id=1, replica_groups=mesh['row1'=2,'row0'=2,'box'=8] {'row0','box'}, dimensions={0} | all-to-all | bytes 262144 | tf_op jit(solution)/shard_map/all_to_all | solution.py:215
  39.8 9.9 %all_to_all.37.got_ref = f32[32,4,128]{2,1,0:T(4,128)S(1)} all-to-all(f32[32,4,128]{2,1,0:T(4,128)S(1)} %get-tuple-element.49), channel_id=1, replica_groups=mesh['row1'=2,'row0'=2,'box'=8] {'row1','row0','box'}, dimensions={0} | all-to-all | bytes 131072 | tf_op jit(solution)/shard_map/all_to_all | solution.py:215
  50.0 9.6 %all_to_all.38.got_ref = f32[32,8,128]{2,1,0:T(8,128)S(1)} all-to-all(f32[32,8,128]{2,1,0:T(8,128)S(1)} %shard_map.129), channel_id=1, replica_groups=mesh['row1'=2,'row0'=2,'box'=8] {'row1','row0','box'}, dimensions={0} | all-to-all | bytes 262144 | tf_op jit(solution)/shard_map/all_to_all | solution.py:215
  60.3 9.9 %all_to_all.39.got_ref = f32[32,8,128]{2,1,0:T(8,128)S(1)} all-to-all(f32[32,8,128]{2,1,0:T(8,128)S(1)} %get-tuple-element.53), channel_id=1, replica_groups=mesh['row1'=2,'row0'=2,'box'=8] {'row1','row0','box'}, dimensions={0} | all-to-all | bytes 262144 | tf_op jit(solution)/shard_map/all_to_all | solution.py:215
  70.3 0.9 collective-permute-start.3
  71.2 0.8 collective-permute-done.3
  72.5 9.9 %all_to_all.40.got_ref = f32[16,16,128]{2,1,0:T(8,128)S(1)} all-to-all(f32[16,16,128]{2,1,0:T(8,128)S(1)} %get-tuple-element.56), channel_id=1, replica_groups=mesh['row1'=2,'row0'=2,'box'=8] {'row0','box'}, dimensions={0} | all-to-all | bytes 262144 | tf_op jit(solution)/shard_map/all_to_all | solution.py:215
  82.5 1.1 %shard_map.134 = (f32[64,128]{1,0:T(8,128)S(1)}, f32[8,64,128]{2,1,0:T(8,128)}) custom-call(f32[64,128]{1,0:T(8,128)S(1)} %get-tuple-element.54.g_ref, f32[64,64]{1,0:T(8,128)S(1)} %get-tuple-element.55.w_ref, f32[16,128]{1,0:T(8,128)S(1)} %shard_map.133.sum_ref, f32[3,64,128]{2,1,0:T(8,128)S(1)} %get-tuple-element.57.xi_ref), custom_call_target="tpu_custom_call" | custom-call | tf_op jit(solution)/shard_map/pallas_call | solution.py:37
  83.6 4.4 %all-to-all-start.6 = ((f32[8,64,128]{2,1,0:T(8,128)}), f32[8,64,128]{2,1,0:T(8,128)S(1)}, u32[]{:S(2)}, u32[]{:S(2)}) async-start(f32[8,64,128]{2,1,0:T(8,128)} %get-tuple-element.59), calls=%async_computation.6 | async-start | bytes 524288 | tf_op jit(solution)/shard_map/all_to_all | solution.py:469
  88.6 5.6 %all-to-all-done.6.got_ref = f32[8,64,128]{2,1,0:T(8,128)S(1)} async-done(((f32[8,64,128]{2,1,0:T(8,128)}), f32[8,64,128]{2,1,0:T(8,128)S(1)}, u32[]{:S(2)}, u32[]{:S(2)}) %all-to-all-start.6) | async-done | bytes 262176 | tf_op jit(solution)/shard_map/all_to_all | solution.py:469
  94.2 1.1 %shard_map.135 = (f32[64,128]{1,0:T(8,128)S(1)}, f32[64,128]{1,0:T(8,128)S(1)}, f32[16,128]{1,0:T(8,128)S(1)}, f32[16,128]{1,0:T(8,128)S(1)}, f32[16,128]{1,0:T(8,128)S(1)}, /*index=5*/f32[16,128]{1,0:T(8,128)S(1)}) custom-call(f32[64,128]{1,0:T(8,128)S(1)} %get-tuple-element.58.g_ref, f32[64,128]{1,0:T(8,128)S(1)} %get-tuple-element.37.h_ref.h0_ref, ...), custom_call_target="tpu_custom_call" | custom-call | tf_op jit(solution)/shard_map/pallas_call | solution.py:37
  95.3 1.0 collective-permute-start.4
  96.2 3.3 %collective-permute-start.5 = (f32[16,128]{1,0:T(8,128)S(1)}, f32[16,128]{1,0:T(8,128)S(1)}, u32[]{:S(2)}, u32[]{:S(2)}) collective-permute-start(f32[16,128]{1,0:T(8,128)S(1)} %get-tuple-element.69), channel_id=1, source_target_pairs={{1,2},{3,4},{5,6},{2,1},{4,3},{6,5},{9,10},{11,12},{13,14},{10,9},... | collective-permute-start | bytes 24584 | tf_op jit(solution)/shard_map/ppermute | solution.py:491
  99.5 3.2 %collective-permute-start.6 = (f32[16,128]{1,0:T(8,128)S(1)}, f32[16,128]{1,0:T(8,128)S(1)}, u32[]{:S(2)}, u32[]{:S(2)}) collective-permute-start(f32[16,128]{1,0:T(8,128)S(1)} %get-tuple-element.70), channel_id=1, source_target_pairs={{0,8},{8,0},{16,24},{24,16},{1,9},{9,1},{17,25},{25,17},{2,10},{10... | collective-permute-start | bytes 24584 | tf_op jit(solution)/shard_map/ppermute | solution.py:492
  102.7 2.1 %collective-permute-start.7 = (f32[16,128]{1,0:T(8,128)S(1)}, f32[16,128]{1,0:T(8,128)S(1)}, u32[]{:S(2)}, u32[]{:S(2)}) collective-permute-start(f32[16,128]{1,0:T(8,128)S(1)} %get-tuple-element.71), channel_id=1, source_target_pairs={{8,16},{16,8},{9,17},{17,9},{10,18},{18,10},{11,19},{19,11},{12,20... | collective-permute-start | bytes 24584 | tf_op jit(solution)/shard_map/ppermute | solution.py:493
  105.1 0.8 copy.14
  105.9 1.7 %collective-permute-done.7.d_ref = f32[16,128]{1,0:T(8,128)S(1)} collective-permute-done((f32[16,128]{1,0:T(8,128)S(1)}, f32[16,128]{1,0:T(8,128)S(1)}, u32[]{:S(2)}, u32[]{:S(2)}) %collective-permute-start.7) | collective-permute-done | bytes 8224 | tf_op jit(solution)/shard_map/ppermute | solution.py:493
  (27 shorter events, 5.7 us)
Async XLA Ops:
  2.5 3.2 %collective-permute-start = (f32[64,256]{1,0:T(8,128)S(1)}, f32[64,256]{1,0:T(8,128)S(1)}, u32[]{:S(2)}, u32[]{:S(2)}) collective-permute-start(f32[64,256]{1,0:T(8,128)S(1)} %get-tuple-element.38.own_ref), channel_id=1, source_target_pairs={{0,1},{1,0},{2,3},{3,2},{4,5},{5,4},{6,7},{7,6},{8,9},{9,8},{10,11... | collective-permute-start | bytes 196616 | tf_op jit(solution)/shard_map/ppermute | solution.py:196
  6.1 2.8 %collective-permute-start.1 = (f32[64,128]{1,0:T(8,128)S(1)}, f32[64,128]{1,0:T(8,128)S(1)}, u32[]{:S(2)}, u32[]{:S(2)}) collective-permute-start(f32[64,128]{1,0:T(8,128)S(1)} %get-tuple-element.42.own_ref), channel_id=1, source_target_pairs={{0,2},{1,3},{2,0},{3,1},{4,6},{5,7},{6,4},{7,5},{8,10},{9,11},{10,... | collective-permute-start | bytes 98312 | tf_op jit(solution)/shard_map/ppermute | solution.py:196
  9.3 3.7 %collective-permute-start.2 = (f32[64,128]{1,0:T(8,128)S(1)}, f32[64,128]{1,0:T(8,128)S(1)}, u32[]{:S(2)}, u32[]{:S(2)}) collective-permute-start(f32[64,128]{1,0:T(8,128)S(1)} %get-tuple-element.44.own_ref), channel_id=1, source_target_pairs={{0,4},{1,5},{2,6},{3,7},{4,0},{5,1},{6,2},{7,3},{8,12},{9,13},{10,... | collective-permute-start | bytes 98312 | tf_op jit(solution)/shard_map/ppermute | solution.py:196
  13.4 46.2 %copy-start = (f32[1,1,128]{2,1,0:T(1,128)S(1)}, f32[1,1,128]{2,1,0:T(1,128)}, u32[]{:S(2)}) copy-start(f32[1,1,128]{2,1,0:T(1,128)} %param.21) | copy-start | bytes 1540
  60.3 27.6 %copy-start.1 = (f32[1,1,512,640]{3,2,1,0:T(8,128)S(1)}, f32[1,1,512,640]{3,2,1,0:T(8,128)}, u32[]{:S(2)}) copy-start(f32[1,1,512,640]{3,2,1,0:T(8,128)} %param.14) | copy-start | bytes 3932164
  60.3 27.6 %copy-start.2 = (f32[64,1,1,512]{3,2,1,0:T(1,128)S(1)}, f32[64,1,1,512]{3,2,1,0:T(1,128)}, u32[]{:S(2)}) copy-start(f32[64,1,1,512]{3,2,1,0:T(1,128)} %load_any.1) | copy-start | bytes 393220
  70.3 1.7 %collective-permute-start.3 = (f32[8,128]{1,0:T(8,128)S(1)}, f32[8,128]{1,0:T(8,128)S(1)}, u32[]{:S(2)}, u32[]{:S(2)}) collective-permute-start(f32[8,128]{1,0:T(8,128)S(1)} %shard_map.131), channel_id=1, source_target_pairs={{0,8},{8,0},{1,9},{9,1},{2,10},{10,2},{3,11},{11,3},{4,12},{12,4},... | collective-permute-start | bytes 12296 | tf_op jit(solution)/shard_map/ppermute | solution.py:339
  83.6 10.6 %all-to-all-start.6 = ((f32[8,64,128]{2,1,0:T(8,128)}), f32[8,64,128]{2,1,0:T(8,128)S(1)}, u32[]{:S(2)}, u32[]{:S(2)}) async-start(f32[8,64,128]{2,1,0:T(8,128)} %get-tuple-element.59), calls=%async_computation.6 | async-start | bytes 524288 | tf_op jit(solution)/shard_map/all_to_all | solution.py:469
  95.3 10.7 %collective-permute-start.4 = (f32[16,128]{1,0:T(8,128)S(1)}, f32[16,128]{1,0:T(8,128)S(1)}, u32[]{:S(2)}, u32[]{:S(2)}) collective-permute-start(f32[16,128]{1,0:T(8,128)S(1)} %get-tuple-element.68), channel_id=1, source_target_pairs={{0,1},{1,0},{2,3},{3,2},{4,5},{5,4},{6,7},{7,6},{8,9},{9,8},{10,11... | collective-permute-start | bytes 24584 | tf_op jit(solution)/shard_map/ppermute | solution.py:490
  96.2 9.7 %collective-permute-start.5 = (f32[16,128]{1,0:T(8,128)S(1)}, f32[16,128]{1,0:T(8,128)S(1)}, u32[]{:S(2)}, u32[]{:S(2)}) collective-permute-start(f32[16,128]{1,0:T(8,128)S(1)} %get-tuple-element.69), channel_id=1, source_target_pairs={{1,2},{3,4},{5,6},{2,1},{4,3},{6,5},{9,10},{11,12},{13,14},{10,9},... | collective-permute-start | bytes 24584 | tf_op jit(solution)/shard_map/ppermute | solution.py:491
  99.5 6.4 %collective-permute-start.6 = (f32[16,128]{1,0:T(8,128)S(1)}, f32[16,128]{1,0:T(8,128)S(1)}, u32[]{:S(2)}, u32[]{:S(2)}) collective-permute-start(f32[16,128]{1,0:T(8,128)S(1)} %get-tuple-element.70), channel_id=1, source_target_pairs={{0,8},{8,0},{16,24},{24,16},{1,9},{9,1},{17,25},{25,17},{2,10},{10... | collective-permute-start | bytes 24584 | tf_op jit(solution)/shard_map/ppermute | solution.py:492
  102.7 5.0 %collective-permute-start.7 = (f32[16,128]{1,0:T(8,128)S(1)}, f32[16,128]{1,0:T(8,128)S(1)}, u32[]{:S(2)}, u32[]{:S(2)}) collective-permute-start(f32[16,128]{1,0:T(8,128)S(1)} %get-tuple-element.71), channel_id=1, source_target_pairs={{8,16},{16,8},{9,17},{17,9},{10,18},{18,10},{11,19},{19,11},{12,20... | collective-permute-start | bytes 24584 | tf_op jit(solution)/shard_map/ppermute | solution.py:493

commit v3 on v2

--- a/solution.py
+++ b/solution.py
@@ -103,7 +103,8 @@
         return x[:, number * edge : (number + 1) * edge]
 
     def exchange_shape(level):
-        lanes = (2 + 2 * (x_levels - 1 - level)) * edge
+        kept = x_levels - 1 - level
+        lanes = (2 + 2 * kept + (x_levels << level if kept else 0)) * edge
         return (pair, -(-lanes // LANES) * LANES)
 
     def pieces_of(x, first, count):
@@ -135,6 +136,10 @@
             for x in (xi, xo)
             for k in range(x_levels - 1)
         ]
+        odd_row = bit(my_row(), 0) == 1
+        travelling += [
+            jnp.where(odd_row, edge_of(xi[k], 0), edge_of(xi[k], 2)) for k in range(x_levels)
+        ]
         out_ref[...] = pad_lanes(
             jnp.concatenate([edge_of(h, 3), edge_of(h, 1)] + travelling, axis=1), out_ref.shape[1]
         )
@@ -173,7 +178,7 @@
         w = dot_t(v, solve_ref[level])
         w_out[...] = w
         if kept:
-            next_ref, ends_ref = rest
+            next_ref, ends_ref, row_ref = rest
             outer = [edge_of(x, 2 + kept) for x in (left_child, right_child)]
             spread = dot(w, jnp.concatenate([xo_ref[level]] + outer, axis=1))
             h_out[...] = h_ref[...] + spread[:, :leaf]
@@ -184,6 +189,14 @@
             )
             mine = jnp.where(bit(my_column(), level + 1) == 1, right_child, left_child)
             travelling = pieces_of(mine, 3, kept - 1) + pieces_of(mine, 3 + kept, kept - 1)
+            known = x_levels << level
+            row = pieces_of(left_child, 2 + 2 * kept, known)
+            row += pieces_of(right_child, 2 + 2 * kept, known)
+            if kept > 1:
+                travelling += row
+                row_ref[...] = jnp.zeros_like(row_ref)
+            else:
+                row_ref[...] = jnp.concatenate(row, axis=1)
             next_ref[...] = pad_lanes(
                 jnp.concatenate([left, right] + travelling, axis=1), next_ref.shape[1]
             )
@@ -196,14 +209,18 @@
         got = lax.ppermute(to_send, "box", [(i, i ^ (1 << level)) for i in range(cols)])
         outs = [(waves, leaf), (waves, pair)]
         if level < x_levels - 1:
+            last = level == x_levels - 2
             outs += [exchange_shape(level + 1), (pair, pair)]
+            outs += [(pair, iface * x_levels // 4) if last else (8, LANES)]
         h, w, *rest = fused(
             functools.partial(x_body, level), outs, h, to_send, got, xs_all, xo_all
         )
         x_keep.append(w)
         if rest:
-            to_send, end = rest
+            to_send, end, row_in = rest
             ends.append(end)
+    top = x_levels - 1
+    other_in = lax.ppermute(row_in, "box", [(i, i ^ (1 << top)) for i in range(cols)])
 
     def group(level):
         return tuple(row_axes[y_levels - 1 - level :]) + ("box",)
@@ -228,7 +245,7 @@
             piece = packed(facing[target * share : (target + 1) * share], edge)
             out[target * cols : (target + 1) * cols] = jnp.broadcast_to(piece, (cols,) + piece.shape)
 
-    def offer_body(level, h_ref, out_ref):
+    def offer_body(level, h_ref, early_ref, out_ref):
         store_offer(level, h_ref[...], out_ref)
 
     def solve_body(level, got_ref, solve_ref, out_ref, v_ref):
@@ -343,25 +360,55 @@
             )
         return total
 
-    x_lanes = -(-x_levels * edge // LANES) * LANES
-
-    def x_terms_body(g_ref, w_ref, sum_ref, xi_ref, g_out, out_ref):
-        g = with_row_edge(0, g_ref[...], w_ref[...], unpacked_parts(0, sum_ref))
+    x_lanes = -(-(x_levels + 1) * edge // LANES) * LANES
+
+    def split_body(g_ref, w_ref, sum_ref, yi_ref, g_out, own_out, other_out):
+        g = with_row_edge(1, g_ref[...], w_ref[...], unpacked_parts(1, sum_ref))
         g_out[...] = g
-        terms = [dot_t(g, xi_ref[k]) for k in range(x_levels)]
+        terms = dot_t(g, yi_ref[0])
+        odd_row = bit(my_row(), 0) == 1
+        low, high = (
+            jnp.concatenate(
+                [terms[:, c * pair + side * edge :][:, :edge] for c in range(cols)], axis=1
+            )
+            for side in range(2)
+        )
+        own_out[...] = jnp.where(odd_row, high, low)
+        other_out[...] = jnp.where(odd_row, low, high)
+
+    def x_terms_body(g_ref, w_ref, own_ref, got_ref, xi_ref, row_ref, other_ref, out_ref):
+        q = own_ref[...] + got_ref[...]
+        g = with_row_edge(0, g_ref[...], w_ref[...], 0.0)
+        is_right = bit(my_column(), top) == 1
+        row, other = row_ref[...], other_ref[...]
+        matrices = [jnp.where(is_right, other, row), jnp.where(is_right, row, other)]
+        half = cols // 2
+        parts = []
+        for k in range(x_levels):
+            known = dot_t(g, xi_ref[k])
+            size = 2 << k
+            nodes = []
+            for first in range(0, cols, size):
+                matrix = jnp.concatenate(
+                    [
+                        edge_of(matrices[c // half], c % half * x_levels + k)
+                        for c in range(first, first + size)
+                    ],
+                    axis=1,
+                )
+                terms = dot_t(q[:, first * edge : (first + size) * edge], matrix)
+                inside = my_column() >> (k + 1) == first >> (k + 1)
+                nodes.append(terms + jnp.where(inside, known, 0.0))
+            parts.append(nodes)
         for c in range(cols):
-            picked = []
-            for k in range(x_levels):
-                start = bit(c, k) * edge
-                same = my_column() >> (k + 1) == c >> (k + 1)
-                picked.append(jnp.where(same, terms[k][:, start : start + edge], 0.0))
-            out_ref[c] = pad_lanes(jnp.concatenate(picked, axis=1), x_lanes)
-
-    def finish_body(g_ref, h0_ref, got_ref, lo_ref, *refs):
+            picked = [edge_of(parts[k][c >> (k + 1)], bit(c, k)) for k in range(x_levels)]
+            out_ref[c] = pad_lanes(jnp.concatenate(picked + [edge_of(q, c)], axis=1), x_lanes)
+
+    def finish_body(g_ref, w_ref, h0_ref, got_ref, lo_ref, *refs):
         keep_ref, ends_ref = refs[:x_levels], refs[x_levels : 2 * x_levels - 1]
         g_out, t_out, *faces = refs[2 * x_levels - 1 :]
-        g = g_ref[...]
         q = jnp.sum(got_ref[...], axis=0)
+        g = with_row_edge(0, g_ref[...], w_ref[...], edge_of(q, x_levels))
         gl = jnp.zeros((waves, edge), f32)
         gr = gl
         for level in reversed(range(x_levels)):
@@ -413,7 +460,7 @@
             axis=1,
         )
 
-    (offer,) = fused(functools.partial(offer_body, 0), [offer_shape(0)], h)
+    (offer,) = fused(functools.partial(offer_body, 0), [offer_shape(0)], h, other_in)
     y_keep = []
     for level in range(y_levels):
         share = waves // span(level)
@@ -446,10 +493,10 @@
                 scratch=[(waves, iface)],
             )
         y_keep.append(w)
-    for level in reversed(range(y_levels)):
+    for level in reversed(range(1, y_levels)):
         (total,) = fused(sum_body, [terms_shape(level)[1:]], swap(terms, level))
         total = collect(total, level)
-        if level > 0:
+        if level > 1:
             g, terms = fused(
                 functools.partial(row_down_body, level),
                 [(waves, leaf), terms_shape(level - 1)],
@@ -458,13 +505,21 @@
                 total,
                 yi_all,
             )
-    g, terms = fused(
+    share = (waves, iface // 2)
+    g, own, other = fused(
+        split_body, [(waves, leaf), share, share], g, y_keep[1], total, yi_all
+    )
+    got = lax.ppermute(other, row_axes[-1], [(0, 1), (1, 0)])
+    (terms,) = fused(
         x_terms_body,
-        [(waves, leaf), (cols, waves, x_lanes)],
+        [(cols, waves, x_lanes)],
         g,
         y_keep[0],
-        total,
+        own,
+        got,
         xi_all,
+        row_in,
+        other_in,
     )
     got = lax.all_to_all(terms, "box", 0, 0, tiled=True)
     face = (waves * edge // LANES, LANES)
@@ -472,6 +527,7 @@
         finish_body,
         [(waves, leaf), (waves, leaf)] + [face] * 4,
         g,
+        y_keep[0],
         h0,
         got,
         out_map,

time: 109 us -> 104 us (0.954)
  blocking collectives: 64.5 us -> 54.2 us
  waiting for transfers between devices: 14.2 us -> 18.1 us
    all_to_all x6 -> x5, blocking collectives: 64.5 us -> 54.2 us  [swap(): return lax.all_to_all(x, group(level), 0, 0, tiled=True)]
    ppermute x3, waiting for transfers between devices: 6.01 us -> 8.99 us  [local(): lax.ppermute(to_send, 'box', [(i, i ^ 1 << level) for i in range(cols)])]
    ppermute x0 -> x2, starting transfers between devices: none -> 2.79 us  [the longest x1 2.38 us: local(): lax.ppermute(row_in, 'box', [(i, i ^ 1 << top) for i in range(cols)])]
    ppermute x3, starting transfers between devices: 3.72 us -> 1.78 us  [local(): lax.ppermute(to_send, 'box', [(i, i ^ 1 << level) for i in range(cols)])]
    pallas_call x14 -> x13, Pallas kernels: 6.25 us -> 6.81 us  [fused(): pl.pallas_call(body, out_shape=[pltpu.VMEM(s, f32) for s in outs], in_spe...]
  transfers between devices with their start and end apart: 9 -> 11, of which waited for: 6 -> 7; matrix products, arithmetic and copies ran while one was open for 2% -> 2% of each run, Pallas kernels for 0% -> 0%
where the time goes in v3:
time: 104 us; the launch traced here: 103 us
  blocking collectives  54.2 us (52%)
  starting transfers between devices  19.1 us (18%)
  waiting for transfers between devices  18.1 us (17%)
  Pallas kernels  8.69 us (8%)
  local copies, waits for them, and re-layouts  1.43 us (1%)
    all_to_all x5, blocking collectives, swap(): return lax.all_to_all(x, group(level), 0, 0, tiled=True)  54.2 us
    ppermute x3, waiting for transfers between devices, local(): lax.ppermute(to_send, 'box', [(i, i ^ 1 << level) for i in range(cols)])  8.99 us
    pallas_call x13, Pallas kernels, fused(): pl.pallas_call(body, out_shape=[pltpu.VMEM(s, f32) for s in outs], in_spe...  6.81 us
    all_to_all x1, waiting for transfers between devices, local(): got = lax.all_to_all(terms, 'box', 0, 0, tiled=True)  6.08 us
    all_to_all x1, starting transfers between devices, local(): got = lax.all_to_all(terms, 'box', 0, 0, tiled=True)  4.05 us
    ppermute x1, starting transfers between devices, local(): lax.ppermute(faces[1], 'box', far(cols))  3.08 us
    ppermute x1, starting transfers between devices, local(): lax.ppermute(faces[3], row_axes, far(rows))  2.58 us
    ppermute x1, starting transfers between devices, local(): lax.ppermute(row_in, 'box', [(i, i ^ 1 << top) for i in range(cols)])  2.38 us
  transfers between devices with their start and end apart: 11, of which 7 were waited for; matrix products, arithmetic and copies ran while one was open for 2% of the time, Pallas kernels for 0%

profile of v3, /device:TPU:9, one launch (start us, length us, event | category | flops | bytes accessed | tf_op | source)
XLA Modules:
  0.0 103.2 jit_solution(15816646118680016133)
XLA Ops:
  0.6 1.9 %shard_map.122 = (f32[64,128]{1,0:T(8,128)S(1)}, f32[64,384]{1,0:T(8,128)S(1)}, f32[3,64,64]{2,1,0:T(8,128)S(1)}, f32[3,64,128]{2,1,0:T(8,128)S(1)}, f32[3,64,12...) custom-call(f32[64,1,1,512]{3,2,1,0:T(1,128)} %load_any.1, ...), custom_call_target="tpu_custom_call" | custom-call | tf_op jit(solution)/shard_map/pallas_call | solution.py:152
  2.5 1.3 %collective-permute-start = (f32[64,384]{1,0:T(8,128)S(1)}, f32[64,384]{1,0:T(8,128)S(1)}, u32[]{:S(2)}, u32[]{:S(2)}) collective-permute-start(f32[64,384]{1,0:T(8,128)S(1)} %get-tuple-element.38.own_ref), channel_id=1, source_target_pairs={{0,1},{1,0},{2,3},{3,2},{4,5},{5,4},{6,7},{7,6},{8,9},{9,8},{10,11... | collective-permute-start | bytes 294920 | tf_op jit(solution)/shard_map/ppermute | solution.py:209
  3.8 2.3 %collective-permute-done.got_ref = f32[64,384]{1,0:T(8,128)S(1)} collective-permute-done((f32[64,384]{1,0:T(8,128)S(1)}, f32[64,384]{1,0:T(8,128)S(1)}, u32[]{:S(2)}, u32[]{:S(2)}) %collective-permute-start) | collective-permute-done | bytes 98336 | tf_op jit(solution)/shard_map/ppermute | solution.py:209
  6.1 0.8 shard_map.123
  7.3 3.0 %collective-permute-done.1.got_ref = f32[64,384]{1,0:T(8,128)S(1)} collective-permute-done((f32[64,384]{1,0:T(8,128)S(1)}, f32[64,384]{1,0:T(8,128)S(1)}, u32[]{:S(2)}, u32[]{:S(2)}) %collective-permute-start.1) | collective-permute-done | bytes 98336 | tf_op jit(solution)/shard_map/ppermute | solution.py:209
  10.8 2.4 %collective-permute-start.3 = (f32[64,384]{1,0:T(8,128)S(1)}, f32[64,384]{1,0:T(8,128)S(1)}, u32[]{:S(2)}, u32[]{:S(2)}) collective-permute-start(f32[64,384]{1,0:T(8,128)S(1)} %get-tuple-element.46.row_ref), channel_id=1, source_target_pairs={{0,4},{1,5},{2,6},{3,7},{4,0},{5,1},{6,2},{7,3},{8,12},{9,13},{10,... | collective-permute-start | bytes 294920 | tf_op jit(solution)/shard_map/ppermute | solution.py:223
  13.2 3.7 %collective-permute-done.2.got_ref = f32[64,128]{1,0:T(8,128)S(1)} collective-permute-done((f32[64,128]{1,0:T(8,128)S(1)}, f32[64,128]{1,0:T(8,128)S(1)}, u32[]{:S(2)}, u32[]{:S(2)}) %collective-permute-start.2) | collective-permute-done | bytes 32800 | tf_op jit(solution)/shard_map/ppermute | solution.py:209
  17.5 14.7 %all_to_all.30.got_ref = f32[16,8,128]{2,1,0:T(8,128)S(1)} all-to-all(f32[16,8,128]{2,1,0:T(8,128)S(1)} %shard_map.126), channel_id=1, replica_groups=mesh['row1'=2,'row0'=2,'box'=8] {'row0','box'}, dimensions={0} | all-to-all | bytes 131072 | tf_op jit(solution)/shard_map/all_to_all | solution.py:232
  32.5 10.1 %all_to_all.31.got_ref = f32[16,16,128]{2,1,0:T(8,128)S(1)} all-to-all(f32[16,16,128]{2,1,0:T(8,128)S(1)} %shard_map.127), channel_id=1, replica_groups=mesh['row1'=2,'row0'=2,'box'=8] {'row0','box'}, dimensions={0} | all-to-all | bytes 262144 | tf_op jit(solution)/shard_map/all_to_all | solution.py:232
  43.3 9.9 %all_to_all.32.got_ref = f32[32,4,128]{2,1,0:T(4,128)S(1)} all-to-all(f32[32,4,128]{2,1,0:T(4,128)S(1)} %get-tuple-element.50), channel_id=1, replica_groups=mesh['row1'=2,'row0'=2,'box'=8] {'row1','row0','box'}, dimensions={0} | all-to-all | bytes 131072 | tf_op jit(solution)/shard_map/all_to_all | solution.py:232
  53.6 9.6 %all_to_all.33.got_ref = f32[32,8,128]{2,1,0:T(8,128)S(1)} all-to-all(f32[32,8,128]{2,1,0:T(8,128)S(1)} %shard_map.129), channel_id=1, replica_groups=mesh['row1'=2,'row0'=2,'box'=8] {'row1','row0','box'}, dimensions={0} | all-to-all | bytes 262144 | tf_op jit(solution)/shard_map/all_to_all | solution.py:232
  63.9 9.9 %all_to_all.34.got_ref = f32[32,8,128]{2,1,0:T(8,128)S(1)} all-to-all(f32[32,8,128]{2,1,0:T(8,128)S(1)} %get-tuple-element.54), channel_id=1, replica_groups=mesh['row1'=2,'row0'=2,'box'=8] {'row1','row0','box'}, dimensions={0} | all-to-all | bytes 262144 | tf_op jit(solution)/shard_map/all_to_all | solution.py:232
  73.8 0.9 collective-permute-start.4
  74.7 0.8 collective-permute-done.4
  76.5 0.9 collective-permute-done.5.got_ref
  77.4 1.3 %shard_map.133 = f32[8,64,128]{2,1,0:T(8,128)} custom-call(f32[64,128]{1,0:T(8,128)S(1)} %get-tuple-element.55.g_ref, f32[64,64]{1,0:T(8,128)S(1)} %get-tuple-element.56.w_ref, f32[64,256]{1,0:T(8,128)S(1)} %get-tuple-element.57.own_ref, f32[64,256]{1,0:T(8,128)S(1)} %collective-permute-done.5.got_ref, f32[3,64,128]{2,1,0:T(8,128)S(1)} %get-tuple-element.59.xi_ref, ...), custom_call_target="tpu_custom_call" | custom-call | tf_op jit(solution)/shard_map/pallas_call | solution.py:37
  78.7 4.1 %all-to-all-start.5 = ((f32[8,64,128]{2,1,0:T(8,128)}), f32[8,64,128]{2,1,0:T(8,128)S(1)}, u32[]{:S(2)}, u32[]{:S(2)}) async-start(f32[8,64,128]{2,1,0:T(8,128)} %shard_map.133), calls=%async_computation.5 | async-start | bytes 524288 | tf_op jit(solution)/shard_map/all_to_all | solution.py:524
  83.3 6.1 %all-to-all-done.5.got_ref = f32[8,64,128]{2,1,0:T(8,128)S(1)} async-done(((f32[8,64,128]{2,1,0:T(8,128)}), f32[8,64,128]{2,1,0:T(8,128)S(1)}, u32[]{:S(2)}, u32[]{:S(2)}) %all-to-all-start.5) | async-done | bytes 262176 | tf_op jit(solution)/shard_map/all_to_all | solution.py:524
  89.4 1.1 %shard_map.134 = (f32[64,128]{1,0:T(8,128)S(1)}, f32[64,128]{1,0:T(8,128)S(1)}, f32[16,128]{1,0:T(8,128)S(1)}, f32[16,128]{1,0:T(8,128)S(1)}, f32[16,128]{1,0:T(8,128)S(1)}, /*index=5*/f32[16,128]{1,0:T(8,128)S(1)}) custom-call(f32[64,128]{1,0:T(8,128)S(1)} %get-tuple-element.55.g_ref, f32[64,64]{1,0:T(8,128)S(1)} %get-tuple-element.56.w_ref, ...), custom_call_target="tpu_custom_call" | custom-call | tf_op jit(solution)/shard_map/pallas_call | solution.py:37
  90.5 1.5 %collective-permute-start.6 = (f32[16,128]{1,0:T(8,128)S(1)}, f32[16,128]{1,0:T(8,128)S(1)}, u32[]{:S(2)}, u32[]{:S(2)}) collective-permute-start(f32[16,128]{1,0:T(8,128)S(1)} %get-tuple-element.68), channel_id=1, source_target_pairs={{0,1},{1,0},{2,3},{3,2},{4,5},{5,4},{6,7},{7,6},{8,9},{9,8},{10,11... | collective-permute-start | bytes 24584 | tf_op jit(solution)/shard_map/ppermute | solution.py:546
  92.0 3.1 %collective-permute-start.7 = (f32[16,128]{1,0:T(8,128)S(1)}, f32[16,128]{1,0:T(8,128)S(1)}, u32[]{:S(2)}, u32[]{:S(2)}) collective-permute-start(f32[16,128]{1,0:T(8,128)S(1)} %get-tuple-element.69), channel_id=1, source_target_pairs={{1,2},{3,4},{5,6},{2,1},{4,3},{6,5},{9,10},{11,12},{13,14},{10,9},... | collective-permute-start | bytes 24584 | tf_op jit(solution)/shard_map/ppermute | solution.py:547
  95.1 2.3 %collective-permute-start.8 = (f32[16,128]{1,0:T(8,128)S(1)}, f32[16,128]{1,0:T(8,128)S(1)}, u32[]{:S(2)}, u32[]{:S(2)}) collective-permute-start(f32[16,128]{1,0:T(8,128)S(1)} %get-tuple-element.70), channel_id=1, source_target_pairs={{0,8},{8,0},{16,24},{24,16},{1,9},{9,1},{17,25},{25,17},{2,10},{10... | collective-permute-start | bytes 24584 | tf_op jit(solution)/shard_map/ppermute | solution.py:548
  97.5 2.6 %collective-permute-start.9 = (f32[16,128]{1,0:T(8,128)S(1)}, f32[16,128]{1,0:T(8,128)S(1)}, u32[]{:S(2)}, u32[]{:S(2)}) collective-permute-start(f32[16,128]{1,0:T(8,128)S(1)} %get-tuple-element.71), channel_id=1, source_target_pairs={{8,16},{16,8},{9,17},{17,9},{10,18},{18,10},{11,19},{19,11},{12,20... | collective-permute-start | bytes 24584 | tf_op jit(solution)/shard_map/ppermute | solution.py:549
  101.1 1.3 %collective-permute-done.9.d_ref = f32[16,128]{1,0:T(8,128)S(1)} collective-permute-done((f32[16,128]{1,0:T(8,128)S(1)}, f32[16,128]{1,0:T(8,128)S(1)}, u32[]{:S(2)}, u32[]{:S(2)}) %collective-permute-start.9) | collective-permute-done | bytes 8224 | tf_op jit(solution)/shard_map/ppermute | solution.py:549
  (29 shorter events, 6.8 us)
Async XLA Ops:
  2.5 3.5 %collective-permute-start = (f32[64,384]{1,0:T(8,128)S(1)}, f32[64,384]{1,0:T(8,128)S(1)}, u32[]{:S(2)}, u32[]{:S(2)}) collective-permute-start(f32[64,384]{1,0:T(8,128)S(1)} %get-tuple-element.38.own_ref), channel_id=1, source_target_pairs={{0,1},{1,0},{2,3},{3,2},{4,5},{5,4},{6,7},{7,6},{8,9},{9,8},{10,11... | collective-permute-start | bytes 294920 | tf_op jit(solution)/shard_map/ppermute | solution.py:209
  6.9 3.5 %collective-permute-start.1 = (f32[64,384]{1,0:T(8,128)S(1)}, f32[64,384]{1,0:T(8,128)S(1)}, u32[]{:S(2)}, u32[]{:S(2)}) collective-permute-start(f32[64,384]{1,0:T(8,128)S(1)} %get-tuple-element.42.own_ref), channel_id=1, source_target_pairs={{0,2},{1,3},{2,0},{3,1},{4,6},{5,7},{6,4},{7,5},{8,10},{9,11},{10,... | collective-permute-start | bytes 294920 | tf_op jit(solution)/shard_map/ppermute | solution.py:209
  10.8 6.5 %collective-permute-start.3 = (f32[64,384]{1,0:T(8,128)S(1)}, f32[64,384]{1,0:T(8,128)S(1)}, u32[]{:S(2)}, u32[]{:S(2)}) collective-permute-start(f32[64,384]{1,0:T(8,128)S(1)} %get-tuple-element.46.row_ref), channel_id=1, source_target_pairs={{0,4},{1,5},{2,6},{3,7},{4,0},{5,1},{6,2},{7,3},{8,12},{9,13},{10,... | collective-permute-start | bytes 294920 | tf_op jit(solution)/shard_map/ppermute | solution.py:223
  13.2 3.8 %collective-permute-start.2 = (f32[64,128]{1,0:T(8,128)S(1)}, f32[64,128]{1,0:T(8,128)S(1)}, u32[]{:S(2)}, u32[]{:S(2)}) collective-permute-start(f32[64,128]{1,0:T(8,128)S(1)} %get-tuple-element.44.own_ref), channel_id=1, source_target_pairs={{0,4},{1,5},{2,6},{3,7},{4,0},{5,1},{6,2},{7,3},{8,12},{9,13},{10,... | collective-permute-start | bytes 98312 | tf_op jit(solution)/shard_map/ppermute | solution.py:209
  17.3 45.9 %copy-start = (f32[1,1,128]{2,1,0:T(1,128)S(1)}, f32[1,1,128]{2,1,0:T(1,128)}, u32[]{:S(2)}) copy-start(f32[1,1,128]{2,1,0:T(1,128)} %param.21) | copy-start | bytes 1540
  63.9 18.8 %copy-start.1 = (f32[1,1,512,640]{3,2,1,0:T(8,128)S(1)}, f32[1,1,512,640]{3,2,1,0:T(8,128)}, u32[]{:S(2)}) copy-start(f32[1,1,512,640]{3,2,1,0:T(8,128)} %param.14) | copy-start | bytes 3932164
  63.9 18.8 %copy-start.2 = (f32[64,1,1,512]{3,2,1,0:T(1,128)S(1)}, f32[64,1,1,512]{3,2,1,0:T(1,128)}, u32[]{:S(2)}) copy-start(f32[64,1,1,512]{3,2,1,0:T(1,128)} %load_any.1) | copy-start | bytes 393220
  73.8 1.7 %collective-permute-start.4 = (f32[8,128]{1,0:T(8,128)S(1)}, f32[8,128]{1,0:T(8,128)S(1)}, u32[]{:S(2)}, u32[]{:S(2)}) collective-permute-start(f32[8,128]{1,0:T(8,128)S(1)} %shard_map.131), channel_id=1, source_target_pairs={{0,8},{8,0},{1,9},{9,1},{2,10},{10,2},{3,11},{11,3},{4,12},{12,4},... | collective-permute-start | bytes 12296 | tf_op jit(solution)/shard_map/ppermute | solution.py:356
  76.0 1.3 %collective-permute-start.5 = (f32[64,256]{1,0:T(8,128)S(1)}, f32[64,256]{1,0:T(8,128)S(1)}, u32[]{:S(2)}, u32[]{:S(2)}) collective-permute-start(f32[64,256]{1,0:T(8,128)S(1)} %get-tuple-element.58), channel_id=1, source_target_pairs={{0,8},{8,0},{1,9},{9,1},{2,10},{10,2},{3,11},{11,3},{4,12},{12,4},... | collective-permute-start | bytes 196616 | tf_op jit(solution)/shard_map/ppermute | solution.py:512
  78.7 10.8 %all-to-all-start.5 = ((f32[8,64,128]{2,1,0:T(8,128)}), f32[8,64,128]{2,1,0:T(8,128)S(1)}, u32[]{:S(2)}, u32[]{:S(2)}) async-start(f32[8,64,128]{2,1,0:T(8,128)} %shard_map.133), calls=%async_computation.5 | async-start | bytes 524288 | tf_op jit(solution)/shard_map/all_to_all | solution.py:524
  90.5 10.6 %collective-permute-start.6 = (f32[16,128]{1,0:T(8,128)S(1)}, f32[16,128]{1,0:T(8,128)S(1)}, u32[]{:S(2)}, u32[]{:S(2)}) collective-permute-start(f32[16,128]{1,0:T(8,128)S(1)} %get-tuple-element.68), channel_id=1, source_target_pairs={{0,1},{1,0},{2,3},{3,2},{4,5},{5,4},{6,7},{7,6},{8,9},{9,8},{10,11... | collective-permute-start | bytes 24584 | tf_op jit(solution)/shard_map/ppermute | solution.py:546
  92.0 9.1 %collective-permute-start.7 = (f32[16,128]{1,0:T(8,128)S(1)}, f32[16,128]{1,0:T(8,128)S(1)}, u32[]{:S(2)}, u32[]{:S(2)}) collective-permute-start(f32[16,128]{1,0:T(8,128)S(1)} %get-tuple-element.69), channel_id=1, source_target_pairs={{1,2},{3,4},{5,6},{2,1},{4,3},{6,5},{9,10},{11,12},{13,14},{10,9},... | collective-permute-start | bytes 24584 | tf_op jit(solution)/shard_map/ppermute | solution.py:547
  95.1 6.0 %collective-permute-start.8 = (f32[16,128]{1,0:T(8,128)S(1)}, f32[16,128]{1,0:T(8,128)S(1)}, u32[]{:S(2)}, u32[]{:S(2)}) collective-permute-start(f32[16,128]{1,0:T(8,128)S(1)} %get-tuple-element.70), channel_id=1, source_target_pairs={{0,8},{8,0},{16,24},{24,16},{1,9},{9,1},{17,25},{25,17},{2,10},{10... | collective-permute-start | bytes 24584 | tf_op jit(solution)/shard_map/ppermute | solution.py:548
  97.5 5.0 %collective-permute-start.9 = (f32[16,128]{1,0:T(8,128)S(1)}, f32[16,128]{1,0:T(8,128)S(1)}, u32[]{:S(2)}, u32[]{:S(2)}) collective-permute-start(f32[16,128]{1,0:T(8,128)S(1)} %get-tuple-element.71), channel_id=1, source_target_pairs={{8,16},{16,8},{9,17},{17,9},{10,18},{18,10},{11,19},{19,11},{12,20... | collective-permute-start | bytes 24584 | tf_op jit(solution)/shard_map/ppermute | solution.py:549

commit v4 on v3

--- a/solution.py
+++ b/solution.py
@@ -32,7 +32,7 @@
     return dot(a, b, 1)
 
 
-def fused(body, outs, *args, scratch=()):
+def fused(body, outs, *args, scratch=(), aliases=None):
     vmem = pl.BlockSpec(memory_space=pltpu.VMEM)
     return pl.pallas_call(
         body,
@@ -40,6 +40,7 @@
         in_specs=[vmem] * len(args),
         out_specs=[vmem] * len(outs),
         scratch_shapes=[pltpu.VMEM(s, f32) for s in scratch],
+        input_output_aliases=aliases or {},
         compiler_params=pltpu.CompilerParams(vmem_limit_bytes=12 << 20),
     )(*args)
 
@@ -104,7 +105,7 @@
 
     def exchange_shape(level):
         kept = x_levels - 1 - level
-        lanes = (2 + 2 * kept + (x_levels << level if kept else 0)) * edge
+        lanes = (2 + 2 * kept) * edge
         return (pair, -(-lanes // LANES) * LANES)
 
     def pieces_of(x, first, count):
@@ -113,15 +114,55 @@
     kept_from_start = [x_solve, jnp.swapaxes(x_out, 3, 4), x_in, y_solve, y_out, y_in]
     kept_from_start = [x[:, 0, 0] for x in kept_from_start] + [leaf_out_map[0, 0]]
 
+    whole_solve = iface * iface <= 1 << 18
+    in_lanes = -(-x_levels * edge // LANES) * LANES
+    width = iface if whole_solve else 4 * in_lanes
+    runs = width // in_lanes
+    in_rows = pair // runs
+    solve_rows = edge if whole_solve else 0
+
+    def held_shape(count):
+        return (count, solve_rows + in_rows, width)
+
+    def passed_on(held, bit_no):
+        return lax.ppermute(held, "box", [(i, i ^ (1 << bit_no)) for i in range(cols)])
+
+    steps = [x_levels - 1] + list(range(x_levels - 1))
+    joined_at = [0] + list(range(2, x_levels))
+
+    def held_of(c, held_ref, moved_ref):
+        place = sum(bit(c, b) << k for k, b in enumerate(steps[:-1]))
+        same = bit(my_column(), steps[-1]) == bit(c, steps[-1])
+        return jnp.where(same, held_ref[place], moved_ref[place])
+
+    def join(step, held_ref, moved_ref, both_ref):
+        high = bit(my_column(), steps[step]) == 1
+        both_ref[: 1 << step] = jnp.where(high, moved_ref[...], held_ref[...])
+        both_ref[1 << step :] = jnp.where(high, held_ref[...], moved_ref[...])
+
     def start_body(load_any, map_any, *refs):
         count = len(kept_from_start)
-        sources, (h_ref, out_ref) = refs[:count], refs[count : count + 2]
-        targets = refs[count + 2 : 2 * count + 2]
-        load_v, map_v, sems = refs[2 * count + 2 :]
+        sources, (h_ref, out_ref, shared_ref) = refs[:count], refs[count : count + 3]
+        targets = refs[count + 3 : 2 * count + 3]
+        load_v, map_v, sems = refs[2 * count + 3 :]
+        odd_row = bit(my_row(), 0)
+        sent = []
+        if whole_solve:
+            sent = [
+                pltpu.make_async_copy(
+                    sources[3].at[0, pl.ds(odd_row * edge, edge)],
+                    shared_ref.at[0, pl.ds(0, edge)],
+                    sems.at[count + 2],
+                )
+            ]
         pairs = [(load_any, load_v), (map_any, map_v)] + list(zip(sources, targets))
         order = [0, 1, 4, 3, 2, 5, 6, 7, 8]
         copies = [pltpu.make_async_copy(a, b, sems.at[i]) for i, (a, b) in enumerate(pairs)]
-        for i in order:
+        for i in order[:4]:
+            copies[i].start()
+        for copy in sent:
+            copy.start()
+        for i in order[4:]:
             copies[i].start()
         copies[0].wait()
         copies[1].wait()
@@ -136,28 +177,40 @@
             for x in (xi, xo)
             for k in range(x_levels - 1)
         ]
-        odd_row = bit(my_row(), 0) == 1
-        travelling += [
-            jnp.where(odd_row, edge_of(xi[k], 0), edge_of(xi[k], 2)) for k in range(x_levels)
-        ]
         out_ref[...] = pad_lanes(
             jnp.concatenate([edge_of(h, 3), edge_of(h, 1)] + travelling, axis=1), out_ref.shape[1]
         )
+        row_in = pad_lanes(
+            jnp.concatenate(
+                [
+                    jnp.where(odd_row == 1, edge_of(xi[k], 0), edge_of(xi[k], 2))
+                    for k in range(x_levels)
+                ],
+                axis=1,
+            ),
+            in_lanes,
+        )
+        row_in = jnp.concatenate(
+            [row_in[i * in_rows : (i + 1) * in_rows] for i in range(runs)], axis=1
+        )
+        shared_ref[0, solve_rows:] = row_in
+        for copy in sent:
+            copy.wait()
         for i in order[4:]:
             copies[i].wait()
 
     anywhere, vmem = (pl.BlockSpec(memory_space=m) for m in (pl.ANY, pltpu.VMEM))
     count = len(kept_from_start)
-    outs = [(waves, leaf), exchange_shape(0)] + [x.shape for x in kept_from_start]
-    h0, to_send, *placed = pl.pallas_call(
+    outs = [(waves, leaf), exchange_shape(0), held_shape(1)] + [x.shape for x in kept_from_start]
+    h0, to_send, held, *placed = pl.pallas_call(
         start_body,
         out_shape=[pltpu.VMEM(s, f32) for s in outs],
         in_specs=[anywhere] * (count + 2),
-        out_specs=[vmem] * (count + 2),
+        out_specs=[vmem] * len(outs),
         scratch_shapes=[
             pltpu.VMEM(load.shape, f32),
             pltpu.VMEM((leaf, inner), f32),
-            pltpu.SemaphoreType.DMA((count + 2,)),
+            pltpu.SemaphoreType.DMA((count + 3,)),
         ],
         compiler_params=pltpu.CompilerParams(
             vmem_limit_bytes=START_ROOM - sum(4 * math.prod(s) for s in outs)
@@ -168,8 +221,12 @@
         "wk,ik->wi", load_here, leaf_field_map[0, 0, :, leaf:], precision=lax.Precision.HIGH
     )
 
-    def x_body(level, h_ref, own_ref, got_ref, solve_ref, xo_ref, h_out, w_out, *rest):
+    def x_body(level, h_ref, own_ref, got_ref, solve_ref, xo_ref, *rest):
         kept = x_levels - 1 - level
+        rest = list(rest)
+        if level in joined_at:
+            join(joined_at.index(level), rest.pop(0), rest.pop(0), rest.pop())
+        h_out, w_out, *rest = rest
         is_right = bit(my_column(), level) == 1
         own, got = own_ref[...], got_ref[...]
         left_child = jnp.where(is_right, got, own)
@@ -178,7 +235,7 @@
         w = dot_t(v, solve_ref[level])
         w_out[...] = w
         if kept:
-            next_ref, ends_ref, row_ref = rest
+            next_ref, ends_ref = rest
             outer = [edge_of(x, 2 + kept) for x in (left_child, right_child)]
             spread = dot(w, jnp.concatenate([xo_ref[level]] + outer, axis=1))
             h_out[...] = h_ref[...] + spread[:, :leaf]
@@ -189,14 +246,6 @@
             )
             mine = jnp.where(bit(my_column(), level + 1) == 1, right_child, left_child)
             travelling = pieces_of(mine, 3, kept - 1) + pieces_of(mine, 3 + kept, kept - 1)
-            known = x_levels << level
-            row = pieces_of(left_child, 2 + 2 * kept, known)
-            row += pieces_of(right_child, 2 + 2 * kept, known)
-            if kept > 1:
-                travelling += row
-                row_ref[...] = jnp.zeros_like(row_ref)
-            else:
-                row_ref[...] = jnp.concatenate(row, axis=1)
             next_ref[...] = pad_lanes(
                 jnp.concatenate([left, right] + travelling, axis=1), next_ref.shape[1]
             )
@@ -205,22 +254,25 @@
 
     h = h0
     x_keep, ends = [], []
+    moved = passed_on(held, steps[0])
     for level in range(x_levels):
         got = lax.ppermute(to_send, "box", [(i, i ^ (1 << level)) for i in range(cols)])
         outs = [(waves, leaf), (waves, pair)]
+        args = [h, to_send, got, xs_all, xo_all]
         if level < x_levels - 1:
-            last = level == x_levels - 2
             outs += [exchange_shape(level + 1), (pair, pair)]
-            outs += [(pair, iface * x_levels // 4) if last else (8, LANES)]
-        h, w, *rest = fused(
-            functools.partial(x_body, level), outs, h, to_send, got, xs_all, xo_all
-        )
+        if level in joined_at:
+            step = joined_at.index(level)
+            outs.append(held_shape(2 << step))
+            args += [held, moved]
+        h, w, *rest = fused(functools.partial(x_body, level), outs, *args)
         x_keep.append(w)
+        if level in joined_at:
+            held = rest.pop()
+            moved = passed_on(held, steps[step + 1])
         if rest:
-            to_send, end, row_in = rest
+            to_send, end = rest
             ends.append(end)
-    top = x_levels - 1
-    other_in = lax.ppermute(row_in, "box", [(i, i ^ (1 << top)) for i in range(cols)])
 
     def group(level):
         return tuple(row_axes[y_levels - 1 - level :]) + ("box",)
@@ -231,24 +283,27 @@
     def swap(x, level):
         return lax.all_to_all(x, group(level), 0, 0, tiled=True)
 
+    def shares(level):
+        return 1 if level == 0 and whole_solve else span(level)
+
     def offer_shape(level):
-        size = span(level)
-        return (size * cols, waves // size * edge // LANES, LANES)
+        return (span(level) * cols, waves // shares(level) * edge // LANES, LANES)
 
     def store_offer(level, h, out):
         size = span(level)
-        share = waves // size
+        share = waves // shares(level)
         facing = jnp.where(
             lax.rem(my_row(), size) == size // 2 - 1, edge_of(h, 2), edge_of(h, 0)
         )
         for target in range(size):
-            piece = packed(facing[target * share : (target + 1) * share], edge)
+            start = target * share % waves
+            piece = packed(facing[start : start + share], edge)
             out[target * cols : (target + 1) * cols] = jnp.broadcast_to(piece, (cols,) + piece.shape)
 
-    def offer_body(level, h_ref, early_ref, out_ref):
+    def offer_body(level, h_ref, out_ref):
         store_offer(level, h_ref[...], out_ref)
 
-    def solve_body(level, got_ref, solve_ref, out_ref, v_ref):
+    def gather_v(level, got_ref, v_ref):
         size = span(level)
         low = (size // 2 - 1) * cols
         run = got_ref.shape[1]
@@ -258,6 +313,9 @@
                 for k in range(LANES // edge):
                     start = c * pair + side * edge
                     v_ref[k * run : (k + 1) * run, start : start + edge] = edge_of(piece, k)
+
+    def solve_body(level, got_ref, solve_ref, out_ref, v_ref):
+        gather_v(level, got_ref, v_ref)
         w = packed(dot_t(v_ref[...], solve_ref[level]), pair)
         out_ref[...] = jnp.broadcast_to(w, out_ref.shape)
 
@@ -281,6 +339,28 @@
                     ]
         return w_ref[...]
 
+    def half_body(got_ref, held_ref, moved_ref, out_ref, v_ref):
+        gather_v(0, got_ref, v_ref)
+        solve = jnp.concatenate(
+            [held_of(c, held_ref, moved_ref)[:solve_rows] for c in range(cols)], axis=0
+        )
+        out_ref[...] = dot_t(v_ref[...], solve)
+
+    def whole_body(h_ref, mine_ref, other_ref, yo_ref, h_out, w_out, next_ref, w_ref):
+        mine, other = mine_ref[...], other_ref[...]
+        odd_row = bit(my_row(), 0) == 1
+        for side, half in enumerate(
+            (jnp.where(odd_row, other, mine), jnp.where(odd_row, mine, other))
+        ):
+            for c in range(cols):
+                start = c * pair + side * edge
+                w_ref[:, start : start + edge] = edge_of(half, c)
+        w_all = w_ref[...]
+        w_out[...] = own_columns(w_all)
+        h = h_ref[...] + dot_t(w_all, yo_ref[0])
+        h_out[...] = h
+        store_offer(1, h, next_ref)
+
     def spread_body(level, h_ref, got_ref, yo_ref, h_out, w_out, next_ref, w_ref):
         w_all = gather_w(level, got_ref, w_ref)
         w_out[...] = own_columns(w_all)
@@ -376,13 +456,17 @@
         own_out[...] = jnp.where(odd_row, high, low)
         other_out[...] = jnp.where(odd_row, low, high)
 
-    def x_terms_body(g_ref, w_ref, own_ref, got_ref, xi_ref, row_ref, other_ref, out_ref):
+    def x_terms_body(g_ref, w_ref, own_ref, got_ref, xi_ref, held_ref, moved_ref, out_ref):
         q = own_ref[...] + got_ref[...]
         g = with_row_edge(0, g_ref[...], w_ref[...], 0.0)
-        is_right = bit(my_column(), top) == 1
-        row, other = row_ref[...], other_ref[...]
-        matrices = [jnp.where(is_right, other, row), jnp.where(is_right, row, other)]
-        half = cols // 2
+        row_in = []
+        for c in range(cols):
+            held = held_of(c, held_ref, moved_ref)[solve_rows:]
+            row_in.append(
+                jnp.concatenate(
+                    [held[:, i * in_lanes : (i + 1) * in_lanes] for i in range(runs)], axis=0
+                )
+            )
         parts = []
         for k in range(x_levels):
             known = dot_t(g, xi_ref[k])
@@ -390,11 +474,7 @@
             nodes = []
             for first in range(0, cols, size):
                 matrix = jnp.concatenate(
-                    [
-                        edge_of(matrices[c // half], c % half * x_levels + k)
-                        for c in range(first, first + size)
-                    ],
-                    axis=1,
+                    [edge_of(row_in[c], k) for c in range(first, first + size)], axis=1
                 )
                 terms = dot_t(q[:, first * edge : (first + size) * edge], matrix)
                 inside = my_column() >> (k + 1) == first >> (k + 1)
@@ -460,9 +540,29 @@
             axis=1,
         )
 
-    (offer,) = fused(functools.partial(offer_body, 0), [offer_shape(0)], h, other_in)
+    (offer,) = fused(functools.partial(offer_body, 0), [offer_shape(0)], h)
     y_keep = []
     for level in range(y_levels):
+        if level == 0 and whole_solve:
+            (mine,) = fused(
+                half_body,
+                [(waves, iface // 2)],
+                swap(offer, 0),
+                held,
+                moved,
+                scratch=[(waves, iface)],
+            )
+            h, w, offer = fused(
+                whole_body,
+                [(waves, leaf), (waves, pair), offer_shape(1)],
+                h,
+                mine,
+                lax.ppermute(mine, row_axes[-1], [(0, 1), (1, 0)]),
+                yo_all,
+                scratch=[(waves, iface)],
+            )
+            y_keep.append(w)
+            continue
         share = waves // span(level)
         (w_offer,) = fused(
             functools.partial(solve_body, level),
@@ -518,8 +618,8 @@
         own,
         got,
         xi_all,
-        row_in,
-        other_in,
+        held,
+        moved,
     )
     got = lax.all_to_all(terms, "box", 0, 0, tiled=True)
     face = (waves * edge // LANES, LANES)

time: 104 us -> 97.1 us (0.934)
  blocking collectives: 54.2 us -> 43.6 us
  starting transfers between devices: 19.1 us -> 23.4 us
    all_to_all x5 -> x4, blocking collectives: 54.2 us -> 43.6 us  [swap(): return lax.all_to_all(x, group(level), 0, 0, tiled=True)]
    ppermute x3, starting transfers between devices: 1.78 us -> 4.38 us  [local(): lax.ppermute(to_send, 'box', [(i, i ^ 1 << level) for i in range(cols)])]
    ppermute x3, waiting for transfers between devices: 8.99 us -> 6.56 us  [local(): lax.ppermute(to_send, 'box', [(i, i ^ 1 << level) for i in range(cols)])]
    ppermute x1 -> x4, starting transfers between devices: 2.38 us -> 4.74 us  [the longest x3 3.72 us: passed_on(): lax.ppermute(held, 'box', [(i, i ^ 1 << bit_no) for i in range(cols)])]
    ppermute x1 -> x4, waiting for transfers between devices: 0.01 us -> 2 us  [the longest x3 1.1 us: passed_on(): lax.ppermute(held, 'box', [(i, i ^ 1 << bit_no) for i in range(cols)])]
    ppermute x1, starting transfers between devices: 1.55 us -> 0.07 us  [local(): lax.ppermute(faces[0], 'box', near(cols))]
  transfers between devices with their start and end apart: 11 -> 14, of which waited for: 7 -> 10; matrix products, arithmetic and copies ran while one was open for 2% -> 2% of each run, Pallas kernels for 0% -> 1%
where the time goes in v4:
time: 97.1 us; the launch traced here: 96.4 us
  blocking collectives  43.6 us (45%)
  starting transfers between devices  23.4 us (24%)
  waiting for transfers between devices  17.8 us (18%)
  Pallas kernels  8.47 us (9%)
  local copies, waits for them, and re-layouts  1.42 us (1%)
    all_to_all x4, blocking collectives, swap(): return lax.all_to_all(x, group(level), 0, 0, tiled=True)  43.6 us
    ppermute x3, waiting for transfers between devices, local(): lax.ppermute(to_send, 'box', [(i, i ^ 1 << level) for i in range(cols)])  6.56 us
    pallas_call x13, Pallas kernels, fused(): pl.pallas_call(body, out_shape=[pltpu.VMEM(s, f32) for s in outs], in_spe...  6.55 us
    all_to_all x1, waiting for transfers between devices, local(): got = lax.all_to_all(terms, 'box', 0, 0, tiled=True)  6.08 us
    ppermute x3, starting transfers between devices, local(): lax.ppermute(to_send, 'box', [(i, i ^ 1 << level) for i in range(cols)])  4.38 us
    all_to_all x1, starting transfers between devices, local(): got = lax.all_to_all(terms, 'box', 0, 0, tiled=True)  4.04 us
    ppermute x3, starting transfers between devices, passed_on(): lax.ppermute(held, 'box', [(i, i ^ 1 << bit_no) for i in range(cols)])  3.72 us
    ppermute x1, starting transfers between devices, local(): lax.ppermute(faces[2], row_axes, near(rows))  3.19 us
  transfers between devices with their start and end apart: 14, of which 10 were waited for; matrix products, arithmetic and copies ran while one was open for 2% of the time, Pallas kernels for 1%

profile of v4, /device:TPU:9, one launch (start us, length us, event | category | flops | bytes accessed | tf_op | source)
XLA Modules:
  0.0 96.4 jit_solution(1027571003048065575)
XLA Ops:
  0.6 1.9 %shard_map.122 = (f32[64,128]{1,0:T(8,128)S(1)}, f32[64,256]{1,0:T(8,128)S(1)}, f32[1,48,512]{2,1,0:T(8,128)S(1)}, f32[3,64,64]{2,1,0:T(8,128)S(1)}, f32[3,64,12...) custom-call(f32[64,1,1,512]{3,2,1,0:T(1,128)} %load_any.1, ...), custom_call_target="tpu_custom_call" | custom-call | tf_op jit(solution)/shard_map/pallas_call | solution.py:205
  2.6 2.4 %collective-permute-start.1 = (f32[1,48,512]{2,1,0:T(8,128)S(1)}, f32[1,48,512]{2,1,0:T(8,128)S(1)}, u32[]{:S(2)}, u32[]{:S(2)}) collective-permute-start(f32[1,48,512]{2,1,0:T(8,128)S(1)} %get-tuple-element.43.rest_0_), channel_id=1, source_target_pairs={{0,4},{1,5},{2,6},{3,7},{4,0},{5,1},{6,2},{7,3},{8,12},{9,13},{10,... | collective-permute-start | bytes 294920 | tf_op jit(solution)/shard_map/ppermute | solution.py:128
  4.9 1.2 %collective-permute-start = (f32[64,256]{1,0:T(8,128)S(1)}, f32[64,256]{1,0:T(8,128)S(1)}, u32[]{:S(2)}, u32[]{:S(2)}) collective-permute-start(f32[64,256]{1,0:T(8,128)S(1)} %get-tuple-element.40.own_ref), channel_id=1, source_target_pairs={{0,1},{1,0},{2,3},{3,2},{4,5},{5,4},{6,7},{7,6},{8,9},{9,8},{10,11... | collective-permute-start | bytes 196616 | tf_op jit(solution)/shard_map/ppermute | solution.py:259
  6.1 2.2 %collective-permute-done.got_ref = f32[64,256]{1,0:T(8,128)S(1)} collective-permute-done((f32[64,256]{1,0:T(8,128)S(1)}, f32[64,256]{1,0:T(8,128)S(1)}, u32[]{:S(2)}, u32[]{:S(2)}) %collective-permute-start) | collective-permute-done | bytes 65568 | tf_op jit(solution)/shard_map/ppermute | solution.py:259
  8.3 1.1 %collective-permute-done.1.rest_1_ = f32[1,48,512]{2,1,0:T(8,128)S(1)} collective-permute-done((f32[1,48,512]{2,1,0:T(8,128)S(1)}, f32[1,48,512]{2,1,0:T(8,128)S(1)}, u32[]{:S(2)}, u32[]{:S(2)}) %collective-permute-start.1) | collective-permute-done | bytes 98336 | tf_op jit(solution)/shard_map/ppermute | solution.py:128
  9.9 1.3 %collective-permute-start.4 = (f32[2,48,512]{2,1,0:T(8,128)S(1)}, f32[2,48,512]{2,1,0:T(8,128)S(1)}, u32[]{:S(2)}, u32[]{:S(2)}) collective-permute-start(f32[2,48,512]{2,1,0:T(8,128)S(1)} %get-tuple-element.48.rest_0_), channel_id=1, source_target_pairs={{0,1},{1,0},{2,3},{3,2},{4,5},{5,4},{6,7},{7,6},{8,9},{9,8},{10,11... | collective-permute-start | bytes 589832 | tf_op jit(solution)/shard_map/ppermute | solution.py:128
  11.1 3.1 %collective-permute-done.2.got_ref = f32[64,128]{1,0:T(8,128)S(1)} collective-permute-done((f32[64,128]{1,0:T(8,128)S(1)}, f32[64,128]{1,0:T(8,128)S(1)}, u32[]{:S(2)}, u32[]{:S(2)}) %collective-permute-start.2) | collective-permute-done | bytes 32800 | tf_op jit(solution)/shard_map/ppermute | solution.py:259
  14.6 3.2 %collective-permute-start.3 = (f32[64,128]{1,0:T(8,128)S(1)}, f32[64,128]{1,0:T(8,128)S(1)}, u32[]{:S(2)}, u32[]{:S(2)}) collective-permute-start(f32[64,128]{1,0:T(8,128)S(1)} %get-tuple-element.47.own_ref), channel_id=1, source_target_pairs={{0,4},{1,5},{2,6},{3,7},{4,0},{5,1},{6,2},{7,3},{8,12},{9,13},{10,... | collective-permute-start | bytes 98312 | tf_op jit(solution)/shard_map/ppermute | solution.py:259
  17.8 1.3 %collective-permute-done.3.got_ref = f32[64,128]{1,0:T(8,128)S(1)} collective-permute-done((f32[64,128]{1,0:T(8,128)S(1)}, f32[64,128]{1,0:T(8,128)S(1)}, u32[]{:S(2)}, u32[]{:S(2)}) %collective-permute-start.3) | collective-permute-done | bytes 32800 | tf_op jit(solution)/shard_map/ppermute | solution.py:259
  19.7 14.0 %all_to_all.25.got_ref = f32[16,16,128]{2,1,0:T(8,128)S(1)} all-to-all(f32[16,16,128]{2,1,0:T(8,128)S(1)} %shard_map.126), channel_id=1, replica_groups=mesh['row1'=2,'row0'=2,'box'=8] {'row0','box'}, dimensions={0} | all-to-all | bytes 262144 | tf_op jit(solution)/shard_map/all_to_all | solution.py:284
  34.1 1.0 %collective-permute-start.6 = (f32[64,256]{1,0:T(8,128)S(1)}, f32[64,256]{1,0:T(8,128)S(1)}, u32[]{:S(2)}, u32[]{:S(2)}) collective-permute-start(f32[64,256]{1,0:T(8,128)S(1)} %shard_map.127.mine_ref), channel_id=1, source_target_pairs={{0,8},{8,0},{1,9},{9,1},{2,10},{10,2},{3,11},{11,3},{4,12},{12,4},... | collective-permute-start | bytes 196616 | tf_op jit(solution)/shard_map/ppermute | solution.py:560
  35.1 0.9 collective-permute-done.6.other_ref
  36.7 10.2 %all_to_all.26.got_ref = f32[32,4,128]{2,1,0:T(4,128)S(1)} all-to-all(f32[32,4,128]{2,1,0:T(4,128)S(1)} %get-tuple-element.53), channel_id=1, replica_groups=mesh['row1'=2,'row0'=2,'box'=8] {'row1','row0','box'}, dimensions={0} | all-to-all | bytes 131072 | tf_op jit(solution)/shard_map/all_to_all | solution.py:284
  47.2 9.6 %all_to_all.27.got_ref = f32[32,8,128]{2,1,0:T(8,128)S(1)} all-to-all(f32[32,8,128]{2,1,0:T(8,128)S(1)} %shard_map.129), channel_id=1, replica_groups=mesh['row1'=2,'row0'=2,'box'=8] {'row1','row0','box'}, dimensions={0} | all-to-all | bytes 262144 | tf_op jit(solution)/shard_map/all_to_all | solution.py:284
  57.5 9.9 %all_to_all.28.got_ref = f32[32,8,128]{2,1,0:T(8,128)S(1)} all-to-all(f32[32,8,128]{2,1,0:T(8,128)S(1)} %get-tuple-element.58), channel_id=1, replica_groups=mesh['row1'=2,'row0'=2,'box'=8] {'row1','row0','box'}, dimensions={0} | all-to-all | bytes 262144 | tf_op jit(solution)/shard_map/all_to_all | solution.py:284
  70.1 0.9 collective-permute-done.8.got_ref
  71.0 1.3 %shard_map.133 = f32[8,64,128]{2,1,0:T(8,128)} custom-call(f32[64,128]{1,0:T(8,128)S(1)} %get-tuple-element.59.g_ref, f32[64,64]{1,0:T(8,128)S(1)} %get-tuple-element.60.w_ref, f32[64,256]{1,0:T(8,128)S(1)} %get-tuple-element.61.own_ref, f32[64,256]{1,0:T(8,128)S(1)} %collective-permute-done.8.got_ref, f32[3,64,128]{2,1,0:T(8,128)S(1)} %get-tuple-element.63.xi_ref, ...), custom_call_target="tpu_custom_call" | custom-call | tf_op jit(solution)/shard_map/pallas_call | solution.py:37
  72.3 4.0 %all-to-all-start.4 = ((f32[8,64,128]{2,1,0:T(8,128)}), f32[8,64,128]{2,1,0:T(8,128)S(1)}, u32[]{:S(2)}, u32[]{:S(2)}) async-start(f32[8,64,128]{2,1,0:T(8,128)} %shard_map.133), calls=%async_computation.4 | async-start | bytes 524288 | tf_op jit(solution)/shard_map/all_to_all | solution.py:624
  76.9 6.1 %all-to-all-done.4.got_ref = f32[8,64,128]{2,1,0:T(8,128)S(1)} async-done(((f32[8,64,128]{2,1,0:T(8,128)}), f32[8,64,128]{2,1,0:T(8,128)S(1)}, u32[]{:S(2)}, u32[]{:S(2)}) %all-to-all-start.4) | async-done | bytes 262176 | tf_op jit(solution)/shard_map/all_to_all | solution.py:624
  83.0 1.1 %shard_map.134 = (f32[64,128]{1,0:T(8,128)S(1)}, f32[64,128]{1,0:T(8,128)S(1)}, f32[16,128]{1,0:T(8,128)S(1)}, f32[16,128]{1,0:T(8,128)S(1)}, f32[16,128]{1,0:T(8,128)S(1)}, /*index=5*/f32[16,128]{1,0:T(8,128)S(1)}) custom-call(f32[64,128]{1,0:T(8,128)S(1)} %get-tuple-element.59.g_ref, f32[64,64]{1,0:T(8,128)S(1)} %get-tuple-element.60.w_ref, ...), custom_call_target="tpu_custom_call" | custom-call | tf_op jit(solution)/shard_map/pallas_call | solution.py:37
  84.1 3.1 %collective-permute-start.10 = (f32[16,128]{1,0:T(8,128)S(1)}, f32[16,128]{1,0:T(8,128)S(1)}, u32[]{:S(2)}, u32[]{:S(2)}) collective-permute-start(f32[16,128]{1,0:T(8,128)S(1)} %get-tuple-element.73), channel_id=1, source_target_pairs={{1,2},{3,4},{5,6},{2,1},{4,3},{6,5},{9,10},{11,12},{13,14},{10,9},... | collective-permute-start | bytes 24584 | tf_op jit(solution)/shard_map/ppermute | solution.py:647
  87.2 3.2 %collective-permute-start.11 = (f32[16,128]{1,0:T(8,128)S(1)}, f32[16,128]{1,0:T(8,128)S(1)}, u32[]{:S(2)}, u32[]{:S(2)}) collective-permute-start(f32[16,128]{1,0:T(8,128)S(1)} %get-tuple-element.74), channel_id=1, source_target_pairs={{0,8},{8,0},{16,24},{24,16},{1,9},{9,1},{17,25},{25,17},{2,10},{10... | collective-permute-start | bytes 24584 | tf_op jit(solution)/shard_map/ppermute | solution.py:648
  90.4 2.6 %collective-permute-start.12 = (f32[16,128]{1,0:T(8,128)S(1)}, f32[16,128]{1,0:T(8,128)S(1)}, u32[]{:S(2)}, u32[]{:S(2)}) collective-permute-start(f32[16,128]{1,0:T(8,128)S(1)} %get-tuple-element.75), channel_id=1, source_target_pairs={{8,16},{16,8},{9,17},{17,9},{10,18},{18,10},{11,19},{19,11},{12,20... | collective-permute-start | bytes 24584 | tf_op jit(solution)/shard_map/ppermute | solution.py:649
  94.2 1.2 %collective-permute-done.12.d_ref = f32[16,128]{1,0:T(8,128)S(1)} collective-permute-done((f32[16,128]{1,0:T(8,128)S(1)}, f32[16,128]{1,0:T(8,128)S(1)}, u32[]{:S(2)}, u32[]{:S(2)}) %collective-permute-start.12) | collective-permute-done | bytes 8224 | tf_op jit(solution)/shard_map/ppermute | solution.py:649
  (34 shorter events, 9.0 us)
Async XLA Ops:
  2.6 6.9 %collective-permute-start.1 = (f32[1,48,512]{2,1,0:T(8,128)S(1)}, f32[1,48,512]{2,1,0:T(8,128)S(1)}, u32[]{:S(2)}, u32[]{:S(2)}) collective-permute-start(f32[1,48,512]{2,1,0:T(8,128)S(1)} %get-tuple-element.43.rest_0_), channel_id=1, source_target_pairs={{0,4},{1,5},{2,6},{3,7},{4,0},{5,1},{6,2},{7,3},{8,12},{9,13},{10,... | collective-permute-start | bytes 294920 | tf_op jit(solution)/shard_map/ppermute | solution.py:128
  4.9 3.4 %collective-permute-start = (f32[64,256]{1,0:T(8,128)S(1)}, f32[64,256]{1,0:T(8,128)S(1)}, u32[]{:S(2)}, u32[]{:S(2)}) collective-permute-start(f32[64,256]{1,0:T(8,128)S(1)} %get-tuple-element.40.own_ref), channel_id=1, source_target_pairs={{0,1},{1,0},{2,3},{3,2},{4,5},{5,4},{6,7},{7,6},{8,9},{9,8},{10,11... | collective-permute-start | bytes 196616 | tf_op jit(solution)/shard_map/ppermute | solution.py:259
  9.9 9.2 %collective-permute-start.4 = (f32[2,48,512]{2,1,0:T(8,128)S(1)}, f32[2,48,512]{2,1,0:T(8,128)S(1)}, u32[]{:S(2)}, u32[]{:S(2)}) collective-permute-start(f32[2,48,512]{2,1,0:T(8,128)S(1)} %get-tuple-element.48.rest_0_), channel_id=1, source_target_pairs={{0,1},{1,0},{2,3},{3,2},{4,5},{5,4},{6,7},{7,6},{8,9},{9,8},{10,11... | collective-permute-start | bytes 589832 | tf_op jit(solution)/shard_map/ppermute | solution.py:128
  11.1 3.1 %collective-permute-start.2 = (f32[64,128]{1,0:T(8,128)S(1)}, f32[64,128]{1,0:T(8,128)S(1)}, u32[]{:S(2)}, u32[]{:S(2)}) collective-permute-start(f32[64,128]{1,0:T(8,128)S(1)} %get-tuple-element.45.own_ref), channel_id=1, source_target_pairs={{0,2},{1,3},{2,0},{3,1},{4,6},{5,7},{6,4},{7,5},{8,10},{9,11},{10,... | collective-permute-start | bytes 98312 | tf_op jit(solution)/shard_map/ppermute | solution.py:259
  14.6 4.5 %collective-permute-start.3 = (f32[64,128]{1,0:T(8,128)S(1)}, f32[64,128]{1,0:T(8,128)S(1)}, u32[]{:S(2)}, u32[]{:S(2)}) collective-permute-start(f32[64,128]{1,0:T(8,128)S(1)} %get-tuple-element.47.own_ref), channel_id=1, source_target_pairs={{0,4},{1,5},{2,6},{3,7},{4,0},{5,1},{6,2},{7,3},{8,12},{9,13},{10,... | collective-permute-start | bytes 98312 | tf_op jit(solution)/shard_map/ppermute | solution.py:259
  19.5 14.2 %collective-permute-start.5 = (f32[4,48,512]{2,1,0:T(8,128)S(1)}, f32[4,48,512]{2,1,0:T(8,128)S(1)}, u32[]{:S(2)}, u32[]{:S(2)}) collective-permute-start(f32[4,48,512]{2,1,0:T(8,128)S(1)} %get-tuple-element.50.held_ref), channel_id=1, source_target_pairs={{0,2},{1,3},{2,0},{3,1},{4,6},{5,7},{6,4},{7,5},{8,10},{9,11},{10,... | collective-permute-start | bytes 1179656 | tf_op jit(solution)/shard_map/ppermute | solution.py:128
  33.6 23.1 %copy-start = (f32[1,1,128]{2,1,0:T(1,128)S(1)}, f32[1,1,128]{2,1,0:T(1,128)}, u32[]{:S(2)}) copy-start(f32[1,1,128]{2,1,0:T(1,128)} %param.21) | copy-start | bytes 1540
  34.1 1.9 %collective-permute-start.6 = (f32[64,256]{1,0:T(8,128)S(1)}, f32[64,256]{1,0:T(8,128)S(1)}, u32[]{:S(2)}, u32[]{:S(2)}) collective-permute-start(f32[64,256]{1,0:T(8,128)S(1)} %shard_map.127.mine_ref), channel_id=1, source_target_pairs={{0,8},{8,0},{1,9},{9,1},{2,10},{10,2},{3,11},{11,3},{4,12},{12,4},... | collective-permute-start | bytes 196616 | tf_op jit(solution)/shard_map/ppermute | solution.py:560
  67.4 8.9 %copy-start.1 = (f32[1,1,512,640]{3,2,1,0:T(8,128)S(1)}, f32[1,1,512,640]{3,2,1,0:T(8,128)}, u32[]{:S(2)}) copy-start(f32[1,1,512,640]{3,2,1,0:T(8,128)} %param.14) | copy-start | bytes 3932164
  67.4 8.9 %copy-start.2 = (f32[64,1,1,512]{3,2,1,0:T(1,128)S(1)}, f32[64,1,1,512]{3,2,1,0:T(1,128)}, u32[]{:S(2)}) copy-start(f32[64,1,1,512]{3,2,1,0:T(1,128)} %load_any.1) | copy-start | bytes 393220
  67.4 1.7 %collective-permute-start.7 = (f32[8,128]{1,0:T(8,128)S(1)}, f32[8,128]{1,0:T(8,128)S(1)}, u32[]{:S(2)}, u32[]{:S(2)}) collective-permute-start(f32[8,128]{1,0:T(8,128)S(1)} %shard_map.131), channel_id=1, source_target_pairs={{0,8},{8,0},{1,9},{9,1},{2,10},{10,2},{3,11},{11,3},{4,12},{12,4},... | collective-permute-start | bytes 12296 | tf_op jit(solution)/shard_map/ppermute | solution.py:436
  69.7 1.3 %collective-permute-start.8 = (f32[64,256]{1,0:T(8,128)S(1)}, f32[64,256]{1,0:T(8,128)S(1)}, u32[]{:S(2)}, u32[]{:S(2)}) collective-permute-start(f32[64,256]{1,0:T(8,128)S(1)} %get-tuple-element.62), channel_id=1, source_target_pairs={{0,8},{8,0},{1,9},{9,1},{2,10},{10,2},{3,11},{11,3},{4,12},{12,4},... | collective-permute-start | bytes 196616 | tf_op jit(solution)/shard_map/ppermute | solution.py:612
  72.3 10.7 %all-to-all-start.4 = ((f32[8,64,128]{2,1,0:T(8,128)}), f32[8,64,128]{2,1,0:T(8,128)S(1)}, u32[]{:S(2)}, u32[]{:S(2)}) async-start(f32[8,64,128]{2,1,0:T(8,128)} %shard_map.133), calls=%async_computation.4 | async-start | bytes 524288 | tf_op jit(solution)/shard_map/all_to_all | solution.py:624
  84.1 10.0 %collective-permute-start.10 = (f32[16,128]{1,0:T(8,128)S(1)}, f32[16,128]{1,0:T(8,128)S(1)}, u32[]{:S(2)}, u32[]{:S(2)}) collective-permute-start(f32[16,128]{1,0:T(8,128)S(1)} %get-tuple-element.73), channel_id=1, source_target_pairs={{1,2},{3,4},{5,6},{2,1},{4,3},{6,5},{9,10},{11,12},{13,14},{10,9},... | collective-permute-start | bytes 24584 | tf_op jit(solution)/shard_map/ppermute | solution.py:647
  87.2 6.9 %collective-permute-start.11 = (f32[16,128]{1,0:T(8,128)S(1)}, f32[16,128]{1,0:T(8,128)S(1)}, u32[]{:S(2)}, u32[]{:S(2)}) collective-permute-start(f32[16,128]{1,0:T(8,128)S(1)} %get-tuple-element.74), channel_id=1, source_target_pairs={{0,8},{8,0},{16,24},{24,16},{1,9},{9,1},{17,25},{25,17},{2,10},{10... | collective-permute-start | bytes 24584 | tf_op jit(solution)/shard_map/ppermute | solution.py:648
  90.4 5.0 %collective-permute-start.12 = (f32[16,128]{1,0:T(8,128)S(1)}, f32[16,128]{1,0:T(8,128)S(1)}, u32[]{:S(2)}, u32[]{:S(2)}) collective-permute-start(f32[16,128]{1,0:T(8,128)S(1)} %get-tuple-element.75), channel_id=1, source_target_pairs={{8,16},{16,8},{9,17},{17,9},{10,18},{18,10},{11,19},{19,11},{12,20... | collective-permute-start | bytes 24584 | tf_op jit(solution)/shard_map/ppermute | solution.py:649
  93.0 2.6 %collective-permute-start.9 = (f32[16,128]{1,0:T(8,128)S(1)}, f32[16,128]{1,0:T(8,128)S(1)}, u32[]{:S(2)}, u32[]{:S(2)}) collective-permute-start(f32[16,128]{1,0:T(8,128)S(1)} %get-tuple-element.72), channel_id=1, source_target_pairs={{0,1},{1,0},{2,3},{3,2},{4,5},{5,4},{6,7},{7,6},{8,9},{9,8},{10,11... | collective-permute-start | bytes 24584 | tf_op jit(solution)/shard_map/ppermute | solution.py:646

commit v5 on v2

--- a/solution.py
+++ b/solution.py
@@ -32,7 +32,7 @@
     return dot(a, b, 1)
 
 
-def fused(body, outs, *args, scratch=()):
+def fused(body, outs, *args, scratch=(), aliases=None):
     vmem = pl.BlockSpec(memory_space=pltpu.VMEM)
     return pl.pallas_call(
         body,
@@ -40,6 +40,7 @@
         in_specs=[vmem] * len(args),
         out_specs=[vmem] * len(outs),
         scratch_shapes=[pltpu.VMEM(s, f32) for s in scratch],
+        input_output_aliases=aliases or {},
         compiler_params=pltpu.CompilerParams(vmem_limit_bytes=12 << 20),
     )(*args)
 
@@ -103,32 +104,127 @@
         return x[:, number * edge : (number + 1) * edge]
 
     def exchange_shape(level):
-        lanes = (2 + 2 * (x_levels - 1 - level)) * edge
+        kept = x_levels - 1 - level
+        lanes = (2 + 2 * kept) * edge
         return (pair, -(-lanes // LANES) * LANES)
 
     def pieces_of(x, first, count):
         return [edge_of(x, first + i) for i in range(count)]
 
-    kept_from_start = [x_solve, jnp.swapaxes(x_out, 3, 4), x_in, y_solve, y_out, y_in]
+    whole_solve = y_levels == 2 and iface * iface <= 1 << 18
+    in_lanes = -(-x_levels * edge // LANES) * LANES
+    width = iface if whole_solve else 4 * in_lanes
+    runs = width // in_lanes
+    in_rows = pair // runs
+    solve_rows = edge if whole_solve else 0
+
+    def held_shape(count, first=True, second=True):
+        first_rows = solve_rows + in_rows
+        return (count, first_rows * first + solve_rows * second, width)
+
+    def passed_on(held, bit_no):
+        return lax.ppermute(held, "box", [(i, i ^ (1 << bit_no)) for i in range(cols)])
+
+    steps = [x_levels - 1] + list(range(x_levels - 1))
+    joined_at = [0] + list(range(2, x_levels))
+
+    def held_of(c, held_ref, moved_ref):
+        place = sum(bit(c, b) << k for k, b in enumerate(steps[:-1]))
+        same = bit(my_column(), steps[-1]) == bit(c, steps[-1])
+        return jnp.where(same, held_ref[place], moved_ref[place])
+
+    def join(step, held_ref, moved_ref, *both_refs):
+        high = bit(my_column(), steps[step]) == 1
+        start = 0
+        for both_ref in both_refs:
+            rows = slice(start, start + both_ref.shape[1])
+            start = rows.stop
+            held, moved = held_ref[:, rows], moved_ref[:, rows]
+            both_ref[: 1 << step] = jnp.where(high, moved, held)
+            both_ref[1 << step :] = jnp.where(high, held, moved)
+
+    def joined_shapes(step):
+        if whole_solve and step == len(joined_at) - 1:
+            return [held_shape(2 << step, True, False), held_shape(2 << step, False, True)]
+        return [held_shape(2 << step)]
+
+    def placing(body, shapes, *args, scratch=()):
+        return pl.pallas_call(
+            body,
+            out_shape=[pltpu.VMEM(s, f32) for s in shapes],
+            in_specs=[pl.BlockSpec(memory_space=pl.ANY)] * len(args),
+            out_specs=[pl.BlockSpec(memory_space=pltpu.VMEM)] * len(shapes),
+            scratch_shapes=[pltpu.VMEM(s, f32) for s in scratch]
+            + [pltpu.SemaphoreType.DMA((len(args) + 1,))],
+            compiler_params=pltpu.CompilerParams(
+                vmem_limit_bytes=START_ROOM - sum(4 * math.prod(s) for s in shapes)
+            ),
+        )(*args)
+
+    def hold_body(solve_any, xi_any, held_ref, solve, xi, sems):
+        copies = [
+            pltpu.make_async_copy(solve_any, solve, sems.at[0]),
+            pltpu.make_async_copy(xi_any, xi, sems.at[1]),
+        ]
+        for copy in copies:
+            copy.start()
+        for copy in copies:
+            copy.wait()
+        odd_row = bit(my_row(), 0) == 1
+        row_in = pad_lanes(
+            jnp.concatenate(
+                [
+                    jnp.where(odd_row, edge_of(xi[k], 0), edge_of(xi[k], 2))
+                    for k in range(x_levels)
+                ],
+                axis=1,
+            ),
+            in_lanes,
+        )
+        held_ref[0, solve_rows : solve_rows + in_rows] = jnp.concatenate(
+            [row_in[i * in_rows : (i + 1) * in_rows] for i in range(runs)], axis=1
+        )
+        if whole_solve:
+            for level, start in ((0, 0), (1, solve_rows + in_rows)):
+                low, high = (
+                    jnp.concatenate(
+                        [edge_of(solve[level], 2 * c + side) for c in range(cols)], axis=1
+                    )
+                    for side in range(2)
+                )
+                mine = jnp.where(odd_row == (level == 0), high, low)
+                held_ref[0, start : start + edge] = jnp.concatenate(
+                    [mine[:edge], mine[edge:]], axis=1
+                )
+
+    ys_here, xi_here = y_solve[:, 0, 0], x_in[:, 0, 0]
+    (held,) = placing(
+        hold_body, [held_shape(1)], ys_here, xi_here, scratch=[ys_here.shape, xi_here.shape]
+    )
+
+    kept_from_start = [jnp.swapaxes(x_out, 3, 4), x_in, x_solve, y_solve, y_out, y_in]
     kept_from_start = [x[:, 0, 0] for x in kept_from_start] + [leaf_out_map[0, 0]]
+    placed_shapes = [x.shape for x in kept_from_start] + [(inner, leaf), (inner, inner)]
+    kept_from_start.append(leaf_field_map[0, 0])
 
     def start_body(load_any, map_any, *refs):
-        count = len(kept_from_start)
-        sources, (h_ref, out_ref) = refs[:count], refs[count : count + 2]
-        targets = refs[count + 2 : 2 * count + 2]
-        load_v, map_v, sems = refs[2 * count + 2 :]
+        *sources, field_any = refs[: len(kept_from_start)]
+        sources += [field_any.at[:, pl.ds(0, leaf)], field_any.at[:, pl.ds(leaf, inner)]]
+        h_ref, out_ref, load_out, *refs = refs[len(kept_from_start) :]
+        targets, (load_v, map_v, sems) = refs[: len(sources)], refs[len(sources) :]
         pairs = [(load_any, load_v), (map_any, map_v)] + list(zip(sources, targets))
-        order = [0, 1, 4, 3, 2, 5, 6, 7, 8]
         copies = [pltpu.make_async_copy(a, b, sems.at[i]) for i, (a, b) in enumerate(pairs)]
-        for i in order:
-            copies[i].start()
+        for copy in copies:
+            copy.start()
         copies[0].wait()
         copies[1].wait()
-        h = dot_t(load_v[...].reshape(waves, inner), map_v[...])
+        loaded = load_v[...].reshape(waves, inner)
+        load_out[...] = loaded
+        h = dot_t(loaded, map_v[...])
         h_ref[...] = h
-        copies[4].wait()
+        copies[2].wait()
         copies[3].wait()
-        xo, xi = targets[1], targets[2]
+        xo, xi = targets[:2]
         is_right = bit(my_column(), 0) == 1
         travelling = [
             jnp.where(is_right, edge_of(x[k], 1), edge_of(x[k], 3))
@@ -138,33 +234,34 @@
         out_ref[...] = pad_lanes(
             jnp.concatenate([edge_of(h, 3), edge_of(h, 1)] + travelling, axis=1), out_ref.shape[1]
         )
-        for i in order[4:]:
-            copies[i].wait()
-
-    anywhere, vmem = (pl.BlockSpec(memory_space=m) for m in (pl.ANY, pltpu.VMEM))
-    count = len(kept_from_start)
-    outs = [(waves, leaf), exchange_shape(0)] + [x.shape for x in kept_from_start]
-    h0, to_send, *placed = pl.pallas_call(
+        for copy in copies[4:]:
+            copy.wait()
+
+    h0, to_send, loaded, *placed = placing(
         start_body,
-        out_shape=[pltpu.VMEM(s, f32) for s in outs],
-        in_specs=[anywhere] * (count + 2),
-        out_specs=[vmem] * (count + 2),
-        scratch_shapes=[
-            pltpu.VMEM(load.shape, f32),
-            pltpu.VMEM((leaf, inner), f32),
-            pltpu.SemaphoreType.DMA((count + 2,)),
-        ],
-        compiler_params=pltpu.CompilerParams(
-            vmem_limit_bytes=START_ROOM - sum(4 * math.prod(s) for s in outs)
-        ),
-    )(load, leaf_load_map[0, 0], *kept_from_start)
-    xs_all, xo_all, xi_all, ys_all, yo_all, yi_all, out_map = placed
-    from_load = jnp.einsum(
-        "wk,ik->wi", load_here, leaf_field_map[0, 0, :, leaf:], precision=lax.Precision.HIGH
+        [(waves, leaf), exchange_shape(0), (waves, inner)] + placed_shapes,
+        load,
+        leaf_load_map[0, 0],
+        *kept_from_start,
+        scratch=[load.shape, (leaf, inner)],
     )
-
-    def x_body(level, h_ref, own_ref, got_ref, solve_ref, xo_ref, h_out, w_out, *rest):
+    xo_all, xi_all, xs_all, ys_all, yo_all, yi_all, out_map, field_edges, field_inner = placed
+
+    def product_body(a_ref, b_ref, out_ref):
+        out_ref[...] = dot_t(a_ref[...], b_ref[...])
+
+    (from_load,) = fused(product_body, [(waves, inner)], loaded, field_inner)
+
+    def x_body(level, h_ref, own_ref, got_ref, solve_ref, xo_ref, *rest):
         kept = x_levels - 1 - level
+        rest = list(rest)
+        if level == 1:
+            rest.pop(0)
+        if level in joined_at:
+            step = joined_at.index(level)
+            both = [rest.pop() for _ in joined_shapes(step)]
+            join(step, rest.pop(0), rest.pop(0), *reversed(both))
+        h_out, w_out, *rest = rest
         is_right = bit(my_column(), level) == 1
         own, got = own_ref[...], got_ref[...]
         left_child = jnp.where(is_right, got, own)
@@ -192,15 +289,25 @@
 
     h = h0
     x_keep, ends = [], []
+    moved = passed_on(held, steps[0])
     for level in range(x_levels):
         got = lax.ppermute(to_send, "box", [(i, i ^ (1 << level)) for i in range(cols)])
         outs = [(waves, leaf), (waves, pair)]
+        args = [h, to_send, got, xs_all, xo_all]
         if level < x_levels - 1:
             outs += [exchange_shape(level + 1), (pair, pair)]
-        h, w, *rest = fused(
-            functools.partial(x_body, level), outs, h, to_send, got, xs_all, xo_all
-        )
+        if level == 1:
+            args.append(from_load)
+        if level in joined_at:
+            step = joined_at.index(level)
+            outs += joined_shapes(step)
+            args += [held, moved]
+        h, w, *rest = fused(functools.partial(x_body, level), outs, *args)
         x_keep.append(w)
+        if level in joined_at:
+            second = rest.pop() if len(joined_shapes(step)) == 2 else None
+            held = rest.pop()
+            moved = passed_on(held, steps[step + 1])
         if rest:
             to_send, end = rest
             ends.append(end)
@@ -215,8 +322,9 @@
         return lax.all_to_all(x, group(level), 0, 0, tiled=True)
 
     def offer_shape(level):
-        size = span(level)
-        return (size * cols, waves // size * edge // LANES, LANES)
+        if whole_solve:
+            return ((1 + level) * cols, waves * edge // LANES, LANES)
+        return (span(level) * cols, waves // span(level) * edge // LANES, LANES)
 
     def store_offer(level, h, out):
         size = span(level)
@@ -224,6 +332,9 @@
         facing = jnp.where(
             lax.rem(my_row(), size) == size // 2 - 1, edge_of(h, 2), edge_of(h, 0)
         )
+        if whole_solve:
+            out[...] = jnp.broadcast_to(packed(facing, edge), out.shape)
+            return
         for target in range(size):
             piece = packed(facing[target * share : (target + 1) * share], edge)
             out[target * cols : (target + 1) * cols] = jnp.broadcast_to(piece, (cols,) + piece.shape)
@@ -231,7 +342,7 @@
     def offer_body(level, h_ref, out_ref):
         store_offer(level, h_ref[...], out_ref)
 
-    def solve_body(level, got_ref, solve_ref, out_ref, v_ref):
+    def gather_v(level, got_ref, v_ref):
         size = span(level)
         low = (size // 2 - 1) * cols
         run = got_ref.shape[1]
@@ -241,6 +352,9 @@
                 for k in range(LANES // edge):
                     start = c * pair + side * edge
                     v_ref[k * run : (k + 1) * run, start : start + edge] = edge_of(piece, k)
+
+    def solve_body(level, got_ref, solve_ref, out_ref, v_ref):
+        gather_v(level, got_ref, v_ref)
         w = packed(dot_t(v_ref[...], solve_ref[level]), pair)
         out_ref[...] = jnp.broadcast_to(w, out_ref.shape)
 
@@ -264,6 +378,27 @@
                     ]
         return w_ref[...]
 
+    def half_body(level, got_ref, held_ref, moved_ref, *refs):
+        out_ref, v_ref = (refs[1], refs[3]) if level == 0 else refs
+        odd_row = bit(my_row(), 0) == 1
+        run = got_ref.shape[1]
+        for c in range(cols):
+            piece = got_ref[c] if level == 0 else jnp.where(odd_row, got_ref[c], got_ref[cols + c])
+            for k in range(LANES // edge):
+                v_ref[k * run : (k + 1) * run, c * edge : (c + 1) * edge] = edge_of(piece, k)
+        solve = []
+        for c in range(cols):
+            block = held_of(c, held_ref, moved_ref)[:edge]
+            solve += [block[:, : iface // 2], block[:, iface // 2 :]]
+        out_ref[...] = dot_t(v_ref[...], jnp.concatenate(solve, axis=0))
+
+    def whole_body(h_ref, mine_ref, other_ref, yo_ref, h_out, w_out, next_ref):
+        w_all = mine_ref[...] + other_ref[...]
+        w_out[...] = own_columns(w_all)
+        h = h_ref[...] + dot_t(w_all, yo_ref[0])
+        h_out[...] = h
+        store_offer(1, h, next_ref)
+
     def spread_body(level, h_ref, got_ref, yo_ref, h_out, w_out, next_ref, w_ref):
         w_all = gather_w(level, got_ref, w_ref)
         w_out[...] = own_columns(w_all)
@@ -290,8 +425,13 @@
                         piece[part * share : (part + 1) * share], edge
                     )
 
-    def turn_body(level, h_ref, got_ref, yo_ref, yi_ref, reflect_ref, w_out, g_out, out_ref, w_ref):
-        w_all = gather_w(level, got_ref, w_ref)
+    def turn_body(level, h_ref, got_ref, *refs):
+        if whole_solve:
+            other_ref, yo_ref, yi_ref, reflect_ref, w_out, g_out, out_ref = refs
+            w_all = got_ref[...] + other_ref[...]
+        else:
+            yo_ref, yi_ref, reflect_ref, w_out, g_out, out_ref, w_ref = refs
+            w_all = gather_w(level, got_ref, w_ref)
         w_out[...] = own_columns(w_all)
         h = h_ref[...] + dot_t(w_all, yo_ref[level])
         lane = lax.broadcasted_iota(jnp.int32, (1, leaf), 1)
@@ -343,25 +483,62 @@
             )
         return total
 
-    x_lanes = -(-x_levels * edge // LANES) * LANES
-
-    def x_terms_body(g_ref, w_ref, sum_ref, xi_ref, g_out, out_ref):
-        g = with_row_edge(0, g_ref[...], w_ref[...], unpacked_parts(0, sum_ref))
+    x_lanes = -(-(x_levels + 1) * edge // LANES) * LANES
+
+    def split_body(g_ref, w_ref, sum_ref, yi_ref, g_out, own_out, other_out):
+        g = with_row_edge(1, g_ref[...], w_ref[...], unpacked_parts(1, sum_ref))
         g_out[...] = g
-        terms = [dot_t(g, xi_ref[k]) for k in range(x_levels)]
+        terms = dot_t(g, yi_ref[0])
+        odd_row = bit(my_row(), 0) == 1
+        low, high = (
+            jnp.concatenate(
+                [terms[:, c * pair + side * edge :][:, :edge] for c in range(cols)], axis=1
+            )
+            for side in range(2)
+        )
+        own_out[...] = jnp.where(odd_row, high, low)
+        other_out[...] = jnp.where(odd_row, low, high)
+
+    node_starts = []
+    for k in range(x_levels):
+        node_starts.append(sum(cols >> (i + 1) for i in range(k)) * pair)
+    node_lanes = (cols - 1) * pair
+
+    def prepare_body(g_ref, w_ref, xi_ref, held_ref, moved_ref, matrix_out, known_out):
+        g = with_row_edge(0, g_ref[...], w_ref[...], 0.0)
+        row = []
+        for c in range(cols):
+            held = held_of(c, held_ref, moved_ref)[solve_rows : solve_rows + in_rows]
+            row.append(
+                jnp.concatenate(
+                    [held[:, i * in_lanes : (i + 1) * in_lanes] for i in range(runs)], axis=0
+                )
+            )
+        matrix_out[...] = jnp.zeros_like(matrix_out)
+        for k in range(x_levels):
+            known = dot_t(g, xi_ref[k])
+            for node in range(cols >> (k + 1)):
+                start = node_starts[k] + node * pair
+                inside = my_column() >> (k + 1) == node
+                known_out[:, start : start + pair] = jnp.where(inside, known, 0.0)
+                for c in range(node << (k + 1), (node + 1) << (k + 1)):
+                    matrix_out[start : start + pair, c * edge : (c + 1) * edge] = edge_of(row[c], k)
+
+    def x_terms_body(own_ref, got_ref, matrix_ref, known_ref, out_ref):
+        q = own_ref[...] + got_ref[...]
+        terms = dot_t(q, matrix_ref[...]) + known_ref[...]
         for c in range(cols):
             picked = []
             for k in range(x_levels):
-                start = bit(c, k) * edge
-                same = my_column() >> (k + 1) == c >> (k + 1)
-                picked.append(jnp.where(same, terms[k][:, start : start + edge], 0.0))
-            out_ref[c] = pad_lanes(jnp.concatenate(picked, axis=1), x_lanes)
-
-    def finish_body(g_ref, h0_ref, got_ref, lo_ref, *refs):
+                start = node_starts[k] + (c >> (k + 1)) * pair + bit(c, k) * edge
+                picked.append(terms[:, start : start + edge])
+            out_ref[c] = pad_lanes(jnp.concatenate(picked + [edge_of(q, c)], axis=1), x_lanes)
+
+    def finish_body(g_ref, w_ref, h0_ref, got_ref, lo_ref, *refs):
         keep_ref, ends_ref = refs[:x_levels], refs[x_levels : 2 * x_levels - 1]
         g_out, t_out, *faces = refs[2 * x_levels - 1 :]
-        g = g_ref[...]
         q = jnp.sum(got_ref[...], axis=0)
+        g = with_row_edge(0, g_ref[...], w_ref[...], edge_of(q, x_levels))
         gl = jnp.zeros((waves, edge), f32)
         gr = gl
         for level in reversed(range(x_levels)):
@@ -403,7 +580,7 @@
         def mean(shared, own, other):
             return jnp.where(shared, 0.5 * (own + other), own)
 
-        out_ref[...] = jnp.concatenate(
+        trace = jnp.concatenate(
             [
                 mean(my_row() > 0, edge_of(t, 0), south),
                 mean(my_column() < cols - 1, edge_of(t, 1), east),
@@ -412,10 +589,49 @@
             ],
             axis=1,
         )
+        out_ref[...] = trace.reshape(out_ref.shape)
 
     (offer,) = fused(functools.partial(offer_body, 0), [offer_shape(0)], h)
     y_keep = []
     for level in range(y_levels):
+        if whole_solve:
+            got = lax.all_to_all(offer, ("box",) if level == 0 else (row_axes[0], "box"), 0, 0, tiled=True)
+            pass_on = [second] if level == 0 else []
+            mine, *pass_on = fused(
+                functools.partial(half_body, level),
+                [(waves, iface)] + [x.shape for x in pass_on],
+                got,
+                *((held, moved) if level == 0 else (second, second_moved)),
+                *pass_on,
+                scratch=[(waves, cols * edge)],
+                aliases={3: 1} if level == 0 else None,
+            )
+            if level == 0:
+                second = pass_on[0]
+                second_moved = passed_on(second, steps[-1])
+            other = lax.ppermute(mine, row_axes[-1], [(0, 1), (1, 0)])
+            if level == 0:
+                h, w, offer = fused(
+                    whole_body,
+                    [(waves, leaf), (waves, pair), offer_shape(1)],
+                    h,
+                    mine,
+                    other,
+                    yo_all,
+                )
+            else:
+                w, g, terms = fused(
+                    functools.partial(turn_body, level),
+                    [(waves, pair), (waves, leaf), terms_shape(level)],
+                    h,
+                    mine,
+                    other,
+                    yo_all,
+                    yi_all,
+                    reflect[0],
+                )
+            y_keep.append(w)
+            continue
         share = waves // span(level)
         (w_offer,) = fused(
             functools.partial(solve_body, level),
@@ -446,10 +662,10 @@
                 scratch=[(waves, iface)],
             )
         y_keep.append(w)
-    for level in reversed(range(y_levels)):
+    for level in reversed(range(1, y_levels)):
         (total,) = fused(sum_body, [terms_shape(level)[1:]], swap(terms, level))
         total = collect(total, level)
-        if level > 0:
+        if level > 1:
             g, terms = fused(
                 functools.partial(row_down_body, level),
                 [(waves, leaf), terms_shape(level - 1)],
@@ -458,20 +674,28 @@
                 total,
                 yi_all,
             )
-    g, terms = fused(
-        x_terms_body,
-        [(waves, leaf), (cols, waves, x_lanes)],
+    share = (waves, iface // 2)
+    g, own, other = fused(
+        split_body, [(waves, leaf), share, share], g, y_keep[1], total, yi_all
+    )
+    got = lax.ppermute(other, row_axes[-1], [(0, 1), (1, 0)])
+    matrix, known = fused(
+        prepare_body,
+        [(node_lanes, cols * edge), (waves, node_lanes)],
         g,
         y_keep[0],
-        total,
         xi_all,
+        held,
+        moved,
     )
+    (terms,) = fused(x_terms_body, [(cols, waves, x_lanes)], own, got, matrix, known)
     got = lax.all_to_all(terms, "box", 0, 0, tiled=True)
     face = (waves * edge // LANES, LANES)
     g, t, *faces = fused(
         finish_body,
         [(waves, leaf), (waves, leaf)] + [face] * 4,
         g,
+        y_keep[0],
         h0,
         got,
         out_map,
@@ -492,11 +716,15 @@
         lax.ppermute(faces[2], row_axes, near(rows)),
         lax.ppermute(faces[3], row_axes, far(rows)),
     ]
-    field_vals = from_load + jnp.einsum(
-        "wk,ik->wi", g, leaf_field_map[0, 0, :, :leaf], precision=lax.Precision.HIGH
+    def field_body(g_ref, map_ref, from_load_ref, out_ref):
+        field = from_load_ref[...] + dot_t(g_ref[...], map_ref[...])
+        out_ref[...] = field.reshape(out_ref.shape)
+
+    (field_vals,) = fused(
+        field_body, [(waves, 1, 1, inner)], g, field_edges, from_load
     )
-    (edge_trace,) = fused(trace_body, [(waves, leaf)], t, *seen)
-    return (field_vals[:, None, None, :], edge_trace[:, None, None, :])
+    (edge_trace,) = fused(trace_body, [(waves, 1, 1, leaf)], t, *seen)
+    return field_vals, edge_trace
 
 
 def solution(mesh):

time: 109 us -> 91.5 us (0.84)
  blocking collectives: 64.5 us -> 30.8 us
  starting transfers between devices: 18.6 us -> 29.9 us
  Pallas kernels: 8.12 us -> 11.5 us
  waiting for transfers between devices: 14.2 us -> 16.8 us
    all_to_all x6 -> x1, blocking collectives: 64.5 us -> 9.41 us  [swap(): return lax.all_to_all(x, group(level), 0, 0, tiled=True)]
    all_to_all x0 -> x2, blocking collectives: none -> 21.4 us  [the longest x1 11.4 us: local(): lax.all_to_all(offer, ('box',) if level == 0 else (row_axes[0], 'box'), 0...]
    ppermute x0 -> x7, starting transfers between devices: none -> 10.5 us  [the longest x4 5.27 us: passed_on(): lax.ppermute(held, 'box', [(i, i ^ 1 << bit_no) for i in range(cols)])]
    ppermute x0 -> x7, waiting for transfers between devices: none -> 3.35 us  [the longest x4 1.85 us: passed_on(): lax.ppermute(held, 'box', [(i, i ^ 1 << bit_no) for i in range(cols)])]
    pallas_call x1 -> x2, Pallas kernels: 1.86 us -> 4.07 us  [placing(): pl.pallas_call(body, out_shape=[pltpu.VMEM(s, f32) for s in shapes], in_s...]
    pallas_call x14 -> x16, Pallas kernels: 6.25 us -> 7.46 us  [fused(): pl.pallas_call(body, out_shape=[pltpu.VMEM(s, f32) for s in outs], in_spe...]
  transfers between devices with their start and end apart: 9 -> 16, of which waited for: 6 -> 10; matrix products, arithmetic and copies ran while one was open for 2% -> 1% of each run, Pallas kernels for 0% -> 6%
where the time goes in v5:
time: 91.5 us; the launch traced here: 91.1 us
  blocking collectives  30.8 us (34%)
  starting transfers between devices  29.9 us (33%)
  waiting for transfers between devices  16.8 us (18%)
  Pallas kernels  11.5 us (13%)
  local copies, waits for them, and re-layouts  1.28 us (1%)
    all_to_all x1, blocking collectives, local(): lax.all_to_all(offer, ('box',) if level == 0 else (row_axes[0], 'box'), 0...  11.4 us
    all_to_all x1, blocking collectives, local(): got = lax.all_to_all(terms, 'box', 0, 0, tiled=True)  10.1 us
    all_to_all x1, blocking collectives, swap(): return lax.all_to_all(x, group(level), 0, 0, tiled=True)  9.41 us
    pallas_call x16, Pallas kernels, fused(): pl.pallas_call(body, out_shape=[pltpu.VMEM(s, f32) for s in outs], in_spe...  7.46 us
    ppermute x3, waiting for transfers between devices, local(): lax.ppermute(to_send, 'box', [(i, i ^ 1 << level) for i in range(cols)])  5.63 us
    ppermute x4, starting transfers between devices, passed_on(): lax.ppermute(held, 'box', [(i, i ^ 1 << bit_no) for i in range(cols)])  5.27 us
    all_to_all x1, waiting for transfers between devices, local(): lax.all_to_all(offer, ('box',) if level == 0 else (row_axes[0], 'box'), 0...  5.14 us
    ppermute x2, starting transfers between devices, local(): other = lax.ppermute(mine, row_axes[-1], [(0, 1), (1, 0)])  4.78 us
  transfers between devices with their start and end apart: 16, of which 10 were waited for; matrix products, arithmetic and copies ran while one was open for 1% of the time, Pallas kernels for 6%

profile of v5, /device:TPU:9, one launch (start us, length us, event | category | flops | bytes accessed | tf_op | source)
XLA Modules:
  0.0 91.1 jit_solution(17487929281480114114)
XLA Ops:
  0.6 1.3 %shard_map.123.rest_0_ = f32[1,80,512]{2,1,0:T(8,128)S(1)} custom-call(f32[2,64,512]{2,1,0:T(8,128)} %bitcast.16, f32[3,64,128]{2,1,0:T(8,128)} %bitcast.20), custom_call_target="tpu_custom_call" | custom-call | tf_op jit(solution)/shard_map/pallas_call | solution.py:152
  1.9 2.4 %collective-permute-start.1 = (f32[1,80,512]{2,1,0:T(8,128)S(1)}, f32[1,80,512]{2,1,0:T(8,128)S(1)}, u32[]{:S(2)}, u32[]{:S(2)}) collective-permute-start(f32[1,80,512]{2,1,0:T(8,128)S(1)} %shard_map.123.rest_0_), channel_id=1, source_target_pairs={{0,4},{1,5},{2,6},{3,7},{4,0},{5,1},{6,2},{7,3},{8,12},{9,13},{10,... | collective-permute-start | bytes 491528 | tf_op jit(solution)/shard_map/ppermute | solution.py:126
  4.3 2.8 %shard_map.122 = (f32[64,128]{1,0:T(8,128)S(1)}, f32[64,256]{1,0:T(8,128)S(1)}, f32[64,512]{1,0:T(8,128)S(1)}, f32[3,64,128]{2,1,0:T(8,128)S(1)}, f32[3,64,128]{...) custom-call(f32[64,1,1,512]{3,2,1,0:T(1,128)} %load_any.1, ...), custom_call_target="tpu_custom_call" | custom-call | tf_op jit(solution)/shard_map/pallas_call | solution.py:152
  7.1 1.3 %collective-permute-start = (f32[64,256]{1,0:T(8,128)S(1)}, f32[64,256]{1,0:T(8,128)S(1)}, u32[]{:S(2)}, u32[]{:S(2)}) collective-permute-start(f32[64,256]{1,0:T(8,128)S(1)} %get-tuple-element.46.own_ref), channel_id=1, source_target_pairs={{0,1},{1,0},{2,3},{3,2},{4,5},{5,4},{6,7},{7,6},{8,9},{9,8},{10,11... | collective-permute-start | bytes 196616 | tf_op jit(solution)/shard_map/ppermute | solution.py:294
  8.4 1.9 %collective-permute-done.got_ref = f32[64,256]{1,0:T(8,128)S(1)} collective-permute-done((f32[64,256]{1,0:T(8,128)S(1)}, f32[64,256]{1,0:T(8,128)S(1)}, u32[]{:S(2)}, u32[]{:S(2)}) %collective-permute-start) | collective-permute-done | bytes 65568 | tf_op jit(solution)/shard_map/ppermute | solution.py:294
  10.3 1.3 %collective-permute-done.1.rest_1_ = f32[1,80,512]{2,1,0:T(8,128)S(1)} collective-permute-done((f32[1,80,512]{2,1,0:T(8,128)S(1)}, f32[1,80,512]{2,1,0:T(8,128)S(1)}, u32[]{:S(2)}, u32[]{:S(2)}) %collective-permute-start.1) | collective-permute-done | bytes 163872 | tf_op jit(solution)/shard_map/ppermute | solution.py:126
  12.0 1.3 %collective-permute-start.4 = (f32[2,80,512]{2,1,0:T(8,128)S(1)}, f32[2,80,512]{2,1,0:T(8,128)S(1)}, u32[]{:S(2)}, u32[]{:S(2)}) collective-permute-start(f32[2,80,512]{2,1,0:T(8,128)S(1)} %get-tuple-element.55.rest_0_), channel_id=1, source_target_pairs={{0,1},{1,0},{2,3},{3,2},{4,5},{5,4},{6,7},{7,6},{8,9},{9,8},{10,11... | collective-permute-start | bytes 983048 | tf_op jit(solution)/shard_map/ppermute | solution.py:126
  13.9 2.4 %collective-permute-done.2.got_ref = f32[64,128]{1,0:T(8,128)S(1)} collective-permute-done((f32[64,128]{1,0:T(8,128)S(1)}, f32[64,128]{1,0:T(8,128)S(1)}, u32[]{:S(2)}, u32[]{:S(2)}) %collective-permute-start.2) | collective-permute-done | bytes 32800 | tf_op jit(solution)/shard_map/ppermute | solution.py:294
  16.8 3.2 %collective-permute-start.3 = (f32[64,128]{1,0:T(8,128)S(1)}, f32[64,128]{1,0:T(8,128)S(1)}, u32[]{:S(2)}, u32[]{:S(2)}) collective-permute-start(f32[64,128]{1,0:T(8,128)S(1)} %get-tuple-element.54.own_ref), channel_id=1, source_target_pairs={{0,4},{1,5},{2,6},{3,7},{4,0},{5,1},{6,2},{7,3},{8,12},{9,13},{10,... | collective-permute-start | bytes 98312 | tf_op jit(solution)/shard_map/ppermute | solution.py:294
  19.9 1.3 %collective-permute-done.3.got_ref = f32[64,128]{1,0:T(8,128)S(1)} collective-permute-done((f32[64,128]{1,0:T(8,128)S(1)}, f32[64,128]{1,0:T(8,128)S(1)}, u32[]{:S(2)}, u32[]{:S(2)}) %collective-permute-start.3) | collective-permute-done | bytes 32800 | tf_op jit(solution)/shard_map/ppermute | solution.py:294
  21.9 11.4 %all_to_all.20.got_ref = f32[8,16,128]{2,1,0:T(8,128)S(1)} all-to-all(f32[8,16,128]{2,1,0:T(8,128)S(1)} %shard_map.128), channel_id=1, replica_groups=mesh['row1'=2,'row0'=2,'box'=8] {'box'}, dimensions={0} | all-to-all | bytes 131072 | tf_op jit(solution)/shard_map/all_to_all | solution.py:598
  33.6 2.9 %collective-permute-start.6 = (f32[64,512]{1,0:T(8,128)S(1)}, f32[64,512]{1,0:T(8,128)S(1)}, u32[]{:S(2)}, u32[]{:S(2)}) collective-permute-start(f32[64,512]{1,0:T(8,128)S(1)} %get-tuple-element.59.mine_ref), channel_id=1, source_target_pairs={{0,8},{8,0},{1,9},{9,1},{2,10},{10,2},{3,11},{11,3},{4,12},{12,4},... | collective-permute-start | bytes 393224 | tf_op jit(solution)/shard_map/ppermute | solution.py:612
  36.5 1.5 %collective-permute-start.7 = (f32[4,32,512]{2,1,0:T(8,128)S(1)}, f32[4,32,512]{2,1,0:T(8,128)S(1)}, u32[]{:S(2)}, u32[]{:S(2)}) collective-permute-start(f32[4,32,512]{2,1,0:T(8,128)S(1)} %get-tuple-element.63.held_ref), channel_id=1, source_target_pairs={{0,2},{1,3},{2,0},{3,1},{4,6},{5,7},{6,4},{7,5},{8,10},{9,11},{10,... | collective-permute-start | bytes 786440 | tf_op jit(solution)/shard_map/ppermute | solution.py:126
  38.1 1.2 %shard_map.130 = (f32[64,128]{1,0:T(8,128)S(1)}, f32[64,64]{1,0:T(8,128)S(1)}, f32[16,16,128]{2,1,0:T(8,128)}) custom-call(f32[64,128]{1,0:T(8,128)S(1)} %get-tuple-element.56.h_ref, f32[64,512]{1,0:T(8,128)S(1)} %get-tuple-element.59.mine_ref, f32[64,512]{1,0:T(8,128)S(1)} %collective-permute-done.6.other_ref, ...), custom_call_target="tpu_custom_call" | custom-call | tf_op jit(solution)/shard_map/pallas_call | solution.py:37
  39.2 4.8 %all-to-all-start.1 = ((f32[16,16,128]{2,1,0:T(8,128)}), f32[16,16,128]{2,1,0:T(8,128)S(1)}, u32[]{:S(2)}, u32[]{:S(2)}) async-start(f32[16,16,128]{2,1,0:T(8,128)} %get-tuple-element.62), calls=%async_computation.1 | async-start | bytes 262144 | tf_op jit(solution)/shard_map/all_to_all | solution.py:598
  44.5 5.1 %all-to-all-done.1.got_ref = f32[16,16,128]{2,1,0:T(8,128)S(1)} async-done(((f32[16,16,128]{2,1,0:T(8,128)}), f32[16,16,128]{2,1,0:T(8,128)S(1)}, u32[]{:S(2)}, u32[]{:S(2)}) %all-to-all-start.1) | async-done | bytes 131104 | tf_op jit(solution)/shard_map/all_to_all | solution.py:598
  50.1 1.9 %collective-permute-start.8 = (f32[64,512]{1,0:T(8,128)S(1)}, f32[64,512]{1,0:T(8,128)S(1)}, u32[]{:S(2)}, u32[]{:S(2)}) collective-permute-start(f32[64,512]{1,0:T(8,128)S(1)} %shard_map.131.got_ref), channel_id=1, source_target_pairs={{0,8},{8,0},{1,9},{9,1},{2,10},{10,2},{3,11},{11,3},{4,12},{12,4},... | collective-permute-start | bytes 393224 | tf_op jit(solution)/shard_map/ppermute | solution.py:612
  53.6 9.4 %all_to_all.21.got_ref = f32[32,8,128]{2,1,0:T(8,128)S(1)} all-to-all(f32[32,8,128]{2,1,0:T(8,128)S(1)} %get-tuple-element.67), channel_id=1, replica_groups=mesh['row1'=2,'row0'=2,'box'=8] {'row1','row0','box'}, dimensions={0} | all-to-all | bytes 262144 | tf_op jit(solution)/shard_map/all_to_all | solution.py:322
  67.1 10.1 %all_to_all.22.got_ref = f32[8,64,128]{2,1,0:T(8,128)S(1)} all-to-all(f32[8,64,128]{2,1,0:T(8,128)S(1)} %shard_map.136), channel_id=1, replica_groups=mesh['row1'=2,'row0'=2,'box'=8] {'box'}, dimensions={0} | all-to-all | bytes 524288 | tf_op jit(solution)/shard_map/all_to_all | solution.py:692
  78.2 1.2 %collective-permute-start.11 = (f32[16,128]{1,0:T(8,128)S(1)}, f32[16,128]{1,0:T(8,128)S(1)}, u32[]{:S(2)}, u32[]{:S(2)}) collective-permute-start(f32[16,128]{1,0:T(8,128)S(1)} %get-tuple-element.84), channel_id=1, source_target_pairs={{0,1},{1,0},{2,3},{3,2},{4,5},{5,4},{6,7},{7,6},{8,9},{9,8},{10,11... | collective-permute-start | bytes 24584 | tf_op jit(solution)/shard_map/ppermute | solution.py:714
  79.4 3.2 %collective-permute-start.12 = (f32[16,128]{1,0:T(8,128)S(1)}, f32[16,128]{1,0:T(8,128)S(1)}, u32[]{:S(2)}, u32[]{:S(2)}) collective-permute-start(f32[16,128]{1,0:T(8,128)S(1)} %get-tuple-element.85), channel_id=1, source_target_pairs={{1,2},{3,4},{5,6},{2,1},{4,3},{6,5},{9,10},{11,12},{13,14},{10,9},... | collective-permute-start | bytes 24584 | tf_op jit(solution)/shard_map/ppermute | solution.py:715
  82.6 2.8 %collective-permute-start.13 = (f32[16,128]{1,0:T(8,128)S(1)}, f32[16,128]{1,0:T(8,128)S(1)}, u32[]{:S(2)}, u32[]{:S(2)}) collective-permute-start(f32[16,128]{1,0:T(8,128)S(1)} %get-tuple-element.86), channel_id=1, source_target_pairs={{0,8},{8,0},{16,24},{24,16},{1,9},{9,1},{17,25},{25,17},{2,10},{10... | collective-permute-start | bytes 24584 | tf_op jit(solution)/shard_map/ppermute | solution.py:716
  85.4 2.2 %collective-permute-start.14 = (f32[16,128]{1,0:T(8,128)S(1)}, f32[16,128]{1,0:T(8,128)S(1)}, u32[]{:S(2)}, u32[]{:S(2)}) collective-permute-start(f32[16,128]{1,0:T(8,128)S(1)} %get-tuple-element.87), channel_id=1, source_target_pairs={{8,16},{16,8},{9,17},{17,9},{10,18},{18,10},{11,19},{19,11},{12,20... | collective-permute-start | bytes 24584 | tf_op jit(solution)/shard_map/ppermute | solution.py:717
  88.5 1.8 %collective-permute-done.14.d_ref = f32[16,128]{1,0:T(8,128)S(1)} collective-permute-done((f32[16,128]{1,0:T(8,128)S(1)}, f32[16,128]{1,0:T(8,128)S(1)}, u32[]{:S(2)}, u32[]{:S(2)}) %collective-permute-start.14) | collective-permute-done | bytes 8224 | tf_op jit(solution)/shard_map/ppermute | solution.py:717
  (35 shorter events, 11.9 us)
Async XLA Ops:
  1.9 9.7 %collective-permute-start.1 = (f32[1,80,512]{2,1,0:T(8,128)S(1)}, f32[1,80,512]{2,1,0:T(8,128)S(1)}, u32[]{:S(2)}, u32[]{:S(2)}) collective-permute-start(f32[1,80,512]{2,1,0:T(8,128)S(1)} %shard_map.123.rest_0_), channel_id=1, source_target_pairs={{0,4},{1,5},{2,6},{3,7},{4,0},{5,1},{6,2},{7,3},{8,12},{9,13},{10,... | collective-permute-start | bytes 491528 | tf_op jit(solution)/shard_map/ppermute | solution.py:126
  7.1 3.2 %collective-permute-start = (f32[64,256]{1,0:T(8,128)S(1)}, f32[64,256]{1,0:T(8,128)S(1)}, u32[]{:S(2)}, u32[]{:S(2)}) collective-permute-start(f32[64,256]{1,0:T(8,128)S(1)} %get-tuple-element.46.own_ref), channel_id=1, source_target_pairs={{0,1},{1,0},{2,3},{3,2},{4,5},{5,4},{6,7},{7,6},{8,9},{9,8},{10,11... | collective-permute-start | bytes 196616 | tf_op jit(solution)/shard_map/ppermute | solution.py:294
  12.0 9.2 %collective-permute-start.4 = (f32[2,80,512]{2,1,0:T(8,128)S(1)}, f32[2,80,512]{2,1,0:T(8,128)S(1)}, u32[]{:S(2)}, u32[]{:S(2)}) collective-permute-start(f32[2,80,512]{2,1,0:T(8,128)S(1)} %get-tuple-element.55.rest_0_), channel_id=1, source_target_pairs={{0,1},{1,0},{2,3},{3,2},{4,5},{5,4},{6,7},{7,6},{8,9},{9,8},{10,11... | collective-permute-start | bytes 983048 | tf_op jit(solution)/shard_map/ppermute | solution.py:126
  13.3 3.1 %collective-permute-start.2 = (f32[64,128]{1,0:T(8,128)S(1)}, f32[64,128]{1,0:T(8,128)S(1)}, u32[]{:S(2)}, u32[]{:S(2)}) collective-permute-start(f32[64,128]{1,0:T(8,128)S(1)} %get-tuple-element.50.own_ref), channel_id=1, source_target_pairs={{0,2},{1,3},{2,0},{3,1},{4,6},{5,7},{6,4},{7,5},{8,10},{9,11},{10,... | collective-permute-start | bytes 98312 | tf_op jit(solution)/shard_map/ppermute | solution.py:294
  16.8 4.5 %collective-permute-start.3 = (f32[64,128]{1,0:T(8,128)S(1)}, f32[64,128]{1,0:T(8,128)S(1)}, u32[]{:S(2)}, u32[]{:S(2)}) collective-permute-start(f32[64,128]{1,0:T(8,128)S(1)} %get-tuple-element.54.own_ref), channel_id=1, source_target_pairs={{0,4},{1,5},{2,6},{3,7},{4,0},{5,1},{6,2},{7,3},{8,12},{9,13},{10,... | collective-permute-start | bytes 98312 | tf_op jit(solution)/shard_map/ppermute | solution.py:294
  21.6 11.6 %collective-permute-start.5 = (f32[4,48,512]{2,1,0:T(8,128)S(1)}, f32[4,48,512]{2,1,0:T(8,128)S(1)}, u32[]{:S(2)}, u32[]{:S(2)}) collective-permute-start(f32[4,48,512]{2,1,0:T(8,128)S(1)} %get-tuple-element.57.held_ref), channel_id=1, source_target_pairs={{0,2},{1,3},{2,0},{3,1},{4,6},{5,7},{6,4},{7,5},{8,10},{9,11},{10,... | collective-permute-start | bytes 1179656 | tf_op jit(solution)/shard_map/ppermute | solution.py:126
  33.2 19.7 %copy-start = (f32[1,1,128]{2,1,0:T(1,128)S(1)}, f32[1,1,128]{2,1,0:T(1,128)}, u32[]{:S(2)}) copy-start(f32[1,1,128]{2,1,0:T(1,128)} %param.21) | copy-start | bytes 1540
  33.6 4.4 %collective-permute-start.6 = (f32[64,512]{1,0:T(8,128)S(1)}, f32[64,512]{1,0:T(8,128)S(1)}, u32[]{:S(2)}, u32[]{:S(2)}) collective-permute-start(f32[64,512]{1,0:T(8,128)S(1)} %get-tuple-element.59.mine_ref), channel_id=1, source_target_pairs={{0,8},{8,0},{1,9},{9,1},{2,10},{10,2},{3,11},{11,3},{4,12},{12,4},... | collective-permute-start | bytes 393224 | tf_op jit(solution)/shard_map/ppermute | solution.py:612
  36.5 8.0 %collective-permute-start.7 = (f32[4,32,512]{2,1,0:T(8,128)S(1)}, f32[4,32,512]{2,1,0:T(8,128)S(1)}, u32[]{:S(2)}, u32[]{:S(2)}) collective-permute-start(f32[4,32,512]{2,1,0:T(8,128)S(1)} %get-tuple-element.63.held_ref), channel_id=1, source_target_pairs={{0,2},{1,3},{2,0},{3,1},{4,6},{5,7},{6,4},{7,5},{8,10},{9,11},{10,... | collective-permute-start | bytes 786440 | tf_op jit(solution)/shard_map/ppermute | solution.py:126
  39.2 10.4 %all-to-all-start.1 = ((f32[16,16,128]{2,1,0:T(8,128)}), f32[16,16,128]{2,1,0:T(8,128)S(1)}, u32[]{:S(2)}, u32[]{:S(2)}) async-start(f32[16,16,128]{2,1,0:T(8,128)} %get-tuple-element.62), calls=%async_computation.1 | async-start | bytes 262144 | tf_op jit(solution)/shard_map/all_to_all | solution.py:598
  50.1 2.9 %collective-permute-start.8 = (f32[64,512]{1,0:T(8,128)S(1)}, f32[64,512]{1,0:T(8,128)S(1)}, u32[]{:S(2)}, u32[]{:S(2)}) collective-permute-start(f32[64,512]{1,0:T(8,128)S(1)} %shard_map.131.got_ref), channel_id=1, source_target_pairs={{0,8},{8,0},{1,9},{9,1},{2,10},{10,2},{3,11},{11,3},{4,12},{12,4},... | collective-permute-start | bytes 393224 | tf_op jit(solution)/shard_map/ppermute | solution.py:612
  63.1 1.7 %collective-permute-start.9 = (f32[8,128]{1,0:T(8,128)S(1)}, f32[8,128]{1,0:T(8,128)S(1)}, u32[]{:S(2)}, u32[]{:S(2)}) collective-permute-start(f32[8,128]{1,0:T(8,128)S(1)} %shard_map.133), channel_id=1, source_target_pairs={{0,8},{8,0},{1,9},{9,1},{2,10},{10,2},{3,11},{11,3},{4,12},{12,4},... | collective-permute-start | bytes 12296 | tf_op jit(solution)/shard_map/ppermute | solution.py:479
  65.3 1.3 %collective-permute-start.10 = (f32[64,256]{1,0:T(8,128)S(1)}, f32[64,256]{1,0:T(8,128)S(1)}, u32[]{:S(2)}, u32[]{:S(2)}) collective-permute-start(f32[64,256]{1,0:T(8,128)S(1)} %get-tuple-element.71), channel_id=1, source_target_pairs={{0,8},{8,0},{1,9},{9,1},{2,10},{10,2},{3,11},{11,3},{4,12},{12,4},... | collective-permute-start | bytes 196616 | tf_op jit(solution)/shard_map/ppermute | solution.py:681
  78.2 10.3 %collective-permute-start.11 = (f32[16,128]{1,0:T(8,128)S(1)}, f32[16,128]{1,0:T(8,128)S(1)}, u32[]{:S(2)}, u32[]{:S(2)}) collective-permute-start(f32[16,128]{1,0:T(8,128)S(1)} %get-tuple-element.84), channel_id=1, source_target_pairs={{0,1},{1,0},{2,3},{3,2},{4,5},{5,4},{6,7},{7,6},{8,9},{9,8},{10,11... | collective-permute-start | bytes 24584 | tf_op jit(solution)/shard_map/ppermute | solution.py:714
  79.4 9.1 %collective-permute-start.12 = (f32[16,128]{1,0:T(8,128)S(1)}, f32[16,128]{1,0:T(8,128)S(1)}, u32[]{:S(2)}, u32[]{:S(2)}) collective-permute-start(f32[16,128]{1,0:T(8,128)S(1)} %get-tuple-element.85), channel_id=1, source_target_pairs={{1,2},{3,4},{5,6},{2,1},{4,3},{6,5},{9,10},{11,12},{13,14},{10,9},... | collective-permute-start | bytes 24584 | tf_op jit(solution)/shard_map/ppermute | solution.py:715
  82.6 5.9 %collective-permute-start.13 = (f32[16,128]{1,0:T(8,128)S(1)}, f32[16,128]{1,0:T(8,128)S(1)}, u32[]{:S(2)}, u32[]{:S(2)}) collective-permute-start(f32[16,128]{1,0:T(8,128)S(1)} %get-tuple-element.86), channel_id=1, source_target_pairs={{0,8},{8,0},{16,24},{24,16},{1,9},{9,1},{17,25},{25,17},{2,10},{10... | collective-permute-start | bytes 24584 | tf_op jit(solution)/shard_map/ppermute | solution.py:716
  85.4 5.0 %collective-permute-start.14 = (f32[16,128]{1,0:T(8,128)S(1)}, f32[16,128]{1,0:T(8,128)S(1)}, u32[]{:S(2)}, u32[]{:S(2)}) collective-permute-start(f32[16,128]{1,0:T(8,128)S(1)} %get-tuple-element.87), channel_id=1, source_target_pairs={{8,16},{16,8},{9,17},{17,9},{10,18},{18,10},{11,19},{19,11},{12,20... | collective-permute-start | bytes 24584 | tf_op jit(solution)/shard_map/ppermute | solution.py:717

commit v6 on v5

--- a/solution.py
+++ b/solution.py
@@ -119,8 +119,7 @@
     solve_rows = edge if whole_solve else 0
 
     def held_shape(count, first=True, second=True):
-        first_rows = solve_rows + in_rows
-        return (count, first_rows * first + solve_rows * second, width)
+        return (count, solve_rows * first + (solve_rows + in_rows) * second, width)
 
     def passed_on(held, bit_no):
         return lax.ppermute(held, "box", [(i, i ^ (1 << bit_no)) for i in range(cols)])
@@ -247,10 +246,19 @@
     )
     xo_all, xi_all, xs_all, ys_all, yo_all, yi_all, out_map, field_edges, field_inner = placed
 
-    def product_body(a_ref, b_ref, out_ref):
-        out_ref[...] = dot_t(a_ref[...], b_ref[...])
-
-    (from_load,) = fused(product_body, [(waves, inner)], loaded, field_inner)
+    def aside_body(load_ref, map_ref, yi_ref, out_ref, columns_ref):
+        out_ref[...] = dot_t(load_ref[...], map_ref[...])
+        columns_ref[...] = packed(
+            jnp.where(my_row() == 1, edge_of(yi_ref[0], 2), edge_of(yi_ref[0], 0)), edge
+        )
+
+    from_load, columns = fused(
+        aside_body,
+        [(waves, inner), (iface * edge // LANES, LANES)],
+        loaded,
+        field_inner,
+        yi_all,
+    )
 
     def x_body(level, h_ref, own_ref, got_ref, solve_ref, xo_ref, *rest):
         kept = x_levels - 1 - level
@@ -379,7 +387,7 @@
         return w_ref[...]
 
     def half_body(level, got_ref, held_ref, moved_ref, *refs):
-        out_ref, v_ref = (refs[1], refs[3]) if level == 0 else refs
+        out_ref, v_ref = (refs[2], refs[5]) if level == 0 else refs
         odd_row = bit(my_row(), 0) == 1
         run = got_ref.shape[1]
         for c in range(cols):
@@ -388,11 +396,12 @@
                 v_ref[k * run : (k + 1) * run, c * edge : (c + 1) * edge] = edge_of(piece, k)
         solve = []
         for c in range(cols):
-            block = held_of(c, held_ref, moved_ref)[:edge]
+            start = in_rows * level
+            block = held_of(c, held_ref, moved_ref)[start : start + edge]
             solve += [block[:, : iface // 2], block[:, iface // 2 :]]
         out_ref[...] = dot_t(v_ref[...], jnp.concatenate(solve, axis=0))
 
-    def whole_body(h_ref, mine_ref, other_ref, yo_ref, h_out, w_out, next_ref):
+    def whole_body(h_ref, mine_ref, other_ref, yo_ref, early_ref, h_out, w_out, next_ref):
         w_all = mine_ref[...] + other_ref[...]
         w_out[...] = own_columns(w_all)
         h = h_ref[...] + dot_t(w_all, yo_ref[0])
@@ -485,19 +494,41 @@
 
     x_lanes = -(-(x_levels + 1) * edge // LANES) * LANES
 
+    def sides_of(terms):
+        low, high = (
+            jnp.concatenate([edge_of(terms, 2 * c + side) for c in range(cols)], axis=1)
+            for side in range(2)
+        )
+        odd_row = bit(my_row(), 0) == 1
+        return jnp.where(odd_row, high, low), jnp.where(odd_row, low, high)
+
     def split_body(g_ref, w_ref, sum_ref, yi_ref, g_out, own_out, other_out):
         g = with_row_edge(1, g_ref[...], w_ref[...], unpacked_parts(1, sum_ref))
         g_out[...] = g
-        terms = dot_t(g, yi_ref[0])
+        own_out[...], other_out[...] = sides_of(dot_t(g, yi_ref[0]))
+
+    def at_upper():
+        return (my_row() == 1) | (my_row() == 2)
+
+    def upper_body(got_ref, g_ref, w_ref, yi_ref, columns_ref, other_ref, own_out, other_out, half_out):
+        q = unpacked(jnp.sum(got_ref[...], axis=0), edge)
+        w = w_ref[...]
+        w = jnp.where(my_row() < 2, w[:, :edge], w[:, edge:])
         odd_row = bit(my_row(), 0) == 1
-        low, high = (
-            jnp.concatenate(
-                [terms[:, c * pair + side * edge :][:, :edge] for c in range(cols)], axis=1
-            )
-            for side in range(2)
-        )
-        own_out[...] = jnp.where(odd_row, high, low)
-        other_out[...] = jnp.where(odd_row, low, high)
+        half = waves // 2
+        value = jnp.where(odd_row, w[half:], w[:half]) + q
+        half_out[...] = value
+        columns = unpacked(jnp.where(at_upper(), columns_ref[...], other_ref[...]), edge)
+        added = dot_t(value, columns)
+        terms = dot_t(g_ref[...], yi_ref[0])
+        terms = jnp.concatenate(
+            [
+                terms[:half] + jnp.where(odd_row, 0.0, added),
+                terms[half:] + jnp.where(odd_row, added, 0.0),
+            ],
+            axis=0,
+        )
+        own_out[...], other_out[...] = sides_of(terms)
 
     node_starts = []
     for k in range(x_levels):
@@ -508,7 +539,7 @@
         g = with_row_edge(0, g_ref[...], w_ref[...], 0.0)
         row = []
         for c in range(cols):
-            held = held_of(c, held_ref, moved_ref)[solve_rows : solve_rows + in_rows]
+            held = held_of(c, held_ref, moved_ref)[:in_rows]
             row.append(
                 jnp.concatenate(
                     [held[:, i * in_lanes : (i + 1) * in_lanes] for i in range(runs)], axis=0
@@ -524,14 +555,38 @@
                 for c in range(node << (k + 1), (node + 1) << (k + 1)):
                     matrix_out[start : start + pair, c * edge : (c + 1) * edge] = edge_of(row[c], k)
 
-    def x_terms_body(own_ref, got_ref, matrix_ref, known_ref, out_ref):
+    def x_terms_body(own_ref, got_ref, matrix_ref, known_ref, *refs):
+        out_ref = refs[-1]
         q = own_ref[...] + got_ref[...]
         terms = dot_t(q, matrix_ref[...]) + known_ref[...]
+        if whole_solve:
+            g_ref, half_ref, other_half_ref, xi_ref, g_out, _ = refs
+            odd_row = bit(my_row(), 0) == 1
+            mine, other = half_ref[...], other_half_ref[...]
+            value = jnp.concatenate(
+                [jnp.where(odd_row, other, mine), jnp.where(odd_row, mine, other)], axis=0
+            )
+            none = jnp.zeros_like(value)
+            upper = jnp.concatenate(
+                [
+                    jnp.where(my_row() == 2, value, 0.0),
+                    none,
+                    jnp.where(my_row() == 1, value, 0.0),
+                    none,
+                ],
+                axis=1,
+            )
+            g_out[...] = g_ref[...] + upper
+            added = dot_t(upper, xi_ref[...].reshape(x_levels * pair, leaf))
         for c in range(cols):
             picked = []
             for k in range(x_levels):
                 start = node_starts[k] + (c >> (k + 1)) * pair + bit(c, k) * edge
-                picked.append(terms[:, start : start + edge])
+                piece = terms[:, start : start + edge]
+                if whole_solve:
+                    inside = my_column() >> (k + 1) == c >> (k + 1)
+                    piece = piece + jnp.where(inside, edge_of(added, 2 * k + bit(c, k)), 0.0)
+                picked.append(piece)
             out_ref[c] = pad_lanes(jnp.concatenate(picked + [edge_of(q, c)], axis=1), x_lanes)
 
     def finish_body(g_ref, w_ref, h0_ref, got_ref, lo_ref, *refs):
@@ -596,7 +651,7 @@
     for level in range(y_levels):
         if whole_solve:
             got = lax.all_to_all(offer, ("box",) if level == 0 else (row_axes[0], "box"), 0, 0, tiled=True)
-            pass_on = [second] if level == 0 else []
+            pass_on = [second, columns] if level == 0 else []
             mine, *pass_on = fused(
                 functools.partial(half_body, level),
                 [(waves, iface)] + [x.shape for x in pass_on],
@@ -604,10 +659,11 @@
                 *((held, moved) if level == 0 else (second, second_moved)),
                 *pass_on,
                 scratch=[(waves, cols * edge)],
-                aliases={3: 1} if level == 0 else None,
+                aliases={3: 1, 4: 2} if level == 0 else None,
             )
             if level == 0:
-                second = pass_on[0]
+                second, columns = pass_on
+                other_columns = lax.ppermute(columns, row_axes[-1], [(0, 1), (1, 0)])
                 second_moved = passed_on(second, steps[-1])
             other = lax.ppermute(mine, row_axes[-1], [(0, 1), (1, 0)])
             if level == 0:
@@ -618,6 +674,7 @@
                     mine,
                     other,
                     yo_all,
+                    other_columns,
                 )
             else:
                 w, g, terms = fused(
@@ -662,7 +719,7 @@
                 scratch=[(waves, iface)],
             )
         y_keep.append(w)
-    for level in reversed(range(1, y_levels)):
+    for level in reversed(range(1, 1 if whole_solve else y_levels)):
         (total,) = fused(sum_body, [terms_shape(level)[1:]], swap(terms, level))
         total = collect(total, level)
         if level > 1:
@@ -675,20 +732,45 @@
                 yi_all,
             )
     share = (waves, iface // 2)
-    g, own, other = fused(
-        split_body, [(waves, leaf), share, share], g, y_keep[1], total, yi_all
-    )
-    got = lax.ppermute(other, row_axes[-1], [(0, 1), (1, 0)])
+    core = row_axes[-1]
+    swapped = [(0, 1), (1, 0)]
+    if whole_solve:
+        own, other, half = fused(
+            upper_body,
+            [share, share, (waves // 2, edge)],
+            swap(terms, 1),
+            g,
+            y_keep[1],
+            yi_all,
+            columns,
+            other_columns,
+        )
+    else:
+        g, own, other = fused(
+            split_body, [(waves, leaf), share, share], g, y_keep[1], total, yi_all
+        )
+    got = lax.ppermute(other, core, swapped)
     matrix, known = fused(
         prepare_body,
         [(node_lanes, cols * edge), (waves, node_lanes)],
         g,
         y_keep[0],
         xi_all,
-        held,
-        moved,
+        *((second, second_moved) if whole_solve else (held, moved)),
     )
-    (terms,) = fused(x_terms_body, [(cols, waves, x_lanes)], own, got, matrix, known)
+    upper = []
+    if whole_solve:
+        upper = [g, half, lax.ppermute(half, core, swapped), xi_all]
+    *g_now, terms = fused(
+        x_terms_body,
+        [(waves, leaf)] * whole_solve + [(cols, waves, x_lanes)],
+        own,
+        got,
+        matrix,
+        known,
+        *upper,
+    )
+    g = g_now[0] if g_now else g
     got = lax.all_to_all(terms, "box", 0, 0, tiled=True)
     face = (waves * edge // LANES, LANES)
     g, t, *faces = fused(

time: 91.5 us -> 89.8 us (0.981)
  blocking collectives: 30.8 us -> 39.2 us
  waiting for transfers between devices: 16.8 us -> 11.8 us
  starting transfers between devices: 29.9 us -> 25.3 us
    all_to_all x1 -> x2, blocking collectives: 11.4 us -> 19.5 us  [local(): lax.all_to_all(offer, ('box',) if level == 0 else (row_axes[0], 'box'), 0...]
    all_to_all x1 -> x0, waiting for transfers between devices: 5.14 us -> none  [local(): lax.all_to_all(offer, ('box',) if level == 0 else (row_axes[0], 'box'), 0...]
    all_to_all x1 -> x0, starting transfers between devices: 4.76 us -> none  [local(): lax.all_to_all(offer, ('box',) if level == 0 else (row_axes[0], 'box'), 0...]
    ppermute x2 -> x3, waiting for transfers between devices: 1.33 us -> 1.96 us  [the longest x1 1.25 us: local(): other_columns = lax.ppermute(columns, row_axes[-1], [(0, 1), (1, 0)])]
    pallas_call x16 -> x15, Pallas kernels: 7.46 us -> 7.14 us  [fused(): pl.pallas_call(body, out_shape=[pltpu.VMEM(s, f32) for s in outs], in_spe...]
  transfers between devices with their start and end apart: 16 -> 16, of which waited for: 10 -> 8; matrix products, arithmetic and copies ran while one was open for 1% -> 1% of each run, Pallas kernels for 6% -> 6%
where the time goes in v6:
time: 89.8 us; the launch traced here: 89.5 us
  blocking collectives  39.2 us (44%)
  starting transfers between devices  25.3 us (28%)
  waiting for transfers between devices  11.8 us (13%)
  Pallas kernels  11.2 us (12%)
  local copies, waits for them, and re-layouts  1.28 us (1%)
    all_to_all x2, blocking collectives, local(): lax.all_to_all(offer, ('box',) if level == 0 else (row_axes[0], 'box'), 0...  19.5 us
    all_to_all x1, blocking collectives, local(): got = lax.all_to_all(terms, 'box', 0, 0, tiled=True)  10.1 us
    all_to_all x1, blocking collectives, swap(): return lax.all_to_all(x, group(level), 0, 0, tiled=True)  9.49 us
    pallas_call x15, Pallas kernels, fused(): pl.pallas_call(body, out_shape=[pltpu.VMEM(s, f32) for s in outs], in_spe...  7.14 us
    ppermute x3, waiting for transfers between devices, local(): lax.ppermute(to_send, 'box', [(i, i ^ 1 << level) for i in range(cols)])  5.63 us
    ppermute x4, starting transfers between devices, passed_on(): lax.ppermute(held, 'box', [(i, i ^ 1 << bit_no) for i in range(cols)])  5.32 us
    ppermute x2, starting transfers between devices, local(): other = lax.ppermute(mine, row_axes[-1], [(0, 1), (1, 0)])  5.28 us
    ppermute x3, starting transfers between devices, local(): lax.ppermute(to_send, 'box', [(i, i ^ 1 << level) for i in range(cols)])  4.48 us
  transfers between devices with their start and end apart: 16, of which 8 were waited for; matrix products, arithmetic and copies ran while one was open for 1% of the time, Pallas kernels for 6%

profile of v6, /device:TPU:9, one launch (start us, length us, event | category | flops | bytes accessed | tf_op | source)
XLA Modules:
  0.0 89.5 jit_solution(16795086141867335666)
XLA Ops:
  0.6 1.3 %shard_map.123.rest_0_ = f32[1,80,512]{2,1,0:T(8,128)S(1)} custom-call(f32[2,64,512]{2,1,0:T(8,128)} %bitcast.16, f32[3,64,128]{2,1,0:T(8,128)} %bitcast.20), custom_call_target="tpu_custom_call" | custom-call | tf_op jit(solution)/shard_map/pallas_call | solution.py:151
  1.9 2.4 %collective-permute-start.1 = (f32[1,80,512]{2,1,0:T(8,128)S(1)}, f32[1,80,512]{2,1,0:T(8,128)S(1)}, u32[]{:S(2)}, u32[]{:S(2)}) collective-permute-start(f32[1,80,512]{2,1,0:T(8,128)S(1)} %shard_map.123.rest_0_), channel_id=1, source_target_pairs={{0,4},{1,5},{2,6},{3,7},{4,0},{5,1},{6,2},{7,3},{8,12},{9,13},{10,... | collective-permute-start | bytes 491528 | tf_op jit(solution)/shard_map/ppermute | solution.py:125
  4.3 2.8 %shard_map.122 = (f32[64,128]{1,0:T(8,128)S(1)}, f32[64,256]{1,0:T(8,128)S(1)}, f32[64,512]{1,0:T(8,128)S(1)}, f32[3,64,128]{2,1,0:T(8,128)S(1)}, f32[3,64,128]{...) custom-call(f32[64,1,1,512]{3,2,1,0:T(1,128)} %load_any.1, ...), custom_call_target="tpu_custom_call" | custom-call | tf_op jit(solution)/shard_map/pallas_call | solution.py:151
  7.1 1.3 %collective-permute-start = (f32[64,256]{1,0:T(8,128)S(1)}, f32[64,256]{1,0:T(8,128)S(1)}, u32[]{:S(2)}, u32[]{:S(2)}) collective-permute-start(f32[64,256]{1,0:T(8,128)S(1)} %get-tuple-element.51.own_ref), channel_id=1, source_target_pairs={{0,1},{1,0},{2,3},{3,2},{4,5},{5,4},{6,7},{7,6},{8,9},{9,8},{10,11... | collective-permute-start | bytes 196616 | tf_op jit(solution)/shard_map/ppermute | solution.py:302
  8.4 1.9 %collective-permute-done.got_ref = f32[64,256]{1,0:T(8,128)S(1)} collective-permute-done((f32[64,256]{1,0:T(8,128)S(1)}, f32[64,256]{1,0:T(8,128)S(1)}, u32[]{:S(2)}, u32[]{:S(2)}) %collective-permute-start) | collective-permute-done | bytes 65568 | tf_op jit(solution)/shard_map/ppermute | solution.py:302
  10.3 1.3 %collective-permute-done.1.rest_1_ = f32[1,80,512]{2,1,0:T(8,128)S(1)} collective-permute-done((f32[1,80,512]{2,1,0:T(8,128)S(1)}, f32[1,80,512]{2,1,0:T(8,128)S(1)}, u32[]{:S(2)}, u32[]{:S(2)}) %collective-permute-start.1) | collective-permute-done | bytes 163872 | tf_op jit(solution)/shard_map/ppermute | solution.py:125
  12.0 1.3 %collective-permute-start.4 = (f32[2,80,512]{2,1,0:T(8,128)S(1)}, f32[2,80,512]{2,1,0:T(8,128)S(1)}, u32[]{:S(2)}, u32[]{:S(2)}) collective-permute-start(f32[2,80,512]{2,1,0:T(8,128)S(1)} %get-tuple-element.62.rest_0_), channel_id=1, source_target_pairs={{0,1},{1,0},{2,3},{3,2},{4,5},{5,4},{6,7},{7,6},{8,9},{9,8},{10,11... | collective-permute-start | bytes 983048 | tf_op jit(solution)/shard_map/ppermute | solution.py:125
  14.0 2.4 %collective-permute-done.2.got_ref = f32[64,128]{1,0:T(8,128)S(1)} collective-permute-done((f32[64,128]{1,0:T(8,128)S(1)}, f32[64,128]{1,0:T(8,128)S(1)}, u32[]{:S(2)}, u32[]{:S(2)}) %collective-permute-start.2) | collective-permute-done | bytes 32800 | tf_op jit(solution)/shard_map/ppermute | solution.py:302
  16.8 3.2 %collective-permute-start.3 = (f32[64,128]{1,0:T(8,128)S(1)}, f32[64,128]{1,0:T(8,128)S(1)}, u32[]{:S(2)}, u32[]{:S(2)}) collective-permute-start(f32[64,128]{1,0:T(8,128)S(1)} %get-tuple-element.61.own_ref), channel_id=1, source_target_pairs={{0,4},{1,5},{2,6},{3,7},{4,0},{5,1},{6,2},{7,3},{8,12},{9,13},{10,... | collective-permute-start | bytes 98312 | tf_op jit(solution)/shard_map/ppermute | solution.py:302
  19.9 1.3 %collective-permute-done.3.got_ref = f32[64,128]{1,0:T(8,128)S(1)} collective-permute-done((f32[64,128]{1,0:T(8,128)S(1)}, f32[64,128]{1,0:T(8,128)S(1)}, u32[]{:S(2)}, u32[]{:S(2)}) %collective-permute-start.3) | collective-permute-done | bytes 32800 | tf_op jit(solution)/shard_map/ppermute | solution.py:302
  21.9 10.4 %all_to_all.20.got_ref = f32[8,16,128]{2,1,0:T(8,128)S(1)} all-to-all(f32[8,16,128]{2,1,0:T(8,128)S(1)} %shard_map.128), channel_id=1, replica_groups=mesh['row1'=2,'row0'=2,'box'=8] {'box'}, dimensions={0} | all-to-all | bytes 131072 | tf_op jit(solution)/shard_map/all_to_all | solution.py:653
  32.7 1.6 %collective-permute-start.8 = (f32[4,48,512]{2,1,0:T(8,128)S(1)}, f32[4,48,512]{2,1,0:T(8,128)S(1)}, u32[]{:S(2)}, u32[]{:S(2)}) collective-permute-start(f32[4,48,512]{2,1,0:T(8,128)S(1)} %get-tuple-element.72.held_ref), channel_id=1, source_target_pairs={{0,2},{1,3},{2,0},{3,1},{4,6},{5,7},{6,4},{7,5},{8,10},{9,11},{10,... | collective-permute-start | bytes 1179656 | tf_op jit(solution)/shard_map/ppermute | solution.py:125
  34.3 3.5 %collective-permute-start.6 = (f32[64,512]{1,0:T(8,128)S(1)}, f32[64,512]{1,0:T(8,128)S(1)}, u32[]{:S(2)}, u32[]{:S(2)}) collective-permute-start(f32[64,512]{1,0:T(8,128)S(1)} %get-tuple-element.67.mine_ref), channel_id=1, source_target_pairs={{0,8},{8,0},{1,9},{9,1},{2,10},{10,2},{3,11},{11,3},{4,12},{12,4},... | collective-permute-start | bytes 393224 | tf_op jit(solution)/shard_map/ppermute | solution.py:668
  37.8 1.3 %collective-permute-done.7.early_ref.other_ref = f32[128,128]{1,0:T(8,128)S(1)} collective-permute-done((f32[128,128]{1,0:T(8,128)S(1)}, f32[128,128]{1,0:T(8,128)S(1)}, u32[]{:S(2)}, u32[]{:S(2)}) %collective-permute-start.7) | collective-permute-done | bytes 65568 | tf_op jit(solution)/shard_map/ppermute | solution.py:666
  39.6 9.1 %all_to_all.21.got_ref = f32[16,16,128]{2,1,0:T(8,128)S(1)} all-to-all(f32[16,16,128]{2,1,0:T(8,128)S(1)} %get-tuple-element.71), channel_id=1, replica_groups=mesh['row1'=2,'row0'=2,'box'=8] {'row1','box'}, dimensions={0} | all-to-all | bytes 262144 | tf_op jit(solution)/shard_map/all_to_all | solution.py:653
  49.2 1.8 %collective-permute-start.9 = (f32[64,512]{1,0:T(8,128)S(1)}, f32[64,512]{1,0:T(8,128)S(1)}, u32[]{:S(2)}, u32[]{:S(2)}) collective-permute-start(f32[64,512]{1,0:T(8,128)S(1)} %shard_map.131.got_ref), channel_id=1, source_target_pairs={{0,8},{8,0},{1,9},{9,1},{2,10},{10,2},{3,11},{11,3},{4,12},{12,4},... | collective-permute-start | bytes 393224 | tf_op jit(solution)/shard_map/ppermute | solution.py:668
  52.6 9.5 %all_to_all.22.got_ref = f32[32,8,128]{2,1,0:T(8,128)S(1)} all-to-all(f32[32,8,128]{2,1,0:T(8,128)S(1)} %get-tuple-element.73), channel_id=1, replica_groups=mesh['row1'=2,'row0'=2,'box'=8] {'row1','row0','box'}, dimensions={0} | all-to-all | bytes 262144 | tf_op jit(solution)/shard_map/all_to_all | solution.py:330
  65.4 10.1 %all_to_all.23.got_ref = f32[8,64,128]{2,1,0:T(8,128)S(1)} all-to-all(f32[8,64,128]{2,1,0:T(8,128)S(1)} %get-tuple-element.84), channel_id=1, replica_groups=mesh['row1'=2,'row0'=2,'box'=8] {'box'}, dimensions={0} | all-to-all | bytes 524288 | tf_op jit(solution)/shard_map/all_to_all | solution.py:774
  75.6 1.1 %shard_map.136 = (f32[64,128]{1,0:T(8,128)S(1)}, f32[64,128]{1,0:T(8,128)S(1)}, f32[16,128]{1,0:T(8,128)S(1)}, f32[16,128]{1,0:T(8,128)S(1)}, f32[16,128]{1,0:T(8,128)S(1)}, /*index=5*/f32[16,128]{1,0:T(8,128)S(1)}) custom-call(f32[64,128]{1,0:T(8,128)S(1)} %get-tuple-element.83.g_ref, f32[64,64]{1,0:T(8,128)S(1)} %get-tuple-element.78.w_ref, ...), custom_call_target="tpu_custom_call" | custom-call | tf_op jit(solution)/shard_map/pallas_call | solution.py:37
  76.7 1.2 %collective-permute-start.12 = (f32[16,128]{1,0:T(8,128)S(1)}, f32[16,128]{1,0:T(8,128)S(1)}, u32[]{:S(2)}, u32[]{:S(2)}) collective-permute-start(f32[16,128]{1,0:T(8,128)S(1)} %get-tuple-element.94), channel_id=1, source_target_pairs={{0,1},{1,0},{2,3},{3,2},{4,5},{5,4},{6,7},{7,6},{8,9},{9,8},{10,11... | collective-permute-start | bytes 24584 | tf_op jit(solution)/shard_map/ppermute | solution.py:796
  77.9 3.3 %collective-permute-start.13 = (f32[16,128]{1,0:T(8,128)S(1)}, f32[16,128]{1,0:T(8,128)S(1)}, u32[]{:S(2)}, u32[]{:S(2)}) collective-permute-start(f32[16,128]{1,0:T(8,128)S(1)} %get-tuple-element.95), channel_id=1, source_target_pairs={{1,2},{3,4},{5,6},{2,1},{4,3},{6,5},{9,10},{11,12},{13,14},{10,9},... | collective-permute-start | bytes 24584 | tf_op jit(solution)/shard_map/ppermute | solution.py:797
  81.2 2.5 %collective-permute-start.14 = (f32[16,128]{1,0:T(8,128)S(1)}, f32[16,128]{1,0:T(8,128)S(1)}, u32[]{:S(2)}, u32[]{:S(2)}) collective-permute-start(f32[16,128]{1,0:T(8,128)S(1)} %get-tuple-element.96), channel_id=1, source_target_pairs={{0,8},{8,0},{16,24},{24,16},{1,9},{9,1},{17,25},{25,17},{2,10},{10... | collective-permute-start | bytes 24584 | tf_op jit(solution)/shard_map/ppermute | solution.py:798
  83.7 2.2 %collective-permute-start.15 = (f32[16,128]{1,0:T(8,128)S(1)}, f32[16,128]{1,0:T(8,128)S(1)}, u32[]{:S(2)}, u32[]{:S(2)}) collective-permute-start(f32[16,128]{1,0:T(8,128)S(1)} %get-tuple-element.97), channel_id=1, source_target_pairs={{8,16},{16,8},{9,17},{17,9},{10,18},{18,10},{11,19},{19,11},{12,20... | collective-permute-start | bytes 24584 | tf_op jit(solution)/shard_map/ppermute | solution.py:799
  86.9 1.8 %collective-permute-done.15.d_ref = f32[16,128]{1,0:T(8,128)S(1)} collective-permute-done((f32[16,128]{1,0:T(8,128)S(1)}, f32[16,128]{1,0:T(8,128)S(1)}, u32[]{:S(2)}, u32[]{:S(2)}) %collective-permute-start.15) | collective-permute-done | bytes 8224 | tf_op jit(solution)/shard_map/ppermute | solution.py:799
  (33 shorter events, 10.2 us)
Async XLA Ops:
  1.9 9.7 %collective-permute-start.1 = (f32[1,80,512]{2,1,0:T(8,128)S(1)}, f32[1,80,512]{2,1,0:T(8,128)S(1)}, u32[]{:S(2)}, u32[]{:S(2)}) collective-permute-start(f32[1,80,512]{2,1,0:T(8,128)S(1)} %shard_map.123.rest_0_), channel_id=1, source_target_pairs={{0,4},{1,5},{2,6},{3,7},{4,0},{5,1},{6,2},{7,3},{8,12},{9,13},{10,... | collective-permute-start | bytes 491528 | tf_op jit(solution)/shard_map/ppermute | solution.py:125
  7.1 3.2 %collective-permute-start = (f32[64,256]{1,0:T(8,128)S(1)}, f32[64,256]{1,0:T(8,128)S(1)}, u32[]{:S(2)}, u32[]{:S(2)}) collective-permute-start(f32[64,256]{1,0:T(8,128)S(1)} %get-tuple-element.51.own_ref), channel_id=1, source_target_pairs={{0,1},{1,0},{2,3},{3,2},{4,5},{5,4},{6,7},{7,6},{8,9},{9,8},{10,11... | collective-permute-start | bytes 196616 | tf_op jit(solution)/shard_map/ppermute | solution.py:302
  12.0 9.2 %collective-permute-start.4 = (f32[2,80,512]{2,1,0:T(8,128)S(1)}, f32[2,80,512]{2,1,0:T(8,128)S(1)}, u32[]{:S(2)}, u32[]{:S(2)}) collective-permute-start(f32[2,80,512]{2,1,0:T(8,128)S(1)} %get-tuple-element.62.rest_0_), channel_id=1, source_target_pairs={{0,1},{1,0},{2,3},{3,2},{4,5},{5,4},{6,7},{7,6},{8,9},{9,8},{10,11... | collective-permute-start | bytes 983048 | tf_op jit(solution)/shard_map/ppermute | solution.py:125
  13.3 3.1 %collective-permute-start.2 = (f32[64,128]{1,0:T(8,128)S(1)}, f32[64,128]{1,0:T(8,128)S(1)}, u32[]{:S(2)}, u32[]{:S(2)}) collective-permute-start(f32[64,128]{1,0:T(8,128)S(1)} %get-tuple-element.55.own_ref), channel_id=1, source_target_pairs={{0,2},{1,3},{2,0},{3,1},{4,6},{5,7},{6,4},{7,5},{8,10},{9,11},{10,... | collective-permute-start | bytes 98312 | tf_op jit(solution)/shard_map/ppermute | solution.py:302
  16.8 4.5 %collective-permute-start.3 = (f32[64,128]{1,0:T(8,128)S(1)}, f32[64,128]{1,0:T(8,128)S(1)}, u32[]{:S(2)}, u32[]{:S(2)}) collective-permute-start(f32[64,128]{1,0:T(8,128)S(1)} %get-tuple-element.61.own_ref), channel_id=1, source_target_pairs={{0,4},{1,5},{2,6},{3,7},{4,0},{5,1},{6,2},{7,3},{8,12},{9,13},{10,... | collective-permute-start | bytes 98312 | tf_op jit(solution)/shard_map/ppermute | solution.py:302
  21.7 10.6 %collective-permute-start.5 = (f32[4,32,512]{2,1,0:T(8,128)S(1)}, f32[4,32,512]{2,1,0:T(8,128)S(1)}, u32[]{:S(2)}, u32[]{:S(2)}) collective-permute-start(f32[4,32,512]{2,1,0:T(8,128)S(1)} %get-tuple-element.64.held_ref), channel_id=1, source_target_pairs={{0,2},{1,3},{2,0},{3,1},{4,6},{5,7},{6,4},{7,5},{8,10},{9,11},{10,... | collective-permute-start | bytes 786440 | tf_op jit(solution)/shard_map/ppermute | solution.py:125
  32.7 19.3 %copy-start = (f32[1,1,128]{2,1,0:T(1,128)S(1)}, f32[1,1,128]{2,1,0:T(1,128)}, u32[]{:S(2)}) copy-start(f32[1,1,128]{2,1,0:T(1,128)} %param.21) | copy-start | bytes 1540
  32.7 16.0 %collective-permute-start.8 = (f32[4,48,512]{2,1,0:T(8,128)S(1)}, f32[4,48,512]{2,1,0:T(8,128)S(1)}, u32[]{:S(2)}, u32[]{:S(2)}) collective-permute-start(f32[4,48,512]{2,1,0:T(8,128)S(1)} %get-tuple-element.72.held_ref), channel_id=1, source_target_pairs={{0,2},{1,3},{2,0},{3,1},{4,6},{5,7},{6,4},{7,5},{8,10},{9,11},{10,... | collective-permute-start | bytes 1179656 | tf_op jit(solution)/shard_map/ppermute | solution.py:125
  34.3 4.7 %collective-permute-start.6 = (f32[64,512]{1,0:T(8,128)S(1)}, f32[64,512]{1,0:T(8,128)S(1)}, u32[]{:S(2)}, u32[]{:S(2)}) collective-permute-start(f32[64,512]{1,0:T(8,128)S(1)} %get-tuple-element.67.mine_ref), channel_id=1, source_target_pairs={{0,8},{8,0},{1,9},{9,1},{2,10},{10,2},{3,11},{11,3},{4,12},{12,4},... | collective-permute-start | bytes 393224 | tf_op jit(solution)/shard_map/ppermute | solution.py:668
  37.8 1.3 %collective-permute-start.7 = (f32[128,128]{1,0:T(8,128)S(1)}, f32[128,128]{1,0:T(8,128)S(1)}, u32[]{:S(2)}, u32[]{:S(2)}) collective-permute-start(f32[128,128]{1,0:T(8,128)S(1)} %get-tuple-element.69.columns_ref), channel_id=1, source_target_pairs={{0,8},{8,0},{1,9},{9,1},{2,10},{10,2},{3,11},{11,3},{4,12},{12,4},... | collective-permute-start | bytes 196616 | tf_op jit(solution)/shard_map/ppermute | solution.py:666
  49.2 2.8 %collective-permute-start.9 = (f32[64,512]{1,0:T(8,128)S(1)}, f32[64,512]{1,0:T(8,128)S(1)}, u32[]{:S(2)}, u32[]{:S(2)}) collective-permute-start(f32[64,512]{1,0:T(8,128)S(1)} %shard_map.131.got_ref), channel_id=1, source_target_pairs={{0,8},{8,0},{1,9},{9,1},{2,10},{10,2},{3,11},{11,3},{4,12},{12,4},... | collective-permute-start | bytes 393224 | tf_op jit(solution)/shard_map/ppermute | solution.py:668
  62.7 2.1 %collective-permute-start.10 = (f32[64,256]{1,0:T(8,128)S(1)}, f32[64,256]{1,0:T(8,128)S(1)}, u32[]{:S(2)}, u32[]{:S(2)}) collective-permute-start(f32[64,256]{1,0:T(8,128)S(1)} %get-tuple-element.77), channel_id=1, source_target_pairs={{0,8},{8,0},{1,9},{9,1},{2,10},{10,2},{3,11},{11,3},{4,12},{12,4},... | collective-permute-start | bytes 196616 | tf_op jit(solution)/shard_map/ppermute | solution.py:752
  63.6 1.2 %collective-permute-start.11 = (f32[32,32]{1,0:T(8,128)S(1)}, f32[32,32]{1,0:T(8,128)S(1)}, u32[]{:S(2)}, u32[]{:S(2)}) collective-permute-start(f32[32,32]{1,0:T(8,128)S(1)} %get-tuple-element.82.refs_1_), channel_id=1, source_target_pairs={{0,8},{8,0},{1,9},{9,1},{2,10},{10,2},{3,11},{11,3},{4,12},{12,4},... | collective-permute-start | bytes 12296 | tf_op jit(solution)/shard_map/ppermute | solution.py:763
  76.7 10.2 %collective-permute-start.12 = (f32[16,128]{1,0:T(8,128)S(1)}, f32[16,128]{1,0:T(8,128)S(1)}, u32[]{:S(2)}, u32[]{:S(2)}) collective-permute-start(f32[16,128]{1,0:T(8,128)S(1)} %get-tuple-element.94), channel_id=1, source_target_pairs={{0,1},{1,0},{2,3},{3,2},{4,5},{5,4},{6,7},{7,6},{8,9},{9,8},{10,11... | collective-permute-start | bytes 24584 | tf_op jit(solution)/shard_map/ppermute | solution.py:796
  77.9 8.9 %collective-permute-start.13 = (f32[16,128]{1,0:T(8,128)S(1)}, f32[16,128]{1,0:T(8,128)S(1)}, u32[]{:S(2)}, u32[]{:S(2)}) collective-permute-start(f32[16,128]{1,0:T(8,128)S(1)} %get-tuple-element.95), channel_id=1, source_target_pairs={{1,2},{3,4},{5,6},{2,1},{4,3},{6,5},{9,10},{11,12},{13,14},{10,9},... | collective-permute-start | bytes 24584 | tf_op jit(solution)/shard_map/ppermute | solution.py:797
  81.2 5.6 %collective-permute-start.14 = (f32[16,128]{1,0:T(8,128)S(1)}, f32[16,128]{1,0:T(8,128)S(1)}, u32[]{:S(2)}, u32[]{:S(2)}) collective-permute-start(f32[16,128]{1,0:T(8,128)S(1)} %get-tuple-element.96), channel_id=1, source_target_pairs={{0,8},{8,0},{16,24},{24,16},{1,9},{9,1},{17,25},{25,17},{2,10},{10... | collective-permute-start | bytes 24584 | tf_op jit(solution)/shard_map/ppermute | solution.py:798
  83.7 5.0 %collective-permute-start.15 = (f32[16,128]{1,0:T(8,128)S(1)}, f32[16,128]{1,0:T(8,128)S(1)}, u32[]{:S(2)}, u32[]{:S(2)}) collective-permute-start(f32[16,128]{1,0:T(8,128)S(1)} %get-tuple-element.97), channel_id=1, source_target_pairs={{8,16},{16,8},{9,17},{17,9},{10,18},{18,10},{11,19},{19,11},{12,20... | collective-permute-start | bytes 24584 | tf_op jit(solution)/shard_map/ppermute | solution.py:799

commit v7 on v6

--- a/solution.py
+++ b/solution.py
@@ -111,15 +111,15 @@
     def pieces_of(x, first, count):
         return [edge_of(x, first + i) for i in range(count)]
 
-    whole_solve = y_levels == 2 and iface * iface <= 1 << 18
+    whole_solve = (x_levels, y_levels) == (3, 2) and iface * iface <= 1 << 18
     in_lanes = -(-x_levels * edge // LANES) * LANES
     width = iface if whole_solve else 4 * in_lanes
     runs = width // in_lanes
     in_rows = pair // runs
     solve_rows = edge if whole_solve else 0
 
-    def held_shape(count, first=True, second=True):
-        return (count, solve_rows * first + (solve_rows + in_rows) * second, width)
+    def held_shape(count, *parts):
+        return (count, sum(parts), width)
 
     def passed_on(held, bit_no):
         return lax.ppermute(held, "box", [(i, i ^ (1 << bit_no)) for i in range(cols)])
@@ -132,22 +132,12 @@
         same = bit(my_column(), steps[-1]) == bit(c, steps[-1])
         return jnp.where(same, held_ref[place], moved_ref[place])
 
-    def join(step, held_ref, moved_ref, *both_refs):
+    def join(step, held, moved, both_ref):
         high = bit(my_column(), steps[step]) == 1
-        start = 0
-        for both_ref in both_refs:
-            rows = slice(start, start + both_ref.shape[1])
-            start = rows.stop
-            held, moved = held_ref[:, rows], moved_ref[:, rows]
-            both_ref[: 1 << step] = jnp.where(high, moved, held)
-            both_ref[1 << step :] = jnp.where(high, held, moved)
-
-    def joined_shapes(step):
-        if whole_solve and step == len(joined_at) - 1:
-            return [held_shape(2 << step, True, False), held_shape(2 << step, False, True)]
-        return [held_shape(2 << step)]
-
-    def placing(body, shapes, *args, scratch=()):
+        both_ref[: 1 << step] = jnp.where(high, moved, held)
+        both_ref[1 << step :] = jnp.where(high, held, moved)
+
+    def placing(body, shapes, *args, scratch=(), live=0):
         return pl.pallas_call(
             body,
             out_shape=[pltpu.VMEM(s, f32) for s in shapes],
@@ -156,11 +146,12 @@
             scratch_shapes=[pltpu.VMEM(s, f32) for s in scratch]
             + [pltpu.SemaphoreType.DMA((len(args) + 1,))],
             compiler_params=pltpu.CompilerParams(
-                vmem_limit_bytes=START_ROOM - sum(4 * math.prod(s) for s in shapes)
+                vmem_limit_bytes=START_ROOM - live - sum(4 * math.prod(s) for s in shapes)
             ),
         )(*args)
 
-    def hold_body(solve_any, xi_any, held_ref, solve, xi, sems):
+    def hold_body(solve_any, xi_any, *refs):
+        *held_refs, solve, xi, sems = refs
         copies = [
             pltpu.make_async_copy(solve_any, solve, sems.at[0]),
             pltpu.make_async_copy(xi_any, xi, sems.at[1]),
@@ -180,11 +171,11 @@
             ),
             in_lanes,
         )
-        held_ref[0, solve_rows : solve_rows + in_rows] = jnp.concatenate(
+        held_refs[0][0, solve_rows:] = jnp.concatenate(
             [row_in[i * in_rows : (i + 1) * in_rows] for i in range(runs)], axis=1
         )
         if whole_solve:
-            for level, start in ((0, 0), (1, solve_rows + in_rows)):
+            for level, held_ref in enumerate(held_refs):
                 low, high = (
                     jnp.concatenate(
                         [edge_of(solve[level], 2 * c + side) for c in range(cols)], axis=1
@@ -192,26 +183,25 @@
                     for side in range(2)
                 )
                 mine = jnp.where(odd_row == (level == 0), high, low)
-                held_ref[0, start : start + edge] = jnp.concatenate(
-                    [mine[:edge], mine[edge:]], axis=1
-                )
+                held_ref[0, :edge] = jnp.concatenate([mine[:edge], mine[edge:]], axis=1)
 
     ys_here, xi_here = y_solve[:, 0, 0], x_in[:, 0, 0]
-    (held,) = placing(
-        hold_body, [held_shape(1)], ys_here, xi_here, scratch=[ys_here.shape, xi_here.shape]
-    )
-
-    kept_from_start = [jnp.swapaxes(x_out, 3, 4), x_in, x_solve, y_solve, y_out, y_in]
-    kept_from_start = [x[:, 0, 0] for x in kept_from_start] + [leaf_out_map[0, 0]]
-    placed_shapes = [x.shape for x in kept_from_start] + [(inner, leaf), (inner, inner)]
-    kept_from_start.append(leaf_field_map[0, 0])
-
-    def start_body(load_any, map_any, *refs):
-        *sources, field_any = refs[: len(kept_from_start)]
-        sources += [field_any.at[:, pl.ds(0, leaf)], field_any.at[:, pl.ds(leaf, inner)]]
-        h_ref, out_ref, load_out, *refs = refs[len(kept_from_start) :]
-        targets, (load_v, map_v, sems) = refs[: len(sources)], refs[len(sources) :]
-        pairs = [(load_any, load_v), (map_any, map_v)] + list(zip(sources, targets))
+    held, *upper_held = placing(
+        hold_body,
+        [held_shape(1, solve_rows, in_rows)] + [held_shape(1, solve_rows)] * whole_solve,
+        ys_here,
+        xi_here,
+        scratch=[ys_here.shape, xi_here.shape],
+    )
+
+    columns_here = [x[:, 0, 0] for x in (jnp.swapaxes(x_out, 3, 4), x_in, x_solve)]
+    rows_here = [x[:, 0, 0] for x in (y_out, y_in)] + [leaf_out_map[0, 0]]
+    if not whole_solve:
+        rows_here.append(ys_here)
+
+    def start_body(load_any, map_any, xo_any, xi_any, xs_any, h_ref, out_ref, load_out, *refs):
+        xo, xi, xs, load_v, map_v, sems = refs
+        pairs = zip((load_any, map_any, xo_any, xi_any, xs_any), (load_v, map_v, xo, xi, xs))
         copies = [pltpu.make_async_copy(a, b, sems.at[i]) for i, (a, b) in enumerate(pairs)]
         for copy in copies:
             copy.start()
@@ -223,7 +213,6 @@
         h_ref[...] = h
         copies[2].wait()
         copies[3].wait()
-        xo, xi = targets[:2]
         is_right = bit(my_column(), 0) == 1
         travelling = [
             jnp.where(is_right, edge_of(x[k], 1), edge_of(x[k], 3))
@@ -233,43 +222,75 @@
         out_ref[...] = pad_lanes(
             jnp.concatenate([edge_of(h, 3), edge_of(h, 1)] + travelling, axis=1), out_ref.shape[1]
         )
-        for copy in copies[4:]:
-            copy.wait()
-
-    h0, to_send, loaded, *placed = placing(
+        copies[4].wait()
+
+    h0, to_send, loaded, xo_all, xi_all, xs_all = placing(
         start_body,
-        [(waves, leaf), exchange_shape(0), (waves, inner)] + placed_shapes,
+        [(waves, leaf), exchange_shape(0), (waves, inner)] + [x.shape for x in columns_here],
         load,
         leaf_load_map[0, 0],
-        *kept_from_start,
+        *columns_here,
         scratch=[load.shape, (leaf, inner)],
     )
-    xo_all, xi_all, xs_all, ys_all, yo_all, yi_all, out_map, field_edges, field_inner = placed
-
-    def aside_body(load_ref, map_ref, yi_ref, out_ref, columns_ref):
+
+    def place_body(field_any, *refs):
+        *refs, sems = refs
+        count = len(rows_here)
+        sources = [field_any.at[:, pl.ds(0, leaf)], field_any.at[:, pl.ds(leaf, inner)]]
+        pairs = zip(sources + list(refs[:count]), refs[count:])
+        copies = [pltpu.make_async_copy(a, b, sems.at[i]) for i, (a, b) in enumerate(pairs)]
+        for copy in copies:
+            copy.start()
+        for copy in copies:
+            copy.wait()
+
+    field_edges, field_inner, yo_all, yi_all, out_map, *ys_all = placing(
+        place_body,
+        [(inner, leaf), (inner, inner)] + [x.shape for x in rows_here],
+        leaf_field_map[0, 0],
+        *rows_here,
+        live=2 << 20,
+    )
+
+    side_rows = iface * edge // LANES
+
+    def at_upper():
+        return (my_row() == 1) | (my_row() == 2)
+
+    def upper_edge(x):
+        return jnp.where(my_row() == 1, x[2 * edge : 3 * edge], x[:edge])
+
+    def aside_body(load_ref, map_ref, yi_ref, yo_ref, out_ref, *side_ref):
         out_ref[...] = dot_t(load_ref[...], map_ref[...])
-        columns_ref[...] = packed(
-            jnp.where(my_row() == 1, edge_of(yi_ref[0], 2), edge_of(yi_ref[0], 0)), edge
-        )
-
-    from_load, columns = fused(
+        for ref in side_ref:
+            ref[:side_rows] = packed(
+                jnp.where(my_row() == 1, edge_of(yi_ref[0], 2), edge_of(yi_ref[0], 0)), edge
+            )
+            out_rows = upper_edge(yo_ref[0])
+            ref[side_rows:] = jnp.concatenate(
+                [out_rows[:, i * LANES : (i + 1) * LANES] for i in range(iface // LANES)], axis=0
+            )
+
+    from_load, *side = fused(
         aside_body,
-        [(waves, inner), (iface * edge // LANES, LANES)],
+        [(waves, inner)] + [(2 * side_rows, LANES)] * whole_solve,
         loaded,
         field_inner,
         yi_all,
-    )
-
-    def x_body(level, h_ref, own_ref, got_ref, solve_ref, xo_ref, *rest):
+        yo_all,
+    )
+
+    core = row_axes[-1]
+    swapped = [(0, 1), (1, 0)]
+
+    def x_body(level, tasks, h_ref, own_ref, got_ref, solve_ref, xo_ref, *refs):
         kept = x_levels - 1 - level
-        rest = list(rest)
-        if level == 1:
-            rest.pop(0)
-        if level in joined_at:
-            step = joined_at.index(level)
-            both = [rest.pop() for _ in joined_shapes(step)]
-            join(step, rest.pop(0), rest.pop(0), *reversed(both))
-        h_out, w_out, *rest = rest
+        count = sum(len(args) for _, args, _ in tasks)
+        ins, (h_out, w_out, *rest) = refs[:count], refs[count:]
+        rest, outs = rest[: 2 if kept else 0], rest[2 if kept else 0 :]
+        for task, args, shapes in tasks:
+            task(*ins[: len(args)], *outs[: len(shapes)])
+            ins, outs = ins[len(args) :], outs[len(shapes) :]
         is_right = bit(my_column(), level) == 1
         own, got = own_ref[...], got_ref[...]
         left_child = jnp.where(is_right, got, own)
@@ -295,30 +316,74 @@
         else:
             h_out[...] = h_ref[...] + dot(w, xo_ref[level])
 
+    def nothing(*refs):
+        pass
+
+    def join_first(held_ref, moved_ref, solve_ref, in_ref):
+        join(0, held_ref[:, :solve_rows], moved_ref[:, :solve_rows], solve_ref)
+        join(0, held_ref[:, solve_rows:], moved_ref[:, solve_rows:], in_ref)
+
+    def join_upper(held_ref, moved_ref, in_ref, both_ref):
+        join(0, held_ref[...], moved_ref[...], both_ref.at[:, in_rows : in_rows + solve_rows])
+        both_ref[:, :in_rows] = in_ref[...]
+        both_ref[:, in_rows + solve_rows :] = jnp.zeros_like(in_ref)
+
+    def join_plain(step, held_ref, moved_ref, both_ref):
+        join(step, held_ref[...], moved_ref[...], both_ref)
+
     h = h0
     x_keep, ends = [], []
     moved = passed_on(held, steps[0])
+    upper_moved = [passed_on(x, steps[0]) for x in upper_held]
     for level in range(x_levels):
         got = lax.ppermute(to_send, "box", [(i, i ^ (1 << level)) for i in range(cols)])
         outs = [(waves, leaf), (waves, pair)]
-        args = [h, to_send, got, xs_all, xo_all]
         if level < x_levels - 1:
             outs += [exchange_shape(level + 1), (pair, pair)]
-        if level == 1:
-            args.append(from_load)
-        if level in joined_at:
+        args = [h, to_send, got, xs_all, xo_all]
+        tasks = []
+        if level < 2:
+            tasks.append((nothing, [(out_map, from_load)[level]], []))
+        if whole_solve and level == 0:
+            shapes = [held_shape(2, solve_rows), held_shape(2, in_rows)]
+            tasks.append((join_first, [held, moved], shapes))
+        elif whole_solve and level == 1:
+            tasks.append((nothing, side, [x.shape for x in side]))
+            shapes = [held_shape(2, in_rows, solve_rows, in_rows)]
+            tasks.append((join_upper, upper_held + upper_moved + [shared_in], shapes))
+        elif whole_solve:
+            tasks.append((nothing, other_side, []))
+            shapes = [held_shape(4, solve_rows)]
+            tasks.append((functools.partial(join_plain, 1), [held, moved], shapes))
+        elif level in joined_at:
             step = joined_at.index(level)
-            outs += joined_shapes(step)
-            args += [held, moved]
-        h, w, *rest = fused(functools.partial(x_body, level), outs, *args)
+            shape = held_shape(2 << step, in_rows)
+            tasks.append((functools.partial(join_plain, step), [held, moved], [shape]))
+        aliases = {len(args) + 1: len(outs)} if level == 1 and whole_solve else None
+        h, w, *rest = fused(
+            functools.partial(x_body, level, tasks),
+            outs + [shape for task in tasks for shape in task[2]],
+            *args,
+            *(x for task in tasks for x in task[1]),
+            aliases=aliases,
+        )
         x_keep.append(w)
-        if level in joined_at:
-            second = rest.pop() if len(joined_shapes(step)) == 2 else None
-            held = rest.pop()
+        if level < x_levels - 1:
+            to_send, end, *rest = rest
+            ends.append(end)
+        if whole_solve and level == 0:
+            held, shared_in = rest
+            moved = passed_on(held, steps[1])
+        elif whole_solve and level == 1:
+            side, upper_held = rest[:1], rest[1]
+            upper_moved = passed_on(upper_held, steps[1])
+            other_side = [lax.ppermute(x, core, swapped) for x in side]
+        elif whole_solve:
+            (held,) = rest
+            moved = passed_on(held, steps[2])
+        elif level in joined_at:
+            (held,) = rest
             moved = passed_on(held, steps[step + 1])
-        if rest:
-            to_send, end = rest
-            ends.append(end)
 
     def group(level):
         return tuple(row_axes[y_levels - 1 - level :]) + ("box",)
@@ -331,7 +396,7 @@
 
     def offer_shape(level):
         if whole_solve:
-            return ((1 + level) * cols, waves * edge // LANES, LANES)
+            return (rows**level * cols, (waves >> level) * edge // LANES, LANES)
         return (span(level) * cols, waves // span(level) * edge // LANES, LANES)
 
     def store_offer(level, h, out):
@@ -347,8 +412,11 @@
             piece = packed(facing[target * share : (target + 1) * share], edge)
             out[target * cols : (target + 1) * cols] = jnp.broadcast_to(piece, (cols,) + piece.shape)
 
-    def offer_body(level, h_ref, out_ref):
-        store_offer(level, h_ref[...], out_ref)
+    def offer_body(level, h_ref, out_ref, *face_ref):
+        h = h_ref[...]
+        store_offer(level, h, out_ref)
+        for ref in face_ref:
+            ref[...] = packed(jnp.where(my_row() == 1, edge_of(h, 2), edge_of(h, 0)), edge)
 
     def gather_v(level, got_ref, v_ref):
         size = span(level)
@@ -387,13 +455,22 @@
         return w_ref[...]
 
     def half_body(level, got_ref, held_ref, moved_ref, *refs):
-        out_ref, v_ref = (refs[2], refs[5]) if level == 0 else refs
+        if level == 0:
+            upper_held_ref, upper_moved_ref, _, out_ref, _, upper_ref, v_ref = refs
+            kept = in_rows + solve_rows
+            join(1, upper_held_ref[:, :kept], upper_moved_ref[:, :kept], upper_ref)
+        else:
+            out_ref, v_ref = refs
         odd_row = bit(my_row(), 0) == 1
         run = got_ref.shape[1]
         for c in range(cols):
-            piece = got_ref[c] if level == 0 else jnp.where(odd_row, got_ref[c], got_ref[cols + c])
-            for k in range(LANES // edge):
-                v_ref[k * run : (k + 1) * run, c * edge : (c + 1) * edge] = edge_of(piece, k)
+            for part in range(1 + level):
+                piece = got_ref[part * cols + c]
+                if level == 1:
+                    piece = jnp.where(odd_row, piece, got_ref[(2 + part) * cols + c])
+                for k in range(LANES // edge):
+                    start = (part * LANES // edge + k) * run
+                    v_ref[start : start + run, c * edge : (c + 1) * edge] = edge_of(piece, k)
         solve = []
         for c in range(cols):
             start = in_rows * level
@@ -401,12 +478,22 @@
             solve += [block[:, : iface // 2], block[:, iface // 2 :]]
         out_ref[...] = dot_t(v_ref[...], jnp.concatenate(solve, axis=0))
 
-    def whole_body(h_ref, mine_ref, other_ref, yo_ref, early_ref, h_out, w_out, next_ref):
+    def whole_body(
+        h_ref, mine_ref, other_ref, yo_ref, face_ref, other_face_ref, side_ref, h_out, w_out, next_ref
+    ):
         w_all = mine_ref[...] + other_ref[...]
         w_out[...] = own_columns(w_all)
-        h = h_ref[...] + dot_t(w_all, yo_ref[0])
-        h_out[...] = h
-        store_offer(1, h, next_ref)
+        out_rows = side_ref[side_rows:]
+        out_rows = jnp.concatenate(
+            [out_rows[i * edge : (i + 1) * edge] for i in range(iface // LANES)], axis=1
+        )
+        out_rows = jnp.where(at_upper(), upper_edge(yo_ref[0]), out_rows)
+        spread = dot_t(w_all, jnp.concatenate([yo_ref[0], out_rows], axis=0))
+        h_out[...] = h_ref[...] + spread[:, :leaf]
+        face = unpacked(jnp.where(at_upper(), face_ref[...], other_face_ref[...]), edge)
+        face = face + spread[:, leaf:]
+        half = jnp.where(bit(my_row(), 0) == 1, face[waves // 2 :], face[: waves // 2])
+        next_ref[...] = jnp.broadcast_to(packed(half, edge), next_ref.shape)
 
     def spread_body(level, h_ref, got_ref, yo_ref, h_out, w_out, next_ref, w_ref):
         w_all = gather_w(level, got_ref, w_ref)
@@ -507,10 +594,7 @@
         g_out[...] = g
         own_out[...], other_out[...] = sides_of(dot_t(g, yi_ref[0]))
 
-    def at_upper():
-        return (my_row() == 1) | (my_row() == 2)
-
-    def upper_body(got_ref, g_ref, w_ref, yi_ref, columns_ref, other_ref, own_out, other_out, half_out):
+    def upper_body(got_ref, g_ref, w_ref, yi_ref, side_ref, other_ref, own_out, other_out, half_out):
         q = unpacked(jnp.sum(got_ref[...], axis=0), edge)
         w = w_ref[...]
         w = jnp.where(my_row() < 2, w[:, :edge], w[:, edge:])
@@ -518,7 +602,8 @@
         half = waves // 2
         value = jnp.where(odd_row, w[half:], w[:half]) + q
         half_out[...] = value
-        columns = unpacked(jnp.where(at_upper(), columns_ref[...], other_ref[...]), edge)
+        columns = jnp.where(at_upper(), side_ref[:side_rows], other_ref[:side_rows])
+        columns = unpacked(columns, edge)
         added = dot_t(value, columns)
         terms = dot_t(g_ref[...], yi_ref[0])
         terms = jnp.concatenate(
@@ -646,26 +731,41 @@
         )
         out_ref[...] = trace.reshape(out_ref.shape)
 
-    (offer,) = fused(functools.partial(offer_body, 0), [offer_shape(0)], h)
+    face = (waves * edge // LANES, LANES)
+    offer, *upper_face = fused(
+        functools.partial(offer_body, 0), [offer_shape(0)] + [face] * whole_solve, h
+    )
     y_keep = []
     for level in range(y_levels):
         if whole_solve:
-            got = lax.all_to_all(offer, ("box",) if level == 0 else (row_axes[0], "box"), 0, 0, tiled=True)
-            pass_on = [second, columns] if level == 0 else []
-            mine, *pass_on = fused(
-                functools.partial(half_body, level),
-                [(waves, iface)] + [x.shape for x in pass_on],
-                got,
-                *((held, moved) if level == 0 else (second, second_moved)),
-                *pass_on,
-                scratch=[(waves, cols * edge)],
-                aliases={3: 1, 4: 2} if level == 0 else None,
-            )
+            axes = "box" if level == 0 else group(1)
+            got = lax.all_to_all(offer, axes, 0, 0, tiled=True)
             if level == 0:
-                second, columns = pass_on
-                other_columns = lax.ppermute(columns, row_axes[-1], [(0, 1), (1, 0)])
-                second_moved = passed_on(second, steps[-1])
-            other = lax.ppermute(mine, row_axes[-1], [(0, 1), (1, 0)])
+                (upper_face,) = upper_face
+                mine, upper_face, second = fused(
+                    functools.partial(half_body, 0),
+                    [(waves, iface), upper_face.shape, held_shape(4, in_rows, solve_rows)],
+                    got,
+                    held,
+                    moved,
+                    upper_held,
+                    upper_moved,
+                    upper_face,
+                    scratch=[(waves, cols * edge)],
+                    aliases={5: 1},
+                )
+                other_face = lax.ppermute(upper_face, core, swapped)
+                second_moved = passed_on(second, steps[2])
+            else:
+                (mine,) = fused(
+                    functools.partial(half_body, 1),
+                    [(waves, iface)],
+                    got,
+                    second,
+                    second_moved,
+                    scratch=[(waves, cols * edge)],
+                )
+            other = lax.ppermute(mine, core, swapped)
             if level == 0:
                 h, w, offer = fused(
                     whole_body,
@@ -674,7 +774,9 @@
                     mine,
                     other,
                     yo_all,
-                    other_columns,
+                    upper_face,
+                    other_face,
+                    *other_side,
                 )
             else:
                 w, g, terms = fused(
@@ -694,7 +796,7 @@
             functools.partial(solve_body, level),
             [(span(level) * cols, share * pair // LANES, LANES)],
             swap(offer, level),
-            ys_all,
+            *ys_all,
             scratch=[(share, iface)],
         )
         got = swap(w_offer, level)
@@ -732,8 +834,6 @@
                 yi_all,
             )
     share = (waves, iface // 2)
-    core = row_axes[-1]
-    swapped = [(0, 1), (1, 0)]
     if whole_solve:
         own, other, half = fused(
             upper_body,
@@ -742,8 +842,8 @@
             g,
             y_keep[1],
             yi_all,
-            columns,
-            other_columns,
+            *side,
+            *other_side,
         )
     else:
         g, own, other = fused(
@@ -772,7 +872,6 @@
     )
     g = g_now[0] if g_now else g
     got = lax.all_to_all(terms, "box", 0, 0, tiled=True)
-    face = (waves * edge // LANES, LANES)
     g, t, *faces = fused(
         finish_body,
         [(waves, leaf), (waves, leaf)] + [face] * 4,

time: 89.8 us -> 87.4 us (0.973)
  waiting for transfers between devices: 11.8 us -> 5.66 us
  starting transfers between devices: 25.3 us -> 27.8 us
    ppermute x3, waiting for transfers between devices: 5.63 us -> 0.74 us  [local(): lax.ppermute(to_send, 'box', [(i, i ^ 1 << level) for i in range(cols)])]
    ppermute x4 -> x6, starting transfers between devices: 5.32 us -> 7.09 us  [passed_on(): lax.ppermute(held, 'box', [(i, i ^ 1 << bit_no) for i in range(cols)])]
    ppermute x4 -> x6, waiting for transfers between devices: 1.33 us -> 0.19 us  [passed_on(): lax.ppermute(held, 'box', [(i, i ^ 1 << bit_no) for i in range(cols)])]
    ppermute x3 -> x4, starting transfers between devices: 5.28 us -> 6.35 us  [the longest x2 3.5 us: local(): other = lax.ppermute(mine, core, swapped)]
    pallas_call x2 -> x3, Pallas kernels: 4.07 us -> 4.75 us  [placing(): pl.pallas_call(body, out_shape=[pltpu.VMEM(s, f32) for s in shapes], in_s...]
    ppermute x3 -> x4, waiting for transfers between devices: 2.24 us -> 2.16 us  [the longest x1 1.17 us: local(): other_face = lax.ppermute(upper_face, core, swapped)]
  transfers between devices with their start and end apart: 16 -> 19, of which waited for: 8 -> 8; matrix products, arithmetic and copies ran while one was open for 1% -> 1% of each run, Pallas kernels for 6% -> 8%
where the time goes in v7:
time: 87.4 us; the launch traced here: 87.1 us
  blocking collectives  39.6 us (45%)
  starting transfers between devices  27.8 us (32%)
  Pallas kernels  11.9 us (14%)
  waiting for transfers between devices  5.66 us (6%)
  local copies, waits for them, and re-layouts  1.28 us (1%)
    all_to_all x2, blocking collectives, local(): got = lax.all_to_all(offer, axes, 0, 0, tiled=True)  20 us
    all_to_all x1, blocking collectives, local(): got = lax.all_to_all(terms, 'box', 0, 0, tiled=True)  10.1 us
    all_to_all x1, blocking collectives, swap(): return lax.all_to_all(x, group(level), 0, 0, tiled=True)  9.55 us
    pallas_call x15, Pallas kernels, fused(): pl.pallas_call(body, out_shape=[pltpu.VMEM(s, f32) for s in outs], in_spe...  7.17 us
    ppermute x6, starting transfers between devices, passed_on(): lax.ppermute(held, 'box', [(i, i ^ 1 << bit_no) for i in range(cols)])  7.09 us
    pallas_call x3, Pallas kernels, placing(): pl.pallas_call(body, out_shape=[pltpu.VMEM(s, f32) for s in shapes], in_s...  4.75 us
    ppermute x3, starting transfers between devices, local(): lax.ppermute(to_send, 'box', [(i, i ^ 1 << level) for i in range(cols)])  4.1 us
    ppermute x2, starting transfers between devices, local(): other = lax.ppermute(mine, core, swapped)  3.5 us
  transfers between devices with their start and end apart: 19, of which 8 were waited for; matrix products, arithmetic and copies ran while one was open for 1% of the time, Pallas kernels for 8%

profile of v7, /device:TPU:9, one launch (start us, length us, event | category | flops | bytes accessed | tf_op | source)
XLA Modules:
  0.0 87.1 jit_solution(1937956863153342545)
XLA Ops:
  0.6 1.3 %shard_map.124 = (f32[1,48,512]{2,1,0:T(8,128)S(1)}, f32[1,32,512]{2,1,0:T(8,128)S(1)}) custom-call(f32[2,64,512]{2,1,0:T(8,128)} %bitcast.20, f32[3,64,128]{2,1,0:T(8,128)} %bitcast.18), custom_call_target="tpu_custom_call" | custom-call | tf_op jit(solution)/shard_map/pallas_call | solution.py:141
  1.9 2.4 %collective-permute-start.1 = (f32[1,48,512]{2,1,0:T(8,128)S(1)}, f32[1,48,512]{2,1,0:T(8,128)S(1)}, u32[]{:S(2)}, u32[]{:S(2)}) collective-permute-start(f32[1,48,512]{2,1,0:T(8,128)S(1)} %get-tuple-element.61.refs_1_), channel_id=1, source_target_pairs={{0,4},{1,5},{2,6},{3,7},{4,0},{5,1},{6,2},{7,3},{8,12},{9,13},{10,... | collective-permute-start | bytes 294920 | tf_op jit(solution)/shard_map/ppermute | solution.py:125
  4.3 1.8 %shard_map.122 = (f32[64,128]{1,0:T(8,128)S(1)}, f32[64,256]{1,0:T(8,128)S(1)}, f32[64,512]{1,0:T(8,128)S(1)}, f32[3,64,128]{2,1,0:T(8,128)S(1)}, f32[3,64,128]{2,1,0:T(8,128)S(1)}, /*index=5*/f32[3,64,64]{2,1,0:T(8,128)S(1)}) custom-call(f32[64,1,1,512]{3,2,1,0:T(1,128)} %load_any.1, f32[128,512]{1,0:T(8,128)} %bitcast.21, f32[3,64,128]{2,1,0:T(8,128)} %bitcast.22, ...), custom_call_target="tpu_custom_call" | custom-call | tf_op jit(solution)/shard_map/pallas_call | solution.py:141
  6.1 1.3 %collective-permute-start = (f32[64,256]{1,0:T(8,128)S(1)}, f32[64,256]{1,0:T(8,128)S(1)}, u32[]{:S(2)}, u32[]{:S(2)}) collective-permute-start(f32[64,256]{1,0:T(8,128)S(1)} %get-tuple-element.57.own_ref), channel_id=1, source_target_pairs={{0,1},{1,0},{2,3},{3,2},{4,5},{5,4},{6,7},{7,6},{8,9},{9,8},{10,11... | collective-permute-start | bytes 196616 | tf_op jit(solution)/shard_map/ppermute | solution.py:339
  7.5 1.6 %shard_map.123 = (f32[512,128]{1,0:T(8,128)S(1)}, f32[512,512]{1,0:T(8,128)S(1)}, f32[2,128,512]{2,1,0:T(8,128)S(1)}, f32[2,512,128]{2,1,0:T(8,128)S(1)}, f32[128,128]{1,0:T(8,128)S(1)}) custom-call(f32[512,640]{1,0:T(8,128)} %bitcast.15, f32[2,128,512]{2,1,0:T(8,128)} %bitcast.16, f32[2,512,128]{2,1,0:T(8,128)} %bitcast.17, f32[128,128]{1,0:T(8,128)} %bitcast.24), custom_call_target="tpu_custom_call" | custom-call | tf_op jit(solution)/shard_map/pallas_call | solution.py:141
  10.9 1.7 %collective-permute-start.6 = (f32[2,32,512]{2,1,0:T(8,128)S(1)}, f32[2,32,512]{2,1,0:T(8,128)S(1)}, u32[]{:S(2)}, u32[]{:S(2)}) collective-permute-start(f32[2,32,512]{2,1,0:T(8,128)S(1)} %get-tuple-element.75.refs_1_), channel_id=1, source_target_pairs={{0,1},{1,0},{2,3},{3,2},{4,5},{5,4},{6,7},{7,6},{8,9},{9,8},{10,11... | collective-permute-start | bytes 393224 | tf_op jit(solution)/shard_map/ppermute | solution.py:125
  13.5 2.8 %collective-permute-start.5 = (f32[256,128]{1,0:T(8,128)S(1)}, f32[256,128]{1,0:T(8,128)S(1)}, u32[]{:S(2)}, u32[]{:S(2)}) collective-permute-start(f32[256,128]{1,0:T(8,128)S(1)} %get-tuple-element.74.side_ref), channel_id=1, source_target_pairs={{0,8},{8,0},{1,9},{9,1},{2,10},{10,2},{3,11},{11,3},{4,12},{12,4},... | collective-permute-start | bytes 393224 | tf_op jit(solution)/shard_map/ppermute | solution.py:380
  16.3 2.5 %collective-permute-start.4 = (f32[64,128]{1,0:T(8,128)S(1)}, f32[64,128]{1,0:T(8,128)S(1)}, u32[]{:S(2)}, u32[]{:S(2)}) collective-permute-start(f32[64,128]{1,0:T(8,128)S(1)} %get-tuple-element.73.own_ref), channel_id=1, source_target_pairs={{0,4},{1,5},{2,6},{3,7},{4,0},{5,1},{6,2},{7,3},{8,12},{9,13},{10,... | collective-permute-start | bytes 98312 | tf_op jit(solution)/shard_map/ppermute | solution.py:339
  18.8 1.2 %collective-permute-start.8 = (f32[2,64,512]{2,1,0:T(8,128)S(1)}, f32[2,64,512]{2,1,0:T(8,128)S(1)}, u32[]{:S(2)}, u32[]{:S(2)}) collective-permute-start(f32[2,64,512]{2,1,0:T(8,128)S(1)} %get-tuple-element.79.refs_0_), channel_id=1, source_target_pairs={{0,1},{1,0},{2,3},{3,2},{4,5},{5,4},{6,7},{7,6},{8,9},{9,8},{10,11... | collective-permute-start | bytes 786440 | tf_op jit(solution)/shard_map/ppermute | solution.py:125
  20.8 10.7 %all_to_all.20.got_ref = f32[8,16,128]{2,1,0:T(8,128)S(1)} all-to-all(f32[8,16,128]{2,1,0:T(8,128)S(1)} %get-tuple-element.77), channel_id=1, replica_groups=mesh['row1'=2,'row0'=2,'box'=8] {'box'}, dimensions={0} | all-to-all | bytes 131072 | tf_op jit(solution)/shard_map/all_to_all | solution.py:742
  32.0 1.6 %collective-permute-start.11 = (f32[4,48,512]{2,1,0:T(8,128)S(1)}, f32[4,48,512]{2,1,0:T(8,128)S(1)}, u32[]{:S(2)}, u32[]{:S(2)}) collective-permute-start(f32[4,48,512]{2,1,0:T(8,128)S(1)} %get-tuple-element.85.held_ref), channel_id=1, source_target_pairs={{0,2},{1,3},{2,0},{3,1},{4,6},{5,7},{6,4},{7,5},{8,10},{9,11},{10,... | collective-permute-start | bytes 1179656 | tf_op jit(solution)/shard_map/ppermute | solution.py:125
  33.6 2.6 %collective-permute-start.9 = (f32[64,512]{1,0:T(8,128)S(1)}, f32[64,512]{1,0:T(8,128)S(1)}, u32[]{:S(2)}, u32[]{:S(2)}) collective-permute-start(f32[64,512]{1,0:T(8,128)S(1)} %get-tuple-element.81.mine_ref), channel_id=1, source_target_pairs={{0,8},{8,0},{1,9},{9,1},{2,10},{10,2},{3,11},{11,3},{4,12},{12,4},... | collective-permute-start | bytes 393224 | tf_op jit(solution)/shard_map/ppermute | solution.py:768
  36.2 1.2 %collective-permute-done.10.other_face_ref = f32[16,128]{1,0:T(8,128)S(1)} collective-permute-done((f32[16,128]{1,0:T(8,128)S(1)}, f32[16,128]{1,0:T(8,128)S(1)}, u32[]{:S(2)}, u32[]{:S(2)}) %collective-permute-start.10) | collective-permute-done | bytes 8224 | tf_op jit(solution)/shard_map/ppermute | solution.py:757
  37.9 9.2 %all_to_all.21.got_ref = f32[32,8,128]{2,1,0:T(8,128)S(1)} all-to-all(f32[32,8,128]{2,1,0:T(8,128)S(1)} %get-tuple-element.84), channel_id=1, replica_groups=mesh['row1'=2,'row0'=2,'box'=8] {'row1','row0','box'}, dimensions={0} | all-to-all | bytes 262144 | tf_op jit(solution)/shard_map/all_to_all | solution.py:742
  48.5 1.0 %collective-permute-done.12.refs_0_ = f32[64,512]{1,0:T(8,128)S(1)} collective-permute-done((f32[64,512]{1,0:T(8,128)S(1)}, f32[64,512]{1,0:T(8,128)S(1)}, u32[]{:S(2)}, u32[]{:S(2)}) %collective-permute-start.12) | collective-permute-done | bytes 131104 | tf_op jit(solution)/shard_map/ppermute | solution.py:768
  50.1 9.6 %all_to_all.22.got_ref = f32[32,8,128]{2,1,0:T(8,128)S(1)} all-to-all(f32[32,8,128]{2,1,0:T(8,128)S(1)} %get-tuple-element.86), channel_id=1, replica_groups=mesh['row1'=2,'row0'=2,'box'=8] {'row1','row0','box'}, dimensions={0} | all-to-all | bytes 262144 | tf_op jit(solution)/shard_map/all_to_all | solution.py:395
  60.3 0.9 %collective-permute-start.13 = (f32[64,256]{1,0:T(8,128)S(1)}, f32[64,256]{1,0:T(8,128)S(1)}, u32[]{:S(2)}, u32[]{:S(2)}) collective-permute-start(f32[64,256]{1,0:T(8,128)S(1)} %get-tuple-element.90), channel_id=1, source_target_pairs={{0,8},{8,0},{1,9},{9,1},{2,10},{10,2},{3,11},{11,3},{4,12},{12,4},... | collective-permute-start | bytes 196616 | tf_op jit(solution)/shard_map/ppermute | solution.py:852
  63.0 10.1 %all_to_all.23.got_ref = f32[8,64,128]{2,1,0:T(8,128)S(1)} all-to-all(f32[8,64,128]{2,1,0:T(8,128)S(1)} %get-tuple-element.97), channel_id=1, replica_groups=mesh['row1'=2,'row0'=2,'box'=8] {'box'}, dimensions={0} | all-to-all | bytes 524288 | tf_op jit(solution)/shard_map/all_to_all | solution.py:874
  73.1 1.1 %shard_map.137 = (f32[64,128]{1,0:T(8,128)S(1)}, f32[64,128]{1,0:T(8,128)S(1)}, f32[16,128]{1,0:T(8,128)S(1)}, f32[16,128]{1,0:T(8,128)S(1)}, f32[16,128]{1,0:T(8,128)S(1)}, /*index=5*/f32[16,128]{1,0:T(8,128)S(1)}) custom-call(f32[64,128]{1,0:T(8,128)S(1)} %get-tuple-element.96.g_ref, f32[64,64]{1,0:T(8,128)S(1)} %get-tuple-element.91.w_ref, ...), custom_call_target="tpu_custom_call" | custom-call | tf_op jit(solution)/shard_map/pallas_call | solution.py:37
  74.2 1.2 %collective-permute-start.15 = (f32[16,128]{1,0:T(8,128)S(1)}, f32[16,128]{1,0:T(8,128)S(1)}, u32[]{:S(2)}, u32[]{:S(2)}) collective-permute-start(f32[16,128]{1,0:T(8,128)S(1)} %get-tuple-element.106), channel_id=1, source_target_pairs={{0,1},{1,0},{2,3},{3,2},{4,5},{5,4},{6,7},{7,6},{8,9},{9,8},{10,11... | collective-permute-start | bytes 24584 | tf_op jit(solution)/shard_map/ppermute | solution.py:895
  75.5 3.3 %collective-permute-start.16 = (f32[16,128]{1,0:T(8,128)S(1)}, f32[16,128]{1,0:T(8,128)S(1)}, u32[]{:S(2)}, u32[]{:S(2)}) collective-permute-start(f32[16,128]{1,0:T(8,128)S(1)} %get-tuple-element.107), channel_id=1, source_target_pairs={{1,2},{3,4},{5,6},{2,1},{4,3},{6,5},{9,10},{11,12},{13,14},{10,9},... | collective-permute-start | bytes 24584 | tf_op jit(solution)/shard_map/ppermute | solution.py:896
  78.8 2.5 %collective-permute-start.17 = (f32[16,128]{1,0:T(8,128)S(1)}, f32[16,128]{1,0:T(8,128)S(1)}, u32[]{:S(2)}, u32[]{:S(2)}) collective-permute-start(f32[16,128]{1,0:T(8,128)S(1)} %get-tuple-element.108), channel_id=1, source_target_pairs={{0,8},{8,0},{16,24},{24,16},{1,9},{9,1},{17,25},{25,17},{2,10},{10... | collective-permute-start | bytes 24584 | tf_op jit(solution)/shard_map/ppermute | solution.py:897
  81.3 2.2 %collective-permute-start.18 = (f32[16,128]{1,0:T(8,128)S(1)}, f32[16,128]{1,0:T(8,128)S(1)}, u32[]{:S(2)}, u32[]{:S(2)}) collective-permute-start(f32[16,128]{1,0:T(8,128)S(1)} %get-tuple-element.109), channel_id=1, source_target_pairs={{8,16},{16,8},{9,17},{17,9},{10,18},{18,10},{11,19},{19,11},{12,20... | collective-permute-start | bytes 24584 | tf_op jit(solution)/shard_map/ppermute | solution.py:898
  84.4 1.8 %collective-permute-done.18.d_ref = f32[16,128]{1,0:T(8,128)S(1)} collective-permute-done((f32[16,128]{1,0:T(8,128)S(1)}, f32[16,128]{1,0:T(8,128)S(1)}, u32[]{:S(2)}, u32[]{:S(2)}) %collective-permute-start.18) | collective-permute-done | bytes 8224 | tf_op jit(solution)/shard_map/ppermute | solution.py:898
  (40 shorter events, 10.6 us)
Async XLA Ops:
  1.9 7.6 %collective-permute-start.1 = (f32[1,48,512]{2,1,0:T(8,128)S(1)}, f32[1,48,512]{2,1,0:T(8,128)S(1)}, u32[]{:S(2)}, u32[]{:S(2)}) collective-permute-start(f32[1,48,512]{2,1,0:T(8,128)S(1)} %get-tuple-element.61.refs_1_), channel_id=1, source_target_pairs={{0,4},{1,5},{2,6},{3,7},{4,0},{5,1},{6,2},{7,3},{8,12},{9,13},{10,... | collective-permute-start | bytes 294920 | tf_op jit(solution)/shard_map/ppermute | solution.py:125
  6.1 3.2 %collective-permute-start = (f32[64,256]{1,0:T(8,128)S(1)}, f32[64,256]{1,0:T(8,128)S(1)}, u32[]{:S(2)}, u32[]{:S(2)}) collective-permute-start(f32[64,256]{1,0:T(8,128)S(1)} %get-tuple-element.57.own_ref), channel_id=1, source_target_pairs={{0,1},{1,0},{2,3},{3,2},{4,5},{5,4},{6,7},{7,6},{8,9},{9,8},{10,11... | collective-permute-start | bytes 196616 | tf_op jit(solution)/shard_map/ppermute | solution.py:339
  7.4 5.2 %collective-permute-start.3 = (f32[1,32,512]{2,1,0:T(8,128)S(1)}, f32[1,32,512]{2,1,0:T(8,128)S(1)}, u32[]{:S(2)}, u32[]{:S(2)}) collective-permute-start(f32[1,32,512]{2,1,0:T(8,128)S(1)} %get-tuple-element.70.refs_2_), channel_id=1, source_target_pairs={{0,4},{1,5},{2,6},{3,7},{4,0},{5,1},{6,2},{7,3},{8,12},{9,13},{10,... | collective-permute-start | bytes 196616 | tf_op jit(solution)/shard_map/ppermute | solution.py:125
  9.9 3.1 %collective-permute-start.2 = (f32[64,128]{1,0:T(8,128)S(1)}, f32[64,128]{1,0:T(8,128)S(1)}, u32[]{:S(2)}, u32[]{:S(2)}) collective-permute-start(f32[64,128]{1,0:T(8,128)S(1)} %get-tuple-element.63.own_ref), channel_id=1, source_target_pairs={{0,2},{1,3},{2,0},{3,1},{4,6},{5,7},{6,4},{7,5},{8,10},{9,11},{10,... | collective-permute-start | bytes 98312 | tf_op jit(solution)/shard_map/ppermute | solution.py:339
  10.9 9.2 %collective-permute-start.6 = (f32[2,32,512]{2,1,0:T(8,128)S(1)}, f32[2,32,512]{2,1,0:T(8,128)S(1)}, u32[]{:S(2)}, u32[]{:S(2)}) collective-permute-start(f32[2,32,512]{2,1,0:T(8,128)S(1)} %get-tuple-element.75.refs_1_), channel_id=1, source_target_pairs={{0,1},{1,0},{2,3},{3,2},{4,5},{5,4},{6,7},{7,6},{8,9},{9,8},{10,11... | collective-permute-start | bytes 393224 | tf_op jit(solution)/shard_map/ppermute | solution.py:125
  13.5 6.6 %collective-permute-start.5 = (f32[256,128]{1,0:T(8,128)S(1)}, f32[256,128]{1,0:T(8,128)S(1)}, u32[]{:S(2)}, u32[]{:S(2)}) collective-permute-start(f32[256,128]{1,0:T(8,128)S(1)} %get-tuple-element.74.side_ref), channel_id=1, source_target_pairs={{0,8},{8,0},{1,9},{9,1},{2,10},{10,2},{3,11},{11,3},{4,12},{12,4},... | collective-permute-start | bytes 393224 | tf_op jit(solution)/shard_map/ppermute | solution.py:380
  16.3 3.8 %collective-permute-start.4 = (f32[64,128]{1,0:T(8,128)S(1)}, f32[64,128]{1,0:T(8,128)S(1)}, u32[]{:S(2)}, u32[]{:S(2)}) collective-permute-start(f32[64,128]{1,0:T(8,128)S(1)} %get-tuple-element.73.own_ref), channel_id=1, source_target_pairs={{0,4},{1,5},{2,6},{3,7},{4,0},{5,1},{6,2},{7,3},{8,12},{9,13},{10,... | collective-permute-start | bytes 98312 | tf_op jit(solution)/shard_map/ppermute | solution.py:339
  18.8 12.7 %collective-permute-start.8 = (f32[2,64,512]{2,1,0:T(8,128)S(1)}, f32[2,64,512]{2,1,0:T(8,128)S(1)}, u32[]{:S(2)}, u32[]{:S(2)}) collective-permute-start(f32[2,64,512]{2,1,0:T(8,128)S(1)} %get-tuple-element.79.refs_0_), channel_id=1, source_target_pairs={{0,1},{1,0},{2,3},{3,2},{4,5},{5,4},{6,7},{7,6},{8,9},{9,8},{10,11... | collective-permute-start | bytes 786440 | tf_op jit(solution)/shard_map/ppermute | solution.py:125
  20.5 11.0 %collective-permute-start.7 = (f32[4,32,512]{2,1,0:T(8,128)S(1)}, f32[4,32,512]{2,1,0:T(8,128)S(1)}, u32[]{:S(2)}, u32[]{:S(2)}) collective-permute-start(f32[4,32,512]{2,1,0:T(8,128)S(1)} %get-tuple-element.78.held_ref), channel_id=1, source_target_pairs={{0,2},{1,3},{2,0},{3,1},{4,6},{5,7},{6,4},{7,5},{8,10},{9,11},{10,... | collective-permute-start | bytes 786440 | tf_op jit(solution)/shard_map/ppermute | solution.py:125
  31.9 17.5 %copy-start = (f32[1,1,128]{2,1,0:T(1,128)S(1)}, f32[1,1,128]{2,1,0:T(1,128)}, u32[]{:S(2)}) copy-start(f32[1,1,128]{2,1,0:T(1,128)} %param.21) | copy-start | bytes 1540
  32.0 15.2 %collective-permute-start.11 = (f32[4,48,512]{2,1,0:T(8,128)S(1)}, f32[4,48,512]{2,1,0:T(8,128)S(1)}, u32[]{:S(2)}, u32[]{:S(2)}) collective-permute-start(f32[4,48,512]{2,1,0:T(8,128)S(1)} %get-tuple-element.85.held_ref), channel_id=1, source_target_pairs={{0,2},{1,3},{2,0},{3,1},{4,6},{5,7},{6,4},{7,5},{8,10},{9,11},{10,... | collective-permute-start | bytes 1179656 | tf_op jit(solution)/shard_map/ppermute | solution.py:125
  33.6 3.8 %collective-permute-start.9 = (f32[64,512]{1,0:T(8,128)S(1)}, f32[64,512]{1,0:T(8,128)S(1)}, u32[]{:S(2)}, u32[]{:S(2)}) collective-permute-start(f32[64,512]{1,0:T(8,128)S(1)} %get-tuple-element.81.mine_ref), channel_id=1, source_target_pairs={{0,8},{8,0},{1,9},{9,1},{2,10},{10,2},{3,11},{11,3},{4,12},{12,4},... | collective-permute-start | bytes 393224 | tf_op jit(solution)/shard_map/ppermute | solution.py:768
  36.2 1.2 %collective-permute-start.10 = (f32[16,128]{1,0:T(8,128)S(1)}, f32[16,128]{1,0:T(8,128)S(1)}, u32[]{:S(2)}, u32[]{:S(2)}) collective-permute-start(f32[16,128]{1,0:T(8,128)S(1)} %get-tuple-element.82.face_ref), channel_id=1, source_target_pairs={{0,8},{8,0},{1,9},{9,1},{2,10},{10,2},{3,11},{11,3},{4,12},{12,4},... | collective-permute-start | bytes 24584 | tf_op jit(solution)/shard_map/ppermute | solution.py:757
  47.6 1.9 %collective-permute-start.12 = (f32[64,512]{1,0:T(8,128)S(1)}, f32[64,512]{1,0:T(8,128)S(1)}, u32[]{:S(2)}, u32[]{:S(2)}) collective-permute-start(f32[64,512]{1,0:T(8,128)S(1)} %shard_map.132.got_ref), channel_id=1, source_target_pairs={{0,8},{8,0},{1,9},{9,1},{2,10},{10,2},{3,11},{11,3},{4,12},{12,4},... | collective-permute-start | bytes 393224 | tf_op jit(solution)/shard_map/ppermute | solution.py:768
  60.3 2.1 %collective-permute-start.13 = (f32[64,256]{1,0:T(8,128)S(1)}, f32[64,256]{1,0:T(8,128)S(1)}, u32[]{:S(2)}, u32[]{:S(2)}) collective-permute-start(f32[64,256]{1,0:T(8,128)S(1)} %get-tuple-element.90), channel_id=1, source_target_pairs={{0,8},{8,0},{1,9},{9,1},{2,10},{10,2},{3,11},{11,3},{4,12},{12,4},... | collective-permute-start | bytes 196616 | tf_op jit(solution)/shard_map/ppermute | solution.py:852
  61.2 1.2 %collective-permute-start.14 = (f32[32,32]{1,0:T(8,128)S(1)}, f32[32,32]{1,0:T(8,128)S(1)}, u32[]{:S(2)}, u32[]{:S(2)}) collective-permute-start(f32[32,32]{1,0:T(8,128)S(1)} %get-tuple-element.95.refs_1_), channel_id=1, source_target_pairs={{0,8},{8,0},{1,9},{9,1},{2,10},{10,2},{3,11},{11,3},{4,12},{12,4},... | collective-permute-start | bytes 12296 | tf_op jit(solution)/shard_map/ppermute | solution.py:863
  74.2 10.2 %collective-permute-start.15 = (f32[16,128]{1,0:T(8,128)S(1)}, f32[16,128]{1,0:T(8,128)S(1)}, u32[]{:S(2)}, u32[]{:S(2)}) collective-permute-start(f32[16,128]{1,0:T(8,128)S(1)} %get-tuple-element.106), channel_id=1, source_target_pairs={{0,1},{1,0},{2,3},{3,2},{4,5},{5,4},{6,7},{7,6},{8,9},{9,8},{10,11... | collective-permute-start | bytes 24584 | tf_op jit(solution)/shard_map/ppermute | solution.py:895
  75.5 8.9 %collective-permute-start.16 = (f32[16,128]{1,0:T(8,128)S(1)}, f32[16,128]{1,0:T(8,128)S(1)}, u32[]{:S(2)}, u32[]{:S(2)}) collective-permute-start(f32[16,128]{1,0:T(8,128)S(1)} %get-tuple-element.107), channel_id=1, source_target_pairs={{1,2},{3,4},{5,6},{2,1},{4,3},{6,5},{9,10},{11,12},{13,14},{10,9},... | collective-permute-start | bytes 24584 | tf_op jit(solution)/shard_map/ppermute | solution.py:896
  78.8 5.6 %collective-permute-start.17 = (f32[16,128]{1,0:T(8,128)S(1)}, f32[16,128]{1,0:T(8,128)S(1)}, u32[]{:S(2)}, u32[]{:S(2)}) collective-permute-start(f32[16,128]{1,0:T(8,128)S(1)} %get-tuple-element.108), channel_id=1, source_target_pairs={{0,8},{8,0},{16,24},{24,16},{1,9},{9,1},{17,25},{25,17},{2,10},{10... | collective-permute-start | bytes 24584 | tf_op jit(solution)/shard_map/ppermute | solution.py:897
  81.3 5.0 %collective-permute-start.18 = (f32[16,128]{1,0:T(8,128)S(1)}, f32[16,128]{1,0:T(8,128)S(1)}, u32[]{:S(2)}, u32[]{:S(2)}) collective-permute-start(f32[16,128]{1,0:T(8,128)S(1)} %get-tuple-element.109), channel_id=1, source_target_pairs={{8,16},{16,8},{9,17},{17,9},{10,18},{18,10},{11,19},{19,11},{12,20... | collective-permute-start | bytes 24584 | tf_op jit(solution)/shard_map/ppermute | solution.py:898

commit v8 on v7

--- a/solution.py
+++ b/solution.py
@@ -25,7 +25,8 @@
 
     a_high, a_low = parts(a)
     b_high, b_low = parts(b)
-    return product(a_high, b_high) + (product(a_high, b_low) + product(a_low, b_high))
+    both = product(jnp.concatenate([a_high, a_low], axis=0), b_high)
+    return both[: a.shape[0]] + (product(a_high, b_low) + both[a.shape[0] :])
 
 
 def dot_t(a, b):
@@ -620,7 +621,39 @@
         node_starts.append(sum(cols >> (i + 1) for i in range(k)) * pair)
     node_lanes = (cols - 1) * pair
 
-    def prepare_body(g_ref, w_ref, xi_ref, held_ref, moved_ref, matrix_out, known_out):
+    inner_lanes = x_levels * edge
+
+    def prepare_body(g_ref, w_ref, xi_ref, held_ref, moved_ref, lo_ref, *refs):
+        keep_ref, ends_ref = refs[:x_levels], refs[x_levels : 2 * x_levels - 1]
+        matrix_out, known_out, chain_out, keep_out = refs[2 * x_levels - 1 :]
+        unit = lax.broadcasted_iota(jnp.int32, (edge, inner_lanes), 0)
+        unit = lax.broadcasted_iota(jnp.int32, (edge, inner_lanes), 1) - unit
+        gl = jnp.zeros((edge, inner_lanes), f32)
+        gr = gl
+        for level in reversed(range(x_levels)):
+            is_right = bit(my_column(), level) == 1
+            keep = keep_ref[level][...]
+            keep_out[:, level * edge : (level + 1) * edge] = jnp.where(
+                is_right, keep[:, edge:], keep[:, :edge]
+            )
+            value = jnp.where(unit == level * edge, 1.0, 0.0)
+            if level < x_levels - 1:
+                end = ends_ref[level][...]
+                end = jnp.where(is_right, end[edge:], end[:edge])
+                value = value + dot(end, jnp.concatenate([gl, gr], axis=0))
+            gl = jnp.where(is_right, value, gl)
+            gr = jnp.where(is_right, gr, value)
+        none = jnp.zeros((edge, inner_lanes), f32)
+        out_map = lo_ref[...]
+        added = dot(out_map, jnp.concatenate([none, gr, none, gl], axis=0))
+        none = jnp.zeros((pair, leaf), f32)
+        chain_out[...] = jnp.concatenate(
+            [
+                jnp.concatenate([out_map, added], axis=1),
+                jnp.concatenate([none, jnp.concatenate([gr, gl], axis=0)], axis=1),
+            ],
+            axis=0,
+        )
         g = with_row_edge(0, g_ref[...], w_ref[...], 0.0)
         row = []
         for c in range(cols):
@@ -674,28 +707,17 @@
                 picked.append(piece)
             out_ref[c] = pad_lanes(jnp.concatenate(picked + [edge_of(q, c)], axis=1), x_lanes)
 
-    def finish_body(g_ref, w_ref, h0_ref, got_ref, lo_ref, *refs):
-        keep_ref, ends_ref = refs[:x_levels], refs[x_levels : 2 * x_levels - 1]
-        g_out, t_out, *faces = refs[2 * x_levels - 1 :]
+    def finish_body(g_ref, w_ref, h0_ref, got_ref, chain_ref, keep_ref, g_out, t_out, *faces):
         q = jnp.sum(got_ref[...], axis=0)
         g = with_row_edge(0, g_ref[...], w_ref[...], edge_of(q, x_levels))
-        gl = jnp.zeros((waves, edge), f32)
-        gr = gl
-        for level in reversed(range(x_levels)):
-            is_right = bit(my_column(), level) == 1
-            keep = keep_ref[level][...]
-            value = edge_of(q, level) + jnp.where(is_right, keep[:, edge:], keep[:, :edge])
-            if level < x_levels - 1:
-                end = ends_ref[level][...]
-                end = jnp.where(is_right, end[edge:], end[:edge])
-                value = value + dot_t(jnp.concatenate([gl, gr], axis=1), end)
-            gl = jnp.where(is_right, value, gl)
-            gr = jnp.where(is_right, gr, value)
+        terms = q[:, :inner_lanes] + keep_ref[...]
+        result = dot_t(jnp.concatenate([g, terms], axis=1), chain_ref[...])
+        gr, gl = edge_of(result, 4), edge_of(result, 5)
         g = jnp.concatenate(
             [edge_of(g, 0), edge_of(g, 1) + gr, edge_of(g, 2), edge_of(g, 3) + gl], axis=1
         )
         g_out[...] = g
-        t = g - (dot_t(g, lo_ref[...]) + h0_ref[...])
+        t = g - (result[:, :leaf] + h0_ref[...])
         t_out[...] = t
         odd_col = bit(my_column(), 0) == 1
         odd_row = bit(my_row(), 0) == 1
@@ -850,13 +872,21 @@
             split_body, [(waves, leaf), share, share], g, y_keep[1], total, yi_all
         )
     got = lax.ppermute(other, core, swapped)
-    matrix, known = fused(
+    matrix, known, chain, keep = fused(
         prepare_body,
-        [(node_lanes, cols * edge), (waves, node_lanes)],
+        [
+            (node_lanes, cols * edge),
+            (waves, node_lanes),
+            (leaf + pair, leaf + inner_lanes),
+            (waves, inner_lanes),
+        ],
         g,
         y_keep[0],
         xi_all,
         *((second, second_moved) if whole_solve else (held, moved)),
+        out_map,
+        *x_keep,
+        *ends,
     )
     upper = []
     if whole_solve:
@@ -879,9 +909,8 @@
         y_keep[0],
         h0,
         got,
-        out_map,
-        *x_keep,
-        *ends,
+        chain,
+        keep,
     )
 
     def near(count):

time: 87.4 us -> 86.2 us (0.986)
  Pallas kernels: 11.9 us -> 10.7 us
    pallas_call x15, Pallas kernels: 7.17 us -> 6 us  [fused(): pl.pallas_call(body, out_shape=[pltpu.VMEM(s, f32) for s in outs], in_spe...]
where the time goes in v8:
time: 86.2 us; the launch traced here: 85.9 us
  blocking collectives  39.7 us (46%)
  starting transfers between devices  27.7 us (32%)
  Pallas kernels  10.7 us (12%)
  waiting for transfers between devices  5.77 us (7%)
  local copies, waits for them, and re-layouts  1.28 us (1%)
    all_to_all x2, blocking collectives, local(): got = lax.all_to_all(offer, axes, 0, 0, tiled=True)  20 us
    all_to_all x1, blocking collectives, local(): got = lax.all_to_all(terms, 'box', 0, 0, tiled=True)  10.1 us
    all_to_all x1, blocking collectives, swap(): return lax.all_to_all(x, group(level), 0, 0, tiled=True)  9.56 us
    ppermute x6, starting transfers between devices, passed_on(): lax.ppermute(held, 'box', [(i, i ^ 1 << bit_no) for i in range(cols)])  7.05 us
    pallas_call x15, Pallas kernels, fused(): pl.pallas_call(body, out_shape=[pltpu.VMEM(s, f32) for s in outs], in_spe...  6 us
    pallas_call x3, Pallas kernels, placing(): pl.pallas_call(body, out_shape=[pltpu.VMEM(s, f32) for s in shapes], in_s...  4.73 us
    ppermute x3, starting transfers between devices, local(): lax.ppermute(to_send, 'box', [(i, i ^ 1 << level) for i in range(cols)])  4.1 us
    ppermute x2, starting transfers between devices, local(): other = lax.ppermute(mine, core, swapped)  3.5 us
  transfers between devices with their start and end apart: 19, of which 8 were waited for; matrix products, arithmetic and copies ran while one was open for 1% of the time, Pallas kernels for 8%

profile of v8, /device:TPU:9, one launch (start us, length us, event | category | flops | bytes accessed | tf_op | source)
XLA Modules:
  0.0 85.9 jit_solution(15103023960944514369)
XLA Ops:
  0.6 1.3 %shard_map.124 = (f32[1,48,512]{2,1,0:T(8,128)S(1)}, f32[1,32,512]{2,1,0:T(8,128)S(1)}) custom-call(f32[2,64,512]{2,1,0:T(8,128)} %bitcast.20, f32[3,64,128]{2,1,0:T(8,128)} %bitcast.18), custom_call_target="tpu_custom_call" | custom-call | tf_op jit(solution)/shard_map/pallas_call | solution.py:142
  1.9 2.4 %collective-permute-start.1 = (f32[1,48,512]{2,1,0:T(8,128)S(1)}, f32[1,48,512]{2,1,0:T(8,128)S(1)}, u32[]{:S(2)}, u32[]{:S(2)}) collective-permute-start(f32[1,48,512]{2,1,0:T(8,128)S(1)} %get-tuple-element.63.refs_1_), channel_id=1, source_target_pairs={{0,4},{1,5},{2,6},{3,7},{4,0},{5,1},{6,2},{7,3},{8,12},{9,13},{10,... | collective-permute-start | bytes 294920 | tf_op jit(solution)/shard_map/ppermute | solution.py:126
  4.3 1.8 %shard_map.122 = (f32[64,128]{1,0:T(8,128)S(1)}, f32[64,256]{1,0:T(8,128)S(1)}, f32[64,512]{1,0:T(8,128)S(1)}, f32[3,64,128]{2,1,0:T(8,128)S(1)}, f32[3,64,128]{2,1,0:T(8,128)S(1)}, /*index=5*/f32[3,64,64]{2,1,0:T(8,128)S(1)}) custom-call(f32[64,1,1,512]{3,2,1,0:T(1,128)} %load_any.1, f32[128,512]{1,0:T(8,128)} %bitcast.21, f32[3,64,128]{2,1,0:T(8,128)} %bitcast.22, ...), custom_call_target="tpu_custom_call" | custom-call | tf_op jit(solution)/shard_map/pallas_call | solution.py:142
  6.1 1.3 %collective-permute-start = (f32[64,256]{1,0:T(8,128)S(1)}, f32[64,256]{1,0:T(8,128)S(1)}, u32[]{:S(2)}, u32[]{:S(2)}) collective-permute-start(f32[64,256]{1,0:T(8,128)S(1)} %get-tuple-element.59.own_ref), channel_id=1, source_target_pairs={{0,1},{1,0},{2,3},{3,2},{4,5},{5,4},{6,7},{7,6},{8,9},{9,8},{10,11... | collective-permute-start | bytes 196616 | tf_op jit(solution)/shard_map/ppermute | solution.py:340
  7.4 1.6 %shard_map.123 = (f32[512,128]{1,0:T(8,128)S(1)}, f32[512,512]{1,0:T(8,128)S(1)}, f32[2,128,512]{2,1,0:T(8,128)S(1)}, f32[2,512,128]{2,1,0:T(8,128)S(1)}, f32[128,128]{1,0:T(8,128)S(1)}) custom-call(f32[512,640]{1,0:T(8,128)} %bitcast.15, f32[2,128,512]{2,1,0:T(8,128)} %bitcast.16, f32[2,512,128]{2,1,0:T(8,128)} %bitcast.17, f32[128,128]{1,0:T(8,128)} %bitcast.24), custom_call_target="tpu_custom_call" | custom-call | tf_op jit(solution)/shard_map/pallas_call | solution.py:142
  10.7 1.7 %collective-permute-start.6 = (f32[2,32,512]{2,1,0:T(8,128)S(1)}, f32[2,32,512]{2,1,0:T(8,128)S(1)}, u32[]{:S(2)}, u32[]{:S(2)}) collective-permute-start(f32[2,32,512]{2,1,0:T(8,128)S(1)} %get-tuple-element.77.refs_1_), channel_id=1, source_target_pairs={{0,1},{1,0},{2,3},{3,2},{4,5},{5,4},{6,7},{7,6},{8,9},{9,8},{10,11... | collective-permute-start | bytes 393224 | tf_op jit(solution)/shard_map/ppermute | solution.py:126
  13.4 2.8 %collective-permute-start.5 = (f32[256,128]{1,0:T(8,128)S(1)}, f32[256,128]{1,0:T(8,128)S(1)}, u32[]{:S(2)}, u32[]{:S(2)}) collective-permute-start(f32[256,128]{1,0:T(8,128)S(1)} %get-tuple-element.76.side_ref), channel_id=1, source_target_pairs={{0,8},{8,0},{1,9},{9,1},{2,10},{10,2},{3,11},{11,3},{4,12},{12,4},... | collective-permute-start | bytes 393224 | tf_op jit(solution)/shard_map/ppermute | solution.py:381
  16.2 2.5 %collective-permute-start.4 = (f32[64,128]{1,0:T(8,128)S(1)}, f32[64,128]{1,0:T(8,128)S(1)}, u32[]{:S(2)}, u32[]{:S(2)}) collective-permute-start(f32[64,128]{1,0:T(8,128)S(1)} %get-tuple-element.75.own_ref), channel_id=1, source_target_pairs={{0,4},{1,5},{2,6},{3,7},{4,0},{5,1},{6,2},{7,3},{8,12},{9,13},{10,... | collective-permute-start | bytes 98312 | tf_op jit(solution)/shard_map/ppermute | solution.py:340
  18.7 1.2 %collective-permute-start.8 = (f32[2,64,512]{2,1,0:T(8,128)S(1)}, f32[2,64,512]{2,1,0:T(8,128)S(1)}, u32[]{:S(2)}, u32[]{:S(2)}) collective-permute-start(f32[2,64,512]{2,1,0:T(8,128)S(1)} %get-tuple-element.81.refs_0_), channel_id=1, source_target_pairs={{0,1},{1,0},{2,3},{3,2},{4,5},{5,4},{6,7},{7,6},{8,9},{9,8},{10,11... | collective-permute-start | bytes 786440 | tf_op jit(solution)/shard_map/ppermute | solution.py:126
  20.6 10.7 %all_to_all.20.got_ref = f32[8,16,128]{2,1,0:T(8,128)S(1)} all-to-all(f32[8,16,128]{2,1,0:T(8,128)S(1)} %get-tuple-element.79), channel_id=1, replica_groups=mesh['row1'=2,'row0'=2,'box'=8] {'box'}, dimensions={0} | all-to-all | bytes 131072 | tf_op jit(solution)/shard_map/all_to_all | solution.py:764
  31.8 1.6 %collective-permute-start.11 = (f32[4,48,512]{2,1,0:T(8,128)S(1)}, f32[4,48,512]{2,1,0:T(8,128)S(1)}, u32[]{:S(2)}, u32[]{:S(2)}) collective-permute-start(f32[4,48,512]{2,1,0:T(8,128)S(1)} %get-tuple-element.87.held_ref), channel_id=1, source_target_pairs={{0,2},{1,3},{2,0},{3,1},{4,6},{5,7},{6,4},{7,5},{8,10},{9,11},{10,... | collective-permute-start | bytes 1179656 | tf_op jit(solution)/shard_map/ppermute | solution.py:126
  33.4 2.6 %collective-permute-start.9 = (f32[64,512]{1,0:T(8,128)S(1)}, f32[64,512]{1,0:T(8,128)S(1)}, u32[]{:S(2)}, u32[]{:S(2)}) collective-permute-start(f32[64,512]{1,0:T(8,128)S(1)} %get-tuple-element.83.mine_ref), channel_id=1, source_target_pairs={{0,8},{8,0},{1,9},{9,1},{2,10},{10,2},{3,11},{11,3},{4,12},{12,4},... | collective-permute-start | bytes 393224 | tf_op jit(solution)/shard_map/ppermute | solution.py:790
  36.0 1.2 %collective-permute-done.10.other_face_ref = f32[16,128]{1,0:T(8,128)S(1)} collective-permute-done((f32[16,128]{1,0:T(8,128)S(1)}, f32[16,128]{1,0:T(8,128)S(1)}, u32[]{:S(2)}, u32[]{:S(2)}) %collective-permute-start.10) | collective-permute-done | bytes 8224 | tf_op jit(solution)/shard_map/ppermute | solution.py:779
  37.7 9.2 %all_to_all.21.got_ref = f32[32,8,128]{2,1,0:T(8,128)S(1)} all-to-all(f32[32,8,128]{2,1,0:T(8,128)S(1)} %get-tuple-element.86), channel_id=1, replica_groups=mesh['row1'=2,'row0'=2,'box'=8] {'row1','row0','box'}, dimensions={0} | all-to-all | bytes 262144 | tf_op jit(solution)/shard_map/all_to_all | solution.py:764
  47.3 0.9 %collective-permute-start.12 = (f32[64,512]{1,0:T(8,128)S(1)}, f32[64,512]{1,0:T(8,128)S(1)}, u32[]{:S(2)}, u32[]{:S(2)}) collective-permute-start(f32[64,512]{1,0:T(8,128)S(1)} %shard_map.132.got_ref), channel_id=1, source_target_pairs={{0,8},{8,0},{1,9},{9,1},{2,10},{10,2},{3,11},{11,3},{4,12},{12,4},... | collective-permute-start | bytes 393224 | tf_op jit(solution)/shard_map/ppermute | solution.py:790
  48.2 1.0 %collective-permute-done.12.refs_0_ = f32[64,512]{1,0:T(8,128)S(1)} collective-permute-done((f32[64,512]{1,0:T(8,128)S(1)}, f32[64,512]{1,0:T(8,128)S(1)}, u32[]{:S(2)}, u32[]{:S(2)}) %collective-permute-start.12) | collective-permute-done | bytes 131104 | tf_op jit(solution)/shard_map/ppermute | solution.py:790
  49.8 9.6 %all_to_all.22.got_ref = f32[32,8,128]{2,1,0:T(8,128)S(1)} all-to-all(f32[32,8,128]{2,1,0:T(8,128)S(1)} %get-tuple-element.88), channel_id=1, replica_groups=mesh['row1'=2,'row0'=2,'box'=8] {'row1','row0','box'}, dimensions={0} | all-to-all | bytes 262144 | tf_op jit(solution)/shard_map/all_to_all | solution.py:396
  59.9 0.9 %collective-permute-start.13 = (f32[64,256]{1,0:T(8,128)S(1)}, f32[64,256]{1,0:T(8,128)S(1)}, u32[]{:S(2)}, u32[]{:S(2)}) collective-permute-start(f32[64,256]{1,0:T(8,128)S(1)} %get-tuple-element.92), channel_id=1, source_target_pairs={{0,8},{8,0},{1,9},{9,1},{2,10},{10,2},{3,11},{11,3},{4,12},{12,4},... | collective-permute-start | bytes 196616 | tf_op jit(solution)/shard_map/ppermute | solution.py:874
  62.5 10.1 %all_to_all.23.got_ref = f32[8,64,128]{2,1,0:T(8,128)S(1)} all-to-all(f32[8,64,128]{2,1,0:T(8,128)S(1)} %get-tuple-element.104), channel_id=1, replica_groups=mesh['row1'=2,'row0'=2,'box'=8] {'box'}, dimensions={0} | all-to-all | bytes 524288 | tf_op jit(solution)/shard_map/all_to_all | solution.py:904
  73.1 1.2 %collective-permute-start.15 = (f32[16,128]{1,0:T(8,128)S(1)}, f32[16,128]{1,0:T(8,128)S(1)}, u32[]{:S(2)}, u32[]{:S(2)}) collective-permute-start(f32[16,128]{1,0:T(8,128)S(1)} %get-tuple-element.110), channel_id=1, source_target_pairs={{0,1},{1,0},{2,3},{3,2},{4,5},{5,4},{6,7},{7,6},{8,9},{9,8},{10,11... | collective-permute-start | bytes 24584 | tf_op jit(solution)/shard_map/ppermute | solution.py:924
  74.3 3.3 %collective-permute-start.16 = (f32[16,128]{1,0:T(8,128)S(1)}, f32[16,128]{1,0:T(8,128)S(1)}, u32[]{:S(2)}, u32[]{:S(2)}) collective-permute-start(f32[16,128]{1,0:T(8,128)S(1)} %get-tuple-element.111), channel_id=1, source_target_pairs={{1,2},{3,4},{5,6},{2,1},{4,3},{6,5},{9,10},{11,12},{13,14},{10,9},... | collective-permute-start | bytes 24584 | tf_op jit(solution)/shard_map/ppermute | solution.py:925
  77.6 2.5 %collective-permute-start.17 = (f32[16,128]{1,0:T(8,128)S(1)}, f32[16,128]{1,0:T(8,128)S(1)}, u32[]{:S(2)}, u32[]{:S(2)}) collective-permute-start(f32[16,128]{1,0:T(8,128)S(1)} %get-tuple-element.112), channel_id=1, source_target_pairs={{0,8},{8,0},{16,24},{24,16},{1,9},{9,1},{17,25},{25,17},{2,10},{10... | collective-permute-start | bytes 24584 | tf_op jit(solution)/shard_map/ppermute | solution.py:926
  80.2 2.2 %collective-permute-start.18 = (f32[16,128]{1,0:T(8,128)S(1)}, f32[16,128]{1,0:T(8,128)S(1)}, u32[]{:S(2)}, u32[]{:S(2)}) collective-permute-start(f32[16,128]{1,0:T(8,128)S(1)} %get-tuple-element.113), channel_id=1, source_target_pairs={{8,16},{16,8},{9,17},{17,9},{10,18},{18,10},{11,19},{19,11},{12,20... | collective-permute-start | bytes 24584 | tf_op jit(solution)/shard_map/ppermute | solution.py:927
  83.2 1.9 %collective-permute-done.18.d_ref = f32[16,128]{1,0:T(8,128)S(1)} collective-permute-done((f32[16,128]{1,0:T(8,128)S(1)}, f32[16,128]{1,0:T(8,128)S(1)}, u32[]{:S(2)}, u32[]{:S(2)}) %collective-permute-start.18) | collective-permute-done | bytes 8224 | tf_op jit(solution)/shard_map/ppermute | solution.py:927
  (40 shorter events, 9.6 us)
Async XLA Ops:
  1.9 7.6 %collective-permute-start.1 = (f32[1,48,512]{2,1,0:T(8,128)S(1)}, f32[1,48,512]{2,1,0:T(8,128)S(1)}, u32[]{:S(2)}, u32[]{:S(2)}) collective-permute-start(f32[1,48,512]{2,1,0:T(8,128)S(1)} %get-tuple-element.63.refs_1_), channel_id=1, source_target_pairs={{0,4},{1,5},{2,6},{3,7},{4,0},{5,1},{6,2},{7,3},{8,12},{9,13},{10,... | collective-permute-start | bytes 294920 | tf_op jit(solution)/shard_map/ppermute | solution.py:126
  6.1 3.2 %collective-permute-start = (f32[64,256]{1,0:T(8,128)S(1)}, f32[64,256]{1,0:T(8,128)S(1)}, u32[]{:S(2)}, u32[]{:S(2)}) collective-permute-start(f32[64,256]{1,0:T(8,128)S(1)} %get-tuple-element.59.own_ref), channel_id=1, source_target_pairs={{0,1},{1,0},{2,3},{3,2},{4,5},{5,4},{6,7},{7,6},{8,9},{9,8},{10,11... | collective-permute-start | bytes 196616 | tf_op jit(solution)/shard_map/ppermute | solution.py:340
  7.4 5.0 %collective-permute-start.3 = (f32[1,32,512]{2,1,0:T(8,128)S(1)}, f32[1,32,512]{2,1,0:T(8,128)S(1)}, u32[]{:S(2)}, u32[]{:S(2)}) collective-permute-start(f32[1,32,512]{2,1,0:T(8,128)S(1)} %get-tuple-element.72.refs_2_), channel_id=1, source_target_pairs={{0,4},{1,5},{2,6},{3,7},{4,0},{5,1},{6,2},{7,3},{8,12},{9,13},{10,... | collective-permute-start | bytes 196616 | tf_op jit(solution)/shard_map/ppermute | solution.py:126
  9.9 3.1 %collective-permute-start.2 = (f32[64,128]{1,0:T(8,128)S(1)}, f32[64,128]{1,0:T(8,128)S(1)}, u32[]{:S(2)}, u32[]{:S(2)}) collective-permute-start(f32[64,128]{1,0:T(8,128)S(1)} %get-tuple-element.65.own_ref), channel_id=1, source_target_pairs={{0,2},{1,3},{2,0},{3,1},{4,6},{5,7},{6,4},{7,5},{8,10},{9,11},{10,... | collective-permute-start | bytes 98312 | tf_op jit(solution)/shard_map/ppermute | solution.py:340
  10.7 9.4 %collective-permute-start.6 = (f32[2,32,512]{2,1,0:T(8,128)S(1)}, f32[2,32,512]{2,1,0:T(8,128)S(1)}, u32[]{:S(2)}, u32[]{:S(2)}) collective-permute-start(f32[2,32,512]{2,1,0:T(8,128)S(1)} %get-tuple-element.77.refs_1_), channel_id=1, source_target_pairs={{0,1},{1,0},{2,3},{3,2},{4,5},{5,4},{6,7},{7,6},{8,9},{9,8},{10,11... | collective-permute-start | bytes 393224 | tf_op jit(solution)/shard_map/ppermute | solution.py:126
  13.4 6.6 %collective-permute-start.5 = (f32[256,128]{1,0:T(8,128)S(1)}, f32[256,128]{1,0:T(8,128)S(1)}, u32[]{:S(2)}, u32[]{:S(2)}) collective-permute-start(f32[256,128]{1,0:T(8,128)S(1)} %get-tuple-element.76.side_ref), channel_id=1, source_target_pairs={{0,8},{8,0},{1,9},{9,1},{2,10},{10,2},{3,11},{11,3},{4,12},{12,4},... | collective-permute-start | bytes 393224 | tf_op jit(solution)/shard_map/ppermute | solution.py:381
  16.2 3.8 %collective-permute-start.4 = (f32[64,128]{1,0:T(8,128)S(1)}, f32[64,128]{1,0:T(8,128)S(1)}, u32[]{:S(2)}, u32[]{:S(2)}) collective-permute-start(f32[64,128]{1,0:T(8,128)S(1)} %get-tuple-element.75.own_ref), channel_id=1, source_target_pairs={{0,4},{1,5},{2,6},{3,7},{4,0},{5,1},{6,2},{7,3},{8,12},{9,13},{10,... | collective-permute-start | bytes 98312 | tf_op jit(solution)/shard_map/ppermute | solution.py:340
  18.7 12.7 %collective-permute-start.8 = (f32[2,64,512]{2,1,0:T(8,128)S(1)}, f32[2,64,512]{2,1,0:T(8,128)S(1)}, u32[]{:S(2)}, u32[]{:S(2)}) collective-permute-start(f32[2,64,512]{2,1,0:T(8,128)S(1)} %get-tuple-element.81.refs_0_), channel_id=1, source_target_pairs={{0,1},{1,0},{2,3},{3,2},{4,5},{5,4},{6,7},{7,6},{8,9},{9,8},{10,11... | collective-permute-start | bytes 786440 | tf_op jit(solution)/shard_map/ppermute | solution.py:126
  20.4 11.0 %collective-permute-start.7 = (f32[4,32,512]{2,1,0:T(8,128)S(1)}, f32[4,32,512]{2,1,0:T(8,128)S(1)}, u32[]{:S(2)}, u32[]{:S(2)}) collective-permute-start(f32[4,32,512]{2,1,0:T(8,128)S(1)} %get-tuple-element.80.held_ref), channel_id=1, source_target_pairs={{0,2},{1,3},{2,0},{3,1},{4,6},{5,7},{6,4},{7,5},{8,10},{9,11},{10,... | collective-permute-start | bytes 786440 | tf_op jit(solution)/shard_map/ppermute | solution.py:126
  31.8 17.4 %copy-start = (f32[1,1,128]{2,1,0:T(1,128)S(1)}, f32[1,1,128]{2,1,0:T(1,128)}, u32[]{:S(2)}) copy-start(f32[1,1,128]{2,1,0:T(1,128)} %param.21) | copy-start | bytes 1540
  31.8 15.2 %collective-permute-start.11 = (f32[4,48,512]{2,1,0:T(8,128)S(1)}, f32[4,48,512]{2,1,0:T(8,128)S(1)}, u32[]{:S(2)}, u32[]{:S(2)}) collective-permute-start(f32[4,48,512]{2,1,0:T(8,128)S(1)} %get-tuple-element.87.held_ref), channel_id=1, source_target_pairs={{0,2},{1,3},{2,0},{3,1},{4,6},{5,7},{6,4},{7,5},{8,10},{9,11},{10,... | collective-permute-start | bytes 1179656 | tf_op jit(solution)/shard_map/ppermute | solution.py:126
  33.4 3.8 %collective-permute-start.9 = (f32[64,512]{1,0:T(8,128)S(1)}, f32[64,512]{1,0:T(8,128)S(1)}, u32[]{:S(2)}, u32[]{:S(2)}) collective-permute-start(f32[64,512]{1,0:T(8,128)S(1)} %get-tuple-element.83.mine_ref), channel_id=1, source_target_pairs={{0,8},{8,0},{1,9},{9,1},{2,10},{10,2},{3,11},{11,3},{4,12},{12,4},... | collective-permute-start | bytes 393224 | tf_op jit(solution)/shard_map/ppermute | solution.py:790
  36.0 1.2 %collective-permute-start.10 = (f32[16,128]{1,0:T(8,128)S(1)}, f32[16,128]{1,0:T(8,128)S(1)}, u32[]{:S(2)}, u32[]{:S(2)}) collective-permute-start(f32[16,128]{1,0:T(8,128)S(1)} %get-tuple-element.84.face_ref), channel_id=1, source_target_pairs={{0,8},{8,0},{1,9},{9,1},{2,10},{10,2},{3,11},{11,3},{4,12},{12,4},... | collective-permute-start | bytes 24584 | tf_op jit(solution)/shard_map/ppermute | solution.py:779
  47.3 1.9 %collective-permute-start.12 = (f32[64,512]{1,0:T(8,128)S(1)}, f32[64,512]{1,0:T(8,128)S(1)}, u32[]{:S(2)}, u32[]{:S(2)}) collective-permute-start(f32[64,512]{1,0:T(8,128)S(1)} %shard_map.132.got_ref), channel_id=1, source_target_pairs={{0,8},{8,0},{1,9},{9,1},{2,10},{10,2},{3,11},{11,3},{4,12},{12,4},... | collective-permute-start | bytes 393224 | tf_op jit(solution)/shard_map/ppermute | solution.py:790
  59.9 2.1 %collective-permute-start.13 = (f32[64,256]{1,0:T(8,128)S(1)}, f32[64,256]{1,0:T(8,128)S(1)}, u32[]{:S(2)}, u32[]{:S(2)}) collective-permute-start(f32[64,256]{1,0:T(8,128)S(1)} %get-tuple-element.92), channel_id=1, source_target_pairs={{0,8},{8,0},{1,9},{9,1},{2,10},{10,2},{3,11},{11,3},{4,12},{12,4},... | collective-permute-start | bytes 196616 | tf_op jit(solution)/shard_map/ppermute | solution.py:874
  60.8 1.2 %collective-permute-start.14 = (f32[32,32]{1,0:T(8,128)S(1)}, f32[32,32]{1,0:T(8,128)S(1)}, u32[]{:S(2)}, u32[]{:S(2)}) collective-permute-start(f32[32,32]{1,0:T(8,128)S(1)} %get-tuple-element.102.refs_1_), channel_id=1, source_target_pairs={{0,8},{8,0},{1,9},{9,1},{2,10},{10,2},{3,11},{11,3},{4,12},{12,4},... | collective-permute-start | bytes 12296 | tf_op jit(solution)/shard_map/ppermute | solution.py:893
  73.1 10.1 %collective-permute-start.15 = (f32[16,128]{1,0:T(8,128)S(1)}, f32[16,128]{1,0:T(8,128)S(1)}, u32[]{:S(2)}, u32[]{:S(2)}) collective-permute-start(f32[16,128]{1,0:T(8,128)S(1)} %get-tuple-element.110), channel_id=1, source_target_pairs={{0,1},{1,0},{2,3},{3,2},{4,5},{5,4},{6,7},{7,6},{8,9},{9,8},{10,11... | collective-permute-start | bytes 24584 | tf_op jit(solution)/shard_map/ppermute | solution.py:924
  74.3 8.9 %collective-permute-start.16 = (f32[16,128]{1,0:T(8,128)S(1)}, f32[16,128]{1,0:T(8,128)S(1)}, u32[]{:S(2)}, u32[]{:S(2)}) collective-permute-start(f32[16,128]{1,0:T(8,128)S(1)} %get-tuple-element.111), channel_id=1, source_target_pairs={{1,2},{3,4},{5,6},{2,1},{4,3},{6,5},{9,10},{11,12},{13,14},{10,9},... | collective-permute-start | bytes 24584 | tf_op jit(solution)/shard_map/ppermute | solution.py:925
  77.6 5.6 %collective-permute-start.17 = (f32[16,128]{1,0:T(8,128)S(1)}, f32[16,128]{1,0:T(8,128)S(1)}, u32[]{:S(2)}, u32[]{:S(2)}) collective-permute-start(f32[16,128]{1,0:T(8,128)S(1)} %get-tuple-element.112), channel_id=1, source_target_pairs={{0,8},{8,0},{16,24},{24,16},{1,9},{9,1},{17,25},{25,17},{2,10},{10... | collective-permute-start | bytes 24584 | tf_op jit(solution)/shard_map/ppermute | solution.py:926
  80.2 5.0 %collective-permute-start.18 = (f32[16,128]{1,0:T(8,128)S(1)}, f32[16,128]{1,0:T(8,128)S(1)}, u32[]{:S(2)}, u32[]{:S(2)}) collective-permute-start(f32[16,128]{1,0:T(8,128)S(1)} %get-tuple-element.113), channel_id=1, source_target_pairs={{8,16},{16,8},{9,17},{17,9},{10,18},{18,10},{11,19},{19,11},{12,20... | collective-permute-start | bytes 24584 | tf_op jit(solution)/shard_map/ppermute | solution.py:927

commit v9 on v8

--- a/solution.py
+++ b/solution.py
@@ -172,11 +172,11 @@
             ),
             in_lanes,
         )
-        held_refs[0][0, solve_rows:] = jnp.concatenate(
+        held_refs[-1][0, :in_rows] = jnp.concatenate(
             [row_in[i * in_rows : (i + 1) * in_rows] for i in range(runs)], axis=1
         )
         if whole_solve:
-            for level, held_ref in enumerate(held_refs):
+            for level, held_ref in enumerate(held_refs[:2]):
                 low, high = (
                     jnp.concatenate(
                         [edge_of(solve[level], 2 * c + side) for c in range(cols)], axis=1
@@ -184,12 +184,15 @@
                     for side in range(2)
                 )
                 mine = jnp.where(odd_row == (level == 0), high, low)
-                held_ref[0, :edge] = jnp.concatenate([mine[:edge], mine[edge:]], axis=1)
+                start = in_rows * level
+                held_ref[0, start : start + edge] = jnp.concatenate(
+                    [mine[:edge], mine[edge:]], axis=1
+                )
 
     ys_here, xi_here = y_solve[:, 0, 0], x_in[:, 0, 0]
     held, *upper_held = placing(
         hold_body,
-        [held_shape(1, solve_rows, in_rows)] + [held_shape(1, solve_rows)] * whole_solve,
+        [held_shape(1, solve_rows)] * whole_solve + [held_shape(1, in_rows, solve_rows)],
         ys_here,
         xi_here,
         scratch=[ys_here.shape, xi_here.shape],
@@ -284,11 +287,39 @@
     core = row_axes[-1]
     swapped = [(0, 1), (1, 0)]
 
+    def group(level):
+        return tuple(row_axes[y_levels - 1 - level :]) + ("box",)
+
+    def span(level):
+        return 2 << level
+
+    def swap(x, level):
+        return lax.all_to_all(x, group(level), 0, 0, tiled=True)
+
+    def offer_shape(level):
+        if whole_solve:
+            return (rows**level * cols, (waves >> level) * edge // LANES, LANES)
+        return (span(level) * cols, waves // span(level) * edge // LANES, LANES)
+
+    def store_offer(level, h, out):
+        size = span(level)
+        share = waves // size
+        facing = jnp.where(
+            lax.rem(my_row(), size) == size // 2 - 1, edge_of(h, 2), edge_of(h, 0)
+        )
+        if whole_solve:
+            out[...] = jnp.broadcast_to(packed(facing, edge), out.shape)
+            return
+        for target in range(size):
+            piece = packed(facing[target * share : (target + 1) * share], edge)
+            out[target * cols : (target + 1) * cols] = jnp.broadcast_to(piece, (cols,) + piece.shape)
+
     def x_body(level, tasks, h_ref, own_ref, got_ref, solve_ref, xo_ref, *refs):
         kept = x_levels - 1 - level
         count = sum(len(args) for _, args, _ in tasks)
         ins, (h_out, w_out, *rest) = refs[:count], refs[count:]
         rest, outs = rest[: 2 if kept else 0], rest[2 if kept else 0 :]
+        offer_ref = outs[-1] if outs else None
         for task, args, shapes in tasks:
             task(*ins[: len(args)], *outs[: len(shapes)])
             ins, outs = ins[len(args) :], outs[len(shapes) :]
@@ -315,19 +346,18 @@
                 jnp.concatenate([left, right] + travelling, axis=1), next_ref.shape[1]
             )
         else:
-            h_out[...] = h_ref[...] + dot(w, xo_ref[level])
+            h = h_ref[...] + dot(w, xo_ref[level])
+            h_out[...] = h
+            if whole_solve:
+                store_offer(0, h, offer_ref)
 
     def nothing(*refs):
         pass
 
-    def join_first(held_ref, moved_ref, solve_ref, in_ref):
-        join(0, held_ref[:, :solve_rows], moved_ref[:, :solve_rows], solve_ref)
-        join(0, held_ref[:, solve_rows:], moved_ref[:, solve_rows:], in_ref)
-
-    def join_upper(held_ref, moved_ref, in_ref, both_ref):
-        join(0, held_ref[...], moved_ref[...], both_ref.at[:, in_rows : in_rows + solve_rows])
-        both_ref[:, :in_rows] = in_ref[...]
-        both_ref[:, in_rows + solve_rows :] = jnp.zeros_like(in_ref)
+    def join_upper(held_ref, moved_ref, both_ref):
+        kept = in_rows + solve_rows
+        join(0, held_ref[...], moved_ref[...], both_ref.at[:, :kept])
+        both_ref[:, kept:] = jnp.zeros((2, in_rows, width), f32)
 
     def join_plain(step, held_ref, moved_ref, both_ref):
         join(step, held_ref[...], moved_ref[...], both_ref)
@@ -346,16 +376,17 @@
         if level < 2:
             tasks.append((nothing, [(out_map, from_load)[level]], []))
         if whole_solve and level == 0:
-            shapes = [held_shape(2, solve_rows), held_shape(2, in_rows)]
-            tasks.append((join_first, [held, moved], shapes))
+            shapes = [held_shape(2, solve_rows)]
+            tasks.append((functools.partial(join_plain, 0), [held, moved], shapes))
         elif whole_solve and level == 1:
             tasks.append((nothing, side, [x.shape for x in side]))
             shapes = [held_shape(2, in_rows, solve_rows, in_rows)]
-            tasks.append((join_upper, upper_held + upper_moved + [shared_in], shapes))
+            tasks.append((join_upper, upper_held + upper_moved, shapes))
         elif whole_solve:
             tasks.append((nothing, other_side, []))
             shapes = [held_shape(4, solve_rows)]
             tasks.append((functools.partial(join_plain, 1), [held, moved], shapes))
+            tasks.append((nothing, [], [offer_shape(0)]))
         elif level in joined_at:
             step = joined_at.index(level)
             shape = held_shape(2 << step, in_rows)
@@ -373,51 +404,27 @@
             to_send, end, *rest = rest
             ends.append(end)
         if whole_solve and level == 0:
-            held, shared_in = rest
+            (held,) = rest
             moved = passed_on(held, steps[1])
         elif whole_solve and level == 1:
             side, upper_held = rest[:1], rest[1]
             upper_moved = passed_on(upper_held, steps[1])
             other_side = [lax.ppermute(x, core, swapped) for x in side]
         elif whole_solve:
-            (held,) = rest
+            held, offer = rest
             moved = passed_on(held, steps[2])
         elif level in joined_at:
             (held,) = rest
             moved = passed_on(held, steps[step + 1])
 
-    def group(level):
-        return tuple(row_axes[y_levels - 1 - level :]) + ("box",)
-
-    def span(level):
-        return 2 << level
-
-    def swap(x, level):
-        return lax.all_to_all(x, group(level), 0, 0, tiled=True)
-
-    def offer_shape(level):
-        if whole_solve:
-            return (rows**level * cols, (waves >> level) * edge // LANES, LANES)
-        return (span(level) * cols, waves // span(level) * edge // LANES, LANES)
-
-    def store_offer(level, h, out):
-        size = span(level)
-        share = waves // size
-        facing = jnp.where(
-            lax.rem(my_row(), size) == size // 2 - 1, edge_of(h, 2), edge_of(h, 0)
-        )
-        if whole_solve:
-            out[...] = jnp.broadcast_to(packed(facing, edge), out.shape)
-            return
-        for target in range(size):
-            piece = packed(facing[target * share : (target + 1) * share], edge)
-            out[target * cols : (target + 1) * cols] = jnp.broadcast_to(piece, (cols,) + piece.shape)
-
-    def offer_body(level, h_ref, out_ref, *face_ref):
-        h = h_ref[...]
-        store_offer(level, h, out_ref)
-        for ref in face_ref:
-            ref[...] = packed(jnp.where(my_row() == 1, edge_of(h, 2), edge_of(h, 0)), edge)
+    def offer_body(level, h_ref, out_ref):
+        store_offer(level, h_ref[...], out_ref)
+
+    def folded(x):
+        return jnp.concatenate([x[i : i + 8] for i in range(0, x.shape[0], 8)], axis=1)
+
+    def unfolded(x, rows):
+        return jnp.concatenate([edge_of(x, i) for i in range(rows // 8)], axis=0)
 
     def gather_v(level, got_ref, v_ref):
         size = span(level)
@@ -455,9 +462,13 @@
                     ]
         return w_ref[...]
 
+    def upper_face(h_ref):
+        return jnp.where(my_row() == 1, edge_of(h_ref[...], 2), edge_of(h_ref[...], 0))
+
     def half_body(level, got_ref, held_ref, moved_ref, *refs):
         if level == 0:
-            upper_held_ref, upper_moved_ref, _, out_ref, _, upper_ref, v_ref = refs
+            upper_held_ref, upper_moved_ref, h_ref, out_ref, face_ref, upper_ref, v_ref = refs
+            face_ref[...] = packed(upper_face(h_ref), edge)
             kept = in_rows + solve_rows
             join(1, upper_held_ref[:, :kept], upper_moved_ref[:, :kept], upper_ref)
         else:
@@ -479,9 +490,7 @@
             solve += [block[:, : iface // 2], block[:, iface // 2 :]]
         out_ref[...] = dot_t(v_ref[...], jnp.concatenate(solve, axis=0))
 
-    def whole_body(
-        h_ref, mine_ref, other_ref, yo_ref, face_ref, other_face_ref, side_ref, h_out, w_out, next_ref
-    ):
+    def whole_body(h_ref, mine_ref, other_ref, yo_ref, face_ref, side_ref, h_out, w_out, next_ref):
         w_all = mine_ref[...] + other_ref[...]
         w_out[...] = own_columns(w_all)
         out_rows = side_ref[side_rows:]
@@ -491,7 +500,7 @@
         out_rows = jnp.where(at_upper(), upper_edge(yo_ref[0]), out_rows)
         spread = dot_t(w_all, jnp.concatenate([yo_ref[0], out_rows], axis=0))
         h_out[...] = h_ref[...] + spread[:, :leaf]
-        face = unpacked(jnp.where(at_upper(), face_ref[...], other_face_ref[...]), edge)
+        face = jnp.where(at_upper(), upper_face(h_ref), unpacked(face_ref[...], edge))
         face = face + spread[:, leaf:]
         half = jnp.where(bit(my_row(), 0) == 1, face[waves // 2 :], face[: waves // 2])
         next_ref[...] = jnp.broadcast_to(packed(half, edge), next_ref.shape)
@@ -614,7 +623,9 @@
             ],
             axis=0,
         )
-        own_out[...], other_out[...] = sides_of(terms)
+        own_out[...], other_out[:waves] = sides_of(terms)
+        other_out[waves:] = jnp.zeros((8, iface // 2), f32)
+        other_out[waves:, : half // 8 * edge] = folded(value)
 
     node_starts = []
     for k in range(x_levels):
@@ -675,12 +686,12 @@
 
     def x_terms_body(own_ref, got_ref, matrix_ref, known_ref, *refs):
         out_ref = refs[-1]
-        q = own_ref[...] + got_ref[...]
+        q = own_ref[...] + got_ref[:waves]
         terms = dot_t(q, matrix_ref[...]) + known_ref[...]
         if whole_solve:
-            g_ref, half_ref, other_half_ref, xi_ref, g_out, _ = refs
+            g_ref, half_ref, xi_ref, g_out, _ = refs
             odd_row = bit(my_row(), 0) == 1
-            mine, other = half_ref[...], other_half_ref[...]
+            mine, other = half_ref[...], unfolded(got_ref[waves:], waves // 2)
             value = jnp.concatenate(
                 [jnp.where(odd_row, other, mine), jnp.where(odd_row, mine, other)], axis=0
             )
@@ -754,29 +765,26 @@
         out_ref[...] = trace.reshape(out_ref.shape)
 
     face = (waves * edge // LANES, LANES)
-    offer, *upper_face = fused(
-        functools.partial(offer_body, 0), [offer_shape(0)] + [face] * whole_solve, h
-    )
+    if not whole_solve:
+        (offer,) = fused(functools.partial(offer_body, 0), [offer_shape(0)], h)
     y_keep = []
     for level in range(y_levels):
         if whole_solve:
             axes = "box" if level == 0 else group(1)
             got = lax.all_to_all(offer, axes, 0, 0, tiled=True)
             if level == 0:
-                (upper_face,) = upper_face
-                mine, upper_face, second = fused(
+                mine, upper, second = fused(
                     functools.partial(half_body, 0),
-                    [(waves, iface), upper_face.shape, held_shape(4, in_rows, solve_rows)],
+                    [(waves, iface), face, held_shape(4, in_rows, solve_rows)],
                     got,
                     held,
                     moved,
                     upper_held,
                     upper_moved,
-                    upper_face,
+                    h,
                     scratch=[(waves, cols * edge)],
-                    aliases={5: 1},
                 )
-                other_face = lax.ppermute(upper_face, core, swapped)
+                upper = lax.ppermute(upper, core, swapped)
                 second_moved = passed_on(second, steps[2])
             else:
                 (mine,) = fused(
@@ -796,8 +804,7 @@
                     mine,
                     other,
                     yo_all,
-                    upper_face,
-                    other_face,
+                    upper,
                     *other_side,
                 )
             else:
@@ -859,7 +866,7 @@
     if whole_solve:
         own, other, half = fused(
             upper_body,
-            [share, share, (waves // 2, edge)],
+            [share, (waves + 8, iface // 2), (waves // 2, edge)],
             swap(terms, 1),
             g,
             y_keep[1],
@@ -890,7 +897,7 @@
     )
     upper = []
     if whole_solve:
-        upper = [g, half, lax.ppermute(half, core, swapped), xi_all]
+        upper = [g, half, xi_all]
     *g_now, terms = fused(
         x_terms_body,
         [(waves, leaf)] * whole_solve + [(cols, waves, x_lanes)],

time: 86.2 us -> 85.7 us (level)
    ppermute x3, starting transfers between devices: 4.1 us -> 3.08 us  [local(): lax.ppermute(to_send, 'box', [(i, i ^ 1 << level) for i in range(cols)])]
    ppermute x2 -> x1, waiting for transfers between devices: 1.79 us -> 1.17 us  [local(): upper = lax.ppermute(upper, core, swapped)]
    pallas_call x15 -> x14, Pallas kernels: 6 us -> 6.03 us  [fused(): pl.pallas_call(body, out_shape=[pltpu.VMEM(s, f32) for s in outs], in_spe...]
  transfers between devices with their start and end apart: 19 -> 18, of which waited for: 8 -> 7; matrix products, arithmetic and copies ran while one was open for 1% -> 1% of each run, Pallas kernels for 8% -> 8%
where the time goes in v9:
time: 85.7 us; the launch traced here: 85.3 us
  blocking collectives  39.2 us (46%)
  starting transfers between devices  27.2 us (32%)
  Pallas kernels  10.8 us (13%)
  waiting for transfers between devices  6.15 us (7%)
  local copies, waits for them, and re-layouts  1.28 us (1%)
    all_to_all x2, blocking collectives, local(): got = lax.all_to_all(offer, axes, 0, 0, tiled=True)  19.5 us
    all_to_all x1, blocking collectives, local(): got = lax.all_to_all(terms, 'box', 0, 0, tiled=True)  10.1 us
    all_to_all x1, blocking collectives, swap(): return lax.all_to_all(x, group(level), 0, 0, tiled=True)  9.56 us
    ppermute x6, starting transfers between devices, passed_on(): lax.ppermute(held, 'box', [(i, i ^ 1 << bit_no) for i in range(cols)])  7.42 us
    pallas_call x14, Pallas kernels, fused(): pl.pallas_call(body, out_shape=[pltpu.VMEM(s, f32) for s in outs], in_spe...  6.03 us
    pallas_call x3, Pallas kernels, placing(): pl.pallas_call(body, out_shape=[pltpu.VMEM(s, f32) for s in shapes], in_s...  4.73 us
    ppermute x2, starting transfers between devices, local(): other = lax.ppermute(mine, core, swapped)  3.5 us
    ppermute x1, starting transfers between devices, local(): lax.ppermute(faces[1], 'box', far(cols))  3.23 us
  transfers between devices with their start and end apart: 18, of which 7 were waited for; matrix products, arithmetic and copies ran while one was open for 1% of the time, Pallas kernels for 8%

profile of v9, /device:TPU:9, one launch (start us, length us, event | category | flops | bytes accessed | tf_op | source)
XLA Modules:
  0.0 85.3 jit_solution(14213871033556932524)
XLA Ops:
  0.6 1.3 %shard_map.124 = (f32[1,32,512]{2,1,0:T(8,128)S(1)}, f32[1,48,512]{2,1,0:T(8,128)S(1)}) custom-call(f32[2,64,512]{2,1,0:T(8,128)} %bitcast.20, f32[3,64,128]{2,1,0:T(8,128)} %bitcast.18), custom_call_target="tpu_custom_call" | custom-call | tf_op jit(solution)/shard_map/pallas_call | solution.py:142
  1.9 2.4 %collective-permute-start.1 = (f32[1,32,512]{2,1,0:T(8,128)S(1)}, f32[1,32,512]{2,1,0:T(8,128)S(1)}, u32[]{:S(2)}, u32[]{:S(2)}) collective-permute-start(f32[1,32,512]{2,1,0:T(8,128)S(1)} %get-tuple-element.61.refs_1_), channel_id=1, source_target_pairs={{0,4},{1,5},{2,6},{3,7},{4,0},{5,1},{6,2},{7,3},{8,12},{9,13},{10,... | collective-permute-start | bytes 196616 | tf_op jit(solution)/shard_map/ppermute | solution.py:126
  4.3 1.8 %shard_map.122 = (f32[64,128]{1,0:T(8,128)S(1)}, f32[64,256]{1,0:T(8,128)S(1)}, f32[64,512]{1,0:T(8,128)S(1)}, f32[3,64,128]{2,1,0:T(8,128)S(1)}, f32[3,64,128]{2,1,0:T(8,128)S(1)}, /*index=5*/f32[3,64,64]{2,1,0:T(8,128)S(1)}) custom-call(f32[64,1,1,512]{3,2,1,0:T(1,128)} %load_any.1, f32[128,512]{1,0:T(8,128)} %bitcast.21, f32[3,64,128]{2,1,0:T(8,128)} %bitcast.22, ...), custom_call_target="tpu_custom_call" | custom-call | tf_op jit(solution)/shard_map/pallas_call | solution.py:142
  6.1 1.3 %collective-permute-start = (f32[64,256]{1,0:T(8,128)S(1)}, f32[64,256]{1,0:T(8,128)S(1)}, u32[]{:S(2)}, u32[]{:S(2)}) collective-permute-start(f32[64,256]{1,0:T(8,128)S(1)} %get-tuple-element.57.own_ref), channel_id=1, source_target_pairs={{0,1},{1,0},{2,3},{3,2},{4,5},{5,4},{6,7},{7,6},{8,9},{9,8},{10,11... | collective-permute-start | bytes 196616 | tf_op jit(solution)/shard_map/ppermute | solution.py:370
  7.4 1.6 %shard_map.123 = (f32[512,128]{1,0:T(8,128)S(1)}, f32[512,512]{1,0:T(8,128)S(1)}, f32[2,128,512]{2,1,0:T(8,128)S(1)}, f32[2,512,128]{2,1,0:T(8,128)S(1)}, f32[128,128]{1,0:T(8,128)S(1)}) custom-call(f32[512,640]{1,0:T(8,128)} %bitcast.15, f32[2,128,512]{2,1,0:T(8,128)} %bitcast.16, f32[2,512,128]{2,1,0:T(8,128)} %bitcast.17, f32[128,128]{1,0:T(8,128)} %bitcast.24), custom_call_target="tpu_custom_call" | custom-call | tf_op jit(solution)/shard_map/pallas_call | solution.py:142
  10.4 1.3 %collective-permute-start.6 = (f32[2,32,512]{2,1,0:T(8,128)S(1)}, f32[2,32,512]{2,1,0:T(8,128)S(1)}, u32[]{:S(2)}, u32[]{:S(2)}) collective-permute-start(f32[2,32,512]{2,1,0:T(8,128)S(1)} %get-tuple-element.74.refs_1_), channel_id=1, source_target_pairs={{0,1},{1,0},{2,3},{3,2},{4,5},{5,4},{6,7},{7,6},{8,9},{9,8},{10,11... | collective-permute-start | bytes 393224 | tf_op jit(solution)/shard_map/ppermute | solution.py:126
  11.6 1.2 %collective-permute-done.2.got_ref = f32[64,128]{1,0:T(8,128)S(1)} collective-permute-done((f32[64,128]{1,0:T(8,128)S(1)}, f32[64,128]{1,0:T(8,128)S(1)}, u32[]{:S(2)}, u32[]{:S(2)}) %collective-permute-start.2) | collective-permute-done | bytes 32800 | tf_op jit(solution)/shard_map/ppermute | solution.py:370
  13.2 3.0 %collective-permute-start.5 = (f32[256,128]{1,0:T(8,128)S(1)}, f32[256,128]{1,0:T(8,128)S(1)}, u32[]{:S(2)}, u32[]{:S(2)}) collective-permute-start(f32[256,128]{1,0:T(8,128)S(1)} %get-tuple-element.73.side_ref), channel_id=1, source_target_pairs={{0,8},{8,0},{1,9},{9,1},{2,10},{10,2},{3,11},{11,3},{4,12},{12,4},... | collective-permute-start | bytes 393224 | tf_op jit(solution)/shard_map/ppermute | solution.py:412
  16.2 1.6 %collective-permute-start.4 = (f32[64,128]{1,0:T(8,128)S(1)}, f32[64,128]{1,0:T(8,128)S(1)}, u32[]{:S(2)}, u32[]{:S(2)}) collective-permute-start(f32[64,128]{1,0:T(8,128)S(1)} %get-tuple-element.72.own_ref), channel_id=1, source_target_pairs={{0,4},{1,5},{2,6},{3,7},{4,0},{5,1},{6,2},{7,3},{8,12},{9,13},{10,... | collective-permute-start | bytes 98312 | tf_op jit(solution)/shard_map/ppermute | solution.py:370
  17.8 1.8 %collective-permute-start.8 = (f32[2,64,512]{2,1,0:T(8,128)S(1)}, f32[2,64,512]{2,1,0:T(8,128)S(1)}, u32[]{:S(2)}, u32[]{:S(2)}) collective-permute-start(f32[2,64,512]{2,1,0:T(8,128)S(1)} %get-tuple-element.78.refs_0_), channel_id=1, source_target_pairs={{0,1},{1,0},{2,3},{3,2},{4,5},{5,4},{6,7},{7,6},{8,9},{9,8},{10,11... | collective-permute-start | bytes 786440 | tf_op jit(solution)/shard_map/ppermute | solution.py:126
  20.7 10.3 %all_to_all.20.got_ref = f32[8,16,128]{2,1,0:T(8,128)S(1)} all-to-all(f32[8,16,128]{2,1,0:T(8,128)S(1)} %get-tuple-element.76), channel_id=1, replica_groups=mesh['row1'=2,'row0'=2,'box'=8] {'box'}, dimensions={0} | all-to-all | bytes 131072 | tf_op jit(solution)/shard_map/all_to_all | solution.py:774
  31.4 1.6 %collective-permute-start.11 = (f32[4,48,512]{2,1,0:T(8,128)S(1)}, f32[4,48,512]{2,1,0:T(8,128)S(1)}, u32[]{:S(2)}, u32[]{:S(2)}) collective-permute-start(f32[4,48,512]{2,1,0:T(8,128)S(1)} %get-tuple-element.83.held_ref), channel_id=1, source_target_pairs={{0,2},{1,3},{2,0},{3,1},{4,6},{5,7},{6,4},{7,5},{8,10},{9,11},{10,... | collective-permute-start | bytes 1179656 | tf_op jit(solution)/shard_map/ppermute | solution.py:126
  33.0 2.6 %collective-permute-start.9 = (f32[64,512]{1,0:T(8,128)S(1)}, f32[64,512]{1,0:T(8,128)S(1)}, u32[]{:S(2)}, u32[]{:S(2)}) collective-permute-start(f32[64,512]{1,0:T(8,128)S(1)} %get-tuple-element.79.mine_ref), channel_id=1, source_target_pairs={{0,8},{8,0},{1,9},{9,1},{2,10},{10,2},{3,11},{11,3},{4,12},{12,4},... | collective-permute-start | bytes 393224 | tf_op jit(solution)/shard_map/ppermute | solution.py:798
  35.6 1.2 %collective-permute-done.10.face_ref = f32[16,128]{1,0:T(8,128)S(1)} collective-permute-done((f32[16,128]{1,0:T(8,128)S(1)}, f32[16,128]{1,0:T(8,128)S(1)}, u32[]{:S(2)}, u32[]{:S(2)}) %collective-permute-start.10) | collective-permute-done | bytes 8224 | tf_op jit(solution)/shard_map/ppermute | solution.py:787
  37.4 9.2 %all_to_all.21.got_ref = f32[32,8,128]{2,1,0:T(8,128)S(1)} all-to-all(f32[32,8,128]{2,1,0:T(8,128)S(1)} %get-tuple-element.82), channel_id=1, replica_groups=mesh['row1'=2,'row0'=2,'box'=8] {'row1','row0','box'}, dimensions={0} | all-to-all | bytes 262144 | tf_op jit(solution)/shard_map/all_to_all | solution.py:774
  46.9 0.9 %collective-permute-start.12 = (f32[64,512]{1,0:T(8,128)S(1)}, f32[64,512]{1,0:T(8,128)S(1)}, u32[]{:S(2)}, u32[]{:S(2)}) collective-permute-start(f32[64,512]{1,0:T(8,128)S(1)} %shard_map.131.got_ref), channel_id=1, source_target_pairs={{0,8},{8,0},{1,9},{9,1},{2,10},{10,2},{3,11},{11,3},{4,12},{12,4},... | collective-permute-start | bytes 393224 | tf_op jit(solution)/shard_map/ppermute | solution.py:798
  47.8 1.0 %collective-permute-done.12.refs_0_ = f32[64,512]{1,0:T(8,128)S(1)} collective-permute-done((f32[64,512]{1,0:T(8,128)S(1)}, f32[64,512]{1,0:T(8,128)S(1)}, u32[]{:S(2)}, u32[]{:S(2)}) %collective-permute-start.12) | collective-permute-done | bytes 131104 | tf_op jit(solution)/shard_map/ppermute | solution.py:798
  49.5 9.6 %all_to_all.22.got_ref = f32[32,8,128]{2,1,0:T(8,128)S(1)} all-to-all(f32[32,8,128]{2,1,0:T(8,128)S(1)} %get-tuple-element.84), channel_id=1, replica_groups=mesh['row1'=2,'row0'=2,'box'=8] {'row1','row0','box'}, dimensions={0} | all-to-all | bytes 262144 | tf_op jit(solution)/shard_map/all_to_all | solution.py:297
  61.9 10.1 %all_to_all.23.got_ref = f32[8,64,128]{2,1,0:T(8,128)S(1)} all-to-all(f32[8,64,128]{2,1,0:T(8,128)S(1)} %get-tuple-element.100), channel_id=1, replica_groups=mesh['row1'=2,'row0'=2,'box'=8] {'box'}, dimensions={0} | all-to-all | bytes 524288 | tf_op jit(solution)/shard_map/all_to_all | solution.py:911
  72.4 1.2 %collective-permute-start.14 = (f32[16,128]{1,0:T(8,128)S(1)}, f32[16,128]{1,0:T(8,128)S(1)}, u32[]{:S(2)}, u32[]{:S(2)}) collective-permute-start(f32[16,128]{1,0:T(8,128)S(1)} %get-tuple-element.106), channel_id=1, source_target_pairs={{0,1},{1,0},{2,3},{3,2},{4,5},{5,4},{6,7},{7,6},{8,9},{9,8},{10,11... | collective-permute-start | bytes 24584 | tf_op jit(solution)/shard_map/ppermute | solution.py:931
  73.6 3.2 %collective-permute-start.15 = (f32[16,128]{1,0:T(8,128)S(1)}, f32[16,128]{1,0:T(8,128)S(1)}, u32[]{:S(2)}, u32[]{:S(2)}) collective-permute-start(f32[16,128]{1,0:T(8,128)S(1)} %get-tuple-element.107), channel_id=1, source_target_pairs={{1,2},{3,4},{5,6},{2,1},{4,3},{6,5},{9,10},{11,12},{13,14},{10,9},... | collective-permute-start | bytes 24584 | tf_op jit(solution)/shard_map/ppermute | solution.py:932
  76.8 2.8 %collective-permute-start.16 = (f32[16,128]{1,0:T(8,128)S(1)}, f32[16,128]{1,0:T(8,128)S(1)}, u32[]{:S(2)}, u32[]{:S(2)}) collective-permute-start(f32[16,128]{1,0:T(8,128)S(1)} %get-tuple-element.108), channel_id=1, source_target_pairs={{0,8},{8,0},{16,24},{24,16},{1,9},{9,1},{17,25},{25,17},{2,10},{10... | collective-permute-start | bytes 24584 | tf_op jit(solution)/shard_map/ppermute | solution.py:933
  79.6 2.2 %collective-permute-start.17 = (f32[16,128]{1,0:T(8,128)S(1)}, f32[16,128]{1,0:T(8,128)S(1)}, u32[]{:S(2)}, u32[]{:S(2)}) collective-permute-start(f32[16,128]{1,0:T(8,128)S(1)} %get-tuple-element.109), channel_id=1, source_target_pairs={{8,16},{16,8},{9,17},{17,9},{10,18},{18,10},{11,19},{19,11},{12,20... | collective-permute-start | bytes 24584 | tf_op jit(solution)/shard_map/ppermute | solution.py:934
  82.7 1.9 %collective-permute-done.17.d_ref = f32[16,128]{1,0:T(8,128)S(1)} collective-permute-done((f32[16,128]{1,0:T(8,128)S(1)}, f32[16,128]{1,0:T(8,128)S(1)}, u32[]{:S(2)}, u32[]{:S(2)}) %collective-permute-start.17) | collective-permute-done | bytes 8224 | tf_op jit(solution)/shard_map/ppermute | solution.py:934
  (37 shorter events, 9.8 us)
Async XLA Ops:
  1.9 7.2 %collective-permute-start.1 = (f32[1,32,512]{2,1,0:T(8,128)S(1)}, f32[1,32,512]{2,1,0:T(8,128)S(1)}, u32[]{:S(2)}, u32[]{:S(2)}) collective-permute-start(f32[1,32,512]{2,1,0:T(8,128)S(1)} %get-tuple-element.61.refs_1_), channel_id=1, source_target_pairs={{0,4},{1,5},{2,6},{3,7},{4,0},{5,1},{6,2},{7,3},{8,12},{9,13},{10,... | collective-permute-start | bytes 196616 | tf_op jit(solution)/shard_map/ppermute | solution.py:126
  6.1 3.2 %collective-permute-start = (f32[64,256]{1,0:T(8,128)S(1)}, f32[64,256]{1,0:T(8,128)S(1)}, u32[]{:S(2)}, u32[]{:S(2)}) collective-permute-start(f32[64,256]{1,0:T(8,128)S(1)} %get-tuple-element.57.own_ref), channel_id=1, source_target_pairs={{0,1},{1,0},{2,3},{3,2},{4,5},{5,4},{6,7},{7,6},{8,9},{9,8},{10,11... | collective-permute-start | bytes 196616 | tf_op jit(solution)/shard_map/ppermute | solution.py:370
  7.4 5.4 %collective-permute-start.3 = (f32[1,48,512]{2,1,0:T(8,128)S(1)}, f32[1,48,512]{2,1,0:T(8,128)S(1)}, u32[]{:S(2)}, u32[]{:S(2)}) collective-permute-start(f32[1,48,512]{2,1,0:T(8,128)S(1)} %get-tuple-element.70.refs_2_), channel_id=1, source_target_pairs={{0,4},{1,5},{2,6},{3,7},{4,0},{5,1},{6,2},{7,3},{8,12},{9,13},{10,... | collective-permute-start | bytes 294920 | tf_op jit(solution)/shard_map/ppermute | solution.py:126
  9.7 3.1 %collective-permute-start.2 = (f32[64,128]{1,0:T(8,128)S(1)}, f32[64,128]{1,0:T(8,128)S(1)}, u32[]{:S(2)}, u32[]{:S(2)}) collective-permute-start(f32[64,128]{1,0:T(8,128)S(1)} %get-tuple-element.63.own_ref), channel_id=1, source_target_pairs={{0,2},{1,3},{2,0},{3,1},{4,6},{5,7},{6,4},{7,5},{8,10},{9,11},{10,... | collective-permute-start | bytes 98312 | tf_op jit(solution)/shard_map/ppermute | solution.py:370
  10.4 9.5 %collective-permute-start.6 = (f32[2,32,512]{2,1,0:T(8,128)S(1)}, f32[2,32,512]{2,1,0:T(8,128)S(1)}, u32[]{:S(2)}, u32[]{:S(2)}) collective-permute-start(f32[2,32,512]{2,1,0:T(8,128)S(1)} %get-tuple-element.74.refs_1_), channel_id=1, source_target_pairs={{0,1},{1,0},{2,3},{3,2},{4,5},{5,4},{6,7},{7,6},{8,9},{9,8},{10,11... | collective-permute-start | bytes 393224 | tf_op jit(solution)/shard_map/ppermute | solution.py:126
  13.2 6.7 %collective-permute-start.5 = (f32[256,128]{1,0:T(8,128)S(1)}, f32[256,128]{1,0:T(8,128)S(1)}, u32[]{:S(2)}, u32[]{:S(2)}) collective-permute-start(f32[256,128]{1,0:T(8,128)S(1)} %get-tuple-element.73.side_ref), channel_id=1, source_target_pairs={{0,8},{8,0},{1,9},{9,1},{2,10},{10,2},{3,11},{11,3},{4,12},{12,4},... | collective-permute-start | bytes 393224 | tf_op jit(solution)/shard_map/ppermute | solution.py:412
  16.2 3.7 %collective-permute-start.4 = (f32[64,128]{1,0:T(8,128)S(1)}, f32[64,128]{1,0:T(8,128)S(1)}, u32[]{:S(2)}, u32[]{:S(2)}) collective-permute-start(f32[64,128]{1,0:T(8,128)S(1)} %get-tuple-element.72.own_ref), channel_id=1, source_target_pairs={{0,4},{1,5},{2,6},{3,7},{4,0},{5,1},{6,2},{7,3},{8,12},{9,13},{10,... | collective-permute-start | bytes 98312 | tf_op jit(solution)/shard_map/ppermute | solution.py:370
  17.8 13.3 %collective-permute-start.8 = (f32[2,64,512]{2,1,0:T(8,128)S(1)}, f32[2,64,512]{2,1,0:T(8,128)S(1)}, u32[]{:S(2)}, u32[]{:S(2)}) collective-permute-start(f32[2,64,512]{2,1,0:T(8,128)S(1)} %get-tuple-element.78.refs_0_), channel_id=1, source_target_pairs={{0,1},{1,0},{2,3},{3,2},{4,5},{5,4},{6,7},{7,6},{8,9},{9,8},{10,11... | collective-permute-start | bytes 786440 | tf_op jit(solution)/shard_map/ppermute | solution.py:126
  20.4 10.6 %collective-permute-start.7 = (f32[4,32,512]{2,1,0:T(8,128)S(1)}, f32[4,32,512]{2,1,0:T(8,128)S(1)}, u32[]{:S(2)}, u32[]{:S(2)}) collective-permute-start(f32[4,32,512]{2,1,0:T(8,128)S(1)} %get-tuple-element.77.held_ref), channel_id=1, source_target_pairs={{0,2},{1,3},{2,0},{3,1},{4,6},{5,7},{6,4},{7,5},{8,10},{9,11},{10,... | collective-permute-start | bytes 786440 | tf_op jit(solution)/shard_map/ppermute | solution.py:126
  31.4 17.4 %copy-start = (f32[1,1,128]{2,1,0:T(1,128)S(1)}, f32[1,1,128]{2,1,0:T(1,128)}, u32[]{:S(2)}) copy-start(f32[1,1,128]{2,1,0:T(1,128)} %param.21) | copy-start | bytes 1540
  31.4 15.2 %collective-permute-start.11 = (f32[4,48,512]{2,1,0:T(8,128)S(1)}, f32[4,48,512]{2,1,0:T(8,128)S(1)}, u32[]{:S(2)}, u32[]{:S(2)}) collective-permute-start(f32[4,48,512]{2,1,0:T(8,128)S(1)} %get-tuple-element.83.held_ref), channel_id=1, source_target_pairs={{0,2},{1,3},{2,0},{3,1},{4,6},{5,7},{6,4},{7,5},{8,10},{9,11},{10,... | collective-permute-start | bytes 1179656 | tf_op jit(solution)/shard_map/ppermute | solution.py:126
  33.0 3.8 %collective-permute-start.9 = (f32[64,512]{1,0:T(8,128)S(1)}, f32[64,512]{1,0:T(8,128)S(1)}, u32[]{:S(2)}, u32[]{:S(2)}) collective-permute-start(f32[64,512]{1,0:T(8,128)S(1)} %get-tuple-element.79.mine_ref), channel_id=1, source_target_pairs={{0,8},{8,0},{1,9},{9,1},{2,10},{10,2},{3,11},{11,3},{4,12},{12,4},... | collective-permute-start | bytes 393224 | tf_op jit(solution)/shard_map/ppermute | solution.py:798
  35.6 1.2 %collective-permute-start.10 = (f32[16,128]{1,0:T(8,128)S(1)}, f32[16,128]{1,0:T(8,128)S(1)}, u32[]{:S(2)}, u32[]{:S(2)}) collective-permute-start(f32[16,128]{1,0:T(8,128)S(1)} %get-tuple-element.80), channel_id=1, source_target_pairs={{0,8},{8,0},{1,9},{9,1},{2,10},{10,2},{3,11},{11,3},{4,12},{12,4},... | collective-permute-start | bytes 24584 | tf_op jit(solution)/shard_map/ppermute | solution.py:787
  46.9 1.9 %collective-permute-start.12 = (f32[64,512]{1,0:T(8,128)S(1)}, f32[64,512]{1,0:T(8,128)S(1)}, u32[]{:S(2)}, u32[]{:S(2)}) collective-permute-start(f32[64,512]{1,0:T(8,128)S(1)} %shard_map.131.got_ref), channel_id=1, source_target_pairs={{0,8},{8,0},{1,9},{9,1},{2,10},{10,2},{3,11},{11,3},{4,12},{12,4},... | collective-permute-start | bytes 393224 | tf_op jit(solution)/shard_map/ppermute | solution.py:798
  59.5 1.8 %collective-permute-start.13 = (f32[72,256]{1,0:T(8,128)S(1)}, f32[72,256]{1,0:T(8,128)S(1)}, u32[]{:S(2)}, u32[]{:S(2)}) collective-permute-start(f32[72,256]{1,0:T(8,128)S(1)} %get-tuple-element.88), channel_id=1, source_target_pairs={{0,8},{8,0},{1,9},{9,1},{2,10},{10,2},{3,11},{11,3},{4,12},{12,4},... | collective-permute-start | bytes 221192 | tf_op jit(solution)/shard_map/ppermute | solution.py:881
  72.4 10.2 %collective-permute-start.14 = (f32[16,128]{1,0:T(8,128)S(1)}, f32[16,128]{1,0:T(8,128)S(1)}, u32[]{:S(2)}, u32[]{:S(2)}) collective-permute-start(f32[16,128]{1,0:T(8,128)S(1)} %get-tuple-element.106), channel_id=1, source_target_pairs={{0,1},{1,0},{2,3},{3,2},{4,5},{5,4},{6,7},{7,6},{8,9},{9,8},{10,11... | collective-permute-start | bytes 24584 | tf_op jit(solution)/shard_map/ppermute | solution.py:931
  73.6 9.1 %collective-permute-start.15 = (f32[16,128]{1,0:T(8,128)S(1)}, f32[16,128]{1,0:T(8,128)S(1)}, u32[]{:S(2)}, u32[]{:S(2)}) collective-permute-start(f32[16,128]{1,0:T(8,128)S(1)} %get-tuple-element.107), channel_id=1, source_target_pairs={{1,2},{3,4},{5,6},{2,1},{4,3},{6,5},{9,10},{11,12},{13,14},{10,9},... | collective-permute-start | bytes 24584 | tf_op jit(solution)/shard_map/ppermute | solution.py:932
  76.8 5.8 %collective-permute-start.16 = (f32[16,128]{1,0:T(8,128)S(1)}, f32[16,128]{1,0:T(8,128)S(1)}, u32[]{:S(2)}, u32[]{:S(2)}) collective-permute-start(f32[16,128]{1,0:T(8,128)S(1)} %get-tuple-element.108), channel_id=1, source_target_pairs={{0,8},{8,0},{16,24},{24,16},{1,9},{9,1},{17,25},{25,17},{2,10},{10... | collective-permute-start | bytes 24584 | tf_op jit(solution)/shard_map/ppermute | solution.py:933
  79.6 5.0 %collective-permute-start.17 = (f32[16,128]{1,0:T(8,128)S(1)}, f32[16,128]{1,0:T(8,128)S(1)}, u32[]{:S(2)}, u32[]{:S(2)}) collective-permute-start(f32[16,128]{1,0:T(8,128)S(1)} %get-tuple-element.109), channel_id=1, source_target_pairs={{8,16},{16,8},{9,17},{17,9},{10,18},{18,10},{11,19},{19,11},{12,20... | collective-permute-start | bytes 24584 | tf_op jit(solution)/shard_map/ppermute | solution.py:934

commit v10 on v9

--- a/solution.py
+++ b/solution.py
@@ -10,7 +10,7 @@
 
 f32 = jnp.float32
 LANES = 128
-START_ROOM = 60 << 20
+PLACING_VMEM = 60 << 20
 
 
 def dot(a, b, over=0):
@@ -147,7 +147,7 @@
             scratch_shapes=[pltpu.VMEM(s, f32) for s in scratch]
             + [pltpu.SemaphoreType.DMA((len(args) + 1,))],
             compiler_params=pltpu.CompilerParams(
-                vmem_limit_bytes=START_ROOM - live - sum(4 * math.prod(s) for s in shapes)
+                vmem_limit_bytes=PLACING_VMEM - live - sum(4 * math.prod(s) for s in shapes)
             ),
         )(*args)
 
@@ -373,8 +373,8 @@
             outs += [exchange_shape(level + 1), (pair, pair)]
         args = [h, to_send, got, xs_all, xo_all]
         tasks = []
-        if level < 2:
-            tasks.append((nothing, [(out_map, from_load)[level]], []))
+        if level == 0:
+            tasks.append((nothing, [from_load], []))
         if whole_solve and level == 0:
             shapes = [held_shape(2, solve_rows)]
             tasks.append((functools.partial(join_plain, 0), [held, moved], shapes))
@@ -391,7 +391,7 @@
             step = joined_at.index(level)
             shape = held_shape(2 << step, in_rows)
             tasks.append((functools.partial(join_plain, step), [held, moved], [shape]))
-        aliases = {len(args) + 1: len(outs)} if level == 1 and whole_solve else None
+        aliases = {len(args): len(outs)} if level == 1 and whole_solve else None
         h, w, *rest = fused(
             functools.partial(x_body, level, tasks),
             outs + [shape for task in tasks for shape in task[2]],

time: 85.7 us -> 85.7 us (level)
  transfers between devices with their start and end apart: 18 -> 18, of which waited for: 7 -> 6; matrix products, arithmetic and copies ran while one was open for 1% -> 1% of each run, Pallas kernels for 8% -> 8%
where the time goes in v10:
time: 85.7 us; the launch traced here: 85.3 us
  blocking collectives  39.1 us (46%)
  starting transfers between devices  26.6 us (31%)
  Pallas kernels  10.8 us (13%)
  waiting for transfers between devices  6.82 us (8%)
  local copies, waits for them, and re-layouts  1.28 us (1%)
    all_to_all x2, blocking collectives, local(): got = lax.all_to_all(offer, axes, 0, 0, tiled=True)  19.4 us
    all_to_all x1, blocking collectives, local(): got = lax.all_to_all(terms, 'box', 0, 0, tiled=True)  10.1 us
    all_to_all x1, blocking collectives, swap(): return lax.all_to_all(x, group(level), 0, 0, tiled=True)  9.56 us
    ppermute x6, starting transfers between devices, passed_on(): lax.ppermute(held, 'box', [(i, i ^ 1 << bit_no) for i in range(cols)])  6.65 us
    pallas_call x14, Pallas kernels, fused(): pl.pallas_call(body, out_shape=[pltpu.VMEM(s, f32) for s in outs], in_spe...  6.03 us
    pallas_call x3, Pallas kernels, placing(): pl.pallas_call(body, out_shape=[pltpu.VMEM(s, f32) for s in shapes], in_s...  4.73 us
    ppermute x3, starting transfers between devices, local(): lax.ppermute(to_send, 'box', [(i, i ^ 1 << level) for i in range(cols)])  3.53 us
    ppermute x2, starting transfers between devices, local(): other = lax.ppermute(mine, core, swapped)  3.5 us
  transfers between devices with their start and end apart: 18, of which 6 were waited for; matrix products, arithmetic and copies ran while one was open for 1% of the time, Pallas kernels for 8%

profile of v10, /device:TPU:9, one launch (start us, length us, event | category | flops | bytes accessed | tf_op | source)
XLA Modules:
  0.0 85.3 jit_solution(6219334226458803099)
XLA Ops:
  0.6 1.3 %shard_map.125 = (f32[1,32,512]{2,1,0:T(8,128)S(1)}, f32[1,48,512]{2,1,0:T(8,128)S(1)}) custom-call(f32[2,64,512]{2,1,0:T(8,128)} %bitcast.20, f32[3,64,128]{2,1,0:T(8,128)} %bitcast.18), custom_call_target="tpu_custom_call" | custom-call | tf_op jit(solution)/shard_map/pallas_call | solution.py:142
  1.9 2.4 %collective-permute-start.1 = (f32[1,32,512]{2,1,0:T(8,128)S(1)}, f32[1,32,512]{2,1,0:T(8,128)S(1)}, u32[]{:S(2)}, u32[]{:S(2)}) collective-permute-start(f32[1,32,512]{2,1,0:T(8,128)S(1)} %get-tuple-element.65.refs_1_), channel_id=1, source_target_pairs={{0,4},{1,5},{2,6},{3,7},{4,0},{5,1},{6,2},{7,3},{8,12},{9,13},{10,... | collective-permute-start | bytes 196616 | tf_op jit(solution)/shard_map/ppermute | solution.py:126
  4.3 1.8 %shard_map.122 = (f32[64,128]{1,0:T(8,128)S(1)}, f32[64,256]{1,0:T(8,128)S(1)}, f32[64,512]{1,0:T(8,128)S(1)}, f32[3,64,128]{2,1,0:T(8,128)S(1)}, f32[3,64,128]{2,1,0:T(8,128)S(1)}, /*index=5*/f32[3,64,64]{2,1,0:T(8,128)S(1)}) custom-call(f32[64,1,1,512]{3,2,1,0:T(1,128)} %load_any.1, f32[128,512]{1,0:T(8,128)} %bitcast.21, f32[3,64,128]{2,1,0:T(8,128)} %bitcast.22, ...), custom_call_target="tpu_custom_call" | custom-call | tf_op jit(solution)/shard_map/pallas_call | solution.py:142
  6.1 1.3 %collective-permute-start = (f32[64,256]{1,0:T(8,128)S(1)}, f32[64,256]{1,0:T(8,128)S(1)}, u32[]{:S(2)}, u32[]{:S(2)}) collective-permute-start(f32[64,256]{1,0:T(8,128)S(1)} %get-tuple-element.57.own_ref), channel_id=1, source_target_pairs={{0,1},{1,0},{2,3},{3,2},{4,5},{5,4},{6,7},{7,6},{8,9},{9,8},{10,11... | collective-permute-start | bytes 196616 | tf_op jit(solution)/shard_map/ppermute | solution.py:370
  7.4 1.6 %shard_map.123 = (f32[512,128]{1,0:T(8,128)S(1)}, f32[512,512]{1,0:T(8,128)S(1)}, f32[2,128,512]{2,1,0:T(8,128)S(1)}, f32[2,512,128]{2,1,0:T(8,128)S(1)}, f32[128,128]{1,0:T(8,128)S(1)}) custom-call(f32[512,640]{1,0:T(8,128)} %bitcast.15, f32[2,128,512]{2,1,0:T(8,128)} %bitcast.16, f32[2,512,128]{2,1,0:T(8,128)} %bitcast.17, f32[128,128]{1,0:T(8,128)} %bitcast.24), custom_call_target="tpu_custom_call" | custom-call | tf_op jit(solution)/shard_map/pallas_call | solution.py:142
  10.2 0.9 %collective-permute-start.6 = (f32[2,32,512]{2,1,0:T(8,128)S(1)}, f32[2,32,512]{2,1,0:T(8,128)S(1)}, u32[]{:S(2)}, u32[]{:S(2)}) collective-permute-start(f32[2,32,512]{2,1,0:T(8,128)S(1)} %get-tuple-element.73.refs_1_), channel_id=1, source_target_pairs={{0,1},{1,0},{2,3},{3,2},{4,5},{5,4},{6,7},{7,6},{8,9},{9,8},{10,11... | collective-permute-start | bytes 393224 | tf_op jit(solution)/shard_map/ppermute | solution.py:126
  11.1 2.0 %collective-permute-done.2.got_ref = f32[64,128]{1,0:T(8,128)S(1)} collective-permute-done((f32[64,128]{1,0:T(8,128)S(1)}, f32[64,128]{1,0:T(8,128)S(1)}, u32[]{:S(2)}, u32[]{:S(2)}) %collective-permute-start.2) | collective-permute-done | bytes 32800 | tf_op jit(solution)/shard_map/ppermute | solution.py:370
  13.5 2.7 %collective-permute-start.5 = (f32[256,128]{1,0:T(8,128)S(1)}, f32[256,128]{1,0:T(8,128)S(1)}, u32[]{:S(2)}, u32[]{:S(2)}) collective-permute-start(f32[256,128]{1,0:T(8,128)S(1)} %get-tuple-element.72.side_ref), channel_id=1, source_target_pairs={{0,8},{8,0},{1,9},{9,1},{2,10},{10,2},{3,11},{11,3},{4,12},{12,4},... | collective-permute-start | bytes 393224 | tf_op jit(solution)/shard_map/ppermute | solution.py:412
  16.2 2.0 %collective-permute-start.4 = (f32[64,128]{1,0:T(8,128)S(1)}, f32[64,128]{1,0:T(8,128)S(1)}, u32[]{:S(2)}, u32[]{:S(2)}) collective-permute-start(f32[64,128]{1,0:T(8,128)S(1)} %get-tuple-element.71.own_ref), channel_id=1, source_target_pairs={{0,4},{1,5},{2,6},{3,7},{4,0},{5,1},{6,2},{7,3},{8,12},{9,13},{10,... | collective-permute-start | bytes 98312 | tf_op jit(solution)/shard_map/ppermute | solution.py:370
  18.3 1.3 %collective-permute-start.8 = (f32[2,64,512]{2,1,0:T(8,128)S(1)}, f32[2,64,512]{2,1,0:T(8,128)S(1)}, u32[]{:S(2)}, u32[]{:S(2)}) collective-permute-start(f32[2,64,512]{2,1,0:T(8,128)S(1)} %get-tuple-element.77.refs_0_), channel_id=1, source_target_pairs={{0,1},{1,0},{2,3},{3,2},{4,5},{5,4},{6,7},{7,6},{8,9},{9,8},{10,11... | collective-permute-start | bytes 786440 | tf_op jit(solution)/shard_map/ppermute | solution.py:126
  20.8 10.2 %all_to_all.20.got_ref = f32[8,16,128]{2,1,0:T(8,128)S(1)} all-to-all(f32[8,16,128]{2,1,0:T(8,128)S(1)} %get-tuple-element.75), channel_id=1, replica_groups=mesh['row1'=2,'row0'=2,'box'=8] {'box'}, dimensions={0} | all-to-all | bytes 131072 | tf_op jit(solution)/shard_map/all_to_all | solution.py:774
  31.4 1.6 %collective-permute-start.11 = (f32[4,48,512]{2,1,0:T(8,128)S(1)}, f32[4,48,512]{2,1,0:T(8,128)S(1)}, u32[]{:S(2)}, u32[]{:S(2)}) collective-permute-start(f32[4,48,512]{2,1,0:T(8,128)S(1)} %get-tuple-element.82.held_ref), channel_id=1, source_target_pairs={{0,2},{1,3},{2,0},{3,1},{4,6},{5,7},{6,4},{7,5},{8,10},{9,11},{10,... | collective-permute-start | bytes 1179656 | tf_op jit(solution)/shard_map/ppermute | solution.py:126
  33.0 2.6 %collective-permute-start.9 = (f32[64,512]{1,0:T(8,128)S(1)}, f32[64,512]{1,0:T(8,128)S(1)}, u32[]{:S(2)}, u32[]{:S(2)}) collective-permute-start(f32[64,512]{1,0:T(8,128)S(1)} %get-tuple-element.78.mine_ref), channel_id=1, source_target_pairs={{0,8},{8,0},{1,9},{9,1},{2,10},{10,2},{3,11},{11,3},{4,12},{12,4},... | collective-permute-start | bytes 393224 | tf_op jit(solution)/shard_map/ppermute | solution.py:798
  35.6 1.2 %collective-permute-done.10.face_ref = f32[16,128]{1,0:T(8,128)S(1)} collective-permute-done((f32[16,128]{1,0:T(8,128)S(1)}, f32[16,128]{1,0:T(8,128)S(1)}, u32[]{:S(2)}, u32[]{:S(2)}) %collective-permute-start.10) | collective-permute-done | bytes 8224 | tf_op jit(solution)/shard_map/ppermute | solution.py:787
  37.4 9.2 %all_to_all.21.got_ref = f32[32,8,128]{2,1,0:T(8,128)S(1)} all-to-all(f32[32,8,128]{2,1,0:T(8,128)S(1)} %get-tuple-element.81), channel_id=1, replica_groups=mesh['row1'=2,'row0'=2,'box'=8] {'row1','row0','box'}, dimensions={0} | all-to-all | bytes 262144 | tf_op jit(solution)/shard_map/all_to_all | solution.py:774
  46.9 0.9 %collective-permute-start.12 = (f32[64,512]{1,0:T(8,128)S(1)}, f32[64,512]{1,0:T(8,128)S(1)}, u32[]{:S(2)}, u32[]{:S(2)}) collective-permute-start(f32[64,512]{1,0:T(8,128)S(1)} %shard_map.131.got_ref), channel_id=1, source_target_pairs={{0,8},{8,0},{1,9},{9,1},{2,10},{10,2},{3,11},{11,3},{4,12},{12,4},... | collective-permute-start | bytes 393224 | tf_op jit(solution)/shard_map/ppermute | solution.py:798
  47.8 1.0 %collective-permute-done.12.refs_0_ = f32[64,512]{1,0:T(8,128)S(1)} collective-permute-done((f32[64,512]{1,0:T(8,128)S(1)}, f32[64,512]{1,0:T(8,128)S(1)}, u32[]{:S(2)}, u32[]{:S(2)}) %collective-permute-start.12) | collective-permute-done | bytes 131104 | tf_op jit(solution)/shard_map/ppermute | solution.py:798
  49.5 9.6 %all_to_all.22.got_ref = f32[32,8,128]{2,1,0:T(8,128)S(1)} all-to-all(f32[32,8,128]{2,1,0:T(8,128)S(1)} %get-tuple-element.83), channel_id=1, replica_groups=mesh['row1'=2,'row0'=2,'box'=8] {'row1','row0','box'}, dimensions={0} | all-to-all | bytes 262144 | tf_op jit(solution)/shard_map/all_to_all | solution.py:297
  61.9 10.1 %all_to_all.23.got_ref = f32[8,64,128]{2,1,0:T(8,128)S(1)} all-to-all(f32[8,64,128]{2,1,0:T(8,128)S(1)} %get-tuple-element.100), channel_id=1, replica_groups=mesh['row1'=2,'row0'=2,'box'=8] {'box'}, dimensions={0} | all-to-all | bytes 524288 | tf_op jit(solution)/shard_map/all_to_all | solution.py:911
  72.4 1.2 %collective-permute-start.14 = (f32[16,128]{1,0:T(8,128)S(1)}, f32[16,128]{1,0:T(8,128)S(1)}, u32[]{:S(2)}, u32[]{:S(2)}) collective-permute-start(f32[16,128]{1,0:T(8,128)S(1)} %get-tuple-element.106), channel_id=1, source_target_pairs={{0,1},{1,0},{2,3},{3,2},{4,5},{5,4},{6,7},{7,6},{8,9},{9,8},{10,11... | collective-permute-start | bytes 24584 | tf_op jit(solution)/shard_map/ppermute | solution.py:931
  73.6 3.2 %collective-permute-start.15 = (f32[16,128]{1,0:T(8,128)S(1)}, f32[16,128]{1,0:T(8,128)S(1)}, u32[]{:S(2)}, u32[]{:S(2)}) collective-permute-start(f32[16,128]{1,0:T(8,128)S(1)} %get-tuple-element.107), channel_id=1, source_target_pairs={{1,2},{3,4},{5,6},{2,1},{4,3},{6,5},{9,10},{11,12},{13,14},{10,9},... | collective-permute-start | bytes 24584 | tf_op jit(solution)/shard_map/ppermute | solution.py:932
  76.8 2.8 %collective-permute-start.16 = (f32[16,128]{1,0:T(8,128)S(1)}, f32[16,128]{1,0:T(8,128)S(1)}, u32[]{:S(2)}, u32[]{:S(2)}) collective-permute-start(f32[16,128]{1,0:T(8,128)S(1)} %get-tuple-element.108), channel_id=1, source_target_pairs={{0,8},{8,0},{16,24},{24,16},{1,9},{9,1},{17,25},{25,17},{2,10},{10... | collective-permute-start | bytes 24584 | tf_op jit(solution)/shard_map/ppermute | solution.py:933
  79.6 2.2 %collective-permute-start.17 = (f32[16,128]{1,0:T(8,128)S(1)}, f32[16,128]{1,0:T(8,128)S(1)}, u32[]{:S(2)}, u32[]{:S(2)}) collective-permute-start(f32[16,128]{1,0:T(8,128)S(1)} %get-tuple-element.109), channel_id=1, source_target_pairs={{8,16},{16,8},{9,17},{17,9},{10,18},{18,10},{11,19},{19,11},{12,20... | collective-permute-start | bytes 24584 | tf_op jit(solution)/shard_map/ppermute | solution.py:934
  82.7 1.9 %collective-permute-done.17.d_ref = f32[16,128]{1,0:T(8,128)S(1)} collective-permute-done((f32[16,128]{1,0:T(8,128)S(1)}, f32[16,128]{1,0:T(8,128)S(1)}, u32[]{:S(2)}, u32[]{:S(2)}) %collective-permute-start.17) | collective-permute-done | bytes 8224 | tf_op jit(solution)/shard_map/ppermute | solution.py:934
  (37 shorter events, 9.7 us)
Async XLA Ops:
  1.9 7.6 %collective-permute-start.1 = (f32[1,32,512]{2,1,0:T(8,128)S(1)}, f32[1,32,512]{2,1,0:T(8,128)S(1)}, u32[]{:S(2)}, u32[]{:S(2)}) collective-permute-start(f32[1,32,512]{2,1,0:T(8,128)S(1)} %get-tuple-element.65.refs_1_), channel_id=1, source_target_pairs={{0,4},{1,5},{2,6},{3,7},{4,0},{5,1},{6,2},{7,3},{8,12},{9,13},{10,... | collective-permute-start | bytes 196616 | tf_op jit(solution)/shard_map/ppermute | solution.py:126
  6.1 3.5 %collective-permute-start = (f32[64,256]{1,0:T(8,128)S(1)}, f32[64,256]{1,0:T(8,128)S(1)}, u32[]{:S(2)}, u32[]{:S(2)}) collective-permute-start(f32[64,256]{1,0:T(8,128)S(1)} %get-tuple-element.57.own_ref), channel_id=1, source_target_pairs={{0,1},{1,0},{2,3},{3,2},{4,5},{5,4},{6,7},{7,6},{8,9},{9,8},{10,11... | collective-permute-start | bytes 196616 | tf_op jit(solution)/shard_map/ppermute | solution.py:370
  7.4 5.7 %collective-permute-start.3 = (f32[1,48,512]{2,1,0:T(8,128)S(1)}, f32[1,48,512]{2,1,0:T(8,128)S(1)}, u32[]{:S(2)}, u32[]{:S(2)}) collective-permute-start(f32[1,48,512]{2,1,0:T(8,128)S(1)} %get-tuple-element.69.refs_1_), channel_id=1, source_target_pairs={{0,4},{1,5},{2,6},{3,7},{4,0},{5,1},{6,2},{7,3},{8,12},{9,13},{10,... | collective-permute-start | bytes 294920 | tf_op jit(solution)/shard_map/ppermute | solution.py:126
  10.0 3.1 %collective-permute-start.2 = (f32[64,128]{1,0:T(8,128)S(1)}, f32[64,128]{1,0:T(8,128)S(1)}, u32[]{:S(2)}, u32[]{:S(2)}) collective-permute-start(f32[64,128]{1,0:T(8,128)S(1)} %get-tuple-element.67.own_ref), channel_id=1, source_target_pairs={{0,2},{1,3},{2,0},{3,1},{4,6},{5,7},{6,4},{7,5},{8,10},{9,11},{10,... | collective-permute-start | bytes 98312 | tf_op jit(solution)/shard_map/ppermute | solution.py:370
  10.2 9.8 %collective-permute-start.6 = (f32[2,32,512]{2,1,0:T(8,128)S(1)}, f32[2,32,512]{2,1,0:T(8,128)S(1)}, u32[]{:S(2)}, u32[]{:S(2)}) collective-permute-start(f32[2,32,512]{2,1,0:T(8,128)S(1)} %get-tuple-element.73.refs_1_), channel_id=1, source_target_pairs={{0,1},{1,0},{2,3},{3,2},{4,5},{5,4},{6,7},{7,6},{8,9},{9,8},{10,11... | collective-permute-start | bytes 393224 | tf_op jit(solution)/shard_map/ppermute | solution.py:126
  13.5 6.5 %collective-permute-start.5 = (f32[256,128]{1,0:T(8,128)S(1)}, f32[256,128]{1,0:T(8,128)S(1)}, u32[]{:S(2)}, u32[]{:S(2)}) collective-permute-start(f32[256,128]{1,0:T(8,128)S(1)} %get-tuple-element.72.side_ref), channel_id=1, source_target_pairs={{0,8},{8,0},{1,9},{9,1},{2,10},{10,2},{3,11},{11,3},{4,12},{12,4},... | collective-permute-start | bytes 393224 | tf_op jit(solution)/shard_map/ppermute | solution.py:412
  16.2 3.7 %collective-permute-start.4 = (f32[64,128]{1,0:T(8,128)S(1)}, f32[64,128]{1,0:T(8,128)S(1)}, u32[]{:S(2)}, u32[]{:S(2)}) collective-permute-start(f32[64,128]{1,0:T(8,128)S(1)} %get-tuple-element.71.own_ref), channel_id=1, source_target_pairs={{0,4},{1,5},{2,6},{3,7},{4,0},{5,1},{6,2},{7,3},{8,12},{9,13},{10,... | collective-permute-start | bytes 98312 | tf_op jit(solution)/shard_map/ppermute | solution.py:370
  18.3 12.8 %collective-permute-start.8 = (f32[2,64,512]{2,1,0:T(8,128)S(1)}, f32[2,64,512]{2,1,0:T(8,128)S(1)}, u32[]{:S(2)}, u32[]{:S(2)}) collective-permute-start(f32[2,64,512]{2,1,0:T(8,128)S(1)} %get-tuple-element.77.refs_0_), channel_id=1, source_target_pairs={{0,1},{1,0},{2,3},{3,2},{4,5},{5,4},{6,7},{7,6},{8,9},{9,8},{10,11... | collective-permute-start | bytes 786440 | tf_op jit(solution)/shard_map/ppermute | solution.py:126
  20.5 10.6 %collective-permute-start.7 = (f32[4,32,512]{2,1,0:T(8,128)S(1)}, f32[4,32,512]{2,1,0:T(8,128)S(1)}, u32[]{:S(2)}, u32[]{:S(2)}) collective-permute-start(f32[4,32,512]{2,1,0:T(8,128)S(1)} %get-tuple-element.76.held_ref), channel_id=1, source_target_pairs={{0,2},{1,3},{2,0},{3,1},{4,6},{5,7},{6,4},{7,5},{8,10},{9,11},{10,... | collective-permute-start | bytes 786440 | tf_op jit(solution)/shard_map/ppermute | solution.py:126
  31.4 17.4 %copy-start = (f32[1,1,128]{2,1,0:T(1,128)S(1)}, f32[1,1,128]{2,1,0:T(1,128)}, u32[]{:S(2)}) copy-start(f32[1,1,128]{2,1,0:T(1,128)} %param.21) | copy-start | bytes 1540
  31.4 15.2 %collective-permute-start.11 = (f32[4,48,512]{2,1,0:T(8,128)S(1)}, f32[4,48,512]{2,1,0:T(8,128)S(1)}, u32[]{:S(2)}, u32[]{:S(2)}) collective-permute-start(f32[4,48,512]{2,1,0:T(8,128)S(1)} %get-tuple-element.82.held_ref), channel_id=1, source_target_pairs={{0,2},{1,3},{2,0},{3,1},{4,6},{5,7},{6,4},{7,5},{8,10},{9,11},{10,... | collective-permute-start | bytes 1179656 | tf_op jit(solution)/shard_map/ppermute | solution.py:126
  33.0 3.8 %collective-permute-start.9 = (f32[64,512]{1,0:T(8,128)S(1)}, f32[64,512]{1,0:T(8,128)S(1)}, u32[]{:S(2)}, u32[]{:S(2)}) collective-permute-start(f32[64,512]{1,0:T(8,128)S(1)} %get-tuple-element.78.mine_ref), channel_id=1, source_target_pairs={{0,8},{8,0},{1,9},{9,1},{2,10},{10,2},{3,11},{11,3},{4,12},{12,4},... | collective-permute-start | bytes 393224 | tf_op jit(solution)/shard_map/ppermute | solution.py:798
  35.6 1.2 %collective-permute-start.10 = (f32[16,128]{1,0:T(8,128)S(1)}, f32[16,128]{1,0:T(8,128)S(1)}, u32[]{:S(2)}, u32[]{:S(2)}) collective-permute-start(f32[16,128]{1,0:T(8,128)S(1)} %get-tuple-element.79), channel_id=1, source_target_pairs={{0,8},{8,0},{1,9},{9,1},{2,10},{10,2},{3,11},{11,3},{4,12},{12,4},... | collective-permute-start | bytes 24584 | tf_op jit(solution)/shard_map/ppermute | solution.py:787
  46.9 1.9 %collective-permute-start.12 = (f32[64,512]{1,0:T(8,128)S(1)}, f32[64,512]{1,0:T(8,128)S(1)}, u32[]{:S(2)}, u32[]{:S(2)}) collective-permute-start(f32[64,512]{1,0:T(8,128)S(1)} %shard_map.131.got_ref), channel_id=1, source_target_pairs={{0,8},{8,0},{1,9},{9,1},{2,10},{10,2},{3,11},{11,3},{4,12},{12,4},... | collective-permute-start | bytes 393224 | tf_op jit(solution)/shard_map/ppermute | solution.py:798
  59.5 1.8 %collective-permute-start.13 = (f32[72,256]{1,0:T(8,128)S(1)}, f32[72,256]{1,0:T(8,128)S(1)}, u32[]{:S(2)}, u32[]{:S(2)}) collective-permute-start(f32[72,256]{1,0:T(8,128)S(1)} %get-tuple-element.87), channel_id=1, source_target_pairs={{0,8},{8,0},{1,9},{9,1},{2,10},{10,2},{3,11},{11,3},{4,12},{12,4},... | collective-permute-start | bytes 221192 | tf_op jit(solution)/shard_map/ppermute | solution.py:881
  72.4 10.2 %collective-permute-start.14 = (f32[16,128]{1,0:T(8,128)S(1)}, f32[16,128]{1,0:T(8,128)S(1)}, u32[]{:S(2)}, u32[]{:S(2)}) collective-permute-start(f32[16,128]{1,0:T(8,128)S(1)} %get-tuple-element.106), channel_id=1, source_target_pairs={{0,1},{1,0},{2,3},{3,2},{4,5},{5,4},{6,7},{7,6},{8,9},{9,8},{10,11... | collective-permute-start | bytes 24584 | tf_op jit(solution)/shard_map/ppermute | solution.py:931
  73.6 9.1 %collective-permute-start.15 = (f32[16,128]{1,0:T(8,128)S(1)}, f32[16,128]{1,0:T(8,128)S(1)}, u32[]{:S(2)}, u32[]{:S(2)}) collective-permute-start(f32[16,128]{1,0:T(8,128)S(1)} %get-tuple-element.107), channel_id=1, source_target_pairs={{1,2},{3,4},{5,6},{2,1},{4,3},{6,5},{9,10},{11,12},{13,14},{10,9},... | collective-permute-start | bytes 24584 | tf_op jit(solution)/shard_map/ppermute | solution.py:932
  76.8 5.8 %collective-permute-start.16 = (f32[16,128]{1,0:T(8,128)S(1)}, f32[16,128]{1,0:T(8,128)S(1)}, u32[]{:S(2)}, u32[]{:S(2)}) collective-permute-start(f32[16,128]{1,0:T(8,128)S(1)} %get-tuple-element.108), channel_id=1, source_target_pairs={{0,8},{8,0},{16,24},{24,16},{1,9},{9,1},{17,25},{25,17},{2,10},{10... | collective-permute-start | bytes 24584 | tf_op jit(solution)/shard_map/ppermute | solution.py:933
  79.6 5.0 %collective-permute-start.17 = (f32[16,128]{1,0:T(8,128)S(1)}, f32[16,128]{1,0:T(8,128)S(1)}, u32[]{:S(2)}, u32[]{:S(2)}) collective-permute-start(f32[16,128]{1,0:T(8,128)S(1)} %get-tuple-element.109), channel_id=1, source_target_pairs={{8,16},{16,8},{9,17},{17,9},{10,18},{18,10},{11,19},{19,11},{12,20... | collective-permute-start | bytes 24584 | tf_op jit(solution)/shard_map/ppermute | solution.py:934

commit v11 on v10

--- a/solution.py
+++ b/solution.py
@@ -199,7 +199,7 @@
     )
 
     columns_here = [x[:, 0, 0] for x in (jnp.swapaxes(x_out, 3, 4), x_in, x_solve)]
-    rows_here = [x[:, 0, 0] for x in (y_out, y_in)] + [leaf_out_map[0, 0]]
+    rows_here = [x[:, 0, 0] for x in (y_out, y_in)] + [leaf_out_map[0, 0], reflect[0]]
     if not whole_solve:
         rows_here.append(ys_here)
 
@@ -248,7 +248,7 @@
         for copy in copies:
             copy.wait()
 
-    field_edges, field_inner, yo_all, yi_all, out_map, *ys_all = placing(
+    field_edges, field_inner, yo_all, yi_all, out_map, mirror, *ys_all = placing(
         place_body,
         [(inner, leaf), (inner, inner)] + [x.shape for x in rows_here],
         leaf_field_map[0, 0],
@@ -816,7 +816,7 @@
                     other,
                     yo_all,
                     yi_all,
-                    reflect[0],
+                    mirror,
                 )
             y_keep.append(w)
             continue
@@ -846,7 +846,7 @@
                 got,
                 yo_all,
                 yi_all,
-                reflect[0],
+                mirror,
                 scratch=[(waves, iface)],
             )
         y_keep.append(w)

time: 85.7 us -> 85.6 us (level)
  no operation moved by 1% of the time
where the time goes in v11:
time: 85.6 us; the launch traced here: 85.3 us
  blocking collectives  39.1 us (46%)
  starting transfers between devices  26.6 us (31%)
  Pallas kernels  10.8 us (13%)
  waiting for transfers between devices  6.83 us (8%)
  local copies, waits for them, and re-layouts  1.28 us (1%)
    all_to_all x2, blocking collectives, local(): got = lax.all_to_all(offer, axes, 0, 0, tiled=True)  19.4 us
    all_to_all x1, blocking collectives, local(): got = lax.all_to_all(terms, 'box', 0, 0, tiled=True)  10.1 us
    all_to_all x1, blocking collectives, swap(): return lax.all_to_all(x, group(level), 0, 0, tiled=True)  9.56 us
    ppermute x6, starting transfers between devices, passed_on(): lax.ppermute(held, 'box', [(i, i ^ 1 << bit_no) for i in range(cols)])  6.63 us
    pallas_call x14, Pallas kernels, fused(): pl.pallas_call(body, out_shape=[pltpu.VMEM(s, f32) for s in outs], in_spe...  6.03 us
    pallas_call x3, Pallas kernels, placing(): pl.pallas_call(body, out_shape=[pltpu.VMEM(s, f32) for s in shapes], in_s...  4.74 us
    ppermute x3, starting transfers between devices, local(): lax.ppermute(to_send, 'box', [(i, i ^ 1 << level) for i in range(cols)])  3.54 us
    ppermute x2, starting transfers between devices, local(): other = lax.ppermute(mine, core, swapped)  3.5 us
  transfers between devices with their start and end apart: 18, of which 6 were waited for; matrix products, arithmetic and copies ran while one was open for 1% of the time, Pallas kernels for 8%

profile of v11, /device:TPU:9, one launch (start us, length us, event | category | flops | bytes accessed | tf_op | source)
XLA Modules:
  0.0 85.3 jit_solution(1102457609903131591)
XLA Ops:
  0.6 1.3 %shard_map.125 = (f32[1,32,512]{2,1,0:T(8,128)S(1)}, f32[1,48,512]{2,1,0:T(8,128)S(1)}) custom-call(f32[2,64,512]{2,1,0:T(8,128)} %bitcast.19, f32[3,64,128]{2,1,0:T(8,128)} %bitcast.17), custom_call_target="tpu_custom_call" | custom-call | tf_op jit(solution)/shard_map/pallas_call | solution.py:142
  1.9 2.4 %collective-permute-start.1 = (f32[1,32,512]{2,1,0:T(8,128)S(1)}, f32[1,32,512]{2,1,0:T(8,128)S(1)}, u32[]{:S(2)}, u32[]{:S(2)}) collective-permute-start(f32[1,32,512]{2,1,0:T(8,128)S(1)} %get-tuple-element.66.refs_1_), channel_id=1, source_target_pairs={{0,4},{1,5},{2,6},{3,7},{4,0},{5,1},{6,2},{7,3},{8,12},{9,13},{10,... | collective-permute-start | bytes 196616 | tf_op jit(solution)/shard_map/ppermute | solution.py:126
  4.3 1.8 %shard_map.122 = (f32[64,128]{1,0:T(8,128)S(1)}, f32[64,256]{1,0:T(8,128)S(1)}, f32[64,512]{1,0:T(8,128)S(1)}, f32[3,64,128]{2,1,0:T(8,128)S(1)}, f32[3,64,128]{2,1,0:T(8,128)S(1)}, /*index=5*/f32[3,64,64]{2,1,0:T(8,128)S(1)}) custom-call(f32[64,1,1,512]{3,2,1,0:T(1,128)} %load_any.1, f32[128,512]{1,0:T(8,128)} %bitcast.20, f32[3,64,128]{2,1,0:T(8,128)} %bitcast.21, ...), custom_call_target="tpu_custom_call" | custom-call | tf_op jit(solution)/shard_map/pallas_call | solution.py:142
  6.1 1.3 %collective-permute-start = (f32[64,256]{1,0:T(8,128)S(1)}, f32[64,256]{1,0:T(8,128)S(1)}, u32[]{:S(2)}, u32[]{:S(2)}) collective-permute-start(f32[64,256]{1,0:T(8,128)S(1)} %get-tuple-element.58.own_ref), channel_id=1, source_target_pairs={{0,1},{1,0},{2,3},{3,2},{4,5},{5,4},{6,7},{7,6},{8,9},{9,8},{10,11... | collective-permute-start | bytes 196616 | tf_op jit(solution)/shard_map/ppermute | solution.py:370
  7.4 1.7 %shard_map.123 = (f32[512,128]{1,0:T(8,128)S(1)}, f32[512,512]{1,0:T(8,128)S(1)}, f32[2,128,512]{2,1,0:T(8,128)S(1)}, f32[2,512,128]{2,1,0:T(8,128)S(1)}, f32[128,128]{1,0:T(8,128)S(1)}, /*index=5*/f32[1,128]{1,0:T(1,128)S(1)}) custom-call(f32[512,640]{1,0:T(8,128)} %bitcast.14, f32[2,128,512]{2,1,0:T(8,128)} %bitcast.15, f32[2,512,128]{2,1,0:T(8,128)} %bitcast.16, ...), custom_call_target="tpu_custom_call" | custom-call | tf_op jit(solution)/shard_map/pallas_call | solution.py:142
  10.2 0.9 %collective-permute-start.6 = (f32[2,32,512]{2,1,0:T(8,128)S(1)}, f32[2,32,512]{2,1,0:T(8,128)S(1)}, u32[]{:S(2)}, u32[]{:S(2)}) collective-permute-start(f32[2,32,512]{2,1,0:T(8,128)S(1)} %get-tuple-element.74.refs_1_), channel_id=1, source_target_pairs={{0,1},{1,0},{2,3},{3,2},{4,5},{5,4},{6,7},{7,6},{8,9},{9,8},{10,11... | collective-permute-start | bytes 393224 | tf_op jit(solution)/shard_map/ppermute | solution.py:126
  11.1 2.0 %collective-permute-done.2.got_ref = f32[64,128]{1,0:T(8,128)S(1)} collective-permute-done((f32[64,128]{1,0:T(8,128)S(1)}, f32[64,128]{1,0:T(8,128)S(1)}, u32[]{:S(2)}, u32[]{:S(2)}) %collective-permute-start.2) | collective-permute-done | bytes 32800 | tf_op jit(solution)/shard_map/ppermute | solution.py:370
  13.5 2.7 %collective-permute-start.5 = (f32[256,128]{1,0:T(8,128)S(1)}, f32[256,128]{1,0:T(8,128)S(1)}, u32[]{:S(2)}, u32[]{:S(2)}) collective-permute-start(f32[256,128]{1,0:T(8,128)S(1)} %get-tuple-element.73.side_ref), channel_id=1, source_target_pairs={{0,8},{8,0},{1,9},{9,1},{2,10},{10,2},{3,11},{11,3},{4,12},{12,4},... | collective-permute-start | bytes 393224 | tf_op jit(solution)/shard_map/ppermute | solution.py:412
  16.2 2.0 %collective-permute-start.4 = (f32[64,128]{1,0:T(8,128)S(1)}, f32[64,128]{1,0:T(8,128)S(1)}, u32[]{:S(2)}, u32[]{:S(2)}) collective-permute-start(f32[64,128]{1,0:T(8,128)S(1)} %get-tuple-element.72.own_ref), channel_id=1, source_target_pairs={{0,4},{1,5},{2,6},{3,7},{4,0},{5,1},{6,2},{7,3},{8,12},{9,13},{10,... | collective-permute-start | bytes 98312 | tf_op jit(solution)/shard_map/ppermute | solution.py:370
  18.3 1.3 %collective-permute-start.8 = (f32[2,64,512]{2,1,0:T(8,128)S(1)}, f32[2,64,512]{2,1,0:T(8,128)S(1)}, u32[]{:S(2)}, u32[]{:S(2)}) collective-permute-start(f32[2,64,512]{2,1,0:T(8,128)S(1)} %get-tuple-element.78.refs_0_), channel_id=1, source_target_pairs={{0,1},{1,0},{2,3},{3,2},{4,5},{5,4},{6,7},{7,6},{8,9},{9,8},{10,11... | collective-permute-start | bytes 786440 | tf_op jit(solution)/shard_map/ppermute | solution.py:126
  20.8 10.2 %all_to_all.20.got_ref = f32[8,16,128]{2,1,0:T(8,128)S(1)} all-to-all(f32[8,16,128]{2,1,0:T(8,128)S(1)} %get-tuple-element.76), channel_id=1, replica_groups=mesh['row1'=2,'row0'=2,'box'=8] {'box'}, dimensions={0} | all-to-all | bytes 131072 | tf_op jit(solution)/shard_map/all_to_all | solution.py:774
  31.4 1.6 %collective-permute-start.11 = (f32[4,48,512]{2,1,0:T(8,128)S(1)}, f32[4,48,512]{2,1,0:T(8,128)S(1)}, u32[]{:S(2)}, u32[]{:S(2)}) collective-permute-start(f32[4,48,512]{2,1,0:T(8,128)S(1)} %get-tuple-element.83.held_ref), channel_id=1, source_target_pairs={{0,2},{1,3},{2,0},{3,1},{4,6},{5,7},{6,4},{7,5},{8,10},{9,11},{10,... | collective-permute-start | bytes 1179656 | tf_op jit(solution)/shard_map/ppermute | solution.py:126
  33.0 2.6 %collective-permute-start.9 = (f32[64,512]{1,0:T(8,128)S(1)}, f32[64,512]{1,0:T(8,128)S(1)}, u32[]{:S(2)}, u32[]{:S(2)}) collective-permute-start(f32[64,512]{1,0:T(8,128)S(1)} %get-tuple-element.79.mine_ref), channel_id=1, source_target_pairs={{0,8},{8,0},{1,9},{9,1},{2,10},{10,2},{3,11},{11,3},{4,12},{12,4},... | collective-permute-start | bytes 393224 | tf_op jit(solution)/shard_map/ppermute | solution.py:798
  35.6 1.2 %collective-permute-done.10.face_ref = f32[16,128]{1,0:T(8,128)S(1)} collective-permute-done((f32[16,128]{1,0:T(8,128)S(1)}, f32[16,128]{1,0:T(8,128)S(1)}, u32[]{:S(2)}, u32[]{:S(2)}) %collective-permute-start.10) | collective-permute-done | bytes 8224 | tf_op jit(solution)/shard_map/ppermute | solution.py:787
  37.3 9.2 %all_to_all.21.got_ref = f32[32,8,128]{2,1,0:T(8,128)S(1)} all-to-all(f32[32,8,128]{2,1,0:T(8,128)S(1)} %get-tuple-element.82), channel_id=1, replica_groups=mesh['row1'=2,'row0'=2,'box'=8] {'row1','row0','box'}, dimensions={0} | all-to-all | bytes 262144 | tf_op jit(solution)/shard_map/all_to_all | solution.py:774
  47.8 1.0 %collective-permute-done.12.refs_0_ = f32[64,512]{1,0:T(8,128)S(1)} collective-permute-done((f32[64,512]{1,0:T(8,128)S(1)}, f32[64,512]{1,0:T(8,128)S(1)}, u32[]{:S(2)}, u32[]{:S(2)}) %collective-permute-start.12) | collective-permute-done | bytes 131104 | tf_op jit(solution)/shard_map/ppermute | solution.py:798
  49.4 9.6 %all_to_all.22.got_ref = f32[32,8,128]{2,1,0:T(8,128)S(1)} all-to-all(f32[32,8,128]{2,1,0:T(8,128)S(1)} %get-tuple-element.85), channel_id=1, replica_groups=mesh['row1'=2,'row0'=2,'box'=8] {'row1','row0','box'}, dimensions={0} | all-to-all | bytes 262144 | tf_op jit(solution)/shard_map/all_to_all | solution.py:297
  59.5 0.9 %collective-permute-start.13 = (f32[72,256]{1,0:T(8,128)S(1)}, f32[72,256]{1,0:T(8,128)S(1)}, u32[]{:S(2)}, u32[]{:S(2)}) collective-permute-start(f32[72,256]{1,0:T(8,128)S(1)} %get-tuple-element.89), channel_id=1, source_target_pairs={{0,8},{8,0},{1,9},{9,1},{2,10},{10,2},{3,11},{11,3},{4,12},{12,4},... | collective-permute-start | bytes 221192 | tf_op jit(solution)/shard_map/ppermute | solution.py:881
  61.9 10.1 %all_to_all.23.got_ref = f32[8,64,128]{2,1,0:T(8,128)S(1)} all-to-all(f32[8,64,128]{2,1,0:T(8,128)S(1)} %get-tuple-element.102), channel_id=1, replica_groups=mesh['row1'=2,'row0'=2,'box'=8] {'box'}, dimensions={0} | all-to-all | bytes 524288 | tf_op jit(solution)/shard_map/all_to_all | solution.py:911
  72.4 1.2 %collective-permute-start.14 = (f32[16,128]{1,0:T(8,128)S(1)}, f32[16,128]{1,0:T(8,128)S(1)}, u32[]{:S(2)}, u32[]{:S(2)}) collective-permute-start(f32[16,128]{1,0:T(8,128)S(1)} %get-tuple-element.108), channel_id=1, source_target_pairs={{0,1},{1,0},{2,3},{3,2},{4,5},{5,4},{6,7},{7,6},{8,9},{9,8},{10,11... | collective-permute-start | bytes 24584 | tf_op jit(solution)/shard_map/ppermute | solution.py:931
  73.6 3.2 %collective-permute-start.15 = (f32[16,128]{1,0:T(8,128)S(1)}, f32[16,128]{1,0:T(8,128)S(1)}, u32[]{:S(2)}, u32[]{:S(2)}) collective-permute-start(f32[16,128]{1,0:T(8,128)S(1)} %get-tuple-element.109), channel_id=1, source_target_pairs={{1,2},{3,4},{5,6},{2,1},{4,3},{6,5},{9,10},{11,12},{13,14},{10,9},... | collective-permute-start | bytes 24584 | tf_op jit(solution)/shard_map/ppermute | solution.py:932
  76.8 2.8 %collective-permute-start.16 = (f32[16,128]{1,0:T(8,128)S(1)}, f32[16,128]{1,0:T(8,128)S(1)}, u32[]{:S(2)}, u32[]{:S(2)}) collective-permute-start(f32[16,128]{1,0:T(8,128)S(1)} %get-tuple-element.110), channel_id=1, source_target_pairs={{0,8},{8,0},{16,24},{24,16},{1,9},{9,1},{17,25},{25,17},{2,10},{10... | collective-permute-start | bytes 24584 | tf_op jit(solution)/shard_map/ppermute | solution.py:933
  79.6 2.2 %collective-permute-start.17 = (f32[16,128]{1,0:T(8,128)S(1)}, f32[16,128]{1,0:T(8,128)S(1)}, u32[]{:S(2)}, u32[]{:S(2)}) collective-permute-start(f32[16,128]{1,0:T(8,128)S(1)} %get-tuple-element.111), channel_id=1, source_target_pairs={{8,16},{16,8},{9,17},{17,9},{10,18},{18,10},{11,19},{19,11},{12,20... | collective-permute-start | bytes 24584 | tf_op jit(solution)/shard_map/ppermute | solution.py:934
  82.6 1.9 %collective-permute-done.17.d_ref = f32[16,128]{1,0:T(8,128)S(1)} collective-permute-done((f32[16,128]{1,0:T(8,128)S(1)}, f32[16,128]{1,0:T(8,128)S(1)}, u32[]{:S(2)}, u32[]{:S(2)}) %collective-permute-start.17) | collective-permute-done | bytes 8224 | tf_op jit(solution)/shard_map/ppermute | solution.py:934
  (35 shorter events, 9.7 us)
Async XLA Ops:
  1.9 7.7 %collective-permute-start.1 = (f32[1,32,512]{2,1,0:T(8,128)S(1)}, f32[1,32,512]{2,1,0:T(8,128)S(1)}, u32[]{:S(2)}, u32[]{:S(2)}) collective-permute-start(f32[1,32,512]{2,1,0:T(8,128)S(1)} %get-tuple-element.66.refs_1_), channel_id=1, source_target_pairs={{0,4},{1,5},{2,6},{3,7},{4,0},{5,1},{6,2},{7,3},{8,12},{9,13},{10,... | collective-permute-start | bytes 196616 | tf_op jit(solution)/shard_map/ppermute | solution.py:126
  6.1 3.5 %collective-permute-start = (f32[64,256]{1,0:T(8,128)S(1)}, f32[64,256]{1,0:T(8,128)S(1)}, u32[]{:S(2)}, u32[]{:S(2)}) collective-permute-start(f32[64,256]{1,0:T(8,128)S(1)} %get-tuple-element.58.own_ref), channel_id=1, source_target_pairs={{0,1},{1,0},{2,3},{3,2},{4,5},{5,4},{6,7},{7,6},{8,9},{9,8},{10,11... | collective-permute-start | bytes 196616 | tf_op jit(solution)/shard_map/ppermute | solution.py:370
  7.4 5.7 %collective-permute-start.3 = (f32[1,48,512]{2,1,0:T(8,128)S(1)}, f32[1,48,512]{2,1,0:T(8,128)S(1)}, u32[]{:S(2)}, u32[]{:S(2)}) collective-permute-start(f32[1,48,512]{2,1,0:T(8,128)S(1)} %get-tuple-element.70.refs_1_), channel_id=1, source_target_pairs={{0,4},{1,5},{2,6},{3,7},{4,0},{5,1},{6,2},{7,3},{8,12},{9,13},{10,... | collective-permute-start | bytes 294920 | tf_op jit(solution)/shard_map/ppermute | solution.py:126
  10.0 3.1 %collective-permute-start.2 = (f32[64,128]{1,0:T(8,128)S(1)}, f32[64,128]{1,0:T(8,128)S(1)}, u32[]{:S(2)}, u32[]{:S(2)}) collective-permute-start(f32[64,128]{1,0:T(8,128)S(1)} %get-tuple-element.68.own_ref), channel_id=1, source_target_pairs={{0,2},{1,3},{2,0},{3,1},{4,6},{5,7},{6,4},{7,5},{8,10},{9,11},{10,... | collective-permute-start | bytes 98312 | tf_op jit(solution)/shard_map/ppermute | solution.py:370
  10.2 9.8 %collective-permute-start.6 = (f32[2,32,512]{2,1,0:T(8,128)S(1)}, f32[2,32,512]{2,1,0:T(8,128)S(1)}, u32[]{:S(2)}, u32[]{:S(2)}) collective-permute-start(f32[2,32,512]{2,1,0:T(8,128)S(1)} %get-tuple-element.74.refs_1_), channel_id=1, source_target_pairs={{0,1},{1,0},{2,3},{3,2},{4,5},{5,4},{6,7},{7,6},{8,9},{9,8},{10,11... | collective-permute-start | bytes 393224 | tf_op jit(solution)/shard_map/ppermute | solution.py:126
  13.5 6.5 %collective-permute-start.5 = (f32[256,128]{1,0:T(8,128)S(1)}, f32[256,128]{1,0:T(8,128)S(1)}, u32[]{:S(2)}, u32[]{:S(2)}) collective-permute-start(f32[256,128]{1,0:T(8,128)S(1)} %get-tuple-element.73.side_ref), channel_id=1, source_target_pairs={{0,8},{8,0},{1,9},{9,1},{2,10},{10,2},{3,11},{11,3},{4,12},{12,4},... | collective-permute-start | bytes 393224 | tf_op jit(solution)/shard_map/ppermute | solution.py:412
  16.2 3.7 %collective-permute-start.4 = (f32[64,128]{1,0:T(8,128)S(1)}, f32[64,128]{1,0:T(8,128)S(1)}, u32[]{:S(2)}, u32[]{:S(2)}) collective-permute-start(f32[64,128]{1,0:T(8,128)S(1)} %get-tuple-element.72.own_ref), channel_id=1, source_target_pairs={{0,4},{1,5},{2,6},{3,7},{4,0},{5,1},{6,2},{7,3},{8,12},{9,13},{10,... | collective-permute-start | bytes 98312 | tf_op jit(solution)/shard_map/ppermute | solution.py:370
  18.3 12.8 %collective-permute-start.8 = (f32[2,64,512]{2,1,0:T(8,128)S(1)}, f32[2,64,512]{2,1,0:T(8,128)S(1)}, u32[]{:S(2)}, u32[]{:S(2)}) collective-permute-start(f32[2,64,512]{2,1,0:T(8,128)S(1)} %get-tuple-element.78.refs_0_), channel_id=1, source_target_pairs={{0,1},{1,0},{2,3},{3,2},{4,5},{5,4},{6,7},{7,6},{8,9},{9,8},{10,11... | collective-permute-start | bytes 786440 | tf_op jit(solution)/shard_map/ppermute | solution.py:126
  20.5 10.6 %collective-permute-start.7 = (f32[4,32,512]{2,1,0:T(8,128)S(1)}, f32[4,32,512]{2,1,0:T(8,128)S(1)}, u32[]{:S(2)}, u32[]{:S(2)}) collective-permute-start(f32[4,32,512]{2,1,0:T(8,128)S(1)} %get-tuple-element.77.held_ref), channel_id=1, source_target_pairs={{0,2},{1,3},{2,0},{3,1},{4,6},{5,7},{6,4},{7,5},{8,10},{9,11},{10,... | collective-permute-start | bytes 786440 | tf_op jit(solution)/shard_map/ppermute | solution.py:126
  31.4 15.2 %collective-permute-start.11 = (f32[4,48,512]{2,1,0:T(8,128)S(1)}, f32[4,48,512]{2,1,0:T(8,128)S(1)}, u32[]{:S(2)}, u32[]{:S(2)}) collective-permute-start(f32[4,48,512]{2,1,0:T(8,128)S(1)} %get-tuple-element.83.held_ref), channel_id=1, source_target_pairs={{0,2},{1,3},{2,0},{3,1},{4,6},{5,7},{6,4},{7,5},{8,10},{9,11},{10,... | collective-permute-start | bytes 1179656 | tf_op jit(solution)/shard_map/ppermute | solution.py:126
  33.0 3.8 %collective-permute-start.9 = (f32[64,512]{1,0:T(8,128)S(1)}, f32[64,512]{1,0:T(8,128)S(1)}, u32[]{:S(2)}, u32[]{:S(2)}) collective-permute-start(f32[64,512]{1,0:T(8,128)S(1)} %get-tuple-element.79.mine_ref), channel_id=1, source_target_pairs={{0,8},{8,0},{1,9},{9,1},{2,10},{10,2},{3,11},{11,3},{4,12},{12,4},... | collective-permute-start | bytes 393224 | tf_op jit(solution)/shard_map/ppermute | solution.py:798
  35.6 1.2 %collective-permute-start.10 = (f32[16,128]{1,0:T(8,128)S(1)}, f32[16,128]{1,0:T(8,128)S(1)}, u32[]{:S(2)}, u32[]{:S(2)}) collective-permute-start(f32[16,128]{1,0:T(8,128)S(1)} %get-tuple-element.80), channel_id=1, source_target_pairs={{0,8},{8,0},{1,9},{9,1},{2,10},{10,2},{3,11},{11,3},{4,12},{12,4},... | collective-permute-start | bytes 24584 | tf_op jit(solution)/shard_map/ppermute | solution.py:787
  46.9 1.9 %collective-permute-start.12 = (f32[64,512]{1,0:T(8,128)S(1)}, f32[64,512]{1,0:T(8,128)S(1)}, u32[]{:S(2)}, u32[]{:S(2)}) collective-permute-start(f32[64,512]{1,0:T(8,128)S(1)} %shard_map.131.got_ref), channel_id=1, source_target_pairs={{0,8},{8,0},{1,9},{9,1},{2,10},{10,2},{3,11},{11,3},{4,12},{12,4},... | collective-permute-start | bytes 393224 | tf_op jit(solution)/shard_map/ppermute | solution.py:798
  59.5 1.8 %collective-permute-start.13 = (f32[72,256]{1,0:T(8,128)S(1)}, f32[72,256]{1,0:T(8,128)S(1)}, u32[]{:S(2)}, u32[]{:S(2)}) collective-permute-start(f32[72,256]{1,0:T(8,128)S(1)} %get-tuple-element.89), channel_id=1, source_target_pairs={{0,8},{8,0},{1,9},{9,1},{2,10},{10,2},{3,11},{11,3},{4,12},{12,4},... | collective-permute-start | bytes 221192 | tf_op jit(solution)/shard_map/ppermute | solution.py:881
  72.4 10.2 %collective-permute-start.14 = (f32[16,128]{1,0:T(8,128)S(1)}, f32[16,128]{1,0:T(8,128)S(1)}, u32[]{:S(2)}, u32[]{:S(2)}) collective-permute-start(f32[16,128]{1,0:T(8,128)S(1)} %get-tuple-element.108), channel_id=1, source_target_pairs={{0,1},{1,0},{2,3},{3,2},{4,5},{5,4},{6,7},{7,6},{8,9},{9,8},{10,11... | collective-permute-start | bytes 24584 | tf_op jit(solution)/shard_map/ppermute | solution.py:931
  73.6 9.1 %collective-permute-start.15 = (f32[16,128]{1,0:T(8,128)S(1)}, f32[16,128]{1,0:T(8,128)S(1)}, u32[]{:S(2)}, u32[]{:S(2)}) collective-permute-start(f32[16,128]{1,0:T(8,128)S(1)} %get-tuple-element.109), channel_id=1, source_target_pairs={{1,2},{3,4},{5,6},{2,1},{4,3},{6,5},{9,10},{11,12},{13,14},{10,9},... | collective-permute-start | bytes 24584 | tf_op jit(solution)/shard_map/ppermute | solution.py:932
  76.8 5.8 %collective-permute-start.16 = (f32[16,128]{1,0:T(8,128)S(1)}, f32[16,128]{1,0:T(8,128)S(1)}, u32[]{:S(2)}, u32[]{:S(2)}) collective-permute-start(f32[16,128]{1,0:T(8,128)S(1)} %get-tuple-element.110), channel_id=1, source_target_pairs={{0,8},{8,0},{16,24},{24,16},{1,9},{9,1},{17,25},{25,17},{2,10},{10... | collective-permute-start | bytes 24584 | tf_op jit(solution)/shard_map/ppermute | solution.py:933
  79.6 5.0 %collective-permute-start.17 = (f32[16,128]{1,0:T(8,128)S(1)}, f32[16,128]{1,0:T(8,128)S(1)}, u32[]{:S(2)}, u32[]{:S(2)}) collective-permute-start(f32[16,128]{1,0:T(8,128)S(1)} %get-tuple-element.111), channel_id=1, source_target_pairs={{8,16},{16,8},{9,17},{17,9},{10,18},{18,10},{11,19},{19,11},{12,20... | collective-permute-start | bytes 24584 | tf_op jit(solution)/shard_map/ppermute | solution.py:934

commit v12 on v11

--- a/solution.py
+++ b/solution.py
@@ -687,7 +687,6 @@
     def x_terms_body(own_ref, got_ref, matrix_ref, known_ref, *refs):
         out_ref = refs[-1]
         q = own_ref[...] + got_ref[:waves]
-        terms = dot_t(q, matrix_ref[...]) + known_ref[...]
         if whole_solve:
             g_ref, half_ref, xi_ref, g_out, _ = refs
             odd_row = bit(my_row(), 0) == 1
@@ -706,16 +705,20 @@
                 axis=1,
             )
             g_out[...] = g_ref[...] + upper
-            added = dot_t(upper, xi_ref[...].reshape(x_levels * pair, leaf))
+            matrix = []
+            for k in range(x_levels):
+                for node in range(cols >> (k + 1)):
+                    inside = my_column() >> (k + 1) == node
+                    matrix.append(jnp.where(inside, xi_ref[k], 0.0))
+            matrix = jnp.concatenate([matrix_ref[...], jnp.concatenate(matrix, axis=0)], axis=1)
+            terms = dot_t(jnp.concatenate([q, upper], axis=1), matrix) + known_ref[...]
+        else:
+            terms = dot_t(q, matrix_ref[...]) + known_ref[...]
         for c in range(cols):
             picked = []
             for k in range(x_levels):
                 start = node_starts[k] + (c >> (k + 1)) * pair + bit(c, k) * edge
-                piece = terms[:, start : start + edge]
-                if whole_solve:
-                    inside = my_column() >> (k + 1) == c >> (k + 1)
-                    piece = piece + jnp.where(inside, edge_of(added, 2 * k + bit(c, k)), 0.0)
-                picked.append(piece)
+                picked.append(terms[:, start : start + edge])
             out_ref[c] = pad_lanes(jnp.concatenate(picked + [edge_of(q, c)], axis=1), x_lanes)
 
     def finish_body(g_ref, w_ref, h0_ref, got_ref, chain_ref, keep_ref, g_out, t_out, *faces):

time: 85.6 us -> 85.7 us (level)
  no operation moved by 1% of the time
where the time goes in v12:
time: 85.7 us; the launch traced here: 85.4 us
  blocking collectives  39.1 us (46%)
  starting transfers between devices  26.6 us (31%)
  Pallas kernels  10.8 us (13%)
  waiting for transfers between devices  6.83 us (8%)
  local copies, waits for them, and re-layouts  1.28 us (1%)
    all_to_all x2, blocking collectives, local(): got = lax.all_to_all(offer, axes, 0, 0, tiled=True)  19.4 us
    all_to_all x1, blocking collectives, local(): got = lax.all_to_all(terms, 'box', 0, 0, tiled=True)  10.1 us
    all_to_all x1, blocking collectives, swap(): return lax.all_to_all(x, group(level), 0, 0, tiled=True)  9.56 us
    ppermute x6, starting transfers between devices, passed_on(): lax.ppermute(held, 'box', [(i, i ^ 1 << bit_no) for i in range(cols)])  6.63 us
    pallas_call x14, Pallas kernels, fused(): pl.pallas_call(body, out_shape=[pltpu.VMEM(s, f32) for s in outs], in_spe...  6.05 us
    pallas_call x3, Pallas kernels, placing(): pl.pallas_call(body, out_shape=[pltpu.VMEM(s, f32) for s in shapes], in_s...  4.74 us
    ppermute x3, starting transfers between devices, local(): lax.ppermute(to_send, 'box', [(i, i ^ 1 << level) for i in range(cols)])  3.54 us
    ppermute x2, starting transfers between devices, local(): other = lax.ppermute(mine, core, swapped)  3.5 us
  transfers between devices with their start and end apart: 18, of which 6 were waited for; matrix products, arithmetic and copies ran while one was open for 1% of the time, Pallas kernels for 8%

profile of v12, /device:TPU:9, one launch (start us, length us, event | category | flops | bytes accessed | tf_op | source)
XLA Modules:
  0.0 85.4 jit_solution(6708829298656108312)
XLA Ops:
  0.6 1.3 %shard_map.125 = (f32[1,32,512]{2,1,0:T(8,128)S(1)}, f32[1,48,512]{2,1,0:T(8,128)S(1)}) custom-call(f32[2,64,512]{2,1,0:T(8,128)} %bitcast.19, f32[3,64,128]{2,1,0:T(8,128)} %bitcast.17), custom_call_target="tpu_custom_call" | custom-call | tf_op jit(solution)/shard_map/pallas_call | solution.py:142
  1.9 2.4 %collective-permute-start.1 = (f32[1,32,512]{2,1,0:T(8,128)S(1)}, f32[1,32,512]{2,1,0:T(8,128)S(1)}, u32[]{:S(2)}, u32[]{:S(2)}) collective-permute-start(f32[1,32,512]{2,1,0:T(8,128)S(1)} %get-tuple-element.66.refs_1_), channel_id=1, source_target_pairs={{0,4},{1,5},{2,6},{3,7},{4,0},{5,1},{6,2},{7,3},{8,12},{9,13},{10,... | collective-permute-start | bytes 196616 | tf_op jit(solution)/shard_map/ppermute | solution.py:126
  4.3 1.8 %shard_map.122 = (f32[64,128]{1,0:T(8,128)S(1)}, f32[64,256]{1,0:T(8,128)S(1)}, f32[64,512]{1,0:T(8,128)S(1)}, f32[3,64,128]{2,1,0:T(8,128)S(1)}, f32[3,64,128]{2,1,0:T(8,128)S(1)}, /*index=5*/f32[3,64,64]{2,1,0:T(8,128)S(1)}) custom-call(f32[64,1,1,512]{3,2,1,0:T(1,128)} %load_any.1, f32[128,512]{1,0:T(8,128)} %bitcast.20, f32[3,64,128]{2,1,0:T(8,128)} %bitcast.21, ...), custom_call_target="tpu_custom_call" | custom-call | tf_op jit(solution)/shard_map/pallas_call | solution.py:142
  6.1 1.3 %collective-permute-start = (f32[64,256]{1,0:T(8,128)S(1)}, f32[64,256]{1,0:T(8,128)S(1)}, u32[]{:S(2)}, u32[]{:S(2)}) collective-permute-start(f32[64,256]{1,0:T(8,128)S(1)} %get-tuple-element.58.own_ref), channel_id=1, source_target_pairs={{0,1},{1,0},{2,3},{3,2},{4,5},{5,4},{6,7},{7,6},{8,9},{9,8},{10,11... | collective-permute-start | bytes 196616 | tf_op jit(solution)/shard_map/ppermute | solution.py:370
  7.4 1.7 %shard_map.123 = (f32[512,128]{1,0:T(8,128)S(1)}, f32[512,512]{1,0:T(8,128)S(1)}, f32[2,128,512]{2,1,0:T(8,128)S(1)}, f32[2,512,128]{2,1,0:T(8,128)S(1)}, f32[128,128]{1,0:T(8,128)S(1)}, /*index=5*/f32[1,128]{1,0:T(1,128)S(1)}) custom-call(f32[512,640]{1,0:T(8,128)} %bitcast.14, f32[2,128,512]{2,1,0:T(8,128)} %bitcast.15, f32[2,512,128]{2,1,0:T(8,128)} %bitcast.16, ...), custom_call_target="tpu_custom_call" | custom-call | tf_op jit(solution)/shard_map/pallas_call | solution.py:142
  10.2 0.9 %collective-permute-start.6 = (f32[2,32,512]{2,1,0:T(8,128)S(1)}, f32[2,32,512]{2,1,0:T(8,128)S(1)}, u32[]{:S(2)}, u32[]{:S(2)}) collective-permute-start(f32[2,32,512]{2,1,0:T(8,128)S(1)} %get-tuple-element.74.refs_1_), channel_id=1, source_target_pairs={{0,1},{1,0},{2,3},{3,2},{4,5},{5,4},{6,7},{7,6},{8,9},{9,8},{10,11... | collective-permute-start | bytes 393224 | tf_op jit(solution)/shard_map/ppermute | solution.py:126
  11.1 2.0 %collective-permute-done.2.got_ref = f32[64,128]{1,0:T(8,128)S(1)} collective-permute-done((f32[64,128]{1,0:T(8,128)S(1)}, f32[64,128]{1,0:T(8,128)S(1)}, u32[]{:S(2)}, u32[]{:S(2)}) %collective-permute-start.2) | collective-permute-done | bytes 32800 | tf_op jit(solution)/shard_map/ppermute | solution.py:370
  13.5 2.7 %collective-permute-start.5 = (f32[256,128]{1,0:T(8,128)S(1)}, f32[256,128]{1,0:T(8,128)S(1)}, u32[]{:S(2)}, u32[]{:S(2)}) collective-permute-start(f32[256,128]{1,0:T(8,128)S(1)} %get-tuple-element.73.side_ref), channel_id=1, source_target_pairs={{0,8},{8,0},{1,9},{9,1},{2,10},{10,2},{3,11},{11,3},{4,12},{12,4},... | collective-permute-start | bytes 393224 | tf_op jit(solution)/shard_map/ppermute | solution.py:412
  16.2 2.0 %collective-permute-start.4 = (f32[64,128]{1,0:T(8,128)S(1)}, f32[64,128]{1,0:T(8,128)S(1)}, u32[]{:S(2)}, u32[]{:S(2)}) collective-permute-start(f32[64,128]{1,0:T(8,128)S(1)} %get-tuple-element.72.own_ref), channel_id=1, source_target_pairs={{0,4},{1,5},{2,6},{3,7},{4,0},{5,1},{6,2},{7,3},{8,12},{9,13},{10,... | collective-permute-start | bytes 98312 | tf_op jit(solution)/shard_map/ppermute | solution.py:370
  18.3 1.3 %collective-permute-start.8 = (f32[2,64,512]{2,1,0:T(8,128)S(1)}, f32[2,64,512]{2,1,0:T(8,128)S(1)}, u32[]{:S(2)}, u32[]{:S(2)}) collective-permute-start(f32[2,64,512]{2,1,0:T(8,128)S(1)} %get-tuple-element.78.refs_0_), channel_id=1, source_target_pairs={{0,1},{1,0},{2,3},{3,2},{4,5},{5,4},{6,7},{7,6},{8,9},{9,8},{10,11... | collective-permute-start | bytes 786440 | tf_op jit(solution)/shard_map/ppermute | solution.py:126
  20.8 10.2 %all_to_all.20.got_ref = f32[8,16,128]{2,1,0:T(8,128)S(1)} all-to-all(f32[8,16,128]{2,1,0:T(8,128)S(1)} %get-tuple-element.76), channel_id=1, replica_groups=mesh['row1'=2,'row0'=2,'box'=8] {'box'}, dimensions={0} | all-to-all | bytes 131072 | tf_op jit(solution)/shard_map/all_to_all | solution.py:777
  31.4 1.6 %collective-permute-start.11 = (f32[4,48,512]{2,1,0:T(8,128)S(1)}, f32[4,48,512]{2,1,0:T(8,128)S(1)}, u32[]{:S(2)}, u32[]{:S(2)}) collective-permute-start(f32[4,48,512]{2,1,0:T(8,128)S(1)} %get-tuple-element.83.held_ref), channel_id=1, source_target_pairs={{0,2},{1,3},{2,0},{3,1},{4,6},{5,7},{6,4},{7,5},{8,10},{9,11},{10,... | collective-permute-start | bytes 1179656 | tf_op jit(solution)/shard_map/ppermute | solution.py:126
  33.0 2.6 %collective-permute-start.9 = (f32[64,512]{1,0:T(8,128)S(1)}, f32[64,512]{1,0:T(8,128)S(1)}, u32[]{:S(2)}, u32[]{:S(2)}) collective-permute-start(f32[64,512]{1,0:T(8,128)S(1)} %get-tuple-element.79.mine_ref), channel_id=1, source_target_pairs={{0,8},{8,0},{1,9},{9,1},{2,10},{10,2},{3,11},{11,3},{4,12},{12,4},... | collective-permute-start | bytes 393224 | tf_op jit(solution)/shard_map/ppermute | solution.py:801
  35.6 1.2 %collective-permute-done.10.face_ref = f32[16,128]{1,0:T(8,128)S(1)} collective-permute-done((f32[16,128]{1,0:T(8,128)S(1)}, f32[16,128]{1,0:T(8,128)S(1)}, u32[]{:S(2)}, u32[]{:S(2)}) %collective-permute-start.10) | collective-permute-done | bytes 8224 | tf_op jit(solution)/shard_map/ppermute | solution.py:790
  37.3 9.2 %all_to_all.21.got_ref = f32[32,8,128]{2,1,0:T(8,128)S(1)} all-to-all(f32[32,8,128]{2,1,0:T(8,128)S(1)} %get-tuple-element.82), channel_id=1, replica_groups=mesh['row1'=2,'row0'=2,'box'=8] {'row1','row0','box'}, dimensions={0} | all-to-all | bytes 262144 | tf_op jit(solution)/shard_map/all_to_all | solution.py:777
  47.8 1.0 %collective-permute-done.12.refs_0_ = f32[64,512]{1,0:T(8,128)S(1)} collective-permute-done((f32[64,512]{1,0:T(8,128)S(1)}, f32[64,512]{1,0:T(8,128)S(1)}, u32[]{:S(2)}, u32[]{:S(2)}) %collective-permute-start.12) | collective-permute-done | bytes 131104 | tf_op jit(solution)/shard_map/ppermute | solution.py:801
  49.4 9.6 %all_to_all.22.got_ref = f32[32,8,128]{2,1,0:T(8,128)S(1)} all-to-all(f32[32,8,128]{2,1,0:T(8,128)S(1)} %get-tuple-element.85), channel_id=1, replica_groups=mesh['row1'=2,'row0'=2,'box'=8] {'row1','row0','box'}, dimensions={0} | all-to-all | bytes 262144 | tf_op jit(solution)/shard_map/all_to_all | solution.py:297
  59.5 0.9 %collective-permute-start.13 = (f32[72,256]{1,0:T(8,128)S(1)}, f32[72,256]{1,0:T(8,128)S(1)}, u32[]{:S(2)}, u32[]{:S(2)}) collective-permute-start(f32[72,256]{1,0:T(8,128)S(1)} %get-tuple-element.89), channel_id=1, source_target_pairs={{0,8},{8,0},{1,9},{9,1},{2,10},{10,2},{3,11},{11,3},{4,12},{12,4},... | collective-permute-start | bytes 221192 | tf_op jit(solution)/shard_map/ppermute | solution.py:884
  61.9 10.1 %all_to_all.23.got_ref = f32[8,64,128]{2,1,0:T(8,128)S(1)} all-to-all(f32[8,64,128]{2,1,0:T(8,128)S(1)} %get-tuple-element.102), channel_id=1, replica_groups=mesh['row1'=2,'row0'=2,'box'=8] {'box'}, dimensions={0} | all-to-all | bytes 524288 | tf_op jit(solution)/shard_map/all_to_all | solution.py:914
  72.4 1.2 %collective-permute-start.14 = (f32[16,128]{1,0:T(8,128)S(1)}, f32[16,128]{1,0:T(8,128)S(1)}, u32[]{:S(2)}, u32[]{:S(2)}) collective-permute-start(f32[16,128]{1,0:T(8,128)S(1)} %get-tuple-element.108), channel_id=1, source_target_pairs={{0,1},{1,0},{2,3},{3,2},{4,5},{5,4},{6,7},{7,6},{8,9},{9,8},{10,11... | collective-permute-start | bytes 24584 | tf_op jit(solution)/shard_map/ppermute | solution.py:934
  73.6 3.2 %collective-permute-start.15 = (f32[16,128]{1,0:T(8,128)S(1)}, f32[16,128]{1,0:T(8,128)S(1)}, u32[]{:S(2)}, u32[]{:S(2)}) collective-permute-start(f32[16,128]{1,0:T(8,128)S(1)} %get-tuple-element.109), channel_id=1, source_target_pairs={{1,2},{3,4},{5,6},{2,1},{4,3},{6,5},{9,10},{11,12},{13,14},{10,9},... | collective-permute-start | bytes 24584 | tf_op jit(solution)/shard_map/ppermute | solution.py:935
  76.8 2.8 %collective-permute-start.16 = (f32[16,128]{1,0:T(8,128)S(1)}, f32[16,128]{1,0:T(8,128)S(1)}, u32[]{:S(2)}, u32[]{:S(2)}) collective-permute-start(f32[16,128]{1,0:T(8,128)S(1)} %get-tuple-element.110), channel_id=1, source_target_pairs={{0,8},{8,0},{16,24},{24,16},{1,9},{9,1},{17,25},{25,17},{2,10},{10... | collective-permute-start | bytes 24584 | tf_op jit(solution)/shard_map/ppermute | solution.py:936
  79.6 2.2 %collective-permute-start.17 = (f32[16,128]{1,0:T(8,128)S(1)}, f32[16,128]{1,0:T(8,128)S(1)}, u32[]{:S(2)}, u32[]{:S(2)}) collective-permute-start(f32[16,128]{1,0:T(8,128)S(1)} %get-tuple-element.111), channel_id=1, source_target_pairs={{8,16},{16,8},{9,17},{17,9},{10,18},{18,10},{11,19},{19,11},{12,20... | collective-permute-start | bytes 24584 | tf_op jit(solution)/shard_map/ppermute | solution.py:937
  82.7 1.9 %collective-permute-done.17.d_ref = f32[16,128]{1,0:T(8,128)S(1)} collective-permute-done((f32[16,128]{1,0:T(8,128)S(1)}, f32[16,128]{1,0:T(8,128)S(1)}, u32[]{:S(2)}, u32[]{:S(2)}) %collective-permute-start.17) | collective-permute-done | bytes 8224 | tf_op jit(solution)/shard_map/ppermute | solution.py:937
  (35 shorter events, 9.7 us)
Async XLA Ops:
  1.9 7.7 %collective-permute-start.1 = (f32[1,32,512]{2,1,0:T(8,128)S(1)}, f32[1,32,512]{2,1,0:T(8,128)S(1)}, u32[]{:S(2)}, u32[]{:S(2)}) collective-permute-start(f32[1,32,512]{2,1,0:T(8,128)S(1)} %get-tuple-element.66.refs_1_), channel_id=1, source_target_pairs={{0,4},{1,5},{2,6},{3,7},{4,0},{5,1},{6,2},{7,3},{8,12},{9,13},{10,... | collective-permute-start | bytes 196616 | tf_op jit(solution)/shard_map/ppermute | solution.py:126
  6.1 3.5 %collective-permute-start = (f32[64,256]{1,0:T(8,128)S(1)}, f32[64,256]{1,0:T(8,128)S(1)}, u32[]{:S(2)}, u32[]{:S(2)}) collective-permute-start(f32[64,256]{1,0:T(8,128)S(1)} %get-tuple-element.58.own_ref), channel_id=1, source_target_pairs={{0,1},{1,0},{2,3},{3,2},{4,5},{5,4},{6,7},{7,6},{8,9},{9,8},{10,11... | collective-permute-start | bytes 196616 | tf_op jit(solution)/shard_map/ppermute | solution.py:370
  7.4 5.7 %collective-permute-start.3 = (f32[1,48,512]{2,1,0:T(8,128)S(1)}, f32[1,48,512]{2,1,0:T(8,128)S(1)}, u32[]{:S(2)}, u32[]{:S(2)}) collective-permute-start(f32[1,48,512]{2,1,0:T(8,128)S(1)} %get-tuple-element.70.refs_1_), channel_id=1, source_target_pairs={{0,4},{1,5},{2,6},{3,7},{4,0},{5,1},{6,2},{7,3},{8,12},{9,13},{10,... | collective-permute-start | bytes 294920 | tf_op jit(solution)/shard_map/ppermute | solution.py:126
  10.0 3.1 %collective-permute-start.2 = (f32[64,128]{1,0:T(8,128)S(1)}, f32[64,128]{1,0:T(8,128)S(1)}, u32[]{:S(2)}, u32[]{:S(2)}) collective-permute-start(f32[64,128]{1,0:T(8,128)S(1)} %get-tuple-element.68.own_ref), channel_id=1, source_target_pairs={{0,2},{1,3},{2,0},{3,1},{4,6},{5,7},{6,4},{7,5},{8,10},{9,11},{10,... | collective-permute-start | bytes 98312 | tf_op jit(solution)/shard_map/ppermute | solution.py:370
  10.2 9.8 %collective-permute-start.6 = (f32[2,32,512]{2,1,0:T(8,128)S(1)}, f32[2,32,512]{2,1,0:T(8,128)S(1)}, u32[]{:S(2)}, u32[]{:S(2)}) collective-permute-start(f32[2,32,512]{2,1,0:T(8,128)S(1)} %get-tuple-element.74.refs_1_), channel_id=1, source_target_pairs={{0,1},{1,0},{2,3},{3,2},{4,5},{5,4},{6,7},{7,6},{8,9},{9,8},{10,11... | collective-permute-start | bytes 393224 | tf_op jit(solution)/shard_map/ppermute | solution.py:126
  13.5 6.5 %collective-permute-start.5 = (f32[256,128]{1,0:T(8,128)S(1)}, f32[256,128]{1,0:T(8,128)S(1)}, u32[]{:S(2)}, u32[]{:S(2)}) collective-permute-start(f32[256,128]{1,0:T(8,128)S(1)} %get-tuple-element.73.side_ref), channel_id=1, source_target_pairs={{0,8},{8,0},{1,9},{9,1},{2,10},{10,2},{3,11},{11,3},{4,12},{12,4},... | collective-permute-start | bytes 393224 | tf_op jit(solution)/shard_map/ppermute | solution.py:412
  16.2 3.7 %collective-permute-start.4 = (f32[64,128]{1,0:T(8,128)S(1)}, f32[64,128]{1,0:T(8,128)S(1)}, u32[]{:S(2)}, u32[]{:S(2)}) collective-permute-start(f32[64,128]{1,0:T(8,128)S(1)} %get-tuple-element.72.own_ref), channel_id=1, source_target_pairs={{0,4},{1,5},{2,6},{3,7},{4,0},{5,1},{6,2},{7,3},{8,12},{9,13},{10,... | collective-permute-start | bytes 98312 | tf_op jit(solution)/shard_map/ppermute | solution.py:370
  18.3 12.8 %collective-permute-start.8 = (f32[2,64,512]{2,1,0:T(8,128)S(1)}, f32[2,64,512]{2,1,0:T(8,128)S(1)}, u32[]{:S(2)}, u32[]{:S(2)}) collective-permute-start(f32[2,64,512]{2,1,0:T(8,128)S(1)} %get-tuple-element.78.refs_0_), channel_id=1, source_target_pairs={{0,1},{1,0},{2,3},{3,2},{4,5},{5,4},{6,7},{7,6},{8,9},{9,8},{10,11... | collective-permute-start | bytes 786440 | tf_op jit(solution)/shard_map/ppermute | solution.py:126
  20.5 10.6 %collective-permute-start.7 = (f32[4,32,512]{2,1,0:T(8,128)S(1)}, f32[4,32,512]{2,1,0:T(8,128)S(1)}, u32[]{:S(2)}, u32[]{:S(2)}) collective-permute-start(f32[4,32,512]{2,1,0:T(8,128)S(1)} %get-tuple-element.77.held_ref), channel_id=1, source_target_pairs={{0,2},{1,3},{2,0},{3,1},{4,6},{5,7},{6,4},{7,5},{8,10},{9,11},{10,... | collective-permute-start | bytes 786440 | tf_op jit(solution)/shard_map/ppermute | solution.py:126
  31.4 15.2 %collective-permute-start.11 = (f32[4,48,512]{2,1,0:T(8,128)S(1)}, f32[4,48,512]{2,1,0:T(8,128)S(1)}, u32[]{:S(2)}, u32[]{:S(2)}) collective-permute-start(f32[4,48,512]{2,1,0:T(8,128)S(1)} %get-tuple-element.83.held_ref), channel_id=1, source_target_pairs={{0,2},{1,3},{2,0},{3,1},{4,6},{5,7},{6,4},{7,5},{8,10},{9,11},{10,... | collective-permute-start | bytes 1179656 | tf_op jit(solution)/shard_map/ppermute | solution.py:126
  33.0 3.8 %collective-permute-start.9 = (f32[64,512]{1,0:T(8,128)S(1)}, f32[64,512]{1,0:T(8,128)S(1)}, u32[]{:S(2)}, u32[]{:S(2)}) collective-permute-start(f32[64,512]{1,0:T(8,128)S(1)} %get-tuple-element.79.mine_ref), channel_id=1, source_target_pairs={{0,8},{8,0},{1,9},{9,1},{2,10},{10,2},{3,11},{11,3},{4,12},{12,4},... | collective-permute-start | bytes 393224 | tf_op jit(solution)/shard_map/ppermute | solution.py:801
  35.6 1.2 %collective-permute-start.10 = (f32[16,128]{1,0:T(8,128)S(1)}, f32[16,128]{1,0:T(8,128)S(1)}, u32[]{:S(2)}, u32[]{:S(2)}) collective-permute-start(f32[16,128]{1,0:T(8,128)S(1)} %get-tuple-element.80), channel_id=1, source_target_pairs={{0,8},{8,0},{1,9},{9,1},{2,10},{10,2},{3,11},{11,3},{4,12},{12,4},... | collective-permute-start | bytes 24584 | tf_op jit(solution)/shard_map/ppermute | solution.py:790
  46.9 1.9 %collective-permute-start.12 = (f32[64,512]{1,0:T(8,128)S(1)}, f32[64,512]{1,0:T(8,128)S(1)}, u32[]{:S(2)}, u32[]{:S(2)}) collective-permute-start(f32[64,512]{1,0:T(8,128)S(1)} %shard_map.131.got_ref), channel_id=1, source_target_pairs={{0,8},{8,0},{1,9},{9,1},{2,10},{10,2},{3,11},{11,3},{4,12},{12,4},... | collective-permute-start | bytes 393224 | tf_op jit(solution)/shard_map/ppermute | solution.py:801
  59.5 1.8 %collective-permute-start.13 = (f32[72,256]{1,0:T(8,128)S(1)}, f32[72,256]{1,0:T(8,128)S(1)}, u32[]{:S(2)}, u32[]{:S(2)}) collective-permute-start(f32[72,256]{1,0:T(8,128)S(1)} %get-tuple-element.89), channel_id=1, source_target_pairs={{0,8},{8,0},{1,9},{9,1},{2,10},{10,2},{3,11},{11,3},{4,12},{12,4},... | collective-permute-start | bytes 221192 | tf_op jit(solution)/shard_map/ppermute | solution.py:884
  72.4 10.2 %collective-permute-start.14 = (f32[16,128]{1,0:T(8,128)S(1)}, f32[16,128]{1,0:T(8,128)S(1)}, u32[]{:S(2)}, u32[]{:S(2)}) collective-permute-start(f32[16,128]{1,0:T(8,128)S(1)} %get-tuple-element.108), channel_id=1, source_target_pairs={{0,1},{1,0},{2,3},{3,2},{4,5},{5,4},{6,7},{7,6},{8,9},{9,8},{10,11... | collective-permute-start | bytes 24584 | tf_op jit(solution)/shard_map/ppermute | solution.py:934
  73.6 9.1 %collective-permute-start.15 = (f32[16,128]{1,0:T(8,128)S(1)}, f32[16,128]{1,0:T(8,128)S(1)}, u32[]{:S(2)}, u32[]{:S(2)}) collective-permute-start(f32[16,128]{1,0:T(8,128)S(1)} %get-tuple-element.109), channel_id=1, source_target_pairs={{1,2},{3,4},{5,6},{2,1},{4,3},{6,5},{9,10},{11,12},{13,14},{10,9},... | collective-permute-start | bytes 24584 | tf_op jit(solution)/shard_map/ppermute | solution.py:935
  76.8 5.8 %collective-permute-start.16 = (f32[16,128]{1,0:T(8,128)S(1)}, f32[16,128]{1,0:T(8,128)S(1)}, u32[]{:S(2)}, u32[]{:S(2)}) collective-permute-start(f32[16,128]{1,0:T(8,128)S(1)} %get-tuple-element.110), channel_id=1, source_target_pairs={{0,8},{8,0},{16,24},{24,16},{1,9},{9,1},{17,25},{25,17},{2,10},{10... | collective-permute-start | bytes 24584 | tf_op jit(solution)/shard_map/ppermute | solution.py:936
  79.6 5.0 %collective-permute-start.17 = (f32[16,128]{1,0:T(8,128)S(1)}, f32[16,128]{1,0:T(8,128)S(1)}, u32[]{:S(2)}, u32[]{:S(2)}) collective-permute-start(f32[16,128]{1,0:T(8,128)S(1)} %get-tuple-element.111), channel_id=1, source_target_pairs={{8,16},{16,8},{9,17},{17,9},{10,18},{18,10},{11,19},{19,11},{12,20... | collective-permute-start | bytes 24584 | tf_op jit(solution)/shard_map/ppermute | solution.py:937
